TPU v7x, 32 devices: a whole 2x2x4 slice. The times are simulated.
32 devices in a mesh: pb: 8 (over z, y), ka: 4 (over x, core).
Axes of the slice: x: 2, y: 2, z: 4, core: 2. Of those that a mesh axis runs over, the one named last changes fastest.
Arguments:
- tokens: bfloat16 [16384, 768], P(('pb', 'ka')), may hold values from -6 to 6
- lengths: int32 [8, 2], P('pb'), may hold values from 0 to 2048, as said below
- block_place: int32 [8, 16], P('pb'), may hold values from 0 to 15, as said below
- qkv_weight: bfloat16 [768, 2304], P(('pb', 'ka')), may hold values from -0.21875 to 0.21875
- out_weight: bfloat16 [768, 768], P(('pb', 'ka')), may hold values from -2.5 to 2.5
- up_weight: bfloat16 [768, 3072], P(('pb', 'ka')), may hold values from -0.21875 to 0.21875
- down_weight: bfloat16 [3072, 768], P(('pb', 'ka')), may hold values from -0.109375 to 0.109375
- attn_gain: bfloat16 [768], P(('pb', 'ka')), may hold values from 0.5 to 1.5
- mlp_gain: bfloat16 [768], P(('pb', 'ka')), may hold values from 0.5 to 1.5
- cotangent: bfloat16 [16384, 768], P(('pb', 'ka')), may hold values from -6 to 6
Outputs:
- mixed: bfloat16 [16384, 768], P(('pb', 'ka'))
- tokens_grad: bfloat16 [16384, 768], P(('pb', 'ka'))
- grad_qkv: float32 [768, 2304], P(('pb', 'ka'))
- grad_out: float32 [768, 768], P(('pb', 'ka'))
- grad_up: float32 [768, 3072], P(('pb', 'ka'))
- grad_down: float32 [3072, 768], P(('pb', 'ka'))
- grad_attn_gain: float32 [768], P(('pb', 'ka'))
- grad_mlp_gain: float32 [768], P(('pb', 'ka'))
Inputs may be any that keep to these rules, and one draw needn't show every extreme that they name: Row g lists the lengths of the sequences of group g: the nonzero entries come first, are equal, each is 1024 times a power of two, and they sum to 2048; in every draw some group holds one sequence of 2048 tokens. `block_place`: row g is a permutation of 0 to 15. Entry k * 4 + t names the block of 128 positions held in slot t of the k-th device of ka. For each t, the blocks t * (4) up to t * 4 + 16 // 4 - 1 fill slot t of the devices of ka, one on each.
All inputs are finite; a program needn't handle non-finite values.
Results may differ from a plain program's by a relative error of at most 0.018.
Values may be sent and summed in bfloat16 or wider, within the bound.
No kernel may reach another device: no remote copies, remote signals or barrier semaphores. Data moves between devices by JAX's collectives and lax.ppermute only.
A program may use at most 192 MiB of HBM per device.

v0:
```python
import math

import jax
import jax.numpy as jnp
from jax import lax
from jax.sharding import PartitionSpec as P

HEADS = 12
HEAD_DIM = 64
BLK = 128
QBLK = 512


epsilon = 1e-05


def norm_rows(values, gain_vec):
    row_mean = jnp.mean(values, axis=-1, keepdims=True)
    centered = values - row_mean
    row_var = jnp.mean(centered * centered, axis=-1, keepdims=True)
    return centered * lax.rsqrt(row_var + epsilon) * gain_vec


def gelu_tanh(values):
    return jax.nn.gelu(values, approximate=True)


def row_layout(lengths_row, place_row):
    offsets = jnp.arange(BLK, dtype=jnp.int32)
    positions = (place_row[:, None] * BLK + offsets[None, :]).reshape(-1)
    doc_ends = jnp.cumsum(lengths_row)
    documents = jnp.sum((positions[:, None] >= doc_ends[None, :]).astype(jnp.int32), axis=1)
    return (positions, documents)


def to_rows(stacked):
    return jnp.transpose(stacked, (1, 0, 2)).reshape(stacked.shape[1], -1)


def body(
    tokens,
    lengths,
    block_place,
    qkv_weight,
    out_weight,
    up_weight,
    down_weight,
    attn_gain,
    mlp_gain,
    cotangent,
):
    score_scale = HEAD_DIM ** (-0.5)
    gathered = (
        lax.all_gather(qkv_weight, ("pb", "ka"), axis=0, tiled=True),
        lax.all_gather(out_weight, ("pb", "ka"), axis=0, tiled=True),
        lax.all_gather(up_weight, ("pb", "ka"), axis=0, tiled=True),
        lax.all_gather(down_weight, ("pb", "ka"), axis=0, tiled=True),
        lax.all_gather(attn_gain, ("pb", "ka"), axis=0, tiled=True),
        lax.all_gather(mlp_gain, ("pb", "ka"), axis=0, tiled=True),
    )
    full_qkv, full_out, full_up, full_down, full_gain_one, full_gain_two = gathered
    tok_rows = tokens.shape[0]
    model_width = tokens.shape[1]
    inputs = tokens.astype(jnp.float32)
    gain_one = full_gain_one.astype(jnp.float32)
    gain_two = full_gain_two.astype(jnp.float32)
    normed_one = norm_rows(inputs, gain_one).astype(jnp.bfloat16)
    projected = jnp.dot(normed_one, full_qkv, preferred_element_type=jnp.float32).astype(
        jnp.bfloat16
    )
    queries = projected[:, :model_width]
    keys_local = projected[:, model_width : 2 * model_width].reshape(tok_rows, HEADS, HEAD_DIM)
    values_local = projected[:, 2 * model_width :].reshape(tok_rows, HEADS, HEAD_DIM)
    all_queries = lax.all_gather(queries, "ka", axis=0, tiled=True)
    row_len = all_queries.shape[0]
    all_heads = all_queries.reshape(row_len, HEADS, HEAD_DIM)
    positions, documents = row_layout(lengths[0], block_place[0])
    key_start = lax.axis_index("ka") * tok_rows
    key_pos = lax.dynamic_slice_in_dim(positions, key_start, tok_rows, 0)
    key_doc = lax.dynamic_slice_in_dim(documents, key_start, tok_rows, 0)
    block_rows = math.gcd(QBLK, row_len)
    block_count = row_len // block_rows
    block_ids = jnp.arange(block_count, dtype=jnp.int32)

    def block_scores(begin, block_size):
        query_rows = lax.dynamic_slice_in_dim(all_heads, begin, block_size, 0)
        query_pos = lax.dynamic_slice_in_dim(positions, begin, block_size, 0)
        query_doc = lax.dynamic_slice_in_dim(documents, begin, block_size, 0)
        scores = (
            jnp.einsum("qhd,khd->hqk", query_rows, keys_local, preferred_element_type=jnp.float32)
            * score_scale
        )
        visible = (
            (query_doc[:, None] == key_doc[None, :]) & (key_pos[None, :] <= query_pos[:, None])
        )[None]
        magnitude = jnp.sqrt(scores * scores + 1.0)
        return (scores, magnitude, visible)

    def local_max(block_id):
        scores, magnitude, visible = block_scores(block_id * block_rows, block_rows)
        return jnp.max(jnp.where(visible, magnitude, 0.0), axis=-1)

    row_peak = lax.pmax(to_rows(lax.map(local_max, block_ids)).astype(jnp.bfloat16), "ka").astype(
        jnp.float32
    )

    def local_sum(block_id):
        begin = block_id * block_rows
        scores, magnitude, visible = block_scores(begin, block_rows)
        peak_rows = lax.dynamic_slice_in_dim(row_peak, begin, block_rows, 1)[:, :, None]
        return jnp.sum(jnp.where(visible, jnp.exp(magnitude - peak_rows), 0.0), axis=-1)

    row_total = lax.psum(to_rows(lax.map(local_sum, block_ids)).astype(jnp.bfloat16), "ka").astype(
        jnp.float32
    )
    block_size = math.gcd(QBLK, tok_rows * lax.axis_size("ka"))

    def one_block(block_id):
        begin = block_id * block_size
        scores, magnitude, visible = block_scores(begin, block_size)
        peak_rows = lax.dynamic_slice_in_dim(row_peak, begin, block_size, 1)[:, :, None]
        total_rows = lax.dynamic_slice_in_dim(row_total, begin, block_size, 1)[:, :, None]
        shares = jnp.where(visible, jnp.exp(magnitude - peak_rows) / total_rows, 0.0)
        mixing = (shares * scores / magnitude).astype(jnp.bfloat16)
        result = jnp.einsum(
            "hqk,khd->qhd", mixing, values_local, preferred_element_type=jnp.float32
        )
        return result.reshape(block_size, model_width)

    inner_ids = jnp.arange(tok_rows * lax.axis_size("ka") // block_size, dtype=jnp.int32)
    attended = lax.psum_scatter(
        lax.map(one_block, inner_ids)
        .reshape(tok_rows * lax.axis_size("ka"), model_width)
        .astype(jnp.bfloat16),
        "ka",
        scatter_dimension=0,
        tiled=True,
    ).astype(jnp.float32)
    attn_low = attended.astype(jnp.bfloat16)
    residual = inputs + jnp.dot(attn_low, full_out, preferred_element_type=jnp.float32)
    normed_two = norm_rows(residual, gain_two).astype(jnp.bfloat16)
    hidden_pre = jnp.dot(normed_two, full_up, preferred_element_type=jnp.float32)
    hidden_act, gelu_back = jax.vjp(gelu_tanh, hidden_pre)
    hidden_low = hidden_act.astype(jnp.bfloat16)
    layer_out = residual + jnp.dot(hidden_low, full_down, preferred_element_type=jnp.float32)
    regathered = (
        lax.all_gather(qkv_weight, ("pb", "ka"), axis=0, tiled=True),
        lax.all_gather(out_weight, ("pb", "ka"), axis=0, tiled=True),
        lax.all_gather(up_weight, ("pb", "ka"), axis=0, tiled=True),
        lax.all_gather(down_weight, ("pb", "ka"), axis=0, tiled=True),
    )
    back_qkv, back_out, back_up, back_down = regathered
    grad_down = jnp.einsum("tf,td->fd", hidden_low, cotangent, preferred_element_type=jnp.float32)
    grad_hidden = jnp.einsum("td,fd->tf", cotangent, back_down, preferred_element_type=jnp.float32)
    (grad_pre,) = gelu_back(grad_hidden)
    grad_pre_low = grad_pre.astype(jnp.bfloat16)
    grad_up = jnp.einsum("tw,tf->wf", normed_two, grad_pre_low, preferred_element_type=jnp.float32)
    grad_normed_two = jnp.einsum(
        "tf,wf->tw", grad_pre_low, back_up, preferred_element_type=jnp.float32
    )
    _, norm_back_two = jax.vjp(norm_rows, residual, gain_two)
    grad_res_norm, grad_gain_two = norm_back_two(grad_normed_two)
    grad_residual = cotangent.astype(jnp.float32) + grad_res_norm
    grad_res_low = grad_residual.astype(jnp.bfloat16)
    grad_out = jnp.einsum("tw,tv->wv", attn_low, grad_res_low, preferred_element_type=jnp.float32)
    grad_attended = jnp.einsum(
        "tv,wv->tw", grad_res_low, back_out, preferred_element_type=jnp.float32
    ).astype(jnp.bfloat16)
    own_delta = jnp.sum(
        grad_attended.astype(jnp.float32).reshape(tok_rows, HEADS, HEAD_DIM)
        * attended.reshape(tok_rows, HEADS, HEAD_DIM),
        axis=-1,
    ).T
    all_upstream = lax.all_gather(grad_attended, "ka", axis=0, tiled=True).reshape(
        row_len, HEADS, HEAD_DIM
    )
    delta_rows = lax.all_gather(own_delta, "ka", axis=1, tiled=True)

    def backward_block(running, block_id):
        grad_keys, grad_values = running
        begin = block_id * block_rows
        scores, magnitude, visible = block_scores(begin, block_rows)
        peak_rows = lax.dynamic_slice_in_dim(row_peak, begin, block_rows, 1)[:, :, None]
        total_rows = lax.dynamic_slice_in_dim(row_total, begin, block_rows, 1)[:, :, None]
        shares = jnp.where(visible, jnp.exp(magnitude - peak_rows) / total_rows, 0.0)
        smooth_sign = scores / magnitude
        upstream_rows = lax.dynamic_slice_in_dim(all_upstream, begin, block_rows, 0)
        effect = jnp.einsum(
            "qhd,khd->hqk", upstream_rows, values_local, preferred_element_type=jnp.float32
        )
        row_delta = lax.dynamic_slice_in_dim(delta_rows, begin, block_rows, 1)[:, :, None]
        grad_scores = shares * (
            (smooth_sign * effect - row_delta) * smooth_sign
            + effect / (magnitude * magnitude * magnitude)
        )
        grad_low = grad_scores.astype(jnp.bfloat16)
        mixing = (shares * smooth_sign).astype(jnp.bfloat16)
        query_rows = lax.dynamic_slice_in_dim(all_heads, begin, block_rows, 0)
        grad_query = (
            jnp.einsum("hqk,khd->qhd", grad_low, keys_local, preferred_element_type=jnp.float32)
            * score_scale
        )
        grad_keys = (
            grad_keys
            + jnp.einsum("hqk,qhd->khd", grad_low, query_rows, preferred_element_type=jnp.float32)
            * score_scale
        )
        grad_values = grad_values + jnp.einsum(
            "hqk,qhd->khd", mixing, upstream_rows, preferred_element_type=jnp.float32
        )
        return ((grad_keys, grad_values), grad_query.reshape(block_rows, model_width))

    zero_heads = jnp.zeros((tok_rows, HEADS, HEAD_DIM), jnp.float32)
    (grad_keys, grad_values), query_blocks = lax.scan(
        backward_block, (zero_heads, zero_heads), block_ids
    )
    grad_queries = lax.psum_scatter(
        query_blocks.reshape(row_len, model_width).astype(jnp.bfloat16),
        "ka",
        scatter_dimension=0,
        tiled=True,
    ).astype(jnp.float32)
    grad_act = jnp.concatenate(
        [
            grad_queries,
            grad_keys.reshape(tok_rows, model_width),
            grad_values.reshape(tok_rows, model_width),
        ],
        axis=1,
    ).astype(jnp.bfloat16)
    grad_qkv = jnp.einsum("tw,tv->wv", normed_one, grad_act, preferred_element_type=jnp.float32)
    grad_normed_one = jnp.einsum(
        "tv,wv->tw", grad_act, back_qkv, preferred_element_type=jnp.float32
    )
    _, norm_back_one = jax.vjp(norm_rows, inputs, gain_one)
    grad_in_norm, grad_gain_one = norm_back_one(grad_normed_one)
    tokens_grad = (grad_residual + grad_in_norm).astype(jnp.bfloat16)
    summed = (
        lax.psum_scatter(grad_qkv, ("pb", "ka"), scatter_dimension=0, tiled=True),
        lax.psum_scatter(grad_out, ("pb", "ka"), scatter_dimension=0, tiled=True),
        lax.psum_scatter(grad_up, ("pb", "ka"), scatter_dimension=0, tiled=True),
        lax.psum_scatter(grad_down, ("pb", "ka"), scatter_dimension=0, tiled=True),
        lax.psum_scatter(grad_gain_one, ("pb", "ka"), scatter_dimension=0, tiled=True),
        lax.psum_scatter(grad_gain_two, ("pb", "ka"), scatter_dimension=0, tiled=True),
    )
    return (
        layer_out.astype(jnp.bfloat16),
        tokens_grad,
        summed[0],
        summed[1],
        summed[2],
        summed[3],
        summed[4],
        summed[5],
    )


def solution(mesh):
    placed = (
        P(("pb", "ka"), None),
        P("pb", None),
        P("pb", None),
        P(("pb", "ka"), None),
        P(("pb", "ka"), None),
        P(("pb", "ka"), None),
        P(("pb", "ka"), None),
        P(("pb", "ka")),
        P(("pb", "ka")),
        P(("pb", "ka"), None),
    )
    return jax.shard_map(
        body,
        mesh=mesh,
        in_specs=placed,
        out_specs=(
            P(("pb", "ka"), None),
            P(("pb", "ka"), None),
            P(("pb", "ka"), None),
            P(("pb", "ka"), None),
            P(("pb", "ka"), None),
            P(("pb", "ka"), None),
            P(("pb", "ka")),
            P(("pb", "ka")),
        ),
        check_vma=False,
    )
```

profile of v0, /device:TPU:0, one launch (start us, length us, event | category | flops | bytes accessed | tf_op | source)
XLA Modules:
  0.0 1201.3 jit_solution(1671825578721346009)
XLA Ops:
  9.6 42.1 %all-reduce.5 = (bf16[768]{0:T(1024)(128)(2,1)S(1)}, bf16[768]{0:T(1024)(128)(2,1)}) all-reduce(bf16[768]{0:T(1024)(128)(2,1)S(1)} %dynamic-update-slice, bf16[768]{0:T(1024)(128)(2,1)S(1)} %dynamic-update-slice.1), channel_id=1, replica_groups=mesh['pb'=8,'ka'=4] {'pb','ka'}, use_global_device_ids=true, to_apply=%add | all-reduce | flops 1536 | bytes 6144
  55.1 18.6 %all-gather.7.cloned.1.call-done = bf16[768,2304]{1,0:T(8,128)(2,1)} async-done(((bf16[24,2304]{1,0:T(8,128)(2,1)}), bf16[768,2304]{1,0:T(8,128)(2,1)}) %all-gather.7.cloned.1.call-update) | async-done | bytes 3538960 | tf_op jit(solution)/shard_map/all_gather | solution.py:54
  73.8 4.4 convolution_convert_fusion
  84.7 22.0 %all-gather.9.cloned.1.call-done = bf16[2048,768]{1,0:T(8,128)(2,1)} async-done(((bf16[512,768]{1,0:T(8,128)(2,1)}), bf16[2048,768]{1,0:T(8,128)(2,1)}) %all-gather.9.cloned.1.call-update) | async-done | bytes 3145744 | tf_op jit(solution)/shard_map/all_gather | solution.py:74
  106.7 3.2 copy.65
  109.9 43.0 %while.45 = (s32[]{:T(128)}, bf16[4,12,512]{2,1,0:T(8,128)(2,1)S(1)}, s32[4]{0:T(128)S(1)}, s32[2048]{0:T(1024)}, s32[512]{0:T(512)S(1)}, /*index=5*/s32[512]{0:...) while((s32[]{:T(128)}, ...), condition=%wide.region_6.7_spmd, body=%wide.region_4.6_spmd.sunk | while | flops 419162112 | bytes 2158799 | solution.py:103
  112.3 8.3 select_reduce_fusion.4
  123.0 8.4 select_reduce_fusion.4
  133.8 8.3 select_reduce_fusion.4
  144.5 8.4 select_reduce_fusion.4
  153.0 12.9 %pmax.7 = bf16[12,2048]{1,0:T(8,128)(2,1)S(1)} all-reduce(bf16[12,2048]{1,0:T(8,128)(2,1)S(1)} %bitcast.125), channel_id=1, replica_groups=mesh['pb'=8,'ka'=4] {'ka'}, use_global_device_ids=true, to_apply=%region_7.8 | all-reduce | flops 24576 | bytes 98304 | tf_op jit(solution)/shard_map/pmax | solution.py:103
  166.0 47.5 %while.46 = (s32[]{:T(128)}, bf16[4,12,512]{2,1,0:T(8,128)(2,1)S(1)}, s32[4]{0:T(128)S(1)}, s32[2048]{0:T(1024)}, s32[512]{0:T(512)S(1)}, /*index=5*/s32[512]{0:...) while((s32[]{:T(128)}, ...), condition=%wide.region_10.11_spmd, body=%wide.region_8.10_spmd.sunk | while | flops 422307840 | bytes 2240731 | solution.py:113
  168.4 9.5 select_reduce_fusion.5
  180.3 9.5 select_reduce_fusion.5
  192.1 9.5 select_reduce_fusion.5
  204.0 9.5 select_reduce_fusion.5
  213.6 12.0 %psum.7 = bf16[12,2048]{1,0:T(8,128)(2,1)S(1)} all-reduce(bf16[12,2048]{1,0:T(8,128)(2,1)S(1)} %bitcast.126), channel_id=1, replica_groups=mesh['pb'=8,'ka'=4] {'ka'}, use_global_device_ids=true, to_apply=%region_11.12 | all-reduce | flops 24576 | bytes 98304 | tf_op jit(solution)/shard_map/psum | solution.py:113
  226.8 91.7 %while.47 = (s32[]{:T(128)}, bf16[4,512,768]{1,2,0:T(8,128)(2,1)}, s32[4]{0:T(128)}, s32[2048]{0:T(1024)}, s32[512]{0:T(512)S(1)}, /*index=5*/s32[512]{0:T(512)S...) while((s32[]{:T(128)}, bf16[4,512,768]{1,2,0:T(8,128)(2,1)}, ...), condition=%wide.region_13.14_spmd, body=%wide.region_12.13_spmd.sunk | while | flops 834404352 | bytes 5406955 | solution.py:132
  231.2 14.5 %fusion.119 = bf16[12,512,64]{1,2,0:T(8,128)(2,1)} fusion(bf16[512,12,64]{0,2,1:T(8,128)(2,1)} %get-tuple-element.895, f32[12,512]{1,0:T(8,128)} %get-tuple-element.751, f32[12,512]{1,0:T(8,128)} %get-tuple-element.752, pred[512,512]{1,0:T(8,128)(4,1)S(1)} %compare_and_fusion.10, bf16[512,12,64]{0,2,1:T(8,128)(2,1)} %get-tuple-element.892, ...), kind=kOutput, calls=%fused_computation.12.clone.1 | convolution fusion | flops 833617920 | bytes 3457028 | tf_op jit(solution)/shard_map/while/body/eval_jaxpr/hqk,khd->qhd/dot_general | solution.py:125
  252.2 14.5 %fusion.119 = bf16[12,512,64]{1,2,0:T(8,128)(2,1)} fusion(bf16[512,12,64]{0,2,1:T(8,128)(2,1)} %get-tuple-element.895, f32[12,512]{1,0:T(8,128)} %get-tuple-element.751, f32[12,512]{1,0:T(8,128)} %get-tuple-element.752, pred[512,512]{1,0:T(8,128)(4,1)S(1)} %compare_and_fusion.10, bf16[512,12,64]{0,2,1:T(8,128)(2,1)} %get-tuple-element.892, ...), kind=kOutput, calls=%fused_computation.12.clone.1 | convolution fusion | flops 833617920 | bytes 3457028 | tf_op jit(solution)/shard_map/while/body/eval_jaxpr/hqk,khd->qhd/dot_general | solution.py:125
  273.2 14.5 %fusion.119 = bf16[12,512,64]{1,2,0:T(8,128)(2,1)} fusion(bf16[512,12,64]{0,2,1:T(8,128)(2,1)} %get-tuple-element.895, f32[12,512]{1,0:T(8,128)} %get-tuple-element.751, f32[12,512]{1,0:T(8,128)} %get-tuple-element.752, pred[512,512]{1,0:T(8,128)(4,1)S(1)} %compare_and_fusion.10, bf16[512,12,64]{0,2,1:T(8,128)(2,1)} %get-tuple-element.892, ...), kind=kOutput, calls=%fused_computation.12.clone.1 | convolution fusion | flops 833617920 | bytes 3457028 | tf_op jit(solution)/shard_map/while/body/eval_jaxpr/hqk,khd->qhd/dot_general | solution.py:125
  294.2 14.5 %fusion.119 = bf16[12,512,64]{1,2,0:T(8,128)(2,1)} fusion(bf16[512,12,64]{0,2,1:T(8,128)(2,1)} %get-tuple-element.895, f32[12,512]{1,0:T(8,128)} %get-tuple-element.751, f32[12,512]{1,0:T(8,128)} %get-tuple-element.752, pred[512,512]{1,0:T(8,128)(4,1)S(1)} %compare_and_fusion.10, bf16[512,12,64]{0,2,1:T(8,128)(2,1)} %get-tuple-element.892, ...), kind=kOutput, calls=%fused_computation.12.clone.1 | convolution fusion | flops 833617920 | bytes 3457028 | tf_op jit(solution)/shard_map/while/body/eval_jaxpr/hqk,khd->qhd/dot_general | solution.py:125
  318.5 5.4 copy.70
  325.1 6.9 fusion.66
  332.0 30.8 %reduce-scatter.7.cloned.1.call-done = bf16[512,768]{1,0:T(8,128)(2,1)} async-done(((bf16[2048,768]{1,0:T(8,128)(2,1)}), bf16[512,768]{1,0:T(8,128)(2,1)}) %reduce-scatter.7.cloned.1.call-update) | async-done | bytes 786448 | tf_op jit(solution)/shard_map/reduce_scatter | solution.py:131
  362.9 2.4 fusion.65
  365.6 64.1 %all-gather.13.cloned.1.call-done = bf16[768,3072]{1,0:T(8,128)(2,1)} async-done(((bf16[24,3072]{1,0:T(8,128)(2,1)}), bf16[768,3072]{1,0:T(8,128)(2,1)}) %all-gather.13.cloned.1.call-update) | async-done | bytes 4718608 | tf_op jit(solution)/shard_map/all_gather | solution.py:56
  429.7 12.5 %fusion.38 = (bf16[512,3072]{1,0:T(8,128)(2,1)S(1)}, f32[512,3072]{1,0:T(8,128)}) fusion(f32[512,3072]{1,0:T(8,128)} %fusion.66, bf16[768,3072]{1,0:T(8,128)(2,1)} %all-gather.13.cloned.1.call-done, f32[512,768]{1,0:T(8,128)S(1)} %get-tuple-element.469, f32[768]{0:T(1024)S(1)} %convert_element_type.111, f32[512]{0:T(512)S(1)} %fusion.54, ...), kind=kOutput, calls=%fused_computation.61 | convolution fusion | flops 2448949248 | bytes 22027264 | tf_op jit(solution)/shard_map/dot_general | solution.py:142
  442.2 3.4 multiply_reduce_fusion
  452.2 5.4 all_gather.39
  457.6 19.9 %all-gather.17.cloned.1.call-done = bf16[2048,768]{1,0:T(8,128)(2,1)} async-done(((bf16[512,768]{1,0:T(8,128)(2,1)}), bf16[2048,768]{1,0:T(8,128)(2,1)}) %all-gather.17.cloned.1.call-update) | async-done | bytes 3145744 | tf_op jit(solution)/shard_map/all_gather | solution.py:174
  477.5 4.7 copy.71
  482.2 160.9 %while.48 = (s32[]{:T(128)}, f32[512,12,64]{0,2,1:T(8,128)S(1)}, f32[512,12,64]{0,2,1:T(8,128)}, bf16[4,512,768]{2,1,0:T(8,128)(2,1)}, s32[4]{0:T(128)S(1)}, /*i...) while((s32[]{:T(128)}, f32[512,12,64]{0,2,1:T(8,128)S(1)}, ...), condition=%wide.region_21.22_spmd.clone, body=%wide.region_20.21_spmd.clone.sunk | while | flops 2095448064 | bytes 98632056 | solution.py:214
  485.7 3.1 fusion.129
  488.9 10.4 bitcast_add_fusion.5
  499.3 15.8 %fusion.130 = bf16[12,512,512]{2,1,0:T(8,128)(2,1)S(1)} fusion(f32[12,512,512]{2,1,0:T(8,128)S(1)} %fusion.129, f32[12,512]{1,0:T(8,128)S(1)} %get-tuple-element.769, f32[12,512]{1,0:T(8,128)S(1)} %get-tuple-element.770, f32[12,512]{1,0:T(8,128)S(1)} %constant_dynamic-slice_fusion.13, pred[512,512]{1,0:T(8,128)(4,1)S(1)} %compare_and_fusion.11, ...), kind=kOutput, calls=%fused_computation.31.clone.1 | convolution fusion | flops 452984832 | bytes 20807684 | tf_op jit(solution)/shard_map/while/body/eval_jaxpr/qhd,khd->hqk/dot_general | solution.py:188
  515.1 2.9 convolution_multiply_fusion.2
  518.0 2.3 bitcast_add_fusion.4
  525.8 3.1 fusion.129
  529.0 10.4 bitcast_add_fusion.5
  539.4 15.8 %fusion.130 = bf16[12,512,512]{2,1,0:T(8,128)(2,1)S(1)} fusion(f32[12,512,512]{2,1,0:T(8,128)S(1)} %fusion.129, f32[12,512]{1,0:T(8,128)S(1)} %get-tuple-element.769, f32[12,512]{1,0:T(8,128)S(1)} %get-tuple-element.770, f32[12,512]{1,0:T(8,128)S(1)} %constant_dynamic-slice_fusion.13, pred[512,512]{1,0:T(8,128)(4,1)S(1)} %compare_and_fusion.11, ...), kind=kOutput, calls=%fused_computation.31.clone.1 | convolution fusion | flops 452984832 | bytes 20807684 | tf_op jit(solution)/shard_map/while/body/eval_jaxpr/qhd,khd->hqk/dot_general | solution.py:188
  555.2 2.9 convolution_multiply_fusion.2
  558.1 2.3 bitcast_add_fusion.4
  565.9 3.1 fusion.129
  569.1 10.4 bitcast_add_fusion.5
  579.5 15.8 %fusion.130 = bf16[12,512,512]{2,1,0:T(8,128)(2,1)S(1)} fusion(f32[12,512,512]{2,1,0:T(8,128)S(1)} %fusion.129, f32[12,512]{1,0:T(8,128)S(1)} %get-tuple-element.769, f32[12,512]{1,0:T(8,128)S(1)} %get-tuple-element.770, f32[12,512]{1,0:T(8,128)S(1)} %constant_dynamic-slice_fusion.13, pred[512,512]{1,0:T(8,128)(4,1)S(1)} %compare_and_fusion.11, ...), kind=kOutput, calls=%fused_computation.31.clone.1 | convolution fusion | flops 452984832 | bytes 20807684 | tf_op jit(solution)/shard_map/while/body/eval_jaxpr/qhd,khd->hqk/dot_general | solution.py:188
  595.3 2.9 convolution_multiply_fusion.2
  598.2 2.3 bitcast_add_fusion.4
  606.0 3.1 fusion.129
  609.1 10.4 bitcast_add_fusion.5
  619.6 15.8 %fusion.130 = bf16[12,512,512]{2,1,0:T(8,128)(2,1)S(1)} fusion(f32[12,512,512]{2,1,0:T(8,128)S(1)} %fusion.129, f32[12,512]{1,0:T(8,128)S(1)} %get-tuple-element.769, f32[12,512]{1,0:T(8,128)S(1)} %get-tuple-element.770, f32[12,512]{1,0:T(8,128)S(1)} %constant_dynamic-slice_fusion.13, pred[512,512]{1,0:T(8,128)(4,1)S(1)} %compare_and_fusion.11, ...), kind=kOutput, calls=%fused_computation.31.clone.1 | convolution fusion | flops 452984832 | bytes 20807684 | tf_op jit(solution)/shard_map/while/body/eval_jaxpr/qhd,khd->hqk/dot_general | solution.py:188
  635.4 2.9 convolution_multiply_fusion.2
  646.7 10.3 fusion.62
  658.4 7.2 fusion.60
  666.7 2.4 copy.74
  671.7 9.5 reduce-scatter.9.cloned.1.call-done
  681.2 6.7 fusion.50
  688.0 8.9 add_convert_fusion.1
  701.1 39.5 %all-reduce.4 = (f32[768]{0:T(1024)S(1)}, f32[768]{0:T(1024)S(1)}) all-reduce(f32[768]{0:T(1024)S(1)} %get-tuple-element.359, f32[768]{0:T(1024)S(1)} %copy-done.39), channel_id=8, replica_groups=mesh['pb'=8,'ka'=4] {'pb','ka'}, use_global_device_ids=true, to_apply=%region_30.31.clone | all-reduce | flops 1536 | bytes 12288
  741.8 3.0 add_convert_fusion
  744.8 41.7 %reduce-scatter.13.cloned.1.call-done = f32[24,768]{1,0:T(8,128)} async-done(((f32[768,768]{1,0:T(8,128)}), f32[24,768]{1,0:T(8,128)}) %reduce-scatter.13.cloned.1.call-update) | async-done | bytes 73744 | tf_op jit(solution)/shard_map/reduce_scatter | solution.py:240
  786.4 141.7 %reduce-scatter.17.cloned.1.call-done = f32[96,768]{1,0:T(8,128)} async-done(((f32[3072,768]{1,0:T(8,128)}), f32[96,768]{1,0:T(8,128)}) %reduce-scatter.17.cloned.1.call-update) | async-done | bytes 294928 | tf_op jit(solution)/shard_map/reduce_scatter | solution.py:242
  928.1 141.3 %reduce-scatter.15.cloned.1.call-done = f32[24,3072]{1,0:T(8,128)} async-done(((f32[768,3072]{1,0:T(8,128)}), f32[24,3072]{1,0:T(8,128)}) %reduce-scatter.15.cloned.1.call-update) | async-done | bytes 294928 | tf_op jit(solution)/shard_map/reduce_scatter | solution.py:241
  1069.4 124.9 %reduce-scatter.11.cloned.1.call-done = f32[24,2304]{1,0:T(8,128)} async-done(((f32[768,2304]{1,0:T(8,128)}), f32[24,2304]{1,0:T(8,128)}) %reduce-scatter.11.cloned.1.call-update) | async-done | bytes 221200 | tf_op jit(solution)/shard_map/reduce_scatter | solution.py:239
  (294 shorter events, 94.1 us)
Async XLA Ops:
  7.2 66.6 %all-gather.7.cloned.1.call-start = ((), (), s32[]{:S(2)}) async-start(), calls=%async_computation.6 | async-start | bytes 3649536 | tf_op jit(solution)/shard_map/all_gather | solution.py:54
  7.9 98.8 %all-gather.9.cloned.1.call-start = ((), (), s32[]{:S(2)}) async-start(), calls=%async_computation.7 | async-start | bytes 3932160 | tf_op jit(solution)/shard_map/all_gather | solution.py:74
  51.7 22.0 %copy-start.29 = (f32[768]{0:T(1024)}, f32[768]{0:T(1024)S(1)}, u32[]{:S(2)}) copy-start(f32[768]{0:T(1024)S(1)} %convert_element_type.98) | copy-start | bytes 9220
  53.1 20.7 %copy-start.31 = (f32[512]{0:T(512)}, f32[512]{0:T(512)S(1)}, u32[]{:S(2)}) copy-start(f32[512]{0:T(512)S(1)} %broadcast_multiply_fusion.1) | copy-start | bytes 6148
  55.1 18.6 %copy-start.33 = (f32[512]{0:T(512)}, f32[512]{0:T(512)S(1)}, u32[]{:S(2)}) copy-start(f32[512]{0:T(512)S(1)} %fusion.53) | copy-start | bytes 6148
  78.1 2.5 copy-start.44
  78.2 2.6 copy-start.45
  79.2 245.5 %all-gather.15.cloned.1.call-start = ((), (), s32[]{:S(2)}) async-start(), calls=%async_computation.11 | async-start | bytes 4866048 | tf_op jit(solution)/shard_map/all_gather | solution.py:57
  80.0 252.1 %all-gather.11.cloned.1.call-start = ((), (), s32[]{:S(2)}) async-start(), calls=%async_computation.9 | async-start | bytes 1216512 | tf_op jit(solution)/shard_map/all_gather | solution.py:55
  80.5 282.3 %reduce-scatter.7.cloned.1.call-start = ((), (), s32[]{:S(2)}) async-start(), calls=%async_computation.8 | async-start | bytes 3932160 | tf_op jit(solution)/shard_map/reduce_scatter | solution.py:131
  318.5 5.5 copy-start
  324.0 1.1 copy-start.15
  324.0 105.7 %all-gather.13.cloned.1.call-start = ((), (), s32[]{:S(2)}) async-start(), calls=%async_computation.10 | async-start | bytes 4866048 | tf_op jit(solution)/shard_map/all_gather | solution.py:56
  324.6 152.9 %all-gather.17.cloned.1.call-start = ((), (), s32[]{:S(2)}) async-start(), calls=%async_computation.12 | async-start | bytes 3932160 | tf_op jit(solution)/shard_map/all_gather | solution.py:174
  324.7 121.0 %copy-start.23 = (f32[768]{0:T(1024)}, f32[768]{0:T(1024)S(1)}, u32[]{:S(2)}) copy-start(f32[768]{0:T(1024)S(1)} %convert_element_type.111) | copy-start | bytes 9220
  324.7 38.2 %copy-start.6 = (bf16[512,768]{1,0:T(8,128)(2,1)S(1)}, bf16[512,768]{1,0:T(8,128)(2,1)}, u32[]{:S(2)}) copy-start(bf16[512,768]{1,0:T(8,128)(2,1)} %param.18) | copy-start | bytes 2359300
  365.3 80.4 %copy-start.4 = (f32[512,768]{1,0:T(8,128)}, f32[512,768]{1,0:T(8,128)S(1)}, u32[]{:S(2)}) copy-start(f32[512,768]{1,0:T(8,128)S(1)} %get-tuple-element.469) | copy-start | bytes 4718596
  365.3 80.4 %copy-start.25 = (f32[512]{0:T(512)}, f32[512]{0:T(512)S(1)}, u32[]{:S(2)}) copy-start(f32[512]{0:T(512)S(1)} %broadcast_multiply_fusion) | copy-start | bytes 6148
  365.6 80.0 %copy-start.27 = (f32[512]{0:T(512)}, f32[512]{0:T(512)S(1)}, u32[]{:S(2)}) copy-start(f32[512]{0:T(512)S(1)} %fusion.54) | copy-start | bytes 6148
  429.7 12.5 %copy-start.41 = (bf16[768,3072]{1,0:T(8,128)(2,1)S(1)}, bf16[768,3072]{1,0:T(8,128)(2,1)}, u32[]{:S(2)}) copy-start(bf16[768,3072]{1,0:T(8,128)(2,1)} %all-gather.13.cloned.1.call-done) | copy-start | bytes 14155780
  442.2 3.4 copy-start.17
  445.7 2.1 copy-start.12
  445.7 2.1 copy-start.20
  446.3 3.7 copy-start.2
  446.3 3.7 copy-start.37
  450.0 231.2 %reduce-scatter.9.cloned.1.call-start = ((), (), s32[]{:S(2)}) async-start(), calls=%async_computation.13 | async-start | bytes 3932160 | tf_op jit(solution)/shard_map/reduce_scatter | solution.py:217
  457.6 24.6 %copy-start.1 = (bf16[512,12,64]{0,2,1:T(8,128)(2,1)S(1)}, bf16[512,12,64]{0,2,1:T(8,128)(2,1)}, u32[]{:S(2)}) copy-start(bf16[512,12,64]{0,2,1:T(8,128)(2,1)} %get-tuple-element.979) | copy-start | bytes 2359300
  485.7 3.1 copy-start.14
  485.7 3.1 copy-start.18
  499.3 15.8 %copy-start.19 = (f32[512,12,64]{0,2,1:T(8,128)}, f32[512,12,64]{0,2,1:T(8,128)S(1)}, u32[]{:S(2)}) copy-start(f32[512,12,64]{0,2,1:T(8,128)S(1)} %bitcast_add_fusion.5) | copy-start | bytes 4718596 | tf_op jit(solution)/shard_map/while
  525.8 3.1 copy-start.14
  525.8 3.1 copy-start.18
  539.4 15.8 %copy-start.19 = (f32[512,12,64]{0,2,1:T(8,128)}, f32[512,12,64]{0,2,1:T(8,128)S(1)}, u32[]{:S(2)}) copy-start(f32[512,12,64]{0,2,1:T(8,128)S(1)} %bitcast_add_fusion.5) | copy-start | bytes 4718596 | tf_op jit(solution)/shard_map/while
  565.9 3.1 copy-start.14
  565.9 3.1 copy-start.18
  579.5 15.8 %copy-start.19 = (f32[512,12,64]{0,2,1:T(8,128)}, f32[512,12,64]{0,2,1:T(8,128)S(1)}, u32[]{:S(2)}) copy-start(f32[512,12,64]{0,2,1:T(8,128)S(1)} %bitcast_add_fusion.5) | copy-start | bytes 4718596 | tf_op jit(solution)/shard_map/while
  606.0 3.1 copy-start.14
  606.0 3.1 copy-start.18
  619.6 15.8 %copy-start.19 = (f32[512,12,64]{0,2,1:T(8,128)}, f32[512,12,64]{0,2,1:T(8,128)S(1)}, u32[]{:S(2)}) copy-start(f32[512,12,64]{0,2,1:T(8,128)S(1)} %bitcast_add_fusion.5) | copy-start | bytes 4718596 | tf_op jit(solution)/shard_map/while
  643.1 1.1 copy-start.10
  643.1 1.4 copy-start.13
  643.1 143.3 %reduce-scatter.13.cloned.1.call-start = ((), (), s32[]{:S(2)}) async-start(), calls=%async_computation.15 | async-start | bytes 2433024 | tf_op jit(solution)/shard_map/reduce_scatter | solution.py:240
  646.7 281.5 %reduce-scatter.17.cloned.1.call-start = ((), (), s32[]{:S(2)}) async-start(), calls=%async_computation.17 | async-start | bytes 9732096 | tf_op jit(solution)/shard_map/reduce_scatter | solution.py:242
  657.0 1.4 copy-start.5
  657.0 1.4 copy-start.24
  657.0 1.4 copy-start.26
  657.0 1.4 copy-start.28
  657.1 412.3 %reduce-scatter.15.cloned.1.call-start = ((), (), s32[]{:S(2)}) async-start(), calls=%async_computation.16 | async-start | bytes 9732096 | tf_op jit(solution)/shard_map/reduce_scatter | solution.py:241
  665.7 528.6 %reduce-scatter.11.cloned.1.call-start = ((), (), s32[]{:S(2)}) async-start(), calls=%async_computation.14 | async-start | bytes 7299072 | tf_op jit(solution)/shard_map/reduce_scatter | solution.py:239
  666.7 14.6 %copy-start.7 = (bf16[512,768]{1,0:T(8,128)(2,1)S(1)}, bf16[512,768]{1,0:T(8,128)(2,1)}, u32[]{:S(2)}) copy-start(bf16[512,768]{1,0:T(8,128)(2,1)} %param.18) | copy-start | bytes 2359300
  666.7 14.6 %copy-start.30 = (f32[768]{0:T(1024)S(1)}, f32[768]{0:T(1024)}, u32[]{:S(2)}) copy-start(f32[768]{0:T(1024)} %copy-done.29) | copy-start | bytes 9220
  666.7 14.6 %copy-start.32 = (f32[512]{0:T(512)S(1)}, f32[512]{0:T(512)}, u32[]{:S(2)}) copy-start(f32[512]{0:T(512)} %copy-done.31) | copy-start | bytes 6148
  666.7 14.6 %copy-start.34 = (f32[512]{0:T(512)S(1)}, f32[512]{0:T(512)}, u32[]{:S(2)}) copy-start(f32[512]{0:T(512)} %copy-done.33) | copy-start | bytes 6148
  688.0 9.0 copy-start.21
  688.0 8.9 copy-start.22
  688.0 8.9 copy-start.42
  688.0 8.9 copy-start.43
  696.9 2.2 copy-start.36
  697.0 3.3 copy-start.8
  697.0 4.1 copy-start.39
  697.0 44.8 %copy-start.16 = (bf16[512,768]{1,0:T(8,128)(2,1)S(1)}, bf16[512,768]{1,0:T(8,128)(2,1)}, u32[]{:S(2)}) copy-start(bf16[512,768]{1,0:T(8,128)(2,1)} %param.27) | copy-start | bytes 2359300
  697.0 44.8 %copy-start.38 = (f32[512]{0:T(512)S(1)}, f32[512]{0:T(512)}, u32[]{:S(2)}) copy-start(f32[512]{0:T(512)} %copy-done.37) | copy-start | bytes 6148
  699.1 1.2 copy-start.11
  699.1 42.6 %copy-start.3 = (f32[512,768]{1,0:T(8,128)S(1)}, f32[512,768]{1,0:T(8,128)}, u32[]{:S(2)}) copy-start(f32[512,768]{1,0:T(8,128)} %copy-done.2) | copy-start | bytes 4718596
  (3 other events, 2.4 us)
Sparse Core Ops, SparseCore 0:
  10.9 62.8 all-gather.6
  79.3 27.3 all-gather.8
  109.6 64.4 all-gather.14
  176.9 52.8 all-gather.10
  324.1 38.7 reduce-scatter.6
  366.1 63.6 all-gather.12
  450.1 27.3 all-gather.16
  643.3 37.9 reduce-scatter.8
  687.1 99.2 reduce-scatter.12
  793.8 134.3 reduce-scatter.16
  934.6 134.7 reduce-scatter.14
  1076.5 117.7 reduce-scatter.10
where the time goes:
time: 1210 us; the launch traced here: 1200 us
  waiting for transfers between devices  617 us (51%)
  matrix products  337 us (28%)
  blocking collectives  112 us (9%)
  local copies, waits for them, and re-layouts  84.2 us (7%)
  loops' own time  19.4 us (2%)
  other arithmetic  16.6 us (1%)
  between operations  15 us (1%)
    reduce_scatter x1, waiting for transfers between devices, body(): lax.psum_scatter(grad_down, ('pb', 'ka'), scatter_dimension=0, tiled=True)  142 us
    reduce_scatter x1, waiting for transfers between devices, body(): lax.psum_scatter(grad_up, ('pb', 'ka'), scatter_dimension=0, tiled=True)  141 us
    reduce_scatter x1, waiting for transfers between devices, body(): lax.psum_scatter(grad_qkv, ('pb', 'ka'), scatter_dimension=0, tiled=True)  125 us
    dot_general x12, matrix products, block_scores(): jnp.einsum('qhd,khd->hqk', query_rows, keys_local, preferred_element_type...  83.8 us
    unnamed x2, blocking collectives  81.6 us
    all_gather x1, waiting for transfers between devices, body(): lax.all_gather(up_weight, ('pb', 'ka'), axis=0, tiled=True)  64.1 us
    dot_general x4, matrix products, backward_block(): jnp.einsum('qhd,khd->hqk', upstream_rows, values_local, preferred_element...  63.3 us
    dot_general x4, matrix products, one_block(): jnp.einsum('hqk,khd->qhd', mixing, values_local, preferred_element_type=j...  58.1 us
  transfers between devices with their start and end apart: 12, of which 10 were waited for; matrix products, arithmetic and copies ran while one was open for 20% of the time, Pallas kernels for 0%

commit v1 on v0

v1 whole, which is shorter than its diff:
```python
import functools
import math

import jax
import jax.numpy as jnp
from jax import lax
from jax.experimental import pallas as pl
from jax.experimental.pallas import tpu as pltpu
from jax.sharding import PartitionSpec as P

HEADS = 12
HEAD_DIM = 64
BLK = 128
TILE = 256
epsilon = 1e-05
f32 = jnp.float32
bf16 = jnp.bfloat16


class Grid:
    def __init__(self, nb, nk):
        nhi = math.gcd(4, nb)
        nc = math.gcd(2, nk)
        self.sizes = {"hi": nhi, "lo": nb // nhi, "x": nk // nc, "c": nc}
        self.nb, self.nk = nb, nk
        pb, ka = lax.axis_index("pb"), lax.axis_index("ka")
        self.pb, self.ka = pb, ka
        self.at = {"hi": pb // self.sizes["lo"], "lo": pb % self.sizes["lo"], "x": ka // nc, "c": ka % nc}

    def fetch(self, value, **steps):
        n = self.sizes
        pairs = []
        for hi in range(n["hi"]):
            for lo in range(n["lo"]):
                for x in range(n["x"]):
                    for c in range(n["c"]):
                        here = {"hi": hi, "lo": lo, "x": x, "c": c}
                        there = {d: (here[d] + steps.get(d, 0)) % n[d] for d in here}
                        flat = [((p["hi"] * n["lo"] + p["lo"]) * n["x"] + p["x"]) * n["c"] + p["c"] for p in (there, here)]
                        pairs.append(tuple(flat))
        return lax.ppermute(value, ("pb", "ka"), pairs)

    def gather(self, value, dim):
        return jnp.stack([value] + [self.fetch(value, **{dim: r}) for r in range(1, self.sizes[dim])])

    def rolled(self, stacked, axis, dim):
        n = self.sizes[dim]
        if n == 1:
            return stacked
        twice = jnp.concatenate([stacked, lax.slice_in_dim(stacked, 0, n - 1, axis=axis)], axis=axis)
        return lax.dynamic_slice_in_dim(twice, (n - self.at[dim]) % n, n, axis=axis)

    def reduce(self, parts, axis, dim, last=False):
        n, me = self.sizes[dim], self.at[dim]
        total = lax.dynamic_index_in_dim(parts, me, axis, keepdims=False).astype(f32)
        for r in range(1, n):
            sent = lax.dynamic_index_in_dim(parts, (me - r) % n, axis, keepdims=False)
            total = total + self.fetch(sent, **{dim: r}).astype(f32)
        return total if last else total.astype(parts.dtype)


def place_kernel(counts, rows, offs_ref, *refs):
    ins, out_ref, sems = refs[: len(counts)], refs[len(counts)], refs[len(counts) + 1]
    copies = []
    for ref, count in zip(ins, counts):
        for i in range(count):
            at = pl.multiple_of(offs_ref[len(copies)], rows)
            copies.append(pltpu.make_async_copy(ref.at[i], out_ref.at[pl.ds(at, rows), :], sems.at[len(copies)]))
    for copy in copies:
        copy.start()
    for copy in copies:
        copy.wait()


def place(stacks, offsets):
    rows, cols = stacks[0].shape[1:]
    counts = [s.shape[0] for s in stacks]
    total = sum(counts)
    return pl.pallas_call(
        functools.partial(place_kernel, counts, rows),
        out_shape=jax.ShapeDtypeStruct((total * rows, cols), stacks[0].dtype),
        in_specs=[pl.BlockSpec(memory_space=pltpu.SMEM)] + [pl.BlockSpec(memory_space=pl.ANY)] * len(stacks),
        out_specs=pl.BlockSpec(memory_space=pl.ANY),
        scratch_shapes=[pltpu.SemaphoreType.DMA((total,))],
        cost_estimate=pl.CostEstimate(flops=0, bytes_accessed=4 * total * rows * cols, transcendentals=0),
    )(offsets.astype(jnp.int32), *stacks)


def gather_rows(grid, piece, order):
    stack = piece[None]
    steps = [dict()]
    stacks = []
    for dim in order:
        got = [grid.fetch(stack, **{dim: r}) for r in range(1, grid.sizes[dim])]
        steps = steps + [{**s, dim: r} for r in range(1, grid.sizes[dim]) for s in steps]
        if dim == order[-1]:
            stacks = [stack] + got
        else:
            stack = jnp.concatenate([stack] + got, axis=0)
    dims = [d for d in ("hi", "lo", "x") if d in order]
    rows = piece.shape[0]
    index = []
    for s in steps:
        at = 0
        for d in dims:
            at = at * grid.sizes[d] + (grid.at[d] + s.get(d, 0)) % grid.sizes[d]
        index.append(at)
    index = jnp.stack(index)
    if rows % 16 == 0:
        return place(stacks, index * rows)
    sizes = [grid.sizes[d] for d in reversed(order)]
    out = jnp.concatenate(stacks, axis=0).reshape(sizes + list(piece.shape))
    for axis, dim in enumerate(reversed(order)):
        out = grid.rolled(out, axis, dim)
    turn = [list(reversed(order)).index(d) for d in dims]
    return jnp.transpose(out, turn + [len(sizes), len(sizes) + 1]).reshape(-1, piece.shape[1])


def reduce_rows(grid, parts, order):
    dims = [d for d in ("hi", "lo", "x") if d in order]
    sizes = [grid.sizes[d] for d in dims]
    rows = parts.shape[0] // math.prod(sizes)
    parts = parts.reshape(sizes + [rows, parts.shape[1]])
    for dim in order:
        parts = grid.reduce(parts, dims.index(dim), dim, last=dim == order[-1])
        dims.remove(dim)
    return parts


def lane_tile(at, size):
    return pl.ds(pl.multiple_of(at, BLK), size)


def tile_scores(keys, queries):
    scores = jnp.dot(keys, queries, preferred_element_type=f32)
    square = scores * scores + 1.0
    return scores, square, lax.rsqrt(square)


def seen_tile(tile):
    return lax.broadcasted_iota(jnp.int32, (tile, tile), 0) <= lax.broadcasted_iota(jnp.int32, (tile, tile), 1)


def forward_kernel(heads, tile, meta_ref, qkv_ref, out_ref, att_ref, lse_ref, sorted_ref, keys_ref):
    row_len = qkv_ref.shape[1]
    width = heads * HEAD_DIM
    blocks = row_len // BLK
    per_device = out_ref.shape[2] // BLK
    for b in range(blocks):
        sorted_ref[:, b * BLK : (b + 1) * BLK] = qkv_ref[: 3 * width, lane_tile(meta_ref[b] * BLK, BLK)]
    for h in range(heads):
        keys_ref[h] = sorted_ref[width + h * HEAD_DIM : width + (h + 1) * HEAD_DIM, :].astype(f32).T.astype(bf16)
    doc_tiles = meta_ref[blocks] // tile
    seen = seen_tile(tile)
    lse_ref[...] = jnp.zeros_like(lse_ref)

    def one_query_tile(i, _):
        first = (i // doc_tiles) * doc_tiles

        def step(j, carry, diagonal):
            new = []
            for h in range(heads):
                peak, total, acc = carry[h]
                keys = keys_ref[h, pl.ds(pl.multiple_of(j * tile, tile), tile), :]
                queries = sorted_ref[h * HEAD_DIM : (h + 1) * HEAD_DIM, lane_tile(i * tile, tile)]
                scores, square, inverse = tile_scores(keys, queries)
                size = square * inverse
                if diagonal:
                    size = jnp.where(seen, size, -1e30)
                top = jnp.maximum(peak, jnp.max(size, axis=0, keepdims=True))
                shares = jnp.exp(size - top)
                fade = jnp.exp(peak - top)
                total = total * fade + jnp.sum(shares, axis=0, keepdims=True)
                mixing = (shares * (scores * inverse)).astype(bf16)
                values = sorted_ref[2 * width + h * HEAD_DIM : 2 * width + (h + 1) * HEAD_DIM, lane_tile(j * tile, tile)]
                acc = acc * fade + jnp.dot(values, mixing, preferred_element_type=f32)
                new.append((top, total, acc))
            return tuple(new)

        start = tuple(
            (jnp.ones((1, tile), f32), jnp.zeros((1, tile), f32), jnp.zeros((HEAD_DIM, tile), f32)) for _ in range(heads)
        )
        carry = lax.fori_loop(first, i, lambda j, c: step(j, c, False), start)
        carry = step(i, carry, True)
        for h in range(heads):
            peak, total, acc = carry[h]
            result = acc / total
            att_ref[h * HEAD_DIM : (h + 1) * HEAD_DIM, lane_tile(i * tile, tile)] = result
            lse_ref[h : h + 1, lane_tile(i * tile, tile)] = peak + jnp.log(total)
            low = result.astype(bf16)
            for part in range(tile // BLK):
                place_at = meta_ref[i * (tile // BLK) + part]
                out_ref[
                    place_at // per_device, h * HEAD_DIM : (h + 1) * HEAD_DIM, lane_tile((place_at % per_device) * BLK, BLK)
                ] = low[:, part * BLK : (part + 1) * BLK]
        return 0

    lax.fori_loop(0, row_len // tile, one_query_tile, 0)


def forward_attention(meta, qkv, heads, devices):
    row_len = qkv.shape[1]
    width = heads * HEAD_DIM
    tile = min(TILE, row_len)
    whole = pl.BlockSpec(memory_space=pltpu.VMEM)
    return pl.pallas_call(
        functools.partial(forward_kernel, heads, tile),
        out_shape=(
            jax.ShapeDtypeStruct((devices, width, row_len // devices), bf16),
            jax.ShapeDtypeStruct((width, row_len), f32),
            jax.ShapeDtypeStruct((8, row_len), f32),
        ),
        in_specs=[pl.BlockSpec(memory_space=pltpu.SMEM), whole],
        out_specs=(whole, whole, whole),
        scratch_shapes=[pltpu.VMEM((3 * width, row_len), bf16), pltpu.VMEM((heads, row_len, HEAD_DIM), bf16)],
        compiler_params=pltpu.CompilerParams(vmem_limit_bytes=40 * 2**20),
        cost_estimate=pl.CostEstimate(
            flops=2 * row_len * row_len * width, bytes_accessed=16 * row_len * width, transcendentals=heads * row_len * row_len
        ),
    )(meta, qkv)


def backward_kernel(
    heads, tile, meta_ref, qkv_ref, up_ref, att_ref, lse_ref, grad_ref, sorted_ref, ups_ref, nat_ref, delta_ref, dq_ref, dkv_ref
):
    row_len = qkv_ref.shape[1]
    width = heads * HEAD_DIM
    blocks = row_len // BLK
    per_device = up_ref.shape[2] // BLK
    for b in range(blocks):
        spot = slice(b * BLK, (b + 1) * BLK)
        sorted_ref[:, spot] = qkv_ref[: 3 * width, lane_tile(meta_ref[b] * BLK, BLK)]
        ups_ref[:, spot] = up_ref[meta_ref[b] // per_device, :, lane_tile((meta_ref[b] % per_device) * BLK, BLK)]
    delta_ref[...] = jnp.zeros_like(delta_ref)
    for h in range(heads):
        rows = slice(h * HEAD_DIM, (h + 1) * HEAD_DIM)
        for part in range(3):
            nat_ref[part * heads + h] = (
                sorted_ref[part * width + h * HEAD_DIM : part * width + (h + 1) * HEAD_DIM, :].astype(f32).T.astype(bf16)
            )
        upstream = ups_ref[rows, :].astype(f32)
        nat_ref[3 * heads + h] = upstream.T.astype(bf16)
        delta_ref[h : h + 1, :] = jnp.sum(upstream * att_ref[rows, :], axis=0, keepdims=True)
    dq_ref[...] = jnp.zeros_like(dq_ref)
    doc_tiles = meta_ref[blocks] // tile
    seen = seen_tile(tile)

    def one_key_tile(j, _):
        last = (j // doc_tiles + 1) * doc_tiles
        key_rows = pl.ds(pl.multiple_of(j * tile, tile), tile)

        def step(i, carry, diagonal):
            new = []
            at = lane_tile(i * tile, tile)
            query_rows = pl.ds(pl.multiple_of(i * tile, tile), tile)
            for h in range(heads):
                grad_keys, grad_values = carry[h]
                rows = slice(h * HEAD_DIM, (h + 1) * HEAD_DIM)
                scores, square, inverse = tile_scores(nat_ref[heads + h, key_rows, :], sorted_ref[rows, at])
                shares = jnp.exp(square * inverse - lse_ref[h : h + 1, at])
                if diagonal:
                    shares = jnp.where(seen, shares, 0.0)
                effect = jnp.dot(nat_ref[2 * heads + h, key_rows, :], ups_ref[rows, at], preferred_element_type=f32)
                sign = scores * inverse
                square_inverse = inverse * inverse
                grad = shares * (
                    effect * (1.0 - square_inverse + square_inverse * inverse) - delta_ref[h : h + 1, at] * sign
                )
                grad = grad.astype(bf16)
                mixing = (shares * sign).astype(bf16)
                grad_keys = grad_keys + jnp.dot(grad, nat_ref[h, query_rows, :], preferred_element_type=f32)
                grad_values = grad_values + jnp.dot(mixing, nat_ref[3 * heads + h, query_rows, :], preferred_element_type=f32)
                keys_t = sorted_ref[width + h * HEAD_DIM : width + (h + 1) * HEAD_DIM, lane_tile(j * tile, tile)]
                dq_ref[rows, at] += jnp.dot(keys_t, grad, preferred_element_type=f32)
                new.append((grad_keys, grad_values))
            return tuple(new)

        start = tuple((jnp.zeros((tile, HEAD_DIM), f32), jnp.zeros((tile, HEAD_DIM), f32)) for _ in range(heads))
        carry = step(j, start, True)
        carry = lax.fori_loop(j + 1, last, lambda i, c: step(i, c, False), carry)
        both = jnp.concatenate([c[0] for c in carry] + [c[1] for c in carry], axis=1).astype(bf16)
        dkv_ref[key_rows, :] = both
        return 0

    lax.fori_loop(0, row_len // tile, one_key_tile, 0)
    scale = HEAD_DIM**-0.5
    for b in range(blocks):
        spot = pl.ds(pl.multiple_of(meta_ref[b] * BLK, BLK), BLK)
        dq = (dq_ref[:, b * BLK : (b + 1) * BLK] * scale).T.astype(bf16)
        grad_ref[spot, :] = jnp.concatenate([dq, dkv_ref[b * BLK : (b + 1) * BLK, :]], axis=1)


def backward_attention(meta, qkv, upstream, att, lse, heads):
    row_len = qkv.shape[1]
    width = heads * HEAD_DIM
    tile = min(TILE, row_len)
    whole = pl.BlockSpec(memory_space=pltpu.VMEM)
    return pl.pallas_call(
        functools.partial(backward_kernel, heads, tile),
        out_shape=jax.ShapeDtypeStruct((row_len, 3 * width), bf16),
        in_specs=[pl.BlockSpec(memory_space=pltpu.SMEM)] + [whole] * 4,
        out_specs=whole,
        scratch_shapes=[
            pltpu.VMEM((3 * width, row_len), bf16),
            pltpu.VMEM((width, row_len), bf16),
            pltpu.VMEM((4 * heads, row_len, HEAD_DIM), bf16),
            pltpu.VMEM((8, row_len), f32),
            pltpu.VMEM((width, row_len), f32),
            pltpu.VMEM((row_len, 2 * width), bf16),
        ],
        compiler_params=pltpu.CompilerParams(vmem_limit_bytes=48 * 2**20),
        cost_estimate=pl.CostEstimate(
            flops=5 * row_len * row_len * width, bytes_accessed=20 * row_len * width, transcendentals=heads * row_len * row_len
        ),
    )(meta, qkv, upstream, att, lse)


def norm_parts(values):
    centered = values - jnp.mean(values, axis=-1, keepdims=True)
    inverse = lax.rsqrt(jnp.mean(centered * centered, axis=-1, keepdims=True) + epsilon)
    return centered * inverse, inverse


def norm_back(normed, inverse, gain, grad):
    c = grad * gain
    return (c - jnp.mean(c, axis=-1, keepdims=True) - normed * jnp.mean(c * normed, axis=-1, keepdims=True)) * inverse


def mm(a, b, dims):
    return lax.dot_general(a, b, ((dims[:1], dims[1:]), ((), ())), preferred_element_type=f32)


def body(
    tokens,
    lengths,
    block_place,
    qkv_weight,
    out_weight,
    up_weight,
    down_weight,
    attn_gain,
    mlp_gain,
    cotangent,
):
    nb, nk = lax.axis_size("pb"), lax.axis_size("ka")
    grid = Grid(nb, nk)
    nx, nc = grid.sizes["x"], grid.sizes["c"]
    x_at, c_at = grid.at["x"], grid.at["c"]
    tok_rows, model = tokens.shape
    shard = qkv_weight.shape[0]
    chips = nb * nx
    heads = -(-HEADS // nk)
    width = heads * HEAD_DIM
    lanes = -(-(3 * width + 2) // BLK) * BLK
    rels = [(xr, cr) for xr in range(nx) for cr in range(nc)]

    def ka_of(xr, cr):
        return ((x_at + xr) % nx) * nc + (c_at + cr) % nc

    def exchange(parts):
        got = [parts(grid.ka)]
        for xr, cr in rels[1:]:
            got.append(grid.fetch(parts(ka_of(-xr, -cr)), x=xr, c=cr))
        return got

    def head_groups(weight):
        split = weight.reshape(weight.shape[0], 3, HEADS, HEAD_DIM)
        if heads * nk != HEADS:
            split = jnp.pad(split, ((0, 0), (0, 0), (0, heads * nk - HEADS), (0, 0)))
        return jnp.transpose(split.reshape(-1, 3, nk, width), (2, 0, 1, 3)).reshape(nk, -1, 3 * width)

    gains = jnp.stack([attn_gain, mlp_gain], axis=1)
    gains = jnp.pad(gains, ((0, 0), (0, lanes - 3 * width - 2)))
    own_qkv = jnp.concatenate([head_groups(qkv_weight), jnp.broadcast_to(gains[None], (nk,) + gains.shape)], axis=2)
    got = exchange(lambda ka: lax.dynamic_index_in_dim(own_qkv, ka, 0, keepdims=False))
    group_qkv = jnp.stack(got).reshape(nx, nc, shard, lanes)
    group_qkv = grid.rolled(grid.rolled(group_qkv, 0, "x"), 1, "c").reshape(nk * shard, lanes)
    full_qkv = gather_rows(grid, group_qkv, ("lo", "hi"))

    by_x = [tokens] + [grid.fetch(tokens, x=r) for r in range(1, nx)]
    row_tokens = jnp.concatenate([p for t in by_x for p in ([t] + [grid.fetch(t, c=r) for r in range(1, nc)])], axis=0)
    row_len = row_tokens.shape[0]

    def core_part(weight):
        mine = lax.dynamic_index_in_dim(weight, c_at, 0, keepdims=False)
        got = [mine] + [
            grid.fetch(lax.dynamic_index_in_dim(weight, (c_at - r) % nc, 0, keepdims=False), c=r) for r in range(1, nc)
        ]
        return grid.rolled(jnp.stack(got), 0, "c").reshape(nc * weight.shape[1], weight.shape[2])

    strip = down_weight.shape[0]
    up_split = jnp.transpose(up_weight.reshape(shard, chips, nc, strip), (2, 0, 1, 3)).reshape(nc, shard, chips * strip)
    out_split = jnp.transpose(out_weight.reshape(shard, nc, model // nc), (1, 0, 2))
    up_out = core_part(jnp.concatenate([up_split, out_split], axis=2))
    full_down = gather_rows(grid, down_weight, ("hi", "x", "lo"))
    full_up_out = gather_rows(grid, up_out, ("hi", "lo", "x"))
    full_up = full_up_out[:, : chips * strip]
    out_own = full_up_out[:, chips * strip :]
    full_out = jnp.concatenate([out_own] + [grid.fetch(out_own, c=r) for r in range(1, nc)], axis=1)
    full_out = grid.rolled(full_out.reshape(model, nc, model // nc), 1, "c").reshape(model, model)
    cots = jnp.concatenate([cotangent] + [grid.fetch(cotangent, c=r) for r in range(1, nc)], axis=0)

    slots = tok_rows // BLK
    holder = jnp.argsort(block_place[0]).astype(jnp.int32)
    holder_ka, holder_slot = holder // slots, holder % slots
    rel = ((holder_ka // nc - x_at) % nx) * nc + (holder_ka % nc - c_at) % nc
    meta = jnp.concatenate([rel * slots + holder_slot, lengths[0, :1]]).astype(jnp.int32)

    gain_one = full_qkv[:, 3 * width].astype(f32)
    gain_two = full_qkv[:, 3 * width + 1].astype(f32)
    head_qkv = full_qkv[:, : 3 * width]
    inputs = tokens.astype(f32)
    normed_row, _ = norm_parts(row_tokens.astype(f32))
    h1 = (normed_row * gain_one).astype(bf16)
    scale = jnp.where(jnp.arange(3 * width) < width, HEAD_DIM**-0.5, 1.0).astype(f32)
    qkv = (mm(head_qkv, h1, (0, 1)) * scale[:, None]).astype(bf16)
    att_parts, att_row, lse = forward_attention(meta, qkv, heads, nk)

    def abs_heads(parts):
        both = jnp.stack(parts).reshape((nx, nc) + parts[0].shape)
        both = grid.rolled(grid.rolled(both, 0, "x"), 1, "c")
        return both.reshape((nk * parts[0].shape[0],) + parts[0].shape[1:])

    got = [att_parts[0]]
    for xr, cr in rels[1:]:
        got.append(grid.fetch(att_parts[((-xr) % nx) * nc + (-cr) % nc], x=xr, c=cr))
    att = abs_heads(got)[: HEADS * HEAD_DIM]

    residual = inputs + mm(att, full_out, (0, 0))
    normed_two, inverse_two = norm_parts(residual)
    h2 = (normed_two * gain_two).astype(bf16)
    h2s = jnp.concatenate([h2] + [grid.fetch(h2, c=r) for r in range(1, nc)], axis=0)

    def core_sum(part):
        pieces = part.reshape((nc, tok_rows) + part.shape[1:])
        total = pieces[0]
        for r in range(1, nc):
            total = total + grid.fetch(pieces[(nc - r) % nc].astype(bf16), c=r).astype(f32)
        return total

    hidden_pre = mm(h2s, full_up, (1, 0))
    hidden_act, gelu_back = jax.vjp(lambda v: jax.nn.gelu(v, approximate=True), hidden_pre)
    hidden_low = hidden_act.astype(bf16)
    (grad_pre,) = gelu_back(mm(cots, full_down, (1, 1)))
    grad_pre = grad_pre.astype(bf16)
    grad_h2 = core_sum(mm(grad_pre, full_up, (1, 1)))
    grad_down = mm(hidden_low, cots, (0, 0)).astype(bf16)
    grad_up = mm(h2s, grad_pre, (0, 0)).astype(bf16)
    mixed = (residual + core_sum(mm(hidden_low, full_down, (1, 0)))).astype(bf16)

    grad_residual = cotangent.astype(f32) + norm_back(normed_two, inverse_two, gain_two, grad_h2)
    grad_res_low = grad_residual.astype(bf16)
    grad_att = mm(full_out, grad_res_low, (1, 1)).astype(bf16)
    if heads * nk != HEADS:
        grad_att = jnp.pad(grad_att, ((0, (heads * nk - HEADS) * HEAD_DIM), (0, 0)))
    grad_att = grad_att.reshape(nk, width, tok_rows)
    upstream = jnp.stack(exchange(lambda ka: lax.dynamic_index_in_dim(grad_att, ka, 0, keepdims=False)))
    grad_out = mm(att, grad_res_low, (1, 0)).astype(bf16)

    grad_qkv_rows = backward_attention(meta, qkv, upstream, att_row, lse, heads)
    grad_qkv = mm(h1, grad_qkv_rows, (0, 0)).astype(bf16)
    grad_h1 = mm(grad_qkv_rows, head_qkv, (1, 1)).astype(bf16).reshape(nx, nc, tok_rows, model)

    half = grad_h1[:, 0].astype(f32)
    for r in range(1, nc):
        half = half + grid.fetch(grad_h1[:, (nc - r) % nc], c=r).astype(f32)
    half = half.astype(bf16)
    grad_normed_one = half[0].astype(f32)
    for r in range(1, nx):
        grad_normed_one = grad_normed_one + grid.fetch(half[(nx - r) % nx], x=r).astype(f32)
    normed_one, inverse_one = norm_parts(inputs)
    tokens_grad = (grad_residual + norm_back(normed_one, inverse_one, gain_one, grad_normed_one)).astype(bf16)

    def from_core_parts(part):
        pieces = part.reshape(nc, part.shape[0] // nc, part.shape[1])
        got = [lax.dynamic_index_in_dim(pieces, c_at, 0, keepdims=False)]
        for r in range(1, nc):
            got.append(grid.fetch(lax.dynamic_index_in_dim(pieces, (c_at - r) % nc, 0, keepdims=False), c=r))
        return grid.rolled(jnp.stack(got), 0, "c")

    sum_down = reduce_rows(grid, grad_down, ("lo", "x", "hi"))
    sum_up = from_core_parts(reduce_rows(grid, grad_up, ("x", "lo", "hi")))
    sum_up = jnp.transpose(sum_up.reshape(nc, shard, chips, strip), (1, 2, 0, 3)).reshape(shard, -1)
    core_out = grid.reduce(grad_out.reshape(model, nc, model // nc), 1, "c")
    sum_out = from_core_parts(reduce_rows(grid, core_out, ("x", "lo", "hi")))
    sum_out = jnp.transpose(sum_out, (1, 0, 2)).reshape(shard, model)
    group_grad = reduce_rows(grid, grad_qkv, ("lo", "hi")).reshape(nk, shard, 3 * width)
    got = exchange(lambda ka: lax.dynamic_index_in_dim(group_grad, ka, 0, keepdims=False))
    sum_qkv = jnp.stack(got).reshape(nx, nc, shard, 3, width)
    sum_qkv = grid.rolled(grid.rolled(sum_qkv, 0, "x"), 1, "c").reshape(nk, shard, 3, width)
    sum_qkv = jnp.transpose(sum_qkv, (1, 2, 0, 3)).reshape(shard, 3, nk * width)[:, :, : HEADS * HEAD_DIM]
    sum_qkv = sum_qkv.reshape(shard, 3 * HEADS * HEAD_DIM)

    grad_gain_one = jnp.sum(sum_qkv * qkv_weight.astype(f32), axis=1) / attn_gain.astype(f32)
    grad_gain_two = jnp.sum(sum_up * up_weight.astype(f32), axis=1) / mlp_gain.astype(f32)
    return (mixed, tokens_grad, sum_qkv, sum_out, sum_up, sum_down, grad_gain_one, grad_gain_two)


def solution(mesh):
    rows = P(("pb", "ka"), None)
    flat = P(("pb", "ka"))
    group = P("pb", None)
    return jax.shard_map(
        body,
        mesh=mesh,
        in_specs=(rows, group, group, rows, rows, rows, rows, flat, flat, rows),
        out_specs=(rows, rows, rows, rows, rows, rows, flat, flat),
        check_vma=False,
    )
```

time: 1210 us -> 576 us (0.48)
  waiting for transfers between devices: 617 us -> 90 us
  matrix products: 337 us -> 43.5 us
  Pallas kernels: 0 us -> 246 us
  blocking collectives: 112 us -> 0 us
  starting transfers between devices: 0.48 us -> 80.5 us
  other arithmetic: 16.6 us -> 53 us
  local copies, waits for them, and re-layouts: 84.2 us -> 56 us
  loops' own time: 19.4 us -> 0 us
  between operations: 15 us -> 2 us
    reduce_scatter x6 -> x0, waiting for transfers between devices: 490 us -> none  [the longest x1 142 us: body(): lax.psum_scatter(grad_down, ('pb', 'ka'), scatter_dimension=0, tiled=True)]
    dot_general x44 -> x12, matrix products: 337 us -> 43.5 us  [mm(): lax.dot_general(a, b, ((dims[:1], dims[1:]), ((), ())), preferred_element...]
    pallas_call x0 -> x5, Pallas kernels: none -> 246 us  [the longest x3 196 us: place(): pl.pallas_call(functools.partial(place_kernel, counts, rows), out_shape=j...]
    all_gather x6 -> x0, waiting for transfers between devices: 125 us -> none  [the longest x1 64.1 us: body(): lax.all_gather(up_weight, ('pb', 'ka'), axis=0, tiled=True)]
    ppermute x0 -> x59, waiting for transfers between devices: none -> 90 us  [fetch(): return lax.ppermute(value, ('pb', 'ka'), pairs)]
    unnamed x2 -> x0, blocking collectives: 81.6 us -> none
    ppermute x0 -> x59, starting transfers between devices: none -> 80.5 us  [fetch(): return lax.ppermute(value, ('pb', 'ka'), pairs)]
    dynamic_slice x66 -> x7, local copies, waits for them, and re-layouts: 34.8 us -> 7.2 us  [the longest x2 3.25 us: reduce(): sent = lax.dynamic_index_in_dim(parts, (me - r) % n, axis, keepdims=False)]
  transfers between devices with their start and end apart: 12 -> 59, of which waited for: 10 -> 24; matrix products, arithmetic and copies ran while one was open for 20% -> 21% of each run, Pallas kernels for 0% -> 43%
where the time goes in v1:
time: 576 us; the launch traced here: 571 us
  Pallas kernels  246 us (43%)
  waiting for transfers between devices  90 us (16%)
  starting transfers between devices  80.5 us (14%)
  local copies, waits for them, and re-layouts  56 us (10%)
  other arithmetic  53 us (9%)
  matrix products  43.5 us (8%)
    pallas_call x3, Pallas kernels, place(): pl.pallas_call(functools.partial(place_kernel, counts, rows), out_shape=j...  196 us
    ppermute x59, waiting for transfers between devices, fetch(): return lax.ppermute(value, ('pb', 'ka'), pairs)  90 us
    ppermute x59, starting transfers between devices, fetch(): return lax.ppermute(value, ('pb', 'ka'), pairs)  80.5 us
    dot_general x12, matrix products, mm(): lax.dot_general(a, b, ((dims[:1], dims[1:]), ((), ())), preferred_element...  43.5 us
    pallas_call x1, Pallas kernels, backward_attention(): pl.pallas_call(functools.partial(backward_kernel, heads, tile), out_shape...  28.6 us
    pallas_call x1, Pallas kernels, forward_attention(): pl.pallas_call(functools.partial(forward_kernel, heads, tile), out_shape=...  21.3 us
    unnamed x110, local copies, waits for them, and re-layouts  17.6 us
  transfers between devices with their start and end apart: 59, of which 24 were waited for; matrix products, arithmetic and copies ran while one was open for 21% of the time, Pallas kernels for 43%

profile of v1, /device:TPU:0, one launch (start us, length us, event | category | flops | bytes accessed | tf_op | source)
XLA Modules:
  0.0 571.1 jit_solution(14407982336665958183)
XLA Ops:
  0.7 3.1 collective-permute-start.23
  3.8 2.6 collective-permute-start.22
  10.0 1.6 collective-permute-start.1
  11.6 1.6 constant_dynamic-update-slice_fusion.9
  14.4 1.9 sort.17
  17.6 1.6 collective-permute-start.8
  25.3 2.9 collective-permute-start.14
  30.5 3.2 collective-permute-done.16
  33.8 7.9 %collective-permute-done.15 = bf16[1,48,1920]{2,1,0:T(8,128)(2,1)S(1)} collective-permute-done((bf16[1,48,1920]{2,1,0:T(8,128)(2,1)S(1)}, bf16[1,48,1920]{2,1,0:T(8,128)(2,1)S(1)}, u32[]{:S(2)}, u32[]{:S(2)}) %collective-permute-start.15) | collective-permute-done | bytes 184352 | tf_op jit(solution)/shard_map/ppermute | solution.py:41
  43.9 3.1 collective-permute-done.6.refs_3_
  49.1 11.3 %collective-permute-done.5.refs_2_ = bf16[2,96,640]{2,1,0:T(8,128)(2,1)S(1)} collective-permute-done((bf16[2,96,640]{2,1,0:T(8,128)(2,1)S(1)}, bf16[2,96,640]{2,1,0:T(8,128)(2,1)S(1)}, u32[]{:S(2)}, u32[]{:S(2)}) %collective-permute-start.5) | collective-permute-done | bytes 245792 | tf_op jit(solution)/shard_map/ppermute | solution.py:41
  60.5 4.8 collective-permute-done.4.refs_1_
  66.1 31.6 %shard_map.161 = bf16[768,640]{1,0:T(8,128)(2,1)} custom-call(s32[8]{0:T(128)} %broadcast_multiply_fusion.9.offs_ref, bf16[2,96,640]{2,1,0:T(8,128)(2,1)} %copy-done.33, bf16[2,96,640]{2,1,0:T(8,128)(2,1)} %copy-done.42, bf16[2,96,640]{2,1,0:T(8,128)(2,1)} %copy-done.41, bf16[2,96,640]{2,1,0:T(8,128)(2,1)} %copy-done.40), custom_call_target="tpu_custom_call" | custom-call | bytes 1966080 | tf_op jit(solution)/shard_map/pallas_call | solution.py:79
  99.1 2.1 constant_dynamic-update-slice_fusion.refs_0_
  101.1 1.8 collective-permute-start.18
  103.8 4.4 fusion.2
  108.2 5.6 multiply_convert_fusion.1.qkv_ref
  113.8 21.3 %shard_map.162 = (bf16[4,192,512]{2,1,0:T(8,128)(2,1)S(1)}, f32[192,2048]{1,0:T(8,128)S(1)}, f32[8,2048]{1,0:T(8,128)S(1)}) custom-call(s32[17]{0:T(128)S(1)} %pad_add_fusion.meta_ref, bf16[576,2048]{1,0:T(8,128)(2,1)S(1)} %multiply_convert_fusion.1.qkv_ref), custom_call_target="tpu_custom_call" | custom-call | flops 1610612736 | bytes 6291456 | tf_op jit(solution)/shard_map/pallas_call | solution.py:206
  137.5 1.8 collective-permute-start.11
  139.3 91.3 %shard_map.163 = bf16[768,1920]{1,0:T(8,128)(2,1)} custom-call(s32[16]{0:T(128)} %broadcast_multiply_fusion.8.offs_ref, bf16[8,48,1920]{2,1,0:T(8,128)(2,1)} %constant_dynamic-update-slice_fusion.refs_0_, bf16[8,48,1920]{2,1,0:T(8,128)(2,1)} %collective-permute-done.18.refs_1_), custom_call_target="tpu_custom_call" | custom-call | bytes 5898240 | tf_op jit(solution)/shard_map/pallas_call | solution.py:79
  231.8 1.9 constant_dynamic-update-slice_fusion.5.refs_0_
  233.7 16.6 %collective-permute-start.25 = (bf16[8,96,768]{2,1,0:T(8,128)(2,1)}, bf16[8,96,768]{2,1,0:T(8,128)(2,1)}, u32[]{:S(2)}, u32[]{:S(2)}) collective-permute-start(bf16[8,96,768]{2,1,0:T(8,128)(2,1)} %constant_dynamic-update-slice_fusion.5.refs_0_), channel_id=1, source_target_pairs={{4,0},{5,1},{6,2},{7,3},{0,4},{1,5},{2,6},{3,7},{12,8},{13,9},{14,... | collective-permute-start | bytes 3538952 | tf_op jit(solution)/shard_map/ppermute | solution.py:41
  255.2 3.9 reshape.211
  259.2 6.0 %fusion.34 = bf16[768,2,384]{2,1,0:T(2,128)(2,1)S(1)} fusion(s32[]{:T(128)S(6)} %select_n.549, bf16[768,2,384]{2,1,0:T(2,128)(2,1)} %reshape.211, bf16[768,1,384]{2,1,0:T(2,128)(2,1)} %bitcast.233), kind=kLoop, calls=%fused_computation.68 | loop fusion | flops 2359296 | bytes 2949124 | tf_op jit(solution)/shard_map/concatenate | solution.py:50
  268.8 2.1 constant_dynamic-update-slice_fusion.11
  272.5 2.1 constant_dynamic-update-slice_fusion.10
  274.6 2.7 collective-permute-done.25.refs_1_
  277.3 73.4 %shard_map.164 = bf16[1536,768]{1,0:T(8,128)(2,1)} custom-call(s32[16]{0:T(128)} %broadcast_multiply_fusion.7.offs_ref, bf16[8,96,768]{2,1,0:T(8,128)(2,1)} %constant_dynamic-update-slice_fusion.5.refs_0_, bf16[8,96,768]{2,1,0:T(8,128)(2,1)} %collective-permute-done.25.refs_1_), custom_call_target="tpu_custom_call" | custom-call | bytes 4718592 | tf_op jit(solution)/shard_map/pallas_call | solution.py:79
  350.7 4.8 fusion.17
  355.6 3.8 convolution_convert_fusion
  359.4 6.5 %fusion.11 = bf16[1024,1536]{1,0:T(8,128)(2,1)S(1)} fusion(f32[1024,1536]{1,0:T(8,128)S(1)} %fusion.17, bf16[1024,768]{1,0:T(8,128)(2,1)S(1)} %copy-done.39, bf16[1536,768]{1,0:T(8,128)(2,1)S(1)} %copy-done.27), kind=kOutput, calls=%fused_computation.15 | convolution fusion | flops 2447376384 | bytes 13369344 | tf_op jit(solution)/shard_map/dot_general | solution.py:330
  365.9 3.8 fusion.89
  372.0 1.7 collective-permute-start.54
  373.8 2.6 fusion.15
  377.2 4.3 convolution_convert_fusion.1
  384.7 2.8 multiply_add_fusion
  389.3 1.7 collective-permute-start.30
  393.1 2.2 copy.77
  395.3 2.1 copy.69
  397.4 16.8 %collective-permute-done.31 = bf16[192,512]{1,0:T(8,128)(2,1)} collective-permute-done((bf16[192,512]{1,0:T(8,128)(2,1)}, bf16[192,512]{1,0:T(8,128)(2,1)}, u32[]{:S(2)}, u32[]{:S(2)}) %collective-permute-start.31) | collective-permute-done | bytes 196640 | tf_op jit(solution)/shard_map/ppermute | solution.py:41
  414.2 1.6 collective-permute-start.41
  415.8 3.5 collective-permute-done.30
  422.0 28.6 %shard_map.165 = bf16[2048,576]{1,0:T(8,128)(2,1)} custom-call(s32[17]{0:T(128)S(1)} %pad_add_fusion.meta_ref, bf16[576,2048]{1,0:T(8,128)(2,1)S(1)} %multiply_convert_fusion.1.qkv_ref, bf16[4,192,512]{2,1,0:T(8,128)(2,1)S(1)} %pad_maximum_fusion.6.up_ref, f32[192,2048]{1,0:T(8,128)S(1)} %copy-done.1, f32[8,2048]{1,0:T(8,128)S(1)} %get-tuple-element.15.lse_ref), custom_call_target="tpu_custom_call" | custom-call | flops 4026531840 | bytes 7864320 | tf_op jit(solution)/shard_map/pallas_call | solution.py:298
  450.6 5.1 convolution_convert_fusion.4
  455.7 1.8 copy.65
  457.6 18.1 %collective-permute-start.34 = (bf16[4,96,576]{2,1,0:T(8,128)(2,1)S(1)}, bf16[4,96,576]{2,1,0:T(8,128)(2,1)S(1)}, u32[]{:S(2)}, u32[]{:S(2)}) collective-permute-start(bf16[4,96,576]{2,1,0:T(8,128)(2,1)S(1)} %dynamic-slice_bitcast_fusion.3), channel_id=1, source_target_pairs={{4,0},{5,1},{6,2},{7,3},{0,4},{1,5},{2,6},{3,7},{12,8},{13,9},{14,... | collective-permute-start | bytes 1327112 | tf_op jit(solution)/shard_map/ppermute | solution.py:41
  475.7 4.4 convolution_convert_fusion.2
  482.3 1.7 fusion.13
  485.2 1.6 fusion.14
  492.5 1.6 collective-permute-done.35
  494.1 3.1 collective-permute-done.37
  497.3 4.5 collective-permute-done.36
  502.5 1.7 collective-permute-start.39
  511.5 1.6 stack.229
  520.3 3.0 collective-permute-done.49
  530.2 2.5 collective-permute-start.52
  534.7 5.5 collective-permute-done.45
  542.2 2.0 collective-permute-start.58
  544.5 1.8 fusion.12
  547.5 3.1 collective-permute-done.56
  550.8 5.4 collective-permute-done.57
  564.0 3.4 collective-permute-done.33
  567.5 1.8 fusion.33
  569.3 1.6 fusion.27
  (303 shorter events, 92.5 us)
Async XLA Ops:
  0.7 23.6 %collective-permute-start.23 = (bf16[1,96,768]{2,1,0:T(8,128)(2,1)}, bf16[1,96,768]{2,1,0:T(8,128)(2,1)S(1)}, u32[]{:S(2)}, u32[]{:S(2)}) collective-permute-start(bf16[1,96,768]{2,1,0:T(8,128)(2,1)} %bitcast.262), channel_id=1, source_target_pairs={{24,0},{25,1},{26,2},{27,3},{28,4},{29,5},{30,6},{31,7},{0,8},{1,9... | collective-permute-start | bytes 442376 | tf_op jit(solution)/shard_map/ppermute | solution.py:41
  3.8 21.3 %collective-permute-start.22 = (bf16[1,96,768]{2,1,0:T(8,128)(2,1)}, bf16[1,96,768]{2,1,0:T(8,128)(2,1)S(1)}, u32[]{:S(2)}, u32[]{:S(2)}) collective-permute-start(bf16[1,96,768]{2,1,0:T(8,128)(2,1)} %bitcast.263), channel_id=1, source_target_pairs={{16,0},{17,1},{18,2},{19,3},{20,4},{21,5},{22,6},{23,7},{24,8},{25... | collective-permute-start | bytes 442376 | tf_op jit(solution)/shard_map/ppermute | solution.py:41
  6.3 19.0 %collective-permute-start.21 = (bf16[1,96,768]{2,1,0:T(8,128)(2,1)}, bf16[1,96,768]{2,1,0:T(8,128)(2,1)S(1)}, u32[]{:S(2)}, u32[]{:S(2)}) collective-permute-start(bf16[1,96,768]{2,1,0:T(8,128)(2,1)} %bitcast.264), channel_id=1, source_target_pairs={{8,0},{9,1},{10,2},{11,3},{12,4},{13,5},{14,6},{15,7},{16,8},{17,9... | collective-permute-start | bytes 442376 | tf_op jit(solution)/shard_map/ppermute | solution.py:41
  9.9 7.3 %collective-permute-start = (bf16[24,640]{1,0:T(8,128)(2,1)S(1)}, bf16[24,640]{1,0:T(8,128)(2,1)S(1)}, u32[]{:S(2)}, u32[]{:S(2)}) collective-permute-start(bf16[24,640]{1,0:T(8,128)(2,1)S(1)} %get-tuple-element.57), channel_id=1, source_target_pairs={{1,0},{0,1},{3,2},{2,3},{5,4},{4,5},{7,6},{6,7},{9,8},{8,9},{11,10... | collective-permute-start | bytes 92168 | tf_op jit(solution)/shard_map/ppermute | solution.py:41
  10.0 7.6 %collective-permute-start.1 = (bf16[24,640]{1,0:T(8,128)(2,1)S(1)}, bf16[24,640]{1,0:T(8,128)(2,1)S(1)}, u32[]{:S(2)}, u32[]{:S(2)}) collective-permute-start(bf16[24,640]{1,0:T(8,128)(2,1)S(1)} %get-tuple-element.58), channel_id=1, source_target_pairs={{2,0},{3,1},{0,2},{1,3},{6,4},{7,5},{4,6},{5,7},{10,8},{11,9},{8,1... | collective-permute-start | bytes 92168 | tf_op jit(solution)/shard_map/ppermute | solution.py:41
  16.6 254.5 %copy-start.45 = (f32[512]{0:T(512)}, f32[512]{0:T(512)S(1)}, u32[]{:S(2)}) copy-start(f32[512]{0:T(512)S(1)} %broadcast_multiply_fusion.2) | copy-start | bytes 6148
  17.2 3.4 collective-permute-start.2
  17.6 30.1 %collective-permute-start.8 = (bf16[512,768]{1,0:T(8,128)(2,1)S(1)}, bf16[512,768]{1,0:T(8,128)(2,1)S(1)}, u32[]{:S(2)}, u32[]{:S(2)}) collective-permute-start(bf16[512,768]{1,0:T(8,128)(2,1)S(1)} %copy-done.2), channel_id=1, source_target_pairs={{2,0},{3,1},{0,2},{1,3},{6,4},{7,5},{4,6},{5,7},{10,8},{11,9},{8,1... | collective-permute-start | bytes 2359304 | tf_op jit(solution)/shard_map/ppermute | solution.py:41
  20.6 1.4 collective-permute-start.13
  22.0 8.5 %collective-permute-start.3 = (bf16[1,96,640]{2,1,0:T(8,128)(2,1)S(1)}, bf16[1,96,640]{2,1,0:T(8,128)(2,1)S(1)}, u32[]{:S(2)}, u32[]{:S(2)}) collective-permute-start(bf16[1,96,640]{2,1,0:T(8,128)(2,1)S(1)} %bitcast.268), channel_id=1, source_target_pairs={{4,0},{5,1},{6,2},{7,3},{0,4},{1,5},{2,6},{3,7},{12,8},{13,9},{14,... | collective-permute-start | bytes 368648 | tf_op jit(solution)/shard_map/ppermute | solution.py:41
  24.3 9.4 %collective-permute-start.16 = (bf16[1,48,1920]{2,1,0:T(8,128)(2,1)S(1)}, bf16[1,48,1920]{2,1,0:T(8,128)(2,1)S(1)}, u32[]{:S(2)}, u32[]{:S(2)}) collective-permute-start(bf16[1,48,1920]{2,1,0:T(8,128)(2,1)S(1)} %bitcast.249), channel_id=1, source_target_pairs={{24,0},{25,1},{26,2},{27,3},{28,4},{29,5},{30,6},{31,7},{0,8},{1,9... | collective-permute-start | bytes 552968 | tf_op jit(solution)/shard_map/ppermute | solution.py:41
  25.0 16.7 %collective-permute-start.15 = (bf16[1,48,1920]{2,1,0:T(8,128)(2,1)S(1)}, bf16[1,48,1920]{2,1,0:T(8,128)(2,1)S(1)}, u32[]{:S(2)}, u32[]{:S(2)}) collective-permute-start(bf16[1,48,1920]{2,1,0:T(8,128)(2,1)S(1)} %bitcast.250), channel_id=1, source_target_pairs={{16,0},{17,1},{18,2},{19,3},{20,4},{21,5},{22,6},{23,7},{24,8},{25... | collective-permute-start | bytes 552968 | tf_op jit(solution)/shard_map/ppermute | solution.py:41
  25.3 16.4 %collective-permute-start.14 = (bf16[1,48,1920]{2,1,0:T(8,128)(2,1)S(1)}, bf16[1,48,1920]{2,1,0:T(8,128)(2,1)S(1)}, u32[]{:S(2)}, u32[]{:S(2)}) collective-permute-start(bf16[1,48,1920]{2,1,0:T(8,128)(2,1)S(1)} %bitcast.251), channel_id=1, source_target_pairs={{8,0},{9,1},{10,2},{11,3},{12,4},{13,5},{14,6},{15,7},{16,8},{17,9... | collective-permute-start | bytes 552968 | tf_op jit(solution)/shard_map/ppermute | solution.py:41
  30.5 72.5 %collective-permute-start.7 = (bf16[512,768]{1,0:T(8,128)(2,1)S(1)}, bf16[512,768]{1,0:T(8,128)(2,1)S(1)}, u32[]{:S(2)}, u32[]{:S(2)}) collective-permute-start(bf16[512,768]{1,0:T(8,128)(2,1)S(1)} %copy-done.2), channel_id=1, source_target_pairs={{1,0},{0,1},{3,2},{2,3},{5,4},{4,5},{7,6},{6,7},{9,8},{8,9},{11,10... | collective-permute-start | bytes 2359304 | tf_op jit(solution)/shard_map/ppermute | solution.py:41
  30.5 35.6 %copy-start.33 = (bf16[2,96,640]{2,1,0:T(8,128)(2,1)}, bf16[2,96,640]{2,1,0:T(8,128)(2,1)S(1)}, u32[]{:S(2)}) copy-start(bf16[2,96,640]{2,1,0:T(8,128)(2,1)S(1)} %pad_maximum_fusion.9.refs_0_) | copy-start | bytes 737284
  33.8 13.2 %collective-permute-start.6 = (bf16[2,96,640]{2,1,0:T(8,128)(2,1)S(1)}, bf16[2,96,640]{2,1,0:T(8,128)(2,1)S(1)}, u32[]{:S(2)}, u32[]{:S(2)}) collective-permute-start(bf16[2,96,640]{2,1,0:T(8,128)(2,1)S(1)} %pad_maximum_fusion.9.refs_0_), channel_id=1, source_target_pairs={{24,0},{25,1},{26,2},{27,3},{28,4},{29,5},{30,6},{31,7},{0,8},{1,9... | collective-permute-start | bytes 737288 | tf_op jit(solution)/shard_map/ppermute | solution.py:41
  41.7 18.8 %collective-permute-start.5 = (bf16[2,96,640]{2,1,0:T(8,128)(2,1)S(1)}, bf16[2,96,640]{2,1,0:T(8,128)(2,1)S(1)}, u32[]{:S(2)}, u32[]{:S(2)}) collective-permute-start(bf16[2,96,640]{2,1,0:T(8,128)(2,1)S(1)} %pad_maximum_fusion.9.refs_0_), channel_id=1, source_target_pairs={{16,0},{17,1},{18,2},{19,3},{20,4},{21,5},{22,6},{23,7},{24,8},{25... | collective-permute-start | bytes 737288 | tf_op jit(solution)/shard_map/ppermute | solution.py:41
  42.7 56.4 %collective-permute-start.17 = (bf16[4,48,1920]{2,1,0:T(8,128)(2,1)}, bf16[4,48,1920]{2,1,0:T(8,128)(2,1)}, u32[]{:S(2)}, u32[]{:S(2)}) collective-permute-start(bf16[4,48,1920]{2,1,0:T(8,128)(2,1)} %pad_maximum_fusion.7), channel_id=1, source_target_pairs={{4,0},{5,1},{6,2},{7,3},{0,4},{1,5},{2,6},{3,7},{12,8},{13,9},{14,... | collective-permute-start | bytes 2211848 | tf_op jit(solution)/shard_map/ppermute | solution.py:41
  47.0 18.2 %collective-permute-start.4 = (bf16[2,96,640]{2,1,0:T(8,128)(2,1)S(1)}, bf16[2,96,640]{2,1,0:T(8,128)(2,1)S(1)}, u32[]{:S(2)}, u32[]{:S(2)}) collective-permute-start(bf16[2,96,640]{2,1,0:T(8,128)(2,1)S(1)} %pad_maximum_fusion.9.refs_0_), channel_id=1, source_target_pairs={{8,0},{9,1},{10,2},{11,3},{12,4},{13,5},{14,6},{15,7},{16,8},{17,9... | collective-permute-start | bytes 737288 | tf_op jit(solution)/shard_map/ppermute | solution.py:41
  47.7 56.1 %copy-start.17 = (bf16[512,768]{1,0:T(8,128)(2,1)}, bf16[512,768]{1,0:T(8,128)(2,1)S(1)}, u32[]{:S(2)}) copy-start(bf16[512,768]{1,0:T(8,128)(2,1)S(1)} %collective-permute-done.8) | copy-start | bytes 2359300
  47.7 55.3 %collective-permute-start.9 = (bf16[512,768]{1,0:T(8,128)(2,1)S(1)}, bf16[512,768]{1,0:T(8,128)(2,1)S(1)}, u32[]{:S(2)}, u32[]{:S(2)}) collective-permute-start(bf16[512,768]{1,0:T(8,128)(2,1)S(1)} %collective-permute-done.8), channel_id=1, source_target_pairs={{1,0},{0,1},{3,2},{2,3},{5,4},{4,5},{7,6},{6,7},{9,8},{8,9},{11,10... | collective-permute-start | bytes 2359304 | tf_op jit(solution)/shard_map/ppermute | solution.py:41
  60.4 212.1 %collective-permute-start.27 = (bf16[512,768]{1,0:T(8,128)(2,1)}, bf16[512,768]{1,0:T(8,128)(2,1)}, u32[]{:S(2)}, u32[]{:S(2)}) collective-permute-start(bf16[512,768]{1,0:T(8,128)(2,1)} %param.19), channel_id=1, source_target_pairs={{1,0},{0,1},{3,2},{2,3},{5,4},{4,5},{7,6},{6,7},{9,8},{8,9},{11,10... | collective-permute-start | bytes 2359304 | tf_op jit(solution)/shard_map/ppermute | solution.py:41
  65.9 165.8 %collective-permute-start.24 = (bf16[4,96,768]{2,1,0:T(8,128)(2,1)}, bf16[4,96,768]{2,1,0:T(8,128)(2,1)}, u32[]{:S(2)}, u32[]{:S(2)}) collective-permute-start(bf16[4,96,768]{2,1,0:T(8,128)(2,1)} %pad_maximum_fusion.8), channel_id=1, source_target_pairs={{2,0},{3,1},{0,2},{1,3},{6,4},{7,5},{4,6},{5,7},{10,8},{11,9},{8,1... | collective-permute-start | bytes 1769480 | tf_op jit(solution)/shard_map/ppermute | solution.py:41
  101.1 36.4 %collective-permute-start.18 = (bf16[8,48,1920]{2,1,0:T(8,128)(2,1)}, bf16[8,48,1920]{2,1,0:T(8,128)(2,1)}, u32[]{:S(2)}, u32[]{:S(2)}) collective-permute-start(bf16[8,48,1920]{2,1,0:T(8,128)(2,1)} %constant_dynamic-update-slice_fusion.refs_0_), channel_id=1, source_target_pairs={{2,0},{3,1},{0,2},{1,3},{6,4},{7,5},{4,6},{5,7},{10,8},{11,9},{8,1... | collective-permute-start | bytes 4423688 | tf_op jit(solution)/shard_map/ppermute | solution.py:41
  136.5 97.2 %collective-permute-start.10 = (bf16[192,512]{1,0:T(8,128)(2,1)}, bf16[192,512]{1,0:T(8,128)(2,1)}, u32[]{:S(2)}, u32[]{:S(2)}) collective-permute-start(bf16[192,512]{1,0:T(8,128)(2,1)} %get-tuple-element.35), channel_id=1, source_target_pairs={{1,0},{0,1},{3,2},{2,3},{5,4},{4,5},{7,6},{6,7},{9,8},{8,9},{11,10... | collective-permute-start | bytes 589832 | tf_op jit(solution)/shard_map/ppermute | solution.py:41
  137.2 114.1 %collective-permute-start.12 = (bf16[192,512]{1,0:T(8,128)(2,1)}, bf16[192,512]{1,0:T(8,128)(2,1)}, u32[]{:S(2)}, u32[]{:S(2)}) collective-permute-start(bf16[192,512]{1,0:T(8,128)(2,1)} %get-tuple-element.33), channel_id=1, source_target_pairs={{3,0},{2,1},{1,2},{0,3},{7,4},{6,5},{5,6},{4,7},{11,8},{10,9},{9,1... | collective-permute-start | bytes 589832 | tf_op jit(solution)/shard_map/ppermute | solution.py:41
  137.5 113.8 %collective-permute-start.11 = (bf16[192,512]{1,0:T(8,128)(2,1)}, bf16[192,512]{1,0:T(8,128)(2,1)}, u32[]{:S(2)}, u32[]{:S(2)}) collective-permute-start(bf16[192,512]{1,0:T(8,128)(2,1)} %get-tuple-element.34), channel_id=1, source_target_pairs={{2,0},{3,1},{0,2},{1,3},{6,4},{7,5},{4,6},{5,7},{10,8},{11,9},{8,1... | collective-permute-start | bytes 589832 | tf_op jit(solution)/shard_map/ppermute | solution.py:41
  231.7 22.4 %collective-permute-start.19 = (bf16[768,384]{1,0:T(8,128)(2,1)S(1)}, bf16[768,384]{1,0:T(8,128)(2,1)S(1)}, u32[]{:S(2)}, u32[]{:S(2)}) collective-permute-start(bf16[768,384]{1,0:T(8,128)(2,1)S(1)} %slice.113), channel_id=1, source_target_pairs={{1,0},{0,1},{3,2},{2,3},{5,4},{4,5},{7,6},{6,7},{9,8},{8,9},{11,10... | collective-permute-start | bytes 1769480 | tf_op jit(solution)/shard_map/ppermute | solution.py:41
  233.7 43.6 %collective-permute-start.25 = (bf16[8,96,768]{2,1,0:T(8,128)(2,1)}, bf16[8,96,768]{2,1,0:T(8,128)(2,1)}, u32[]{:S(2)}, u32[]{:S(2)}) collective-permute-start(bf16[8,96,768]{2,1,0:T(8,128)(2,1)} %constant_dynamic-update-slice_fusion.5.refs_0_), channel_id=1, source_target_pairs={{4,0},{5,1},{6,2},{7,3},{0,4},{1,5},{2,6},{3,7},{12,8},{13,9},{14,... | collective-permute-start | bytes 3538952 | tf_op jit(solution)/shard_map/ppermute | solution.py:41
  268.6 82.1 %collective-permute-start.20 = (bf16[512,768]{1,0:T(8,128)(2,1)}, bf16[512,768]{1,0:T(8,128)(2,1)}, u32[]{:S(2)}, u32[]{:S(2)}) collective-permute-start(bf16[512,768]{1,0:T(8,128)(2,1)} %multiply_convert_fusion.2), channel_id=1, source_target_pairs={{1,0},{0,1},{3,2},{2,3},{5,4},{4,5},{7,6},{6,7},{9,8},{8,9},{11,10... | collective-permute-start | bytes 2359304 | tf_op jit(solution)/shard_map/ppermute | solution.py:41
  372.0 109.3 %collective-permute-start.54 = (bf16[4,2,96,768]{3,2,0,1:T(8,128)(2,1)}, bf16[4,2,96,768]{3,2,0,1:T(8,128)(2,1)}, u32[]{:S(2)}, u32[]{:S(2)}) collective-permute-start(bf16[4,2,96,768]{3,2,0,1:T(8,128)(2,1)} %bitcast.226), channel_id=1, source_target_pairs={{4,0},{5,1},{6,2},{7,3},{0,4},{1,5},{2,6},{3,7},{12,8},{13,9},{14,... | collective-permute-start | bytes 3538952 | tf_op jit(solution)/shard_map/ppermute | solution.py:41
  376.6 8.1 %collective-permute-start.26 = (bf16[512,768]{1,0:T(8,128)(2,1)S(1)}, bf16[512,768]{1,0:T(8,128)(2,1)S(1)}, u32[]{:S(2)}, u32[]{:S(2)}) collective-permute-start(bf16[512,768]{1,0:T(8,128)(2,1)S(1)} %slice.168), channel_id=1, source_target_pairs={{1,0},{0,1},{3,2},{2,3},{5,4},{4,5},{7,6},{6,7},{9,8},{8,9},{11,10... | collective-permute-start | bytes 2359304 | tf_op jit(solution)/shard_map/ppermute | solution.py:41
  376.7 6.1 %collective-permute-start.28 = (bf16[512,768]{1,0:T(8,128)(2,1)S(1)}, bf16[512,768]{1,0:T(8,128)(2,1)S(1)}, u32[]{:S(2)}, u32[]{:S(2)}) collective-permute-start(bf16[512,768]{1,0:T(8,128)(2,1)S(1)} %slice.167), channel_id=1, source_target_pairs={{1,0},{0,1},{3,2},{2,3},{5,4},{4,5},{7,6},{6,7},{9,8},{8,9},{11,10... | collective-permute-start | bytes 2359304 | tf_op jit(solution)/shard_map/ppermute | solution.py:41
  382.6 102.6 %collective-permute-start.48 = (bf16[4,2,48,1536]{3,2,1,0:T(8,128)(2,1)}, bf16[4,2,48,1536]{3,2,1,0:T(8,128)(2,1)}, u32[]{:S(2)}, u32[]{:S(2)}) collective-permute-start(bf16[4,2,48,1536]{3,2,1,0:T(8,128)(2,1)} %dynamic-slice_bitcast_fusion), channel_id=1, source_target_pairs={{2,0},{3,1},{0,2},{1,3},{6,4},{7,5},{4,6},{5,7},{10,8},{11,9},{8,1... | collective-permute-start | bytes 3538952 | tf_op jit(solution)/shard_map/ppermute | solution.py:41
  389.3 25.0 %collective-permute-start.31 = (bf16[192,512]{1,0:T(8,128)(2,1)}, bf16[192,512]{1,0:T(8,128)(2,1)}, u32[]{:S(2)}, u32[]{:S(2)}) collective-permute-start(bf16[192,512]{1,0:T(8,128)(2,1)} %get-tuple-element.29), channel_id=1, source_target_pairs={{3,0},{2,1},{1,2},{0,3},{7,4},{6,5},{5,6},{4,7},{11,8},{10,9},{9,1... | collective-permute-start | bytes 589832 | tf_op jit(solution)/shard_map/ppermute | solution.py:41
  389.3 30.1 %collective-permute-start.30 = (bf16[192,512]{1,0:T(8,128)(2,1)}, bf16[192,512]{1,0:T(8,128)(2,1)}, u32[]{:S(2)}, u32[]{:S(2)}) collective-permute-start(bf16[192,512]{1,0:T(8,128)(2,1)} %get-tuple-element.30), channel_id=1, source_target_pairs={{2,0},{3,1},{0,2},{1,3},{6,4},{7,5},{4,6},{5,7},{10,8},{11,9},{8,1... | collective-permute-start | bytes 589832 | tf_op jit(solution)/shard_map/ppermute | solution.py:41
  391.0 28.4 %collective-permute-start.29 = (bf16[192,512]{1,0:T(8,128)(2,1)}, bf16[192,512]{1,0:T(8,128)(2,1)}, u32[]{:S(2)}, u32[]{:S(2)}) collective-permute-start(bf16[192,512]{1,0:T(8,128)(2,1)} %get-tuple-element.31), channel_id=1, source_target_pairs={{1,0},{0,1},{3,2},{2,3},{5,4},{4,5},{7,6},{6,7},{9,8},{8,9},{11,10... | collective-permute-start | bytes 589832 | tf_op jit(solution)/shard_map/ppermute | solution.py:41
  414.2 75.8 %collective-permute-start.41 = (bf16[768,384]{1,0:T(8,128)(2,1)}, bf16[768,384]{1,0:T(8,128)(2,1)}, u32[]{:S(2)}, u32[]{:S(2)}) collective-permute-start(bf16[768,384]{1,0:T(8,128)(2,1)} %bitcast.266), channel_id=1, source_target_pairs={{1,0},{0,1},{3,2},{2,3},{5,4},{4,5},{7,6},{6,7},{9,8},{8,9},{11,10... | collective-permute-start | bytes 1769480 | tf_op jit(solution)/shard_map/ppermute | solution.py:41
  421.9 28.6 %copy-start.20 = (bf16[512,768]{1,0:T(8,128)(2,1)S(1)}, bf16[512,768]{1,0:T(8,128)(2,1)}, u32[]{:S(2)}) copy-start(bf16[512,768]{1,0:T(8,128)(2,1)} %copy-done.19) | copy-start | bytes 2359300
  421.9 28.6 %copy-start.22 = (bf16[512,768]{1,0:T(8,128)(2,1)S(1)}, bf16[512,768]{1,0:T(8,128)(2,1)}, u32[]{:S(2)}) copy-start(bf16[512,768]{1,0:T(8,128)(2,1)} %copy-done.21) | copy-start | bytes 2359300
  457.6 30.2 %collective-permute-start.34 = (bf16[4,96,576]{2,1,0:T(8,128)(2,1)S(1)}, bf16[4,96,576]{2,1,0:T(8,128)(2,1)S(1)}, u32[]{:S(2)}, u32[]{:S(2)}) collective-permute-start(bf16[4,96,576]{2,1,0:T(8,128)(2,1)S(1)} %dynamic-slice_bitcast_fusion.3), channel_id=1, source_target_pairs={{4,0},{5,1},{6,2},{7,3},{0,4},{1,5},{2,6},{3,7},{12,8},{13,9},{14,... | collective-permute-start | bytes 1327112 | tf_op jit(solution)/shard_map/ppermute | solution.py:41
  481.4 63.1 %collective-permute-start.32 = (bf16[2,512,768]{2,1,0:T(8,128)(2,1)}, bf16[2,512,768]{2,1,0:T(8,128)(2,1)}, u32[]{:S(2)}, u32[]{:S(2)}) collective-permute-start(bf16[2,512,768]{2,1,0:T(8,128)(2,1)} %slice_bitcast_fusion), channel_id=1, source_target_pairs={{1,0},{0,1},{3,2},{2,3},{5,4},{4,5},{7,6},{6,7},{9,8},{8,9},{11,10... | collective-permute-start | bytes 4718600 | tf_op jit(solution)/shard_map/ppermute | solution.py:41
  484.9 43.2 %collective-permute-start.55 = (bf16[4,96,768]{2,1,0:T(8,128)(2,1)}, bf16[4,96,768]{2,1,0:T(8,128)(2,1)}, u32[]{:S(2)}, u32[]{:S(2)}) collective-permute-start(bf16[4,96,768]{2,1,0:T(8,128)(2,1)} %dynamic-slice_bitcast_fusion.1), channel_id=1, source_target_pairs={{2,0},{3,1},{0,2},{1,3},{6,4},{7,5},{4,6},{5,7},{10,8},{11,9},{8,1... | collective-permute-start | bytes 1769480 | tf_op jit(solution)/shard_map/ppermute | solution.py:41
  487.9 6.2 %collective-permute-start.35 = (bf16[96,576]{1,0:T(8,128)(2,1)S(1)}, bf16[96,576]{1,0:T(8,128)(2,1)S(1)}, u32[]{:S(2)}, u32[]{:S(2)}) collective-permute-start(bf16[96,576]{1,0:T(8,128)(2,1)S(1)} %get-tuple-element.42), channel_id=1, source_target_pairs={{8,0},{9,1},{10,2},{11,3},{12,4},{13,5},{14,6},{15,7},{16,8},{17,9... | collective-permute-start | bytes 331784 | tf_op jit(solution)/shard_map/ppermute | solution.py:41
  488.6 8.6 %collective-permute-start.37 = (bf16[96,576]{1,0:T(8,128)(2,1)S(1)}, bf16[96,576]{1,0:T(8,128)(2,1)S(1)}, u32[]{:S(2)}, u32[]{:S(2)}) collective-permute-start(bf16[96,576]{1,0:T(8,128)(2,1)S(1)} %get-tuple-element.43), channel_id=1, source_target_pairs={{24,0},{25,1},{26,2},{27,3},{28,4},{29,5},{30,6},{31,7},{0,8},{1,9... | collective-permute-start | bytes 331784 | tf_op jit(solution)/shard_map/ppermute | solution.py:41
  490.0 11.8 %collective-permute-start.36 = (bf16[96,576]{1,0:T(8,128)(2,1)S(1)}, bf16[96,576]{1,0:T(8,128)(2,1)S(1)}, u32[]{:S(2)}, u32[]{:S(2)}) collective-permute-start(bf16[96,576]{1,0:T(8,128)(2,1)S(1)} %get-tuple-element.44), channel_id=1, source_target_pairs={{16,0},{17,1},{18,2},{19,3},{20,4},{21,5},{22,6},{23,7},{24,8},{25... | collective-permute-start | bytes 331784 | tf_op jit(solution)/shard_map/ppermute | solution.py:41
  502.5 4.3 collective-permute-start.40
  502.5 5.8 %collective-permute-start.39 = (f32[24,576]{1,0:T(8,128)S(1)}, f32[24,576]{1,0:T(8,128)S(1)}, u32[]{:S(2)}, u32[]{:S(2)}) collective-permute-start(f32[24,576]{1,0:T(8,128)S(1)} %get-tuple-element.49), channel_id=1, source_target_pairs={{2,0},{3,1},{0,2},{1,3},{6,4},{7,5},{4,6},{5,7},{10,8},{11,9},{8,1... | collective-permute-start | bytes 165896 | tf_op jit(solution)/shard_map/ppermute | solution.py:41
  504.2 4.8 collective-permute-start.38
  506.8 16.5 %collective-permute-start.49 = (bf16[4,48,1536]{2,1,0:T(8,128)(2,1)}, bf16[4,48,1536]{2,1,0:T(8,128)(2,1)}, u32[]{:S(2)}, u32[]{:S(2)}) collective-permute-start(bf16[4,48,1536]{2,1,0:T(8,128)(2,1)} %dynamic-slice_bitcast_fusion.2), channel_id=1, source_target_pairs={{4,0},{5,1},{6,2},{7,3},{0,4},{1,5},{2,6},{3,7},{12,8},{13,9},{14,... | collective-permute-start | bytes 1769480 | tf_op jit(solution)/shard_map/ppermute | solution.py:41
  508.4 9.3 %collective-permute-start.42 = (bf16[4,2,48,384]{3,2,1,0:T(8,128)(2,1)}, bf16[4,2,48,384]{3,2,1,0:T(8,128)(2,1)}, u32[]{:S(2)}, u32[]{:S(2)}) collective-permute-start(bf16[4,2,48,384]{3,2,1,0:T(8,128)(2,1)} %dynamic-slice_bitcast_fusion.4), channel_id=1, source_target_pairs={{2,0},{3,1},{0,2},{1,3},{6,4},{7,5},{4,6},{5,7},{10,8},{11,9},{8,1... | collective-permute-start | bytes 884744 | tf_op jit(solution)/shard_map/ppermute | solution.py:41
  518.8 7.1 %collective-permute-start.43 = (bf16[4,48,384]{2,1,0:T(8,128)(2,1)S(1)}, bf16[4,48,384]{2,1,0:T(8,128)(2,1)S(1)}, u32[]{:S(2)}, u32[]{:S(2)}) collective-permute-start(bf16[4,48,384]{2,1,0:T(8,128)(2,1)S(1)} %dynamic-slice_bitcast_fusion.15), channel_id=1, source_target_pairs={{4,0},{5,1},{6,2},{7,3},{0,4},{1,5},{2,6},{3,7},{12,8},{13,9},{14,... | collective-permute-start | bytes 442376 | tf_op jit(solution)/shard_map/ppermute | solution.py:41
  524.6 17.6 %collective-permute-start.50 = (bf16[48,1536]{1,0:T(8,128)(2,1)S(1)}, bf16[48,1536]{1,0:T(8,128)(2,1)S(1)}, u32[]{:S(2)}, u32[]{:S(2)}) collective-permute-start(bf16[48,1536]{1,0:T(8,128)(2,1)S(1)} %get-tuple-element.39), channel_id=1, source_target_pairs={{8,0},{9,1},{10,2},{11,3},{12,4},{13,5},{14,6},{15,7},{16,8},{17,9... | collective-permute-start | bytes 442376 | tf_op jit(solution)/shard_map/ppermute | solution.py:41
  526.0 4.2 collective-permute-start.44
  527.1 6.2 %collective-permute-start.46 = (bf16[48,384]{1,0:T(8,128)(2,1)S(1)}, bf16[48,384]{1,0:T(8,128)(2,1)S(1)}, u32[]{:S(2)}, u32[]{:S(2)}) collective-permute-start(bf16[48,384]{1,0:T(8,128)(2,1)S(1)} %get-tuple-element.54), channel_id=1, source_target_pairs={{24,0},{25,1},{26,2},{27,3},{28,4},{29,5},{30,6},{31,7},{0,8},{1,9... | collective-permute-start | bytes 110600 | tf_op jit(solution)/shard_map/ppermute | solution.py:41
  528.1 12.1 %collective-permute-start.45 = (bf16[48,384]{1,0:T(8,128)(2,1)S(1)}, bf16[48,384]{1,0:T(8,128)(2,1)S(1)}, u32[]{:S(2)}, u32[]{:S(2)}) collective-permute-start(bf16[48,384]{1,0:T(8,128)(2,1)S(1)} %get-tuple-element.55), channel_id=1, source_target_pairs={{16,0},{17,1},{18,2},{19,3},{20,4},{21,5},{22,6},{23,7},{24,8},{25... | collective-permute-start | bytes 110600 | tf_op jit(solution)/shard_map/ppermute | solution.py:41
  530.2 14.0 %collective-permute-start.52 = (bf16[48,1536]{1,0:T(8,128)(2,1)S(1)}, bf16[48,1536]{1,0:T(8,128)(2,1)S(1)}, u32[]{:S(2)}, u32[]{:S(2)}) collective-permute-start(bf16[48,1536]{1,0:T(8,128)(2,1)S(1)} %get-tuple-element.40), channel_id=1, source_target_pairs={{24,0},{25,1},{26,2},{27,3},{28,4},{29,5},{30,6},{31,7},{0,8},{1,9... | collective-permute-start | bytes 442376 | tf_op jit(solution)/shard_map/ppermute | solution.py:41
  533.3 10.9 %collective-permute-start.51 = (bf16[48,1536]{1,0:T(8,128)(2,1)S(1)}, bf16[48,1536]{1,0:T(8,128)(2,1)S(1)}, u32[]{:S(2)}, u32[]{:S(2)}) collective-permute-start(bf16[48,1536]{1,0:T(8,128)(2,1)S(1)} %get-tuple-element.41), channel_id=1, source_target_pairs={{16,0},{17,1},{18,2},{19,3},{20,4},{21,5},{22,6},{23,7},{24,8},{25... | collective-permute-start | bytes 442376 | tf_op jit(solution)/shard_map/ppermute | solution.py:41
  540.3 1.3 collective-permute-start.47
  541.5 9.0 %collective-permute-start.56 = (bf16[96,768]{1,0:T(8,128)(2,1)S(1)}, bf16[96,768]{1,0:T(8,128)(2,1)S(1)}, u32[]{:S(2)}, u32[]{:S(2)}) collective-permute-start(bf16[96,768]{1,0:T(8,128)(2,1)S(1)} %get-tuple-element.36), channel_id=1, source_target_pairs={{8,0},{9,1},{10,2},{11,3},{12,4},{13,5},{14,6},{15,7},{16,8},{17,9... | collective-permute-start | bytes 442376 | tf_op jit(solution)/shard_map/ppermute | solution.py:41
  542.2 8.6 %collective-permute-start.58 = (bf16[96,768]{1,0:T(8,128)(2,1)S(1)}, bf16[96,768]{1,0:T(8,128)(2,1)S(1)}, u32[]{:S(2)}, u32[]{:S(2)}) collective-permute-start(bf16[96,768]{1,0:T(8,128)(2,1)S(1)} %get-tuple-element.37), channel_id=1, source_target_pairs={{24,0},{25,1},{26,2},{27,3},{28,4},{29,5},{30,6},{31,7},{0,8},{1,9... | collective-permute-start | bytes 442376 | tf_op jit(solution)/shard_map/ppermute | solution.py:41
  544.2 12.1 %collective-permute-start.57 = (bf16[96,768]{1,0:T(8,128)(2,1)S(1)}, bf16[96,768]{1,0:T(8,128)(2,1)S(1)}, u32[]{:S(2)}, u32[]{:S(2)}) collective-permute-start(bf16[96,768]{1,0:T(8,128)(2,1)S(1)} %get-tuple-element.38), channel_id=1, source_target_pairs={{16,0},{17,1},{18,2},{19,3},{20,4},{21,5},{22,6},{23,7},{24,8},{25... | collective-permute-start | bytes 442376 | tf_op jit(solution)/shard_map/ppermute | solution.py:41
  544.4 12.7 %collective-permute-start.53 = (f32[24,1536]{1,0:T(8,128)S(1)}, f32[24,1536]{1,0:T(8,128)S(1)}, u32[]{:S(2)}, u32[]{:S(2)}) collective-permute-start(f32[24,1536]{1,0:T(8,128)S(1)} %get-tuple-element.45), channel_id=1, source_target_pairs={{1,0},{0,1},{3,2},{2,3},{5,4},{4,5},{7,6},{6,7},{9,8},{8,9},{11,10... | collective-permute-start | bytes 442376 | tf_op jit(solution)/shard_map/ppermute | solution.py:41
  547.3 20.1 %collective-permute-start.33 = (bf16[512,768]{1,0:T(8,128)(2,1)}, bf16[512,768]{1,0:T(8,128)(2,1)S(1)}, u32[]{:S(2)}, u32[]{:S(2)}) collective-permute-start(bf16[512,768]{1,0:T(8,128)(2,1)} %slice_bitcast_fusion.2), channel_id=1, source_target_pairs={{2,0},{3,1},{0,2},{1,3},{6,4},{7,5},{4,6},{5,7},{10,8},{11,9},{8,1... | collective-permute-start | bytes 2359304 | tf_op jit(solution)/shard_map/ppermute | solution.py:41
  (44 other events, 367.7 us)

commit v2 on v1

v2 whole, which is shorter than its diff:
```python
import functools
import math

import jax
import jax.numpy as jnp
from jax import lax
from jax.experimental import pallas as pl
from jax.experimental.pallas import tpu as pltpu
from jax.sharding import PartitionSpec as P

HEADS = 12
HEAD_DIM = 64
BLK = 128
SEQ_UNIT = 1024
epsilon = 1e-05
f32 = jnp.float32
bf16 = jnp.bfloat16


class Grid:
    def __init__(self, nb, nk):
        nhi = math.gcd(4, nb)
        nc = math.gcd(2, nk)
        self.sizes = {"hi": nhi, "lo": nb // nhi, "x": nk // nc, "c": nc}
        self.nb, self.nk = nb, nk
        pb, ka = lax.axis_index("pb"), lax.axis_index("ka")
        self.pb, self.ka = pb, ka
        self.at = {"hi": pb // self.sizes["lo"], "lo": pb % self.sizes["lo"], "x": ka // nc, "c": ka % nc}

    def fetch(self, value, flip=0, **steps):
        n = self.sizes
        pairs = []
        for hi in range(n["hi"]):
            for lo in range(n["lo"]):
                for x in range(n["x"]):
                    for c in range(n["c"]):
                        here = {"hi": hi, "lo": lo, "x": x, "c": c}
                        there = {d: here[d] ^ steps[d] if flip and d in steps else (here[d] + steps.get(d, 0)) % n[d] for d in here}
                        flat = [((p["hi"] * n["lo"] + p["lo"]) * n["x"] + p["x"]) * n["c"] + p["c"] for p in (there, here)]
                        pairs.append(tuple(flat))
        return lax.ppermute(value, ("pb", "ka"), pairs)

    def gather(self, value, dim):
        return jnp.stack([value] + [self.fetch(value, **{dim: r}) for r in range(1, self.sizes[dim])])

    def in_order(self, pieces, dim):
        n, me = self.sizes[dim], self.at[dim]
        if n == 1:
            return pieces
        if n == 2:
            return [jnp.where(me == 0, pieces[0], pieces[1]), jnp.where(me == 0, pieces[1], pieces[0])]
        stacked = jnp.stack(pieces)
        return [lax.dynamic_index_in_dim(stacked, (i - me) % n, 0, keepdims=False) for i in range(n)]

    def group_in_order(self, pieces):
        nx, nc = self.sizes["x"], self.sizes["c"]
        by_x = [self.in_order(pieces[i * nc : (i + 1) * nc], "c") for i in range(nx)]
        by_c = [self.in_order([row[c] for row in by_x], "x") for c in range(nc)]
        return [by_c[c][x] for x in range(nx) for c in range(nc)]

    def split(self, parts, axis, dim):
        n, me = self.sizes[dim], self.at[dim]
        own = lax.dynamic_index_in_dim(parts, me, axis, keepdims=False)
        return own, [lax.dynamic_index_in_dim(parts, (me - r) % n, axis, keepdims=False) for r in range(1, n)]

    def halve(self, parts, dim, bit):
        mine = (self.at[dim] >> bit) % 2
        parts = parts.reshape((2, -1) + parts.shape[1:])
        kept = lax.dynamic_index_in_dim(parts, mine, 0, keepdims=False)
        return kept, lax.dynamic_index_in_dim(parts, 1 - mine, 0, keepdims=False)

    def swap(self, value, dim, bit):
        return self.fetch(value, 1, **{dim: 1 << bit})

    def send(self, sends, dim):
        return [self.fetch(sent, **{dim: r + 1}) for r, sent in enumerate(sends)]


def added(own, received, last=False):
    total = own.astype(f32)
    for one in received:
        total = total + one.astype(f32)
    return total if last else total.astype(own.dtype)


def together(*values):
    return lax.optimization_barrier(values)


def place_kernel(counts, rows, offs_ref, *refs):
    ins, out_ref, sems = refs[: len(counts)], refs[len(counts)], refs[len(counts) + 1]
    copies = []
    for ref, count in zip(ins, counts):
        for i in range(count):
            at = pl.multiple_of(offs_ref[len(copies)], rows)
            copies.append(pltpu.make_async_copy(ref.at[i], out_ref.at[pl.ds(at, rows), :], sems.at[len(copies)]))
    for copy in copies:
        copy.start()
    for copy in copies:
        copy.wait()


def place(stacks, offsets):
    rows, cols = stacks[0].shape[1:]
    counts = [s.shape[0] for s in stacks]
    total = sum(counts)
    return pl.pallas_call(
        functools.partial(place_kernel, counts, rows),
        out_shape=jax.ShapeDtypeStruct((total * rows, cols), stacks[0].dtype),
        in_specs=[pl.BlockSpec(memory_space=pltpu.SMEM)] + [pl.BlockSpec(memory_space=pl.ANY)] * len(stacks),
        out_specs=pl.BlockSpec(memory_space=pltpu.VMEM),
        scratch_shapes=[pltpu.SemaphoreType.DMA((total,))],
        compiler_params=pltpu.CompilerParams(vmem_limit_bytes=16 * 2**20),
        cost_estimate=pl.CostEstimate(flops=10**6, bytes_accessed=10**5, transcendentals=0),
    )(offsets.astype(jnp.int32), *stacks)


def tie(value, *before):
    return lax.optimization_barrier((value,) + before)[0]


def gather_rows(grid, piece, order, gates=None, begun=None, done=("hi",)):
    if begun is None:
        stack, steps = piece[None], [dict()]
    else:
        stack, steps = begun, [dict()]
        for dim in done:
            steps = steps + [{**s, dim: r} for r in range(1, grid.sizes[dim]) for s in steps]
        piece = stack[0]
    stacks = []
    received = {}
    for dim in order:
        if gates and dim in gates:
            stack = tie(stack, *gates[dim])
        got = [grid.fetch(stack, **{dim: r}) for r in range(1, grid.sizes[dim])]
        received[dim] = got
        steps = steps + [{**s, dim: r} for r in range(1, grid.sizes[dim]) for s in steps]
        if dim == order[-1]:
            stacks = [stack] + got
        else:
            stack = jnp.concatenate([stack] + got, axis=0)
    dims = [d for d in ("hi", "lo", "x") if d in order or (begun is not None and d in done)]
    rows = piece.shape[0]
    index = []
    for s in steps:
        at = 0
        for d in dims:
            at = at * grid.sizes[d] + (grid.at[d] + s.get(d, 0)) % grid.sizes[d]
        index.append(at)
    index = jnp.stack(index)
    if gates and "place" in gates:
        stacks, _ = together(stacks, gates["place"])
    if rows % 16 == 0:
        return place(stacks, index * rows), received
    order_back = jnp.argsort(index)
    out = jnp.concatenate(stacks, axis=0)
    out = jnp.concatenate([lax.dynamic_index_in_dim(out, order_back[i], 0, keepdims=False) for i in range(len(steps))], axis=0)
    return out, received


def lane_tile(at, size):
    return pl.ds(pl.multiple_of(at, BLK), size)


def head_rows(sets, kind, head):
    at = 0
    for one in sets:
        if head in one:
            return slice(at + (kind * len(one) + one.index(head)) * HEAD_DIM, at + (kind * len(one) + one.index(head) + 1) * HEAD_DIM)
        at += 3 * len(one) * HEAD_DIM


def pipeline(work, first, second, third):
    held = {}
    for t in range(len(work) + 2):
        if t < len(work):
            held[t] = first(work[t])
        if 1 <= t <= len(work):
            held[t - 1] = second(work[t - 1], held[t - 1])
        if t >= 2:
            third(work[t - 2], held.pop(t - 2))


def spans_to(begin, end, chunk):
    spans = []
    while begin < end:
        size = min(chunk, end - begin)
        spans.append((begin, size, begin + size == end))
        begin += size
    return spans


def forward_kernel(sets, tile, chunk, unit, meta_ref, qkv_ref, out_ref, att_ref, lse_ref, sorted_ref, keys_ref):
    heads = sum(len(one) for one in sets)
    row_len = qkv_ref.shape[1]
    blocks = row_len // BLK
    per_device = out_ref.shape[2] // BLK
    for b in range(blocks):
        sorted_ref[:, b * BLK : (b + 1) * BLK] = qkv_ref[:, lane_tile(meta_ref[b] * BLK, BLK)]
    for h in range(heads):
        keys_ref[h] = sorted_ref[head_rows(sets, 1, h), :].astype(f32).T.astype(bf16)
    doc_units = meta_ref[blocks] // unit
    seen = lax.broadcasted_iota(jnp.int32, (tile, tile), 0) <= lax.broadcasted_iota(jnp.int32, (tile, tile), 1)
    lse_ref[...] = jnp.zeros_like(lse_ref)
    for i in range(row_len // tile):
        lanes = slice(i * tile, (i + 1) * tile)
        queries = [sorted_ref[head_rows(sets, 0, h), lanes] for h in range(heads)]

        def run(spans, carry):
            carry = list(carry)

            def first(item):
                h, begin, size, _ = item
                return jnp.dot(keys_ref[h, pl.ds(begin, size), :], queries[h], preferred_element_type=f32)

            def second(item, scores):
                h, _, size, diagonal = item
                peak, total, acc = carry[h]
                square = scores * scores + 1.0
                inverse = lax.rsqrt(square)
                reach = square * inverse
                if diagonal:
                    low = jnp.where(seen, reach[size - tile :], -1e30)
                    reach = low if size == tile else jnp.concatenate([reach[: size - tile], low], axis=0)
                top = jnp.maximum(peak, jnp.max(reach, axis=0, keepdims=True))
                shares = jnp.exp(reach - top)
                fade = jnp.exp(peak - top)
                total = total * fade + jnp.sum(shares, axis=0, keepdims=True)
                carry[h] = (top, total, acc)
                return (shares * (scores * inverse)).astype(bf16), fade

            def third(item, kept):
                h, begin, size, _ = item
                mixing, fade = kept
                top, total, acc = carry[h]
                values = sorted_ref[head_rows(sets, 2, h), pl.ds(begin, size)]
                carry[h] = (top, total, acc * fade + jnp.dot(values, mixing, preferred_element_type=f32))

            pipeline([(h,) + span for span in spans for h in range(heads)], first, second, third)
            return tuple(carry)

        here = i * tile // unit
        start = (jnp.ones((1, tile), f32), jnp.zeros((1, tile), f32), jnp.zeros((HEAD_DIM, tile), f32))
        carry = run(spans_to(here * unit, (i + 1) * tile, chunk), (start,) * heads)
        if here > 0:

            def earlier(k, carry):
                base = pl.multiple_of(k * unit, unit)
                return run([(base + o, chunk, False) for o in range(0, unit, chunk)], carry)

            carry = lax.fori_loop(here // doc_units * doc_units, here, earlier, carry)
        for h in range(heads):
            peak, total, acc = carry[h]
            rows = slice(h * HEAD_DIM, (h + 1) * HEAD_DIM)
            result = acc / total
            att_ref[rows, lanes] = result
            lse_ref[h : h + 1, lanes] = peak + jnp.log(total)
            low = result.astype(bf16)
            for part in range(tile // BLK):
                spot = meta_ref[i * (tile // BLK) + part]
                out_ref[spot // per_device, rows, lane_tile((spot % per_device) * BLK, BLK)] = low[:, part * BLK : (part + 1) * BLK]


def forward_attention(meta, qkv, sets, devices):
    row_len = qkv.shape[1]
    heads = sum(len(one) for one in sets)
    width = heads * HEAD_DIM
    whole = pl.BlockSpec(memory_space=pltpu.VMEM)
    return pl.pallas_call(
        functools.partial(forward_kernel, sets, 256, 512, SEQ_UNIT),
        out_shape=(
            jax.ShapeDtypeStruct((devices, width, row_len // devices), bf16),
            jax.ShapeDtypeStruct((width, row_len), f32),
            jax.ShapeDtypeStruct((8, row_len), f32),
        ),
        in_specs=[pl.BlockSpec(memory_space=pltpu.SMEM), whole],
        out_specs=(whole, whole, whole),
        scratch_shapes=[pltpu.VMEM((3 * width, row_len), bf16), pltpu.VMEM((heads, row_len, HEAD_DIM), bf16)],
        compiler_params=pltpu.CompilerParams(vmem_limit_bytes=40 * 2**20),
        cost_estimate=pl.CostEstimate(
            flops=10**6, bytes_accessed=10**5, transcendentals=0),
    )(meta, qkv)


def backward_kernel(
    sets, which, tile, chunk, unit, meta_ref, qkv_ref, up_ref, att_ref, lse_ref, grad_ref, sorted_ref, ups_ref, nat_ref, stat_ref, dq_ref, dkv_ref
):
    heads = sets[which]
    count = len(heads)
    row_len = qkv_ref.shape[1]
    width = count * HEAD_DIM
    blocks = row_len // BLK
    per_device = up_ref.shape[2] // BLK
    base_row = head_rows(sets, 0, heads[0]).start
    ups_rows = slice(heads[0] * HEAD_DIM, (heads[-1] + 1) * HEAD_DIM)
    for b in range(blocks):
        spot = slice(b * BLK, (b + 1) * BLK)
        sorted_ref[:, spot] = qkv_ref[base_row : base_row + 3 * width, lane_tile(meta_ref[b] * BLK, BLK)]
        ups_ref[:, spot] = up_ref[meta_ref[b] // per_device, ups_rows, lane_tile((meta_ref[b] % per_device) * BLK, BLK)]
    own = [slice(h * HEAD_DIM, (h + 1) * HEAD_DIM) for h in range(3 * count)]
    for h in range(count):
        for part in range(2):
            nat_ref[part * count + h] = sorted_ref[own[part * count + h], :].astype(f32).T.astype(bf16)
        upstream = ups_ref[own[h], :].astype(f32)
        nat_ref[2 * count + h] = upstream.T.astype(bf16)
        att = att_ref[heads[h] * HEAD_DIM : (heads[h] + 1) * HEAD_DIM, :]
        delta = jnp.sum(upstream * att, axis=0, keepdims=True)
        stats = [lse_ref[heads[h] : heads[h] + 1, :], delta, jnp.zeros((6, row_len), f32)]
        stat_ref[h] = jnp.concatenate(stats, axis=0).T
    dkv_ref[...] = jnp.zeros_like(dkv_ref)
    doc_units = meta_ref[blocks] // unit
    seen = lax.broadcasted_iota(jnp.int32, (tile, tile), 0) >= lax.broadcasted_iota(jnp.int32, (tile, tile), 1)
    for i in range(row_len // tile):
        at = slice(i * tile, (i + 1) * tile)

        def run(spans, carry):
            carry = list(carry)

            def first(item):
                h, begin, size, _ = item
                lanes = pl.ds(begin, size)
                scores = jnp.dot(nat_ref[h, at, :], sorted_ref[own[count + h], lanes], preferred_element_type=f32)
                effect = jnp.dot(nat_ref[2 * count + h, at, :], sorted_ref[own[2 * count + h], lanes], preferred_element_type=f32)
                return scores, effect

            def second(item, kept):
                h, _, size, diagonal = item
                scores, effect = kept
                square = scores * scores + 1.0
                inverse = lax.rsqrt(square)
                shares = jnp.exp(square * inverse - stat_ref[h, at, 0:1])
                if diagonal:
                    low = jnp.where(seen, shares[:, size - tile :], 0.0)
                    shares = low if size == tile else jnp.concatenate([shares[:, : size - tile], low], axis=1)
                sign = scores * inverse
                twice = inverse * inverse
                grad = shares * (effect * (1.0 - twice + twice * inverse) - stat_ref[h, at, 1:2] * sign)
                return grad.astype(bf16), (shares * sign).astype(bf16)

            def third(item, kept):
                h, begin, size, _ = item
                grad, mixing = kept
                lanes = pl.ds(begin, size)
                carry[h] = carry[h] + jnp.dot(grad, nat_ref[count + h, pl.ds(begin, size), :], preferred_element_type=f32)
                dkv_ref[own[h], lanes] += jnp.dot(sorted_ref[own[h], at], grad, preferred_element_type=f32)
                dkv_ref[own[count + h], lanes] += jnp.dot(ups_ref[own[h], at], mixing, preferred_element_type=f32)

            pipeline([(h,) + span for span in spans for h in range(count)], first, second, third)
            return tuple(carry)

        here = i * tile // unit
        carry = run(spans_to(here * unit, (i + 1) * tile, chunk), (jnp.zeros((tile, HEAD_DIM), f32),) * count)
        if here > 0:

            def earlier(k, carry):
                base = pl.multiple_of(k * unit, unit)
                return run([(base + o, chunk, False) for o in range(0, unit, chunk)], carry)

            carry = lax.fori_loop(here // doc_units * doc_units, here, earlier, carry)
        dq_ref[at, :] = carry[0] if count == 1 else jnp.concatenate(carry, axis=1)
    scale = HEAD_DIM**-0.5
    for b in range(blocks):
        here = slice(b * BLK, (b + 1) * BLK)
        both = jnp.concatenate([dq_ref[here, :] * scale, dkv_ref[:, here].T], axis=1)
        grad_ref[pl.ds(pl.multiple_of(meta_ref[b] * BLK, BLK), BLK), :] = both.astype(bf16)


def backward_attention(meta, qkv, upstream, att, lse, sets, which):
    row_len = qkv.shape[1]
    count = len(sets[which])
    width = count * HEAD_DIM
    whole = pl.BlockSpec(memory_space=pltpu.VMEM)
    return pl.pallas_call(
        functools.partial(backward_kernel, sets, which, 256, 256, SEQ_UNIT),
        out_shape=jax.ShapeDtypeStruct((row_len, 3 * width), bf16),
        in_specs=[pl.BlockSpec(memory_space=pltpu.SMEM)] + [whole] * 4,
        out_specs=whole,
        scratch_shapes=[
            pltpu.VMEM((3 * width, row_len), bf16),
            pltpu.VMEM((width, row_len), bf16),
            pltpu.VMEM((3 * count, row_len, HEAD_DIM), bf16),
            pltpu.VMEM((count, row_len, 8), f32),
            pltpu.VMEM((row_len, width), f32),
            pltpu.VMEM((2 * width, row_len), f32),
        ],
        compiler_params=pltpu.CompilerParams(vmem_limit_bytes=48 * 2**20),
        cost_estimate=pl.CostEstimate(
            flops=10**6, bytes_accessed=10**5, transcendentals=0),
    )(meta, qkv, upstream, att, lse)


def project_kernel(sets, gain_lane, count, *refs):
    weight_ref, h1_ref, qkv_ref, turned_ref, gain_ref = refs[count:]
    columns = qkv_ref.shape[0]

    @pl.when(pl.program_id(0) == 0)
    def _():
        turned = weight_ref[...].astype(f32).T
        gain_ref[...] = turned[gain_lane : gain_lane + 8]
        turned = turned[:columns]
        for one in sets:
            begin = head_rows(sets, 0, one[0]).start
            end = begin + len(one) * HEAD_DIM
            stop = begin + 3 * len(one) * HEAD_DIM
            turned_ref[begin:end] = (turned[begin:end] * HEAD_DIM**-0.5).astype(bf16)
            turned_ref[end:stop] = turned[end:stop].astype(bf16)

    for i in range(count):

        @pl.when(pl.program_id(0) == i)
        def _(tokens_ref=refs[i]):
            values = tokens_ref[...].astype(f32)
            centered = values - jnp.mean(values, axis=-1, keepdims=True)
            inverse = lax.rsqrt(jnp.mean(centered * centered, axis=-1, keepdims=True) + epsilon)
            h1 = (centered * inverse * gain_ref[0:1]).T.astype(bf16)
            h1_ref[...] = h1
            qkv_ref[...] = jnp.dot(turned_ref[...], h1, preferred_element_type=f32).astype(bf16)


def project(pieces, weight, sets):
    step, model = pieces[0].shape
    count = len(pieces)
    row_len = count * step
    columns = 3 * HEAD_DIM * sum(len(one) for one in sets)
    return pl.pallas_call(
        functools.partial(project_kernel, sets, columns, count),
        grid=(count,),
        out_shape=(jax.ShapeDtypeStruct((model, row_len), bf16), jax.ShapeDtypeStruct((columns, row_len), bf16)),
        in_specs=[pl.BlockSpec((step, model), lambda i: (0, 0))] * count + [pl.BlockSpec(weight.shape, lambda i: (0, 0))],
        out_specs=(pl.BlockSpec((model, step), lambda i: (0, i)), pl.BlockSpec((columns, step), lambda i: (0, i))),
        scratch_shapes=[pltpu.VMEM((columns, model), bf16), pltpu.VMEM((8, model), f32)],
        compiler_params=pltpu.CompilerParams(vmem_limit_bytes=40 * 2**20),
        cost_estimate=pl.CostEstimate(flops=10**6, bytes_accessed=10**5, transcendentals=0),
    )(*pieces, weight)


def rows_kernel(count, strides, me_ref, left_ref, right_ref, *refs):
    outs, total_ref = refs[:-1], refs[-1]
    total_ref[...] = jnp.dot(left_ref[...], right_ref[...], preferred_element_type=f32)
    outer, inner = strides
    rows = outs[0].shape[-2]
    for r in range(count):
        entry = (me_ref[0] + count - r) % count
        for a in range(outer):
            for b in range(inner):
                at = pl.multiple_of(((a * count + entry) * inner + b) * rows, 8)
                outs[r][a, b] = total_ref[pl.ds(at, rows), :].astype(bf16)


def split_product(grid, left, right, dim, with_x=False):
    rows_all, cols = left.shape[0], right.shape[1]
    outer = grid.sizes["hi"] if dim == "lo" else grid.nb
    inner = grid.sizes["x"] if dim == "lo" and with_x else 1
    count = grid.sizes[dim]
    rows = rows_all // (outer * inner * count)
    whole = pl.BlockSpec(memory_space=pltpu.VMEM)
    outs = pl.pallas_call(
        functools.partial(rows_kernel, count, (outer, inner)),
        out_shape=tuple(jax.ShapeDtypeStruct((outer, inner, rows, cols), bf16) for _ in range(count)),
        in_specs=[pl.BlockSpec(memory_space=pltpu.SMEM), whole, whole],
        out_specs=(whole,) * count,
        scratch_shapes=[pltpu.VMEM((rows_all, cols), f32)],
        compiler_params=pltpu.CompilerParams(vmem_limit_bytes=48 * 2**20),
        cost_estimate=pl.CostEstimate(flops=10**6, bytes_accessed=10**5, transcendentals=0),
    )(grid.at[dim].reshape(1).astype(jnp.int32), left, right)
    if inner == 1:
        outs = [one.reshape(outer, rows, cols) for one in outs]
    return outs[0], list(outs[1:])


def back_kernel(bounds, count, *refs):
    parts, weight_ref, outs = refs[:count], refs[count], refs[count + 1 :]
    pieces, rows = outs[0].shape[0], outs[0].shape[1]
    for x in range(pieces):
        for c, out_ref in enumerate(outs):
            here = slice((x * len(outs) + c) * rows, (x * len(outs) + c + 1) * rows)
            total = 0.0
            for i in range(count):
                weight = weight_ref[:, bounds[i] : bounds[i + 1]]
                total = total + lax.dot_general(parts[i][here, :], weight, (((1,), (1,)), ((), ())), preferred_element_type=f32)
            out_ref[x] = total.astype(bf16)


def back_project(grid, parts, weight, bounds):
    nx, nc = grid.sizes["x"], grid.sizes["c"]
    rows = parts[0].shape[0] // (nx * nc)
    whole = pl.BlockSpec(memory_space=pltpu.VMEM)
    return pl.pallas_call(
        functools.partial(back_kernel, bounds, len(parts)),
        out_shape=tuple(jax.ShapeDtypeStruct((nx, rows, weight.shape[0]), bf16) for _ in range(nc)),
        in_specs=[whole] * (len(parts) + 1),
        out_specs=(whole,) * nc,
        compiler_params=pltpu.CompilerParams(vmem_limit_bytes=48 * 2**20),
        cost_estimate=pl.CostEstimate(flops=10**6, bytes_accessed=10**5, transcendentals=0),
    )(*parts, weight)


def norm_parts(values):
    centered = values - jnp.mean(values, axis=-1, keepdims=True)
    inverse = lax.rsqrt(jnp.mean(centered * centered, axis=-1, keepdims=True) + epsilon)
    return centered * inverse, inverse


def norm_back(normed, inverse, gain, grad):
    c = grad * gain
    return (c - jnp.mean(c, axis=-1, keepdims=True) - normed * jnp.mean(c * normed, axis=-1, keepdims=True)) * inverse


def mm(a, b, dims):
    return lax.dot_general(a, b, ((dims[:1], dims[1:]), ((), ())), preferred_element_type=f32)


def body(
    tokens,
    lengths,
    block_place,
    qkv_weight,
    out_weight,
    up_weight,
    down_weight,
    attn_gain,
    mlp_gain,
    cotangent,
):
    nb, nk = lax.axis_size("pb"), lax.axis_size("ka")
    grid = Grid(nb, nk)
    nx, nc = grid.sizes["x"], grid.sizes["c"]
    x_at, c_at = grid.at["x"], grid.at["c"]
    tok_rows, model = tokens.shape
    shard = qkv_weight.shape[0]
    chips = nb * nx
    heads = -(-HEADS // nk)
    width = heads * HEAD_DIM
    lanes = -(-(3 * width + 2) // BLK) * BLK
    rels = [(xr, cr) for xr in range(nx) for cr in range(nc)]

    def ka_of(xr, cr):
        return ((x_at + xr) % nx) * nc + (c_at + cr) % nc

    def exchange(parts):
        got = [parts(grid.ka)]
        for xr, cr in rels[1:]:
            got.append(grid.fetch(parts(ka_of(-xr, -cr)), x=xr, c=cr))
        return got

    cut = max(1, heads - 1)
    sets = [tuple(range(cut)), tuple(range(cut, heads))] if heads > 1 else [(0,)]
    bounds = [0]
    for one in sets:
        bounds.append(bounds[-1] + 3 * len(one) * HEAD_DIM)

    def head_groups(weight):
        split = weight.reshape(weight.shape[0], 3, HEADS, HEAD_DIM)
        if heads * nk != HEADS:
            split = jnp.pad(split, ((0, 0), (0, 0), (0, heads * nk - HEADS), (0, 0)))
        split = split.reshape(-1, 3, nk, heads, HEAD_DIM)
        chosen = [split[:, :, :, one[0] : one[-1] + 1].transpose(2, 0, 1, 3, 4).reshape(nk, weight.shape[0], -1) for one in sets]
        return jnp.concatenate(chosen, axis=2)

    gains = jnp.stack([attn_gain, mlp_gain], axis=1)
    gains = jnp.pad(gains, ((0, 0), (0, lanes - 3 * width - 2)))
    own_qkv = jnp.concatenate([head_groups(qkv_weight), jnp.broadcast_to(gains[None], (nk,) + gains.shape)], axis=2)
    got = exchange(lambda ka: lax.dynamic_index_in_dim(own_qkv, ka, 0, keepdims=False))
    group_qkv = jnp.concatenate(grid.group_in_order(got), axis=0)

    first_tokens = tie(tokens, *got)
    by_x = [tokens] + [grid.fetch(first_tokens, x=r) for r in range(1, nx)]
    got_hi = [grid.fetch(group_qkv[None], hi=r) for r in range(1, grid.sizes["hi"])]
    stack = tie(jnp.stack(by_x), *got_hi)
    by_c = [by_x] + [list(grid.fetch(stack, c=r)) for r in range(1, nc)]
    row_tokens = [by_c[c][x] for x in range(nx) for c in range(nc)]
    full_qkv, _ = gather_rows(grid, None, ("lo",), {"place": row_tokens}, jnp.concatenate([group_qkv[None]] + got_hi, axis=0))

    full_out = lax.all_gather(tie(out_weight, *got_hi), ("pb", "ka"), axis=0, tiled=True)

    strip = down_weight.shape[0]
    up_split = jnp.transpose(up_weight.reshape(shard, chips, nc, strip), (2, 0, 1, 3)).reshape(nc, shard, chips * strip)
    own, sends = grid.split(up_split, 0, "c")
    up_part = jnp.concatenate(grid.in_order([own] + grid.send(sends, "c"), "c"), axis=0)
    folds = chips * strip // model
    up_part = jnp.concatenate([up_part[:, i * model : (i + 1) * model] for i in range(folds)], axis=0)
    both = tie(jnp.concatenate([up_part, down_weight], axis=0), *got_hi, *by_x)
    both = grid.gather(both, "hi")

    slots = tok_rows // BLK
    holder = jnp.argsort(block_place[0]).astype(jnp.int32)
    holder_ka, holder_slot = holder // slots, holder % slots
    rel = ((holder_ka // nc - x_at) % nx) * nc + (holder_ka % nc - c_at) % nc
    meta = jnp.concatenate([rel * slots + holder_slot, lengths[0, :1]]).astype(jnp.int32)

    gain_one = full_qkv[:, 3 * width].astype(f32)
    gain_two = full_qkv[:, 3 * width + 1].astype(f32)
    inputs = tokens.astype(f32)
    h1, qkv = project(row_tokens, full_qkv, sets)
    row_len = h1.shape[1]
    both = tie(both, qkv)
    up_rows = up_part.shape[0]
    up_stack, down_stack = both[:, :up_rows], both[:, up_rows:]
    up_stack = jnp.concatenate([up_stack] + [grid.fetch(up_stack, lo=r) for r in range(1, grid.sizes["lo"])], axis=0)
    down_stack = jnp.concatenate([down_stack] + [grid.fetch(down_stack, x=r) for r in range(1, nx)], axis=0)
    att_parts, att_row, lse = forward_attention(meta, tie(qkv, both), sets, nk)
    att_parts, up_stack, down_stack = together(att_parts, up_stack, down_stack)
    full_up, _ = gather_rows(grid, None, ("x",), begun=up_stack, done=("hi", "lo"))
    full_up = jnp.transpose(full_up.reshape(chips, folds, nc * shard, model), (0, 2, 1, 3)).reshape(model, folds * model)
    full_down, _ = gather_rows(grid, None, ("lo",), begun=down_stack, done=("hi", "x"))

    got = [att_parts[0]]
    for xr, cr in rels[1:]:
        got.append(grid.fetch(att_parts[((-xr) % nx) * nc + (-cr) % nc], x=xr, c=cr))
    att = jnp.concatenate(grid.group_in_order(got), axis=0)[: HEADS * HEAD_DIM]

    late_cot = tie(cotangent, att_parts)
    cots = jnp.concatenate([cotangent] + [grid.fetch(late_cot, c=r) for r in range(1, nc)], axis=0)
    residual = inputs + mm(att, full_out, (0, 0))
    normed_two, inverse_two = norm_parts(residual)
    h2 = (normed_two * gain_two).astype(bf16)
    h2s = jnp.concatenate([h2] + [grid.fetch(h2, c=r) for r in range(1, nc)], axis=0)

    def core_sum(part):
        pieces = part.reshape((nc, tok_rows) + part.shape[1:])
        total = pieces[0]
        for r in range(1, nc):
            total = total + grid.fetch(pieces[(nc - r) % nc].astype(bf16), c=r).astype(f32)
        return total

    hidden_pre = mm(h2s, full_up, (1, 0))
    hidden_act, gelu_back = jax.vjp(lambda v: jax.nn.gelu(v, approximate=True), hidden_pre)
    hidden_low = hidden_act.astype(bf16)
    (grad_pre,) = gelu_back(mm(cots, full_down, (1, 1)))
    grad_pre = grad_pre.astype(bf16)
    grad_h2 = core_sum(mm(grad_pre, full_up, (1, 1)))
    grad_up = mm(h2s, grad_pre, (0, 0)).astype(bf16)
    grad_residual = cotangent.astype(f32) + norm_back(normed_two, inverse_two, gain_two, grad_h2)
    grad_res_low = grad_residual.astype(bf16)
    grad_att = mm(full_out, grad_res_low, (1, 1)).astype(bf16)
    if heads * nk != HEADS:
        grad_att = jnp.pad(grad_att, ((0, (heads * nk - HEADS) * HEAD_DIM), (0, 0)))
    grad_att = grad_att.reshape(nk, width, tok_rows)
    upstream = jnp.stack(exchange(lambda ka: lax.dynamic_index_in_dim(grad_att, ka, 0, keepdims=False)))
    grad_down = mm(hidden_low, cots, (0, 0)).astype(bf16)
    grad_out = mm(att, grad_res_low, (1, 0)).astype(bf16)
    mixed = (residual + core_sum(mm(hidden_low, full_down, (1, 0)))).astype(bf16)

    n = grid.sizes

    def placed(grad):
        return grad.reshape(n["hi"], n["lo"], n["x"], -1, grad.shape[1])

    up_own, up_send = grid.split(placed(grad_up), 1, "lo")
    up_got = grid.send(up_send, "lo")
    sum_out = lax.psum_scatter(grad_out, ("pb", "ka"), scatter_dimension=0, tiled=True)
    down_own, down_send = grid.split(placed(grad_down), 2, "x")
    down_send, _ = together(down_send, upstream)
    down_got = grid.send(down_send, "x")

    parts, qkv_rest, qkv_got = [], [], []
    last = len(sets) - 1
    for which in range(len(sets)):
        part = backward_attention(meta, qkv, upstream, att_row, lse, sets, which)
        if which == last:
            part, down_got, qkv_got = together(part, down_got, qkv_got)
        parts.append(part)
        own, sends = split_product(grid, h1, part, "lo")
        qkv_rest.append(own)
        if which < last:
            qkv_got.append(grid.send(sends, "lo"))
        if which == 0:
            up_own, up_send = grid.split(added(up_own, up_got), 0, "hi")
            up_got = grid.send(up_send, "hi")
            upstream, *_ = together(upstream, *sends, *up_send)

    qkv_got.append(grid.send(sends, "lo"))
    down_own, down_send = grid.split(added(down_own, down_got), 1, "lo")
    down_send, _ = together(down_send, sends)
    down_got = grid.send(down_send, "lo")
    grad_h1 = back_project(grid, parts, full_qkv, bounds)
    h1_send = [grad_h1[(nc - r) % nc] for r in range(1, nc)]

    sums = [added(own, got) for own, got in zip(qkv_rest, qkv_got)]
    by_kind = []
    for kind in range(3):
        for i, one in enumerate(sets):
            begin = kind * len(one) * HEAD_DIM
            by_kind.append(sums[i][:, :, begin : begin + len(one) * HEAD_DIM])
    qkv_own, qkv_send = grid.split(jnp.concatenate(by_kind, axis=2), 0, "hi")
    up_got, qkv_send, h1_send = together(up_got, qkv_send, h1_send)
    up_own, up_send = grid.split(added(up_own, up_got), 0, "x")
    qkv_got = grid.send(qkv_send, "hi")
    h1_got = grid.send(h1_send, "c")
    up_got = grid.send(up_send, "x")
    h1_own = added(grad_h1[0], h1_got)
    h1_send = [h1_own[(nx - r) % nx] for r in range(1, nx)]
    up_own, up_send = grid.split(added(up_own, up_got, True).reshape(nc, shard, -1), 0, "c")
    h1_send, up_send = together(h1_send, up_send)
    h1_got = grid.send(h1_send, "x")
    up_got = grid.send(up_send, "c")

    down_own, down_send = grid.split(added(down_own, down_got), 0, "hi")
    group_grad = added(qkv_own, qkv_got, True).reshape(nx, nc, shard, 3 * width)
    group_grad, down_send, up_got = together(group_grad, down_send, up_got)
    group_own, group_send = grid.split(group_grad, 0, "x")
    by_x = grid.in_order([group_own] + grid.send(group_send, "x"), "x")
    down_got = grid.send(down_send, "hi")
    group_own, group_send = grid.split(jnp.stack(by_x), 1, "c")
    by_c = grid.in_order([group_own] + grid.send(group_send, "c"), "c")
    got = [by_c[c][x] for x in range(nx) for c in range(nc)]
    sum_up = grid.in_order([up_own] + up_got, "c")

    kept = min(nk * width, HEADS * HEAD_DIM)
    sum_qkv = []
    for kind in range(3):
        for i, one in enumerate(got):
            size = min(width, kept - i * width)
            if size > 0:
                sum_qkv.append(one[:, kind * width : kind * width + size])
    sum_qkv = jnp.concatenate(sum_qkv, axis=1)
    sum_up = jnp.stack([one.reshape(shard, chips, strip) for one in sum_up], axis=2).reshape(shard, -1)
    sum_down = added(down_own, down_got, True)
    normed_one, inverse_one = norm_parts(inputs)
    tokens_grad = added(h1_own[0], h1_got, True)
    tokens_grad = (grad_residual + norm_back(normed_one, inverse_one, gain_one, tokens_grad)).astype(bf16)

    grad_gain_one = jnp.sum(sum_qkv * qkv_weight.astype(f32), axis=1) / attn_gain.astype(f32)
    grad_gain_two = jnp.sum(sum_up * up_weight.astype(f32), axis=1) / mlp_gain.astype(f32)
    sum_out = tie(sum_out, tokens_grad).astype(f32)
    return (mixed, tokens_grad, sum_qkv, sum_out, sum_up, sum_down, grad_gain_one, grad_gain_two)


def solution(mesh):
    rows = P(("pb", "ka"), None)
    flat = P(("pb", "ka"))
    group = P("pb", None)
    return jax.shard_map(
        body,
        mesh=mesh,
        in_specs=(rows, group, group, rows, rows, rows, rows, flat, flat, rows),
        out_specs=(rows, rows, rows, rows, rows, rows, flat, flat),
        check_vma=False,
    )
```

time: 576 us -> 325 us (0.56)
  Pallas kernels: 246 us -> 73.9 us
  starting transfers between devices: 80.5 us -> 49.7 us
  local copies, waits for them, and re-layouts: 56 us -> 32.6 us
  other arithmetic: 53 us -> 32.1 us
  between operations: 2 us -> 15.8 us
  matrix products: 43.5 us -> 31.6 us
    pallas_call x3, Pallas kernels: 196 us -> 8.01 us  [place(): pl.pallas_call(functools.partial(place_kernel, counts, rows), out_shape=j...]
    ppermute x59 -> x47, starting transfers between devices: 80.5 us -> 49.5 us  [fetch(): return lax.ppermute(value, ('pb', 'ka'), pairs)]
    pallas_call x2 -> x7, Pallas kernels: 49.9 us -> 65.9 us  [the longest x2 34.5 us: backward_attention(): pl.pallas_call(functools.partial(backward_kernel, sets, which, 256, 256,...]
    dot_general x12 -> x9, matrix products: 43.5 us -> 31.6 us  [mm(): lax.dot_general(a, b, ((dims[:1], dims[1:]), ((), ())), preferred_element...]
    concatenate x13 -> x5, other arithmetic: 12.7 us -> 4.78 us  [the longest x1 1.93 us: body(): jnp.concatenate([down_stack] + [grid.fetch(down_stack, x=r) for r in rang...]
    unnamed x110 -> x101, local copies, waits for them, and re-layouts: 17.6 us -> 10.8 us
    ppermute x59 -> x47, waiting for transfers between devices: 90 us -> 86.6 us  [fetch(): return lax.ppermute(value, ('pb', 'ka'), pairs)]
    convert_element_type x11 -> x10, other arithmetic: 13.2 us -> 10.2 us  [the longest x7 6.9 us: added(): return total if last else total.astype(own.dtype)]
  transfers between devices with their start and end apart: 59 -> 49, of which waited for: 24 -> 14; matrix products, arithmetic and copies ran while one was open for 21% -> 21% of each run, Pallas kernels for 43% -> 23%
where the time goes in v2:
time: 325 us; the launch traced here: 322 us
  waiting for transfers between devices  86.6 us (27%)
  Pallas kernels  73.9 us (23%)
  starting transfers between devices  49.7 us (15%)
  local copies, waits for them, and re-layouts  32.6 us (10%)
  other arithmetic  32.1 us (10%)
  matrix products  31.6 us (10%)
  between operations  15.8 us (5%)
    ppermute x47, waiting for transfers between devices, fetch(): return lax.ppermute(value, ('pb', 'ka'), pairs)  86.6 us
    ppermute x47, starting transfers between devices, fetch(): return lax.ppermute(value, ('pb', 'ka'), pairs)  49.5 us
    pallas_call x2, Pallas kernels, backward_attention(): pl.pallas_call(functools.partial(backward_kernel, sets, which, 256, 256,...  34.5 us
    dot_general x9, matrix products, mm(): lax.dot_general(a, b, ((dims[:1], dims[1:]), ((), ())), preferred_element...  31.6 us
    pallas_call x1, Pallas kernels, forward_attention(): pl.pallas_call(functools.partial(forward_kernel, sets, 256, 512, SEQ_UNIT...  18.9 us
    unnamed x101, local copies, waits for them, and re-layouts  10.8 us
    pallas_call x3, Pallas kernels, place(): pl.pallas_call(functools.partial(place_kernel, counts, rows), out_shape=j...  8.01 us
    convert_element_type x7, other arithmetic, added(): return total if last else total.astype(own.dtype)  6.9 us
  transfers between devices with their start and end apart: 49, of which 14 were waited for; matrix products, arithmetic and copies ran while one was open for 21% of the time, Pallas kernels for 23%

profile of v2, /device:TPU:0, one launch (start us, length us, event | category | flops | bytes accessed | tf_op | source)
XLA Modules:
  0.0 322.3 jit_solution(3030999434810740179)
XLA Ops:
  10.2 2.4 collective-permute-start.2
  14.3 2.2 collective-permute-done.1
  17.6 1.6 collective-permute-start.6
  19.2 2.6 collective-permute-start.5
  21.8 1.3 collective-permute-start.4
  23.2 12.7 %collective-permute-done.3.refs_2_ = bf16[512,768]{1,0:T(8,128)(2,1)S(1)} collective-permute-done((bf16[512,768]{1,0:T(8,128)(2,1)S(1)}, bf16[512,768]{1,0:T(8,128)(2,1)S(1)}, u32[]{:S(2)}, u32[]{:S(2)}) %collective-permute-start.3) | collective-permute-done | bytes 786464 | tf_op jit(solution)/shard_map/ppermute | solution.py:41
  38.2 2.2 collective-permute-done.9
  41.2 1.6 collective-permute-start.12
  42.8 2.6 collective-permute-start.11
  45.3 1.3 collective-permute-start.10
  47.7 1.6 collective-permute-start.8
  49.5 3.8 %collective-permute-done.12 = bf16[192,768]{1,0:T(8,128)(2,1)} collective-permute-done((bf16[192,768]{1,0:T(8,128)(2,1)}, bf16[192,768]{1,0:T(8,128)(2,1)}, u32[]{:S(2)}, u32[]{:S(2)}) %collective-permute-start.12) | collective-permute-done | bytes 294944 | tf_op jit(solution)/shard_map/ppermute | solution.py:41
  53.3 12.3 %collective-permute-done.11 = bf16[192,768]{1,0:T(8,128)(2,1)} collective-permute-done((bf16[192,768]{1,0:T(8,128)(2,1)}, bf16[192,768]{1,0:T(8,128)(2,1)}, u32[]{:S(2)}, u32[]{:S(2)}) %collective-permute-start.11) | collective-permute-done | bytes 294944 | tf_op jit(solution)/shard_map/ppermute | solution.py:41
  65.6 1.4 pad_maximum_fusion.2
  67.0 1.5 slice_bitcast_fusion.2
  68.5 1.9 shard_map.161.refs_4_.refs_2_
  70.4 5.4 %shard_map.162 = (bf16[768,2048]{1,0:T(8,128)(2,1)S(1)}, bf16[576,2048]{1,0:T(8,128)(2,1)S(1)}) custom-call(bf16[512,768]{1,0:T(8,128)(2,1)S(1)} %copy-done, bf16[512,768]{1,0:T(8,128)(2,1)S(1)} %get-tuple-element.111.refs_1_, bf16[512,768]{1,0:T(8,128)(2,1)S(1)} %copy-done.12, bf16[512,768]{1,0:T(8,128)(2,1)S(1)} %get-tuple-element.110.refs_3_, ...), custom_call_target="tpu_custom_call" | custom-call | flops 1000000 | bytes 100000 | tf_op jit(solution)/shard_map/pallas_call | solution.py:425
  75.9 1.6 copy-done.4
  78.7 1.2 collective-permute-start.14
  79.9 1.2 sort.17
  81.1 1.5 collective-permute-start.13
  83.0 18.9 %shard_map.163 = (bf16[4,192,512]{2,1,0:T(8,128)(2,1)S(1)}, f32[192,2048]{1,0:T(8,128)S(1)}, f32[8,2048]{1,0:T(8,128)S(1)}) custom-call(s32[17]{0:T(128)S(1)} %pad_add_fusion.meta_ref, bf16[576,2048]{1,0:T(8,128)(2,1)S(1)} %get-tuple-element.61.qkv_ref), custom_call_target="tpu_custom_call" | custom-call | flops 1000000 | bytes 100000 | tf_op jit(solution)/shard_map/pallas_call | solution.py:269
  101.9 1.9 pad_maximum_fusion.4.refs_0_
  106.1 1.2 collective-permute-start.16
  108.6 3.3 %collective-permute-done.17 = bf16[192,512]{1,0:T(8,128)(2,1)S(1)} collective-permute-done((bf16[192,512]{1,0:T(8,128)(2,1)S(1)}, bf16[192,512]{1,0:T(8,128)(2,1)S(1)}, u32[]{:S(2)}, u32[]{:S(2)}) %collective-permute-start.17) | collective-permute-done | bytes 196640 | tf_op jit(solution)/shard_map/ppermute | solution.py:41
  111.8 5.3 %collective-permute-done.16 = bf16[192,512]{1,0:T(8,128)(2,1)S(1)} collective-permute-done((bf16[192,512]{1,0:T(8,128)(2,1)S(1)}, bf16[192,512]{1,0:T(8,128)(2,1)S(1)}, u32[]{:S(2)}, u32[]{:S(2)}) %collective-permute-start.16) | collective-permute-done | bytes 196640 | tf_op jit(solution)/shard_map/ppermute | solution.py:41
  118.0 2.4 fusion.65
  121.9 2.1 constant_dynamic-update-slice_fusion.1
  124.6 2.1 constant_dynamic-update-slice_fusion
  126.7 15.3 %collective-permute-done.19.refs_1_ = bf16[8,96,768]{2,1,0:T(8,128)(2,1)} collective-permute-done((bf16[8,96,768]{2,1,0:T(8,128)(2,1)}, bf16[8,96,768]{2,1,0:T(8,128)(2,1)}, u32[]{:S(2)}, u32[]{:S(2)}) %collective-permute-start.19) | collective-permute-done | bytes 1179680 | tf_op jit(solution)/shard_map/ppermute | solution.py:41
  142.0 2.4 shard_map.164
  144.4 2.2 copy.46
  147.0 3.7 %shard_map.165 = bf16[1536,768]{1,0:T(8,128)(2,1)S(1)} custom-call(s32[16]{0:T(128)S(1)} %broadcast_multiply_fusion.6.offs_ref, bf16[8,96,768]{2,1,0:T(8,128)(2,1)S(1)} %pad_maximum_fusion.4.refs_0_, bf16[8,96,768]{2,1,0:T(8,128)(2,1)} %collective-permute-done.20.refs_1_), custom_call_target="tpu_custom_call" | custom-call | flops 1000000 | bytes 100000 | tf_op jit(solution)/shard_map/pallas_call | solution.py:107
  150.8 4.0 %fusion.25 = f32[1024,1536]{1,0:T(8,128)S(1)} fusion(bf16[768,1536]{1,0:T(8,128)(2,1)S(1)} %bitcast.229, bf16[512,768]{1,0:T(8,128)(2,1)} %collective-permute-done.18, bf16[512,768]{1,0:T(8,128)(2,1)} %multiply_convert_fusion.1), kind=kOutput, calls=%fused_computation.57 | convolution fusion | flops 2419064832 | bytes 10223616 | tf_op jit(solution)/shard_map/dot_general | solution.py:510
  154.8 3.8 %fusion.57 = f32[1024,768]{1,0:T(8,128)S(1)} fusion(bf16[1536,768]{1,0:T(8,128)(2,1)S(1)} %shard_map.165, f32[1024,1536]{1,0:T(8,128)S(1)} %fusion.25), kind=kOutput, calls=%fused_computation.206 | convolution fusion | flops 2430074880 | bytes 11796480 | tf_op jit(solution)/shard_map/dot_general | solution.py:510
  158.5 6.4 %fusion.6 = bf16[1024,1536]{1,0:T(8,128)(2,1)S(1)} fusion(f32[1024,1536]{1,0:T(8,128)S(1)} %fusion.25, bf16[1024,768]{1,0:T(8,128)(2,1)S(1)} %copy-done.34, bf16[1536,768]{1,0:T(8,128)(2,1)S(1)} %shard_map.165), kind=kOutput, calls=%fused_computation.8 | convolution fusion | flops 2447376384 | bytes 13369344 | tf_op jit(solution)/shard_map/dot_general | solution.py:510
  164.9 2.6 fusion.66
  168.3 4.3 %convolution_convert_fusion.1 = bf16[768,1536]{1,0:T(8,128)(2,1)S(1)} fusion(bf16[1024,1536]{1,0:T(8,128)(2,1)S(1)} %fusion.6, bf16[512,768]{1,0:T(8,128)(2,1)} %collective-permute-done.18, bf16[512,768]{1,0:T(8,128)(2,1)} %multiply_convert_fusion.1), kind=kOutput, calls=%fused_computation.11 | convolution fusion | flops 2420244480 | bytes 7077888 | tf_op jit(solution)/shard_map/dot_general | solution.py:510
  173.8 1.4 copy-done.15
  175.9 2.8 multiply_add_fusion
  181.5 4.0 %convolution_convert_fusion = bf16[1536,768]{1,0:T(8,128)(2,1)S(1)} fusion(bf16[1024,768]{1,0:T(8,128)(2,1)S(1)} %copy-done.34, f32[1024,1536]{1,0:T(8,128)S(1)} %fusion.25), kind=kOutput, calls=%fused_computation.10 | convolution fusion | flops 2431254528 | bytes 10223616 | tf_op jit(solution)/shard_map/dot_general | solution.py:510
  187.9 3.2 collective-permute-done.25
  192.7 3.4 %convolution_convert_fusion.2 = bf16[768,768]{1,0:T(8,128)(2,1)} fusion(f32[512,768]{1,0:T(8,128)} %copy-done.18, bf16[192,512]{1,0:T(8,128)(2,1)} %get-tuple-element.115, bf16[192,512]{1,0:T(8,128)(2,1)S(1)} %copy-done.39, bf16[192,512]{1,0:T(8,128)(2,1)S(1)} %copy-done.38, bf16[192,512]{1,0:T(8,128)(2,1)S(1)} %get-tuple-element.112), kind=kOutput, calls=%fused_computation.45 | convolution fusion | flops 608108544 | bytes 3538944 | tf_op jit(solution)/shard_map/dot_general | solution.py:510
  196.1 1.4 copy-done.9
  197.5 22.5 %shard_map.166.right_ref.refs_0_ = bf16[2048,384]{1,0:T(8,128)(2,1)S(1)} custom-call(s32[17]{0:T(128)S(1)} %pad_add_fusion.meta_ref, bf16[576,2048]{1,0:T(8,128)(2,1)} %copy-done.1, bf16[4,192,512]{2,1,0:T(8,128)(2,1)S(1)} %pad_maximum_fusion.8.up_ref, f32[192,2048]{1,0:T(8,128)S(1)} %copy-done.9, f32[8,2048]{1,0:T(8,128)S(1)} %get-tuple-element.69.lse_ref), custom_call_target="tpu_custom_call" | custom-call | flops 1000000 | bytes 100000 | tf_op jit(solution)/shard_map/pallas_call | solution.py:373
  220.0 1.9 shard_map.167
  222.3 1.7 fusion.8
  225.0 9.0 %collective-permute-start.31 = (bf16[2,48,1536]{2,1,0:T(8,128)(2,1)}, bf16[2,48,1536]{2,1,0:T(8,128)(2,1)}, u32[]{:S(2)}, u32[]{:S(2)}) collective-permute-start(bf16[2,48,1536]{2,1,0:T(8,128)(2,1)} %get-tuple-element.117), channel_id=1, source_target_pairs={{16,0},{17,1},{18,2},{19,3},{20,4},{21,5},{22,6},{23,7},{24,8},{25... | collective-permute-start | bytes 884744 | tf_op jit(solution)/shard_map/ppermute | solution.py:41
  234.4 12.0 %shard_map.168.refs_1_.right_ref = bf16[2048,192]{1,0:T(8,128)(2,1)S(1)} custom-call(s32[17]{0:T(128)S(1)} %pad_add_fusion.meta_ref, bf16[576,2048]{1,0:T(8,128)(2,1)S(1)} %copy-done.2, bf16[4,192,512]{2,1,0:T(8,128)(2,1)S(1)} %pad_maximum_fusion.8.up_ref, f32[192,2048]{1,0:T(8,128)S(1)} %copy-done.10, f32[8,2048]{1,0:T(8,128)S(1)} %get-tuple-element.69.lse_ref), custom_call_target="tpu_custom_call" | custom-call | flops 1000000 | bytes 100000 | tf_op jit(solution)/shard_map/pallas_call | solution.py:373
  248.2 4.2 %shard_map.169 = (bf16[2,512,768]{2,1,0:T(8,128)(2,1)S(1)}, bf16[2,512,768]{2,1,0:T(8,128)(2,1)S(1)}) custom-call(bf16[2048,384]{1,0:T(8,128)(2,1)} %copy-done.3, bf16[2048,192]{1,0:T(8,128)(2,1)S(1)} %shard_map.168.refs_1_.right_ref, bf16[768,640]{1,0:T(8,128)(2,1)S(1)} %copy-done.7), custom_call_target="tpu_custom_call" | custom-call | flops 1000000 | bytes 100000 | tf_op jit(solution)/shard_map/pallas_call | solution.py:488
  252.4 2.0 fusion.7
  255.4 1.6 collective-permute-start.40
  257.1 2.2 collective-permute-done.33
  259.9 2.8 collective-permute-start.37
  262.7 1.7 collective-permute-start.38
  264.4 1.4 fusion.28
  267.6 8.8 %collective-permute-done.38 = bf16[96,576]{1,0:T(8,128)(2,1)S(1)} collective-permute-done((bf16[96,576]{1,0:T(8,128)(2,1)S(1)}, bf16[96,576]{1,0:T(8,128)(2,1)S(1)}, u32[]{:S(2)}, u32[]{:S(2)}) %collective-permute-start.38) | collective-permute-done | bytes 110624 | tf_op jit(solution)/shard_map/ppermute | solution.py:41
  284.3 4.4 %collective-permute-start.45 = (bf16[96,768]{1,0:T(8,128)(2,1)}, bf16[96,768]{1,0:T(8,128)(2,1)}, u32[]{:S(2)}, u32[]{:S(2)}) collective-permute-start(bf16[96,768]{1,0:T(8,128)(2,1)} %get-tuple-element.96), channel_id=1, source_target_pairs={{16,0},{17,1},{18,2},{19,3},{20,4},{21,5},{22,6},{23,7},{24,8},{25... | collective-permute-start | bytes 442376 | tf_op jit(solution)/shard_map/ppermute | solution.py:41
  290.4 13.5 %collective-permute-done.42 = f32[2,24,576]{2,1,0:T(8,128)S(1)} collective-permute-done((f32[2,24,576]{2,1,0:T(8,128)S(1)}, f32[2,24,576]{2,1,0:T(8,128)S(1)}, u32[]{:S(2)}, u32[]{:S(2)}) %collective-permute-start.42) | collective-permute-done | bytes 110624 | tf_op jit(solution)/shard_map/ppermute | solution.py:41
  304.1 2.0 fusion.36
  309.5 1.3 convert_divide_fusion.1
  310.9 1.3 fusion.23
  312.3 1.6 fusion.17
  313.9 1.4 convert_element_type.274
  (264 shorter events, 47.0 us)
Async XLA Ops:
  7.2 9.4 %copy-start = (bf16[512,768]{1,0:T(8,128)(2,1)S(1)}, bf16[512,768]{1,0:T(8,128)(2,1)}, u32[]{:S(2)}) copy-start(bf16[512,768]{1,0:T(8,128)(2,1)} %refs_0_.1) | copy-start | bytes 2359300
  7.2 110.8 %all-gather.2.cloned.1.call-start = ((), (), s32[]{:S(2)}) async-start(), calls=%async_computation.1 | async-start | bytes 1216512 | tf_op jit(solution)/shard_map/all_gather | solution.py:574
  10.2 4.2 %collective-permute-start.2 = (bf16[24,640]{1,0:T(8,128)(2,1)S(1)}, bf16[24,640]{1,0:T(8,128)(2,1)S(1)}, u32[]{:S(2)}, u32[]{:S(2)}) collective-permute-start(bf16[24,640]{1,0:T(8,128)(2,1)S(1)} %get-tuple-element.155), channel_id=1, source_target_pairs={{3,0},{2,1},{1,2},{0,3},{7,4},{6,5},{5,6},{4,7},{11,8},{10,9},{9,1... | collective-permute-start | bytes 92168 | tf_op jit(solution)/shard_map/ppermute | solution.py:41
  12.6 3.9 %collective-permute-start.1 = (bf16[24,640]{1,0:T(8,128)(2,1)S(1)}, bf16[24,640]{1,0:T(8,128)(2,1)S(1)}, u32[]{:S(2)}, u32[]{:S(2)}) collective-permute-start(bf16[24,640]{1,0:T(8,128)(2,1)S(1)} %get-tuple-element.156), channel_id=1, source_target_pairs={{2,0},{3,1},{0,2},{1,3},{6,4},{7,5},{4,6},{5,7},{10,8},{11,9},{8,1... | collective-permute-start | bytes 92168 | tf_op jit(solution)/shard_map/ppermute | solution.py:41
  13.2 3.3 %collective-permute-start = (bf16[24,640]{1,0:T(8,128)(2,1)S(1)}, bf16[24,640]{1,0:T(8,128)(2,1)S(1)}, u32[]{:S(2)}, u32[]{:S(2)}) collective-permute-start(bf16[24,640]{1,0:T(8,128)(2,1)S(1)} %get-tuple-element.157), channel_id=1, source_target_pairs={{1,0},{0,1},{3,2},{2,3},{5,4},{4,5},{7,6},{6,7},{9,8},{8,9},{11,10... | collective-permute-start | bytes 92168 | tf_op jit(solution)/shard_map/ppermute | solution.py:41
  16.6 19.3 %collective-permute-start.3 = (bf16[512,768]{1,0:T(8,128)(2,1)S(1)}, bf16[512,768]{1,0:T(8,128)(2,1)S(1)}, u32[]{:S(2)}, u32[]{:S(2)}) collective-permute-start(bf16[512,768]{1,0:T(8,128)(2,1)S(1)} %copy-done), channel_id=1, source_target_pairs={{2,0},{3,1},{0,2},{1,3},{6,4},{7,5},{4,6},{5,7},{10,8},{11,9},{8,1... | collective-permute-start | bytes 2359304 | tf_op jit(solution)/shard_map/ppermute | solution.py:41
  17.6 19.2 %collective-permute-start.6 = (bf16[1,96,640]{2,1,0:T(8,128)(2,1)S(1)}, bf16[1,96,640]{2,1,0:T(8,128)(2,1)S(1)}, u32[]{:S(2)}, u32[]{:S(2)}) collective-permute-start(bf16[1,96,640]{2,1,0:T(8,128)(2,1)S(1)} %maximum_bitcast_fusion), channel_id=1, source_target_pairs={{24,0},{25,1},{26,2},{27,3},{28,4},{29,5},{30,6},{31,7},{0,8},{1,9... | collective-permute-start | bytes 368648 | tf_op jit(solution)/shard_map/ppermute | solution.py:41
  19.2 17.5 %collective-permute-start.5 = (bf16[1,96,640]{2,1,0:T(8,128)(2,1)S(1)}, bf16[1,96,640]{2,1,0:T(8,128)(2,1)S(1)}, u32[]{:S(2)}, u32[]{:S(2)}) collective-permute-start(bf16[1,96,640]{2,1,0:T(8,128)(2,1)S(1)} %maximum_bitcast_fusion), channel_id=1, source_target_pairs={{16,0},{17,1},{18,2},{19,3},{20,4},{21,5},{22,6},{23,7},{24,8},{25... | collective-permute-start | bytes 368648 | tf_op jit(solution)/shard_map/ppermute | solution.py:41
  21.8 15.0 %collective-permute-start.4 = (bf16[1,96,640]{2,1,0:T(8,128)(2,1)S(1)}, bf16[1,96,640]{2,1,0:T(8,128)(2,1)S(1)}, u32[]{:S(2)}, u32[]{:S(2)}) collective-permute-start(bf16[1,96,640]{2,1,0:T(8,128)(2,1)S(1)} %maximum_bitcast_fusion), channel_id=1, source_target_pairs={{8,0},{9,1},{10,2},{11,3},{12,4},{13,5},{14,6},{15,7},{16,8},{17,9... | collective-permute-start | bytes 368648 | tf_op jit(solution)/shard_map/ppermute | solution.py:41
  36.8 30.2 %collective-permute-start.7 = (bf16[2,512,768]{2,1,0:T(8,128)(2,1)S(1)}, bf16[2,512,768]{2,1,0:T(8,128)(2,1)}, u32[]{:S(2)}, u32[]{:S(2)}) collective-permute-start(bf16[2,512,768]{2,1,0:T(8,128)(2,1)S(1)} %pad_maximum_fusion), channel_id=1, source_target_pairs={{1,0},{0,1},{3,2},{2,3},{5,4},{4,5},{7,6},{6,7},{9,8},{8,9},{11,10... | collective-permute-start | bytes 4718600 | tf_op jit(solution)/shard_map/ppermute | solution.py:41
  37.9 2.5 collective-permute-start.9
  41.2 12.1 %collective-permute-start.12 = (bf16[192,768]{1,0:T(8,128)(2,1)}, bf16[192,768]{1,0:T(8,128)(2,1)}, u32[]{:S(2)}, u32[]{:S(2)}) collective-permute-start(bf16[192,768]{1,0:T(8,128)(2,1)} %fusion.34), channel_id=1, source_target_pairs={{24,0},{25,1},{26,2},{27,3},{28,4},{29,5},{30,6},{31,7},{0,8},{1,9... | collective-permute-start | bytes 884744 | tf_op jit(solution)/shard_map/ppermute | solution.py:41
  42.8 22.9 %collective-permute-start.11 = (bf16[192,768]{1,0:T(8,128)(2,1)}, bf16[192,768]{1,0:T(8,128)(2,1)}, u32[]{:S(2)}, u32[]{:S(2)}) collective-permute-start(bf16[192,768]{1,0:T(8,128)(2,1)} %fusion.34), channel_id=1, source_target_pairs={{16,0},{17,1},{18,2},{19,3},{20,4},{21,5},{22,6},{23,7},{24,8},{25... | collective-permute-start | bytes 884744 | tf_op jit(solution)/shard_map/ppermute | solution.py:41
  45.3 20.3 %collective-permute-start.10 = (bf16[192,768]{1,0:T(8,128)(2,1)}, bf16[192,768]{1,0:T(8,128)(2,1)}, u32[]{:S(2)}, u32[]{:S(2)}) collective-permute-start(bf16[192,768]{1,0:T(8,128)(2,1)} %fusion.34), channel_id=1, source_target_pairs={{8,0},{9,1},{10,2},{11,3},{12,4},{13,5},{14,6},{15,7},{16,8},{17,9... | collective-permute-start | bytes 884744 | tf_op jit(solution)/shard_map/ppermute | solution.py:41
  47.7 20.8 %collective-permute-start.8 = (bf16[4,96,640]{2,1,0:T(8,128)(2,1)S(1)}, bf16[4,96,640]{2,1,0:T(8,128)(2,1)S(1)}, u32[]{:S(2)}, u32[]{:S(2)}) collective-permute-start(bf16[4,96,640]{2,1,0:T(8,128)(2,1)S(1)} %pad_maximum_fusion.9.refs_0_), channel_id=1, source_target_pairs={{4,0},{5,1},{6,2},{7,3},{0,4},{1,5},{2,6},{3,7},{12,8},{13,9},{14,... | collective-permute-start | bytes 1474568 | tf_op jit(solution)/shard_map/ppermute | solution.py:41
  49.3 264.6 %reduce-scatter.2.cloned.1.call-start = ((), (), s32[]{:S(2)}) async-start(), calls=%async_computation.2 | async-start | bytes 1216512 | tf_op jit(solution)/shard_map/reduce_scatter | solution.py:651
  70.4 5.4 %copy-start.6 = (bf16[768,640]{1,0:T(8,128)(2,1)}, bf16[768,640]{1,0:T(8,128)(2,1)S(1)}, u32[]{:S(2)}) copy-start(bf16[768,640]{1,0:T(8,128)(2,1)S(1)} %shard_map.161.refs_4_.refs_2_) | copy-start | bytes 2949124
  77.5 5.5 %copy-start.1 = (bf16[576,2048]{1,0:T(8,128)(2,1)}, bf16[576,2048]{1,0:T(8,128)(2,1)S(1)}, u32[]{:S(2)}) copy-start(bf16[576,2048]{1,0:T(8,128)(2,1)S(1)} %get-tuple-element.61.qkv_ref) | copy-start | bytes 7077892
  78.7 23.2 %collective-permute-start.14 = (bf16[4,96,768]{2,1,0:T(8,128)(2,1)}, bf16[4,96,768]{2,1,0:T(8,128)(2,1)}, u32[]{:S(2)}, u32[]{:S(2)}) collective-permute-start(bf16[4,96,768]{2,1,0:T(8,128)(2,1)} %get-tuple-element.119), channel_id=1, source_target_pairs={{2,0},{3,1},{0,2},{1,3},{6,4},{7,5},{4,6},{5,7},{10,8},{11,9},{8,1... | collective-permute-start | bytes 1769480 | tf_op jit(solution)/shard_map/ppermute | solution.py:41
  81.1 22.7 %collective-permute-start.13 = (bf16[4,96,768]{2,1,0:T(8,128)(2,1)}, bf16[4,96,768]{2,1,0:T(8,128)(2,1)S(1)}, u32[]{:S(2)}, u32[]{:S(2)}) collective-permute-start(bf16[4,96,768]{2,1,0:T(8,128)(2,1)} %get-tuple-element.120), channel_id=1, source_target_pairs={{4,0},{5,1},{6,2},{7,3},{0,4},{1,5},{2,6},{3,7},{12,8},{13,9},{14,... | collective-permute-start | bytes 1769480 | tf_op jit(solution)/shard_map/ppermute | solution.py:41
  105.1 3.5 %collective-permute-start.15 = (bf16[192,512]{1,0:T(8,128)(2,1)S(1)}, bf16[192,512]{1,0:T(8,128)(2,1)S(1)}, u32[]{:S(2)}, u32[]{:S(2)}) collective-permute-start(bf16[192,512]{1,0:T(8,128)(2,1)S(1)} %get-tuple-element.125), channel_id=1, source_target_pairs={{1,0},{0,1},{3,2},{2,3},{5,4},{4,5},{7,6},{6,7},{9,8},{8,9},{11,10... | collective-permute-start | bytes 589832 | tf_op jit(solution)/shard_map/ppermute | solution.py:41
  105.1 6.7 %collective-permute-start.17 = (bf16[192,512]{1,0:T(8,128)(2,1)S(1)}, bf16[192,512]{1,0:T(8,128)(2,1)S(1)}, u32[]{:S(2)}, u32[]{:S(2)}) collective-permute-start(bf16[192,512]{1,0:T(8,128)(2,1)S(1)} %get-tuple-element.126), channel_id=1, source_target_pairs={{3,0},{2,1},{1,2},{0,3},{7,4},{6,5},{5,6},{4,7},{11,8},{10,9},{9,1... | collective-permute-start | bytes 589832 | tf_op jit(solution)/shard_map/ppermute | solution.py:41
  106.1 11.1 %collective-permute-start.16 = (bf16[192,512]{1,0:T(8,128)(2,1)S(1)}, bf16[192,512]{1,0:T(8,128)(2,1)S(1)}, u32[]{:S(2)}, u32[]{:S(2)}) collective-permute-start(bf16[192,512]{1,0:T(8,128)(2,1)S(1)} %get-tuple-element.127), channel_id=1, source_target_pairs={{2,0},{3,1},{0,2},{1,3},{6,4},{7,5},{4,6},{5,7},{10,8},{11,9},{8,1... | collective-permute-start | bytes 589832 | tf_op jit(solution)/shard_map/ppermute | solution.py:41
  107.3 16.9 %copy-start.42 = (f32[512]{0:T(512)}, f32[512]{0:T(512)S(1)}, u32[]{:S(2)}) copy-start(f32[512]{0:T(512)S(1)} %broadcast_multiply_fusion.1) | copy-start | bytes 6148
  107.6 17.0 %collective-permute-start.22 = (bf16[512,768]{1,0:T(8,128)(2,1)}, bf16[512,768]{1,0:T(8,128)(2,1)}, u32[]{:S(2)}, u32[]{:S(2)}) collective-permute-start(bf16[512,768]{1,0:T(8,128)(2,1)} %param.19), channel_id=1, source_target_pairs={{1,0},{0,1},{3,2},{2,3},{5,4},{4,5},{7,6},{6,7},{9,8},{8,9},{11,10... | collective-permute-start | bytes 2359304 | tf_op jit(solution)/shard_map/ppermute | solution.py:41
  107.7 34.3 %collective-permute-start.19 = (bf16[8,96,768]{2,1,0:T(8,128)(2,1)}, bf16[8,96,768]{2,1,0:T(8,128)(2,1)}, u32[]{:S(2)}, u32[]{:S(2)}) collective-permute-start(bf16[8,96,768]{2,1,0:T(8,128)(2,1)} %pad_maximum_fusion.3.refs_0_), channel_id=1, source_target_pairs={{2,0},{3,1},{0,2},{1,3},{6,4},{7,5},{4,6},{5,7},{10,8},{11,9},{8,1... | collective-permute-start | bytes 3538952 | tf_op jit(solution)/shard_map/ppermute | solution.py:41
  108.5 38.5 %collective-permute-start.20 = (bf16[8,96,768]{2,1,0:T(8,128)(2,1)S(1)}, bf16[8,96,768]{2,1,0:T(8,128)(2,1)}, u32[]{:S(2)}, u32[]{:S(2)}) collective-permute-start(bf16[8,96,768]{2,1,0:T(8,128)(2,1)S(1)} %pad_maximum_fusion.4.refs_0_), channel_id=1, source_target_pairs={{4,0},{5,1},{6,2},{7,3},{0,4},{1,5},{2,6},{3,7},{12,8},{13,9},{14,... | collective-permute-start | bytes 3538952 | tf_op jit(solution)/shard_map/ppermute | solution.py:41
  121.9 28.8 %collective-permute-start.18 = (bf16[512,768]{1,0:T(8,128)(2,1)}, bf16[512,768]{1,0:T(8,128)(2,1)}, u32[]{:S(2)}, u32[]{:S(2)}) collective-permute-start(bf16[512,768]{1,0:T(8,128)(2,1)} %multiply_convert_fusion.1), channel_id=1, source_target_pairs={{1,0},{0,1},{3,2},{2,3},{5,4},{4,5},{7,6},{6,7},{9,8},{8,9},{11,10... | collective-permute-start | bytes 2359304 | tf_op jit(solution)/shard_map/ppermute | solution.py:41
  167.7 8.1 %collective-permute-start.21 = (bf16[512,768]{1,0:T(8,128)(2,1)S(1)}, bf16[512,768]{1,0:T(8,128)(2,1)S(1)}, u32[]{:S(2)}, u32[]{:S(2)}) collective-permute-start(bf16[512,768]{1,0:T(8,128)(2,1)S(1)} %slice.256), channel_id=1, source_target_pairs={{1,0},{0,1},{3,2},{2,3},{5,4},{4,5},{7,6},{6,7},{9,8},{8,9},{11,10... | collective-permute-start | bytes 2359304 | tf_op jit(solution)/shard_map/ppermute | solution.py:41
  167.8 5.9 %collective-permute-start.23 = (bf16[512,768]{1,0:T(8,128)(2,1)S(1)}, bf16[512,768]{1,0:T(8,128)(2,1)S(1)}, u32[]{:S(2)}, u32[]{:S(2)}) collective-permute-start(bf16[512,768]{1,0:T(8,128)(2,1)S(1)} %slice.255), channel_id=1, source_target_pairs={{1,0},{0,1},{3,2},{2,3},{5,4},{4,5},{7,6},{6,7},{9,8},{8,9},{11,10... | collective-permute-start | bytes 2359304 | tf_op jit(solution)/shard_map/ppermute | solution.py:41
  173.7 48.3 %collective-permute-start.27 = (bf16[4,2,48,1536]{3,2,1,0:T(8,128)(2,1)}, bf16[4,2,48,1536]{3,2,1,0:T(8,128)(2,1)}, u32[]{:S(2)}, u32[]{:S(2)}) collective-permute-start(bf16[4,2,48,1536]{3,2,1,0:T(8,128)(2,1)} %dynamic-slice_bitcast_fusion), channel_id=1, source_target_pairs={{4,0},{5,1},{6,2},{7,3},{0,4},{1,5},{2,6},{3,7},{12,8},{13,9},{14,... | collective-permute-start | bytes 3538952 | tf_op jit(solution)/shard_map/ppermute | solution.py:41
  178.7 6.8 %copy-start.18 = (f32[512,768]{1,0:T(8,128)}, f32[512,768]{1,0:T(8,128)S(1)}, u32[]{:S(2)}) copy-start(f32[512,768]{1,0:T(8,128)S(1)} %get-tuple-element.108) | copy-start | bytes 4718596
  179.6 8.3 %collective-permute-start.26 = (bf16[192,512]{1,0:T(8,128)(2,1)S(1)}, bf16[192,512]{1,0:T(8,128)(2,1)S(1)}, u32[]{:S(2)}, u32[]{:S(2)}) collective-permute-start(bf16[192,512]{1,0:T(8,128)(2,1)S(1)} %get-tuple-element.122), channel_id=1, source_target_pairs={{3,0},{2,1},{1,2},{0,3},{7,4},{6,5},{5,6},{4,7},{11,8},{10,9},{9,1... | collective-permute-start | bytes 589832 | tf_op jit(solution)/shard_map/ppermute | solution.py:41
  180.2 10.9 %collective-permute-start.25 = (bf16[192,512]{1,0:T(8,128)(2,1)S(1)}, bf16[192,512]{1,0:T(8,128)(2,1)S(1)}, u32[]{:S(2)}, u32[]{:S(2)}) collective-permute-start(bf16[192,512]{1,0:T(8,128)(2,1)S(1)} %get-tuple-element.123), channel_id=1, source_target_pairs={{2,0},{3,1},{0,2},{1,3},{6,4},{7,5},{4,6},{5,7},{10,8},{11,9},{8,1... | collective-permute-start | bytes 589832 | tf_op jit(solution)/shard_map/ppermute | solution.py:41
  181.4 9.7 %collective-permute-start.24 = (bf16[192,512]{1,0:T(8,128)(2,1)S(1)}, bf16[192,512]{1,0:T(8,128)(2,1)S(1)}, u32[]{:S(2)}, u32[]{:S(2)}) collective-permute-start(bf16[192,512]{1,0:T(8,128)(2,1)S(1)} %get-tuple-element.124), channel_id=1, source_target_pairs={{1,0},{0,1},{3,2},{2,3},{5,4},{4,5},{7,6},{6,7},{9,8},{8,9},{11,10... | collective-permute-start | bytes 589832 | tf_op jit(solution)/shard_map/ppermute | solution.py:41
  191.2 55.2 %collective-permute-start.28 = (bf16[4,2,96,768]{3,2,0,1:T(8,128)(2,1)}, bf16[4,2,96,768]{3,2,0,1:T(8,128)(2,1)}, u32[]{:S(2)}, u32[]{:S(2)}) collective-permute-start(bf16[4,2,96,768]{3,2,0,1:T(8,128)(2,1)} %bitcast.218), channel_id=1, source_target_pairs={{2,0},{3,1},{0,2},{1,3},{6,4},{7,5},{4,6},{5,7},{10,8},{11,9},{8,1... | collective-permute-start | bytes 3538952 | tf_op jit(solution)/shard_map/ppermute | solution.py:41
  197.5 22.5 %copy-start.5 = (bf16[768,2048]{1,0:T(8,128)(2,1)S(1)}, bf16[768,2048]{1,0:T(8,128)(2,1)}, u32[]{:S(2)}) copy-start(bf16[768,2048]{1,0:T(8,128)(2,1)} %copy-done.4) | copy-start | bytes 9437188
  221.9 24.4 %collective-permute-start.29 = (bf16[4,96,384]{2,1,0:T(8,128)(2,1)S(1)}, bf16[4,96,384]{2,1,0:T(8,128)(2,1)S(1)}, u32[]{:S(2)}, u32[]{:S(2)}) collective-permute-start(bf16[4,96,384]{2,1,0:T(8,128)(2,1)S(1)} %bitcast.223), channel_id=1, source_target_pairs={{4,0},{5,1},{6,2},{7,3},{0,4},{1,5},{2,6},{3,7},{12,8},{13,9},{14,... | collective-permute-start | bytes 884744 | tf_op jit(solution)/shard_map/ppermute | solution.py:41
  222.3 12.1 %copy-start.2 = (bf16[576,2048]{1,0:T(8,128)(2,1)S(1)}, bf16[576,2048]{1,0:T(8,128)(2,1)}, u32[]{:S(2)}) copy-start(bf16[576,2048]{1,0:T(8,128)(2,1)} %copy-done.1) | copy-start | bytes 7077892
  224.0 22.4 %copy-start.23 = (bf16[4,2,48,1536]{3,2,1,0:T(8,128)(2,1)}, bf16[4,2,48,1536]{3,2,1,0:T(8,128)(2,1)S(1)}, u32[]{:S(2)}) copy-start(bf16[4,2,48,1536]{3,2,1,0:T(8,128)(2,1)S(1)} %fusion.8) | copy-start | bytes 3538948
  224.0 10.3 %copy-start.10 = (f32[192,2048]{1,0:T(8,128)S(1)}, f32[192,2048]{1,0:T(8,128)}, u32[]{:S(2)}) copy-start(f32[192,2048]{1,0:T(8,128)} %copy-done.8) | copy-start | bytes 4718596
  225.0 34.9 %collective-permute-start.32 = (bf16[2,48,1536]{2,1,0:T(8,128)(2,1)}, bf16[2,48,1536]{2,1,0:T(8,128)(2,1)}, u32[]{:S(2)}, u32[]{:S(2)}) collective-permute-start(bf16[2,48,1536]{2,1,0:T(8,128)(2,1)} %get-tuple-element.116), channel_id=1, source_target_pairs={{24,0},{25,1},{26,2},{27,3},{28,4},{29,5},{30,6},{31,7},{0,8},{1,9... | collective-permute-start | bytes 884744 | tf_op jit(solution)/shard_map/ppermute | solution.py:41
  225.0 34.9 %collective-permute-start.31 = (bf16[2,48,1536]{2,1,0:T(8,128)(2,1)}, bf16[2,48,1536]{2,1,0:T(8,128)(2,1)}, u32[]{:S(2)}, u32[]{:S(2)}) collective-permute-start(bf16[2,48,1536]{2,1,0:T(8,128)(2,1)} %get-tuple-element.117), channel_id=1, source_target_pairs={{16,0},{17,1},{18,2},{19,3},{20,4},{21,5},{22,6},{23,7},{24,8},{25... | collective-permute-start | bytes 884744 | tf_op jit(solution)/shard_map/ppermute | solution.py:41
  234.0 25.9 %collective-permute-start.30 = (bf16[2,48,1536]{2,1,0:T(8,128)(2,1)}, bf16[2,48,1536]{2,1,0:T(8,128)(2,1)}, u32[]{:S(2)}, u32[]{:S(2)}) collective-permute-start(bf16[2,48,1536]{2,1,0:T(8,128)(2,1)} %get-tuple-element.118), channel_id=1, source_target_pairs={{8,0},{9,1},{10,2},{11,3},{12,4},{13,5},{14,6},{15,7},{16,8},{17,9... | collective-permute-start | bytes 884744 | tf_op jit(solution)/shard_map/ppermute | solution.py:41
  252.3 7.0 %copy-start.13 = (bf16[2,512,768]{2,1,0:T(8,128)(2,1)}, bf16[2,512,768]{2,1,0:T(8,128)(2,1)S(1)}, u32[]{:S(2)}) copy-start(bf16[2,512,768]{2,1,0:T(8,128)(2,1)S(1)} %get-tuple-element.81) | copy-start | bytes 4718596
  252.3 7.0 %collective-permute-start.33 = (bf16[4,96,192]{2,1,0:T(8,128)(2,1)S(1)}, bf16[4,96,192]{2,1,0:T(8,128)(2,1)S(1)}, u32[]{:S(2)}, u32[]{:S(2)}) collective-permute-start(bf16[4,96,192]{2,1,0:T(8,128)(2,1)S(1)} %bitcast.224), channel_id=1, source_target_pairs={{4,0},{5,1},{6,2},{7,3},{0,4},{1,5},{2,6},{3,7},{12,8},{13,9},{14,... | collective-permute-start | bytes 442376 | tf_op jit(solution)/shard_map/ppermute | solution.py:41
  255.4 23.2 %collective-permute-start.40 = (bf16[4,96,768]{2,1,0:T(8,128)(2,1)}, bf16[4,96,768]{2,1,0:T(8,128)(2,1)}, u32[]{:S(2)}, u32[]{:S(2)}) collective-permute-start(bf16[4,96,768]{2,1,0:T(8,128)(2,1)} %dynamic-slice_bitcast_fusion.1), channel_id=1, source_target_pairs={{4,0},{5,1},{6,2},{7,3},{0,4},{1,5},{2,6},{3,7},{12,8},{13,9},{14,... | collective-permute-start | bytes 1769480 | tf_op jit(solution)/shard_map/ppermute | solution.py:41
  259.9 6.5 %collective-permute-start.37 = (bf16[96,576]{1,0:T(8,128)(2,1)S(1)}, bf16[96,576]{1,0:T(8,128)(2,1)S(1)}, u32[]{:S(2)}, u32[]{:S(2)}) collective-permute-start(bf16[96,576]{1,0:T(8,128)(2,1)S(1)} %get-tuple-element.86), channel_id=1, source_target_pairs={{8,0},{9,1},{10,2},{11,3},{12,4},{13,5},{14,6},{15,7},{16,8},{17,9... | collective-permute-start | bytes 331784 | tf_op jit(solution)/shard_map/ppermute | solution.py:41
  262.7 13.7 %collective-permute-start.38 = (bf16[96,576]{1,0:T(8,128)(2,1)S(1)}, bf16[96,576]{1,0:T(8,128)(2,1)S(1)}, u32[]{:S(2)}, u32[]{:S(2)}) collective-permute-start(bf16[96,576]{1,0:T(8,128)(2,1)S(1)} %get-tuple-element.87), channel_id=1, source_target_pairs={{16,0},{17,1},{18,2},{19,3},{20,4},{21,5},{22,6},{23,7},{24,8},{25... | collective-permute-start | bytes 331784 | tf_op jit(solution)/shard_map/ppermute | solution.py:41
  264.4 12.0 %collective-permute-start.39 = (bf16[96,576]{1,0:T(8,128)(2,1)S(1)}, bf16[96,576]{1,0:T(8,128)(2,1)S(1)}, u32[]{:S(2)}, u32[]{:S(2)}) collective-permute-start(bf16[96,576]{1,0:T(8,128)(2,1)S(1)} %get-tuple-element.88), channel_id=1, source_target_pairs={{24,0},{25,1},{26,2},{27,3},{28,4},{29,5},{30,6},{31,7},{0,8},{1,9... | collective-permute-start | bytes 331784 | tf_op jit(solution)/shard_map/ppermute | solution.py:41
  264.4 12.8 %collective-permute-start.34 = (bf16[2,512,768]{2,1,0:T(8,128)(2,1)}, bf16[2,512,768]{2,1,0:T(8,128)(2,1)S(1)}, u32[]{:S(2)}, u32[]{:S(2)}) collective-permute-start(bf16[2,512,768]{2,1,0:T(8,128)(2,1)} %copy-done.13), channel_id=1, source_target_pairs={{1,0},{0,1},{3,2},{2,3},{5,4},{4,5},{7,6},{6,7},{9,8},{8,9},{11,10... | collective-permute-start | bytes 4718600 | tf_op jit(solution)/shard_map/ppermute | solution.py:41
  266.4 10.7 %collective-permute-start.35 = (bf16[48,1536]{1,0:T(8,128)(2,1)S(1)}, bf16[48,1536]{1,0:T(8,128)(2,1)S(1)}, u32[]{:S(2)}, u32[]{:S(2)}) collective-permute-start(bf16[48,1536]{1,0:T(8,128)(2,1)S(1)} %dynamic-slice_bitcast_fusion.12), channel_id=1, source_target_pairs={{2,0},{3,1},{0,2},{1,3},{6,4},{7,5},{4,6},{5,7},{10,8},{11,9},{8,1... | collective-permute-start | bytes 442376 | tf_op jit(solution)/shard_map/ppermute | solution.py:41
  278.6 4.5 %collective-permute-start.41 = (f32[24,1536]{1,0:T(8,128)S(1)}, f32[24,1536]{1,0:T(8,128)S(1)}, u32[]{:S(2)}, u32[]{:S(2)}) collective-permute-start(f32[24,1536]{1,0:T(8,128)S(1)} %dynamic-slice_bitcast_fusion.11), channel_id=1, source_target_pairs={{1,0},{0,1},{3,2},{2,3},{5,4},{4,5},{7,6},{6,7},{9,8},{8,9},{11,10... | collective-permute-start | bytes 442376 | tf_op jit(solution)/shard_map/ppermute | solution.py:41
  282.0 28.9 %collective-permute-start.36 = (bf16[512,768]{1,0:T(8,128)(2,1)}, bf16[512,768]{1,0:T(8,128)(2,1)S(1)}, u32[]{:S(2)}, u32[]{:S(2)}) collective-permute-start(bf16[512,768]{1,0:T(8,128)(2,1)} %slice_bitcast_fusion), channel_id=1, source_target_pairs={{2,0},{3,1},{0,2},{1,3},{6,4},{7,5},{4,6},{5,7},{10,8},{11,9},{8,1... | collective-permute-start | bytes 2359304 | tf_op jit(solution)/shard_map/ppermute | solution.py:41
  283.1 6.6 %copy-start.32 = (bf16[24,3072]{1,0:T(8,128)(2,1)S(1)}, bf16[24,3072]{1,0:T(8,128)(2,1)}, u32[]{:S(2)}) copy-start(bf16[24,3072]{1,0:T(8,128)(2,1)} %param.15) | copy-start | bytes 442372
  283.3 6.6 %copy-start.48 = (bf16[24]{0:T(256)(128)(2,1)S(1)}, bf16[24]{0:T(256)(128)(2,1)}, u32[]{:S(2)}) copy-start(bf16[24]{0:T(256)(128)(2,1)} %param.18) | copy-start | bytes 148
  283.3 20.6 %collective-permute-start.42 = (f32[2,24,576]{2,1,0:T(8,128)S(1)}, f32[2,24,576]{2,1,0:T(8,128)S(1)}, u32[]{:S(2)}, u32[]{:S(2)}) collective-permute-start(f32[2,24,576]{2,1,0:T(8,128)S(1)} %dynamic-slice_bitcast_fusion.13), channel_id=1, source_target_pairs={{2,0},{3,1},{0,2},{1,3},{6,4},{7,5},{4,6},{5,7},{10,8},{11,9},{8,1... | collective-permute-start | bytes 331784 | tf_op jit(solution)/shard_map/ppermute | solution.py:41
  284.3 19.7 %collective-permute-start.44 = (bf16[96,768]{1,0:T(8,128)(2,1)}, bf16[96,768]{1,0:T(8,128)(2,1)}, u32[]{:S(2)}, u32[]{:S(2)}) collective-permute-start(bf16[96,768]{1,0:T(8,128)(2,1)} %get-tuple-element.95), channel_id=1, source_target_pairs={{8,0},{9,1},{10,2},{11,3},{12,4},{13,5},{14,6},{15,7},{16,8},{17,9... | collective-permute-start | bytes 442376 | tf_op jit(solution)/shard_map/ppermute | solution.py:41
  284.3 19.8 %collective-permute-start.45 = (bf16[96,768]{1,0:T(8,128)(2,1)}, bf16[96,768]{1,0:T(8,128)(2,1)}, u32[]{:S(2)}, u32[]{:S(2)}) collective-permute-start(bf16[96,768]{1,0:T(8,128)(2,1)} %get-tuple-element.96), channel_id=1, source_target_pairs={{16,0},{17,1},{18,2},{19,3},{20,4},{21,5},{22,6},{23,7},{24,8},{25... | collective-permute-start | bytes 442376 | tf_op jit(solution)/shard_map/ppermute | solution.py:41
  288.7 15.4 %collective-permute-start.46 = (bf16[96,768]{1,0:T(8,128)(2,1)}, bf16[96,768]{1,0:T(8,128)(2,1)}, u32[]{:S(2)}, u32[]{:S(2)}) collective-permute-start(bf16[96,768]{1,0:T(8,128)(2,1)} %get-tuple-element.97), channel_id=1, source_target_pairs={{24,0},{25,1},{26,2},{27,3},{28,4},{29,5},{30,6},{31,7},{0,8},{1,9... | collective-permute-start | bytes 442376 | tf_op jit(solution)/shard_map/ppermute | solution.py:41
  289.7 17.2 %copy-start.28 = (f32[24,3072]{1,0:T(8,128)}, f32[24,3072]{1,0:T(8,128)S(1)}, u32[]{:S(2)}) copy-start(f32[24,3072]{1,0:T(8,128)S(1)} %reshape.163) | copy-start | bytes 884740
  304.0 5.4 %copy-start.33 = (bf16[24,2304]{1,0:T(8,128)(2,1)S(1)}, bf16[24,2304]{1,0:T(8,128)(2,1)}, u32[]{:S(2)}) copy-start(bf16[24,2304]{1,0:T(8,128)(2,1)} %param.13) | copy-start | bytes 331780
  304.0 6.9 %copy-start.17 = (bf16[2,512,768]{2,1,0:T(8,128)(2,1)S(1)}, bf16[2,512,768]{2,1,0:T(8,128)(2,1)}, u32[]{:S(2)}) copy-start(bf16[2,512,768]{2,1,0:T(8,128)(2,1)} %copy-done.16) | copy-start | bytes 4718596
  304.0 2.1 collective-permute-start.43
  (34 other events, 96.7 us)
Sparse Core Ops, SparseCore 0:
  49.4 58.4 all-gather.1
  196.2 105.6 reduce-scatter.1

commit v3 on v2

--- a/solution.py
+++ b/solution.py
@@ -65,9 +65,9 @@
 
     def halve(self, parts, dim, bit):
         mine = (self.at[dim] >> bit) % 2
-        parts = parts.reshape((2, -1) + parts.shape[1:])
-        kept = lax.dynamic_index_in_dim(parts, mine, 0, keepdims=False)
-        return kept, lax.dynamic_index_in_dim(parts, 1 - mine, 0, keepdims=False)
+        parts = parts.reshape((-1, 2) + parts.shape[1:])
+        kept = lax.dynamic_index_in_dim(parts, mine, 1, keepdims=False)
+        return kept, lax.dynamic_index_in_dim(parts, 1 - mine, 1, keepdims=False)
 
     def swap(self, value, dim, bit):
         return self.fetch(value, 1, **{dim: 1 << bit})
@@ -119,7 +119,16 @@
     return lax.optimization_barrier((value,) + before)[0]
 
 
-def gather_rows(grid, piece, order, gates=None, begun=None, done=("hi",)):
+def put_in_place(stacks, index):
+    rows = stacks[0].shape[1]
+    if rows % 16 == 0:
+        return place(stacks, index * rows)
+    order = jnp.argsort(index)
+    out = jnp.concatenate(stacks, axis=0)
+    return jnp.concatenate([lax.dynamic_index_in_dim(out, order[i], 0, keepdims=False) for i in range(index.shape[0])], axis=0)
+
+
+def gather_rows(grid, piece, order, gates=None, begun=None, done=("hi",), raw=False):
     if begun is None:
         stack, steps = piece[None], [dict()]
     else:
@@ -147,15 +156,12 @@
         for d in dims:
             at = at * grid.sizes[d] + (grid.at[d] + s.get(d, 0)) % grid.sizes[d]
         index.append(at)
-    index = jnp.stack(index)
+    index = jnp.stack(index).astype(jnp.int32)
+    if begun is not None and len(order) == 1 and raw:
+        return stacks, index
     if gates and "place" in gates:
         stacks, _ = together(stacks, gates["place"])
-    if rows % 16 == 0:
-        return place(stacks, index * rows), received
-    order_back = jnp.argsort(index)
-    out = jnp.concatenate(stacks, axis=0)
-    out = jnp.concatenate([lax.dynamic_index_in_dim(out, order_back[i], 0, keepdims=False) for i in range(len(steps))], axis=0)
-    return out, received
+    return put_in_place(stacks, index), received
 
 
 def lane_tile(at, size):
@@ -277,8 +283,7 @@
         out_specs=(whole, whole, whole),
         scratch_shapes=[pltpu.VMEM((3 * width, row_len), bf16), pltpu.VMEM((heads, row_len, HEAD_DIM), bf16)],
         compiler_params=pltpu.CompilerParams(vmem_limit_bytes=40 * 2**20),
-        cost_estimate=pl.CostEstimate(
-            flops=10**6, bytes_accessed=10**5, transcendentals=0),
+        cost_estimate=pl.CostEstimate(flops=7 * 10**9 * heads, bytes_accessed=10**6, transcendentals=0),
     )(meta, qkv)
 
 
@@ -384,8 +389,7 @@
             pltpu.VMEM((2 * width, row_len), f32),
         ],
         compiler_params=pltpu.CompilerParams(vmem_limit_bytes=48 * 2**20),
-        cost_estimate=pl.CostEstimate(
-            flops=10**6, bytes_accessed=10**5, transcendentals=0),
+        cost_estimate=pl.CostEstimate(flops=13 * 10**9 * count if which == 0 else 10**6, bytes_accessed=10**5, transcendentals=0),
     )(meta, qkv, upstream, att, lse)
 
 
@@ -434,37 +438,40 @@
     )(*pieces, weight)
 
 
-def rows_kernel(count, strides, me_ref, left_ref, right_ref, *refs):
+def rows_kernel(count, strides, more, me_ref, left_ref, right_ref, *refs):
     outs, total_ref = refs[:-1], refs[-1]
-    total_ref[...] = jnp.dot(left_ref[...], right_ref[...], preferred_element_type=f32)
-    outer, inner = strides
+    cols = right_ref.shape[1]
+    total_ref[:, :cols] = jnp.dot(left_ref[...], right_ref[...], preferred_element_type=f32)
+    if more:
+        total_ref[:, cols:] = refs[0][...].astype(f32)
+        outs = outs[1:]
+    outer = strides
     rows = outs[0].shape[-2]
     for r in range(count):
         entry = (me_ref[0] + count - r) % count
         for a in range(outer):
-            for b in range(inner):
-                at = pl.multiple_of(((a * count + entry) * inner + b) * rows, 8)
-                outs[r][a, b] = total_ref[pl.ds(at, rows), :].astype(bf16)
-
-
-def split_product(grid, left, right, dim, with_x=False):
+            at = pl.multiple_of((a * count + entry) * rows, 8)
+            outs[r][a] = total_ref[pl.ds(at, rows), :].astype(bf16)
+
+
+def split_product(grid, left, right, dim, more=None):
     rows_all, cols = left.shape[0], right.shape[1]
-    outer = grid.sizes["hi"] if dim == "lo" else grid.nb
-    inner = grid.sizes["x"] if dim == "lo" and with_x else 1
-    count = grid.sizes[dim]
-    rows = rows_all // (outer * inner * count)
+    operands = [left, right]
+    if more is not None:
+        operands.append(more)
+        cols += more.shape[1]
+    outer, count = grid.sizes["hi"], grid.sizes[dim]
+    rows = rows_all // (outer * count)
     whole = pl.BlockSpec(memory_space=pltpu.VMEM)
     outs = pl.pallas_call(
-        functools.partial(rows_kernel, count, (outer, inner)),
-        out_shape=tuple(jax.ShapeDtypeStruct((outer, inner, rows, cols), bf16) for _ in range(count)),
-        in_specs=[pl.BlockSpec(memory_space=pltpu.SMEM), whole, whole],
+        functools.partial(rows_kernel, count, outer, more is not None),
+        out_shape=tuple(jax.ShapeDtypeStruct((outer, rows, cols), bf16) for _ in range(count)),
+        in_specs=[pl.BlockSpec(memory_space=pltpu.SMEM)] + [whole] * len(operands),
         out_specs=(whole,) * count,
         scratch_shapes=[pltpu.VMEM((rows_all, cols), f32)],
         compiler_params=pltpu.CompilerParams(vmem_limit_bytes=48 * 2**20),
         cost_estimate=pl.CostEstimate(flops=10**6, bytes_accessed=10**5, transcendentals=0),
-    )(grid.at[dim].reshape(1).astype(jnp.int32), left, right)
-    if inner == 1:
-        outs = [one.reshape(outer, rows, cols) for one in outs]
+    )(grid.at[dim].reshape(1).astype(jnp.int32), *operands)
     return outs[0], list(outs[1:])
 
 
@@ -493,6 +500,85 @@
         compiler_params=pltpu.CompilerParams(vmem_limit_bytes=48 * 2**20),
         cost_estimate=pl.CostEstimate(flops=10**6, bytes_accessed=10**5, transcendentals=0),
     )(*parts, weight)
+
+
+def hidden_kernel(counts, folds, up_at, down_at, *refs):
+    up_refs, down_refs = refs[: counts[0]], refs[counts[0] : counts[0] + counts[1]]
+    rest = refs[counts[0] + counts[1] :]
+    h2_refs, cot_refs = rest[:2], rest[2:4]
+    act_ref, pre_ref, own_ref, sent_ref, up_ref, down_ref, up_sem, down_sem = rest[4:]
+    model = up_ref.shape[0]
+    rows = up_refs[0].shape[1] // folds
+    strip = down_refs[0].shape[1]
+    copies, later = [], []
+    for ref in up_refs:
+        for i in range(ref.shape[0]):
+            at = pl.multiple_of(up_at[len(copies) // folds] * rows, rows)
+            for f in range(folds):
+                piece = ref.at[i, pl.ds(f * rows, rows), :]
+                spot = up_ref.at[pl.ds(at, rows), pl.ds(f * model, model)]
+                copies.append(pltpu.make_async_copy(piece, spot, up_sem.at[len(copies)]))
+    for ref in down_refs:
+        for i in range(ref.shape[0]):
+            at = pl.multiple_of(down_at[len(later)] * strip, strip)
+            later.append(pltpu.make_async_copy(ref.at[i], down_ref.at[pl.ds(at, strip), :], down_sem.at[len(later)]))
+    for copy in copies + later:
+        copy.start()
+    for copy in copies + later:
+        copy.wait()
+    half = h2_refs[0].shape[0]
+    hidden = up_ref.shape[1]
+    width = 256
+    root = (2.0 / math.pi) ** 0.5
+
+    def first(item):
+        i, at = item
+        pre = jnp.dot(h2_refs[i][...], up_ref[:, at : at + width], preferred_element_type=f32)
+        back = lax.dot_general(cot_refs[i][...], down_ref[at : at + width, :], (((1,), (1,)), ((), ())), preferred_element_type=f32)
+        return pre, back
+
+    def second(item, kept):
+        i, at = item
+        pre, back = kept
+        square = pre * pre
+        slope = jnp.tanh(pre * (root + root * 0.044715 * square))
+        side = 0.5 + 0.5 * slope
+        act_ref[i * half : (i + 1) * half, at : at + width] = (pre * side).astype(bf16)
+        steep = side + (0.5 * pre) * (1.0 - slope * slope) * (root + 3 * root * 0.044715 * square)
+        pre_ref[i * half : (i + 1) * half, at : at + width] = (steep * back).astype(bf16)
+
+    pipeline([(i, at) for i in range(2) for at in range(0, hidden, width)], first, second, lambda item, kept: None)
+    for i, ref in enumerate((own_ref, sent_ref)):
+        for at in range(0, half, 256):
+            left = pre_ref[i * half + at : i * half + at + 256, :]
+            total = lax.dot_general(left, up_ref[...], (((1,), (1,)), ((), ())), preferred_element_type=f32)
+            ref[at : at + 256, :] = total.astype(ref.dtype)
+
+
+def hidden_layer(up_stacks, up_at, down_stacks, down_at, h2_pair, cot_pair, folds):
+    half, model = h2_pair[0].shape
+    up_count, down_count = sum(one.shape[0] for one in up_stacks), sum(one.shape[0] for one in down_stacks)
+    hidden = folds * model
+    whole, smem, far = (pl.BlockSpec(memory_space=m) for m in (pltpu.VMEM, pltpu.SMEM, pl.ANY))
+    return pl.pallas_call(
+        functools.partial(hidden_kernel, (len(up_stacks), len(down_stacks)), folds),
+        out_shape=(
+            jax.ShapeDtypeStruct((2 * half, hidden), bf16),
+            jax.ShapeDtypeStruct((2 * half, hidden), bf16),
+            jax.ShapeDtypeStruct((half, model), f32),
+            jax.ShapeDtypeStruct((half, model), bf16),
+        ),
+        in_specs=[smem, smem] + [far] * (len(up_stacks) + len(down_stacks)) + [whole] * 4,
+        out_specs=(whole,) * 4,
+        scratch_shapes=[
+            pltpu.VMEM((model, hidden), bf16),
+            pltpu.VMEM((hidden, model), bf16),
+            pltpu.SemaphoreType.DMA((up_count * folds,)),
+            pltpu.SemaphoreType.DMA((down_count,)),
+        ],
+        compiler_params=pltpu.CompilerParams(vmem_limit_bytes=50 * 2**20),
+        cost_estimate=pl.CostEstimate(flops=14 * 10**9, bytes_accessed=10**6, transcendentals=0),
+    )(up_at, down_at, *up_stacks, *down_stacks, *h2_pair, *cot_pair)
 
 
 def norm_parts(values):
@@ -565,21 +651,24 @@
 
     first_tokens = tie(tokens, *got)
     by_x = [tokens] + [grid.fetch(first_tokens, x=r) for r in range(1, nx)]
-    got_hi = [grid.fetch(group_qkv[None], hi=r) for r in range(1, grid.sizes["hi"])]
-    stack = tie(jnp.stack(by_x), *got_hi)
-    by_c = [by_x] + [list(grid.fetch(stack, c=r)) for r in range(1, nc)]
-    row_tokens = [by_c[c][x] for x in range(nx) for c in range(nc)]
-    full_qkv, _ = gather_rows(grid, None, ("lo",), {"place": row_tokens}, jnp.concatenate([group_qkv[None]] + got_hi, axis=0))
-
-    full_out = lax.all_gather(tie(out_weight, *got_hi), ("pb", "ka"), axis=0, tiled=True)
-
     strip = down_weight.shape[0]
     up_split = jnp.transpose(up_weight.reshape(shard, chips, nc, strip), (2, 0, 1, 3)).reshape(nc, shard, chips * strip)
     own, sends = grid.split(up_split, 0, "c")
     up_part = jnp.concatenate(grid.in_order([own] + grid.send(sends, "c"), "c"), axis=0)
     folds = chips * strip // model
     up_part = jnp.concatenate([up_part[:, i * model : (i + 1) * model] for i in range(folds)], axis=0)
-    both = tie(jnp.concatenate([up_part, down_weight], axis=0), *got_hi, *by_x)
+    both = jnp.concatenate([up_part, down_weight], axis=0)
+    group_qkv, both = together(group_qkv, both)
+    got_hi = [grid.fetch(group_qkv[None], hi=r) for r in range(1, grid.sizes["hi"])]
+    stack = tie(jnp.stack(by_x), *got_hi)
+    by_c = [by_x] + [list(grid.fetch(stack, c=r)) for r in range(1, nc)]
+    row_tokens = [by_c[c][x] for x in range(nx) for c in range(nc)]
+    qkv_stack = jnp.concatenate([group_qkv[None]] + got_hi, axis=0)
+    full_qkv, _ = gather_rows(grid, None, ("lo",), {"place": row_tokens}, qkv_stack)
+
+    full_out = lax.all_gather(tie(out_weight, *got_hi), ("pb", "ka"), axis=0, tiled=True)
+
+    both = tie(both, qkv_stack, *row_tokens)
     both = grid.gather(both, "hi")
 
     slots = tok_rows // BLK
@@ -593,28 +682,30 @@
     inputs = tokens.astype(f32)
     h1, qkv = project(row_tokens, full_qkv, sets)
     row_len = h1.shape[1]
-    both = tie(both, qkv)
     up_rows = up_part.shape[0]
-    up_stack, down_stack = both[:, :up_rows], both[:, up_rows:]
-    up_stack = jnp.concatenate([up_stack] + [grid.fetch(up_stack, lo=r) for r in range(1, grid.sizes["lo"])], axis=0)
-    down_stack = jnp.concatenate([down_stack] + [grid.fetch(down_stack, x=r) for r in range(1, nx)], axis=0)
-    att_parts, att_row, lse = forward_attention(meta, tie(qkv, both), sets, nk)
+    up_stack, down_stack, _ = together(both[:, :up_rows], both[:, up_rows:], qkv)
+    qkv = tie(qkv, up_stack, down_stack)
+    up_stack = [up_stack] + [grid.fetch(up_stack, x=r) for r in range(1, nx)]
+    down_stack = [down_stack] + [grid.fetch(down_stack, lo=r) for r in range(1, grid.sizes["lo"])]
+    att_parts, att_row, lse = forward_attention(meta, qkv, sets, nk)
     att_parts, up_stack, down_stack = together(att_parts, up_stack, down_stack)
-    full_up, _ = gather_rows(grid, None, ("x",), begun=up_stack, done=("hi", "lo"))
-    full_up = jnp.transpose(full_up.reshape(chips, folds, nc * shard, model), (0, 2, 1, 3)).reshape(model, folds * model)
-    full_down, _ = gather_rows(grid, None, ("lo",), begun=down_stack, done=("hi", "x"))
-
+    up_stack, down_stack = jnp.concatenate(up_stack, axis=0), jnp.concatenate(down_stack, axis=0)
+    up_stacks, up_at = gather_rows(grid, None, ("lo",), begun=up_stack, done=("hi", "x"), raw=True)
+    down_stacks, down_at = gather_rows(grid, None, ("x",), begun=down_stack, done=("hi", "lo"), raw=True)
     got = [att_parts[0]]
     for xr, cr in rels[1:]:
         got.append(grid.fetch(att_parts[((-xr) % nx) * nc + (-cr) % nc], x=xr, c=cr))
     att = jnp.concatenate(grid.group_in_order(got), axis=0)[: HEADS * HEAD_DIM]
 
     late_cot = tie(cotangent, att_parts)
-    cots = jnp.concatenate([cotangent] + [grid.fetch(late_cot, c=r) for r in range(1, nc)], axis=0)
+    cot_pair = [cotangent] + [grid.fetch(late_cot, c=r) for r in range(1, nc)]
+    cots = jnp.concatenate(cot_pair, axis=0)
+    att = tie(att, up_stack, down_stack)
     residual = inputs + mm(att, full_out, (0, 0))
     normed_two, inverse_two = norm_parts(residual)
     h2 = (normed_two * gain_two).astype(bf16)
-    h2s = jnp.concatenate([h2] + [grid.fetch(h2, c=r) for r in range(1, nc)], axis=0)
+    h2_pair = [h2] + [grid.fetch(h2, c=r) for r in range(1, nc)]
+    h2s = jnp.concatenate(h2_pair, axis=0)
 
     def core_sum(part):
         pieces = part.reshape((nc, tok_rows) + part.shape[1:])
@@ -623,12 +714,17 @@
             total = total + grid.fetch(pieces[(nc - r) % nc].astype(bf16), c=r).astype(f32)
         return total
 
-    hidden_pre = mm(h2s, full_up, (1, 0))
-    hidden_act, gelu_back = jax.vjp(lambda v: jax.nn.gelu(v, approximate=True), hidden_pre)
-    hidden_low = hidden_act.astype(bf16)
-    (grad_pre,) = gelu_back(mm(cots, full_down, (1, 1)))
-    grad_pre = grad_pre.astype(bf16)
-    grad_h2 = core_sum(mm(grad_pre, full_up, (1, 1)))
+    if nc == 2 and strip % 16 == 0 and (nc * shard) % 16 == 0 and tok_rows % 256 == 0:
+        hidden_low, grad_pre, grad_h2, grad_sent = hidden_layer(up_stacks, up_at, down_stacks, down_at, h2_pair, cot_pair, folds)
+        grad_h2 = added(grad_h2, [grid.fetch(grad_sent, c=1)], True)
+    else:
+        full_up = put_in_place(up_stacks, up_at).reshape(chips, folds, nc * shard, model)
+        full_up = jnp.transpose(full_up, (0, 2, 1, 3)).reshape(model, folds * model)
+        hidden_act, gelu_back = jax.vjp(lambda v: jax.nn.gelu(v, approximate=True), mm(h2s, full_up, (1, 0)))
+        hidden_low = hidden_act.astype(bf16)
+        (grad_pre,) = gelu_back(mm(cots, put_in_place(down_stacks, down_at), (1, 1)))
+        grad_pre = grad_pre.astype(bf16)
+        grad_h2 = core_sum(mm(grad_pre, full_up, (1, 1)))
     grad_up = mm(h2s, grad_pre, (0, 0)).astype(bf16)
     grad_residual = cotangent.astype(f32) + norm_back(normed_two, inverse_two, gain_two, grad_h2)
     grad_res_low = grad_residual.astype(bf16)
@@ -637,9 +733,9 @@
         grad_att = jnp.pad(grad_att, ((0, (heads * nk - HEADS) * HEAD_DIM), (0, 0)))
     grad_att = grad_att.reshape(nk, width, tok_rows)
     upstream = jnp.stack(exchange(lambda ka: lax.dynamic_index_in_dim(grad_att, ka, 0, keepdims=False)))
-    grad_down = mm(hidden_low, cots, (0, 0)).astype(bf16)
-    grad_out = mm(att, grad_res_low, (1, 0)).astype(bf16)
-    mixed = (residual + core_sum(mm(hidden_low, full_down, (1, 0)))).astype(bf16)
+    late_low, late_res, _ = together(hidden_low, grad_res_low, grad_att)
+    grad_down = mm(late_low, cots, (0, 0)).astype(bf16)
+    grad_out = mm(att, late_res, (1, 0)).astype(bf16)
 
     n = grid.sizes
 
@@ -648,9 +744,12 @@
 
     up_own, up_send = grid.split(placed(grad_up), 1, "lo")
     up_got = grid.send(up_send, "lo")
-    sum_out = lax.psum_scatter(grad_out, ("pb", "ka"), scatter_dimension=0, tiled=True)
     down_own, down_send = grid.split(placed(grad_down), 2, "x")
-    down_send, _ = together(down_send, upstream)
+    out_own, out_send = grid.split(grad_out.reshape(model, nc, model // nc), 1, "c")
+    out_sum = added(out_own, grid.send(out_send, "c"))
+    upstream, out_sum, down_send = together(upstream, out_sum, down_send)
+    out_own, out_send = grid.split(out_sum.reshape(model, nx, model // nk), 1, "x")
+    out_got = grid.send(out_send, "x")
     down_got = grid.send(down_send, "x")
 
     parts, qkv_rest, qkv_got = [], [], []
@@ -658,54 +757,70 @@
     for which in range(len(sets)):
         part = backward_attention(meta, qkv, upstream, att_row, lse, sets, which)
         if which == last:
-            part, down_got, qkv_got = together(part, down_got, qkv_got)
+            part, qkv_got, up_got = together(part, qkv_got, up_got)
+        if which == 0:
+            part, up_got, out_got = together(part, up_got, out_got)
+            out_sum = added(out_own, out_got)
         parts.append(part)
-        own, sends = split_product(grid, h1, part, "lo")
+        own, sends = split_product(grid, h1, part, "lo", out_sum if which == 0 else None)
         qkv_rest.append(own)
-        if which < last:
-            qkv_got.append(grid.send(sends, "lo"))
+        qkv_got.append(grid.send(sends, "lo"))
         if which == 0:
-            up_own, up_send = grid.split(added(up_own, up_got), 0, "hi")
-            up_got = grid.send(up_send, "hi")
-            upstream, *_ = together(upstream, *sends, *up_send)
-
-    qkv_got.append(grid.send(sends, "lo"))
+            up_own, up_send = grid.halve(added(up_own, up_got), "hi", 0)
+            up_got = [grid.swap(up_send, "hi", 0)]
+            upstream, down_got, *_ = together(upstream, down_got, up_send, *sends)
+
+    up_own, up_send = grid.halve(added(up_own, up_got), "hi", 1)
     down_own, down_send = grid.split(added(down_own, down_got), 1, "lo")
-    down_send, _ = together(down_send, sends)
+    up_got = [grid.swap(up_send, "hi", 1)]
     down_got = grid.send(down_send, "lo")
-    grad_h1 = back_project(grid, parts, full_qkv, bounds)
-    h1_send = [grad_h1[(nc - r) % nc] for r in range(1, nc)]
-
+    late_part, *_ = together(parts[-1], *sends)
+    grad_h1 = back_project(grid, parts[:-1] + [late_part], full_qkv, bounds)
+    h1_got = grid.send([grad_h1[(nc - r) % nc] for r in range(1, nc)], "c")
+
+    qkv_got, h1_got = together(qkv_got, h1_got)
     sums = [added(own, got) for own, got in zip(qkv_rest, qkv_got)]
     by_kind = []
     for kind in range(3):
         for i, one in enumerate(sets):
             begin = kind * len(one) * HEAD_DIM
             by_kind.append(sums[i][:, :, begin : begin + len(one) * HEAD_DIM])
-    qkv_own, qkv_send = grid.split(jnp.concatenate(by_kind, axis=2), 0, "hi")
-    up_got, qkv_send, h1_send = together(up_got, qkv_send, h1_send)
-    up_own, up_send = grid.split(added(up_own, up_got), 0, "x")
-    qkv_got = grid.send(qkv_send, "hi")
-    h1_got = grid.send(h1_send, "c")
+    by_kind.append(sums[0][:, :, 3 * len(sets[0]) * HEAD_DIM :])
+    qkv_own, qkv_send = grid.halve(jnp.concatenate(by_kind, axis=2), "hi", 0)
+    qkv_got = [grid.swap(qkv_send, "hi", 0)]
+    h1_own = added(grad_h1[0], h1_got)
+    h1_got = grid.send([h1_own[(nx - r) % nx] for r in range(1, nx)], "x")
+
+    qkv_got, up_got, down_got = together(qkv_got, up_got, down_got)
+    qkv_own, qkv_send = grid.halve(added(qkv_own, qkv_got), "hi", 1)
+    qkv_got = [grid.swap(qkv_send, "hi", 1)]
+    up_own, up_send = grid.split(added(up_own, up_got)[0], 0, "x")
     up_got = grid.send(up_send, "x")
-    h1_own = added(grad_h1[0], h1_got)
-    h1_send = [h1_own[(nx - r) % nx] for r in range(1, nx)]
+    down_own, down_send = grid.halve(added(down_own, down_got), "hi", 0)
+    down_got = [grid.swap(down_send, "hi", 0)]
+
+    low, stacks, _ = together(hidden_low, down_stacks, qkv_send)
+    mixed = mm(low, put_in_place(stacks, down_at), (1, 0)).reshape(nc, tok_rows, model)
+    mixed_got = [grid.fetch(mixed[(nc - r) % nc].astype(bf16), c=r) for r in range(1, nc)]
+    mixed = (residual + added(mixed[0], mixed_got, True)).astype(bf16)
+
+    qkv_got, h1_got, up_got, down_got = together(qkv_got, h1_got, up_got, down_got)
+    group_grad = added(qkv_own, qkv_got, True).reshape(nx, nc, shard, -1)
+    group_own, group_send = grid.split(group_grad, 0, "x")
+    group_got = grid.send(group_send, "x")
     up_own, up_send = grid.split(added(up_own, up_got, True).reshape(nc, shard, -1), 0, "c")
-    h1_send, up_send = together(h1_send, up_send)
-    h1_got = grid.send(h1_send, "x")
     up_got = grid.send(up_send, "c")
-
-    down_own, down_send = grid.split(added(down_own, down_got), 0, "hi")
-    group_grad = added(qkv_own, qkv_got, True).reshape(nx, nc, shard, 3 * width)
-    group_grad, down_send, up_got = together(group_grad, down_send, up_got)
-    group_own, group_send = grid.split(group_grad, 0, "x")
-    by_x = grid.in_order([group_own] + grid.send(group_send, "x"), "x")
-    down_got = grid.send(down_send, "hi")
+    down_own, down_send = grid.halve(added(down_own, down_got), "hi", 1)
+    down_got = [grid.swap(down_send, "hi", 1)]
+
+    group_got, up_got = together(group_got, up_got)
+    by_x = grid.in_order([group_own] + group_got, "x")
     group_own, group_send = grid.split(jnp.stack(by_x), 1, "c")
     by_c = grid.in_order([group_own] + grid.send(group_send, "c"), "c")
     got = [by_c[c][x] for x in range(nx) for c in range(nc)]
     sum_up = grid.in_order([up_own] + up_got, "c")
 
+    sum_out = jnp.concatenate([got[x * nc + c][:, 3 * width :] for c in range(nc) for x in range(nx)], axis=1)
     kept = min(nk * width, HEADS * HEAD_DIM)
     sum_qkv = []
     for kind in range(3):
@@ -715,14 +830,13 @@
                 sum_qkv.append(one[:, kind * width : kind * width + size])
     sum_qkv = jnp.concatenate(sum_qkv, axis=1)
     sum_up = jnp.stack([one.reshape(shard, chips, strip) for one in sum_up], axis=2).reshape(shard, -1)
-    sum_down = added(down_own, down_got, True)
+    sum_down = added(down_own, down_got, True)[0]
     normed_one, inverse_one = norm_parts(inputs)
     tokens_grad = added(h1_own[0], h1_got, True)
     tokens_grad = (grad_residual + norm_back(normed_one, inverse_one, gain_one, tokens_grad)).astype(bf16)
 
     grad_gain_one = jnp.sum(sum_qkv * qkv_weight.astype(f32), axis=1) / attn_gain.astype(f32)
     grad_gain_two = jnp.sum(sum_up * up_weight.astype(f32), axis=1) / mlp_gain.astype(f32)
-    sum_out = tie(sum_out, tokens_grad).astype(f32)
     return (mixed, tokens_grad, sum_qkv, sum_out, sum_up, sum_down, grad_gain_one, grad_gain_two)
 
 

time: 325 us -> 299 us (0.920)
  matrix products: 31.6 us -> 16.5 us
  waiting for transfers between devices: 86.6 us -> 77.6 us
  local copies, waits for them, and re-layouts: 32.6 us -> 26.4 us
    dot_general x9 -> x6, matrix products: 31.6 us -> 16.5 us  [mm(): lax.dot_general(a, b, ((dims[:1], dims[1:]), ((), ())), preferred_element...]
    pallas_call x2 -> x3, Pallas kernels: 2.94 us -> 17.2 us  [the longest x1 14.2 us: hidden_layer(): pl.pallas_call(functools.partial(hidden_kernel, (len(up_stacks), len(down...]
    ppermute x47 -> x46, waiting for transfers between devices: 86.6 us -> 75.8 us  [fetch(): return lax.ppermute(value, ('pb', 'ka'), pairs)]
    pallas_call x2, Pallas kernels: 34.5 us -> 25.1 us  [backward_attention(): pl.pallas_call(functools.partial(backward_kernel, sets, which, 256, 256,...]
    convert_element_type x1 -> x2, other arithmetic: 1.41 us -> 5.61 us  [the longest x1 3.07 us: body(): grad_res_low = grad_residual.astype(bf16)]
    convert_element_type x7 -> x12, other arithmetic: 6.9 us -> 11.1 us  [added(): return total if last else total.astype(own.dtype)]
    pallas_call x1, Pallas kernels: 18.9 us -> 15.1 us  [forward_attention(): pl.pallas_call(functools.partial(forward_kernel, sets, 256, 512, SEQ_UNIT...]
    ppermute x47 -> x46, starting transfers between devices: 49.5 us -> 52.4 us  [fetch(): return lax.ppermute(value, ('pb', 'ka'), pairs)]
  transfers between devices with their start and end apart: 49 -> 47, of which waited for: 14 -> 20; matrix products, arithmetic and copies ran while one was open for 21% -> 21% of each run, Pallas kernels for 23% -> 18%
where the time goes in v3:
time: 299 us; the launch traced here: 293 us
  waiting for transfers between devices  77.6 us (26%)
  Pallas kernels  73.4 us (25%)
  starting transfers between devices  52.5 us (18%)
  other arithmetic  31 us (10%)
  local copies, waits for them, and re-layouts  26.4 us (9%)
  matrix products  16.5 us (6%)
  between operations  16 us (5%)
    ppermute x46, waiting for transfers between devices, fetch(): return lax.ppermute(value, ('pb', 'ka'), pairs)  75.8 us
    ppermute x46, starting transfers between devices, fetch(): return lax.ppermute(value, ('pb', 'ka'), pairs)  52.4 us
    pallas_call x2, Pallas kernels, backward_attention(): pl.pallas_call(functools.partial(backward_kernel, sets, which, 256, 256,...  25.1 us
    dot_general x6, matrix products, mm(): lax.dot_general(a, b, ((dims[:1], dims[1:]), ((), ())), preferred_element...  16.5 us
    pallas_call x1, Pallas kernels, forward_attention(): pl.pallas_call(functools.partial(forward_kernel, sets, 256, 512, SEQ_UNIT...  15.1 us
    pallas_call x1, Pallas kernels, hidden_layer(): pl.pallas_call(functools.partial(hidden_kernel, (len(up_stacks), len(down...  14.2 us
    convert_element_type x12, other arithmetic, added(): return total if last else total.astype(own.dtype)  11.1 us
    unnamed x106, local copies, waits for them, and re-layouts  8.82 us
  transfers between devices with their start and end apart: 47, of which 20 were waited for; matrix products, arithmetic and copies ran while one was open for 21% of the time, Pallas kernels for 18%

profile of v3, /device:TPU:0, one launch (start us, length us, event | category | flops | bytes accessed | tf_op | source)
XLA Modules:
  0.0 293.5 jit_solution(9399760926554476750)
XLA Ops:
  10.0 2.6 collective-permute-start.1
  13.3 1.2 collective-permute-done.1
  14.5 1.4 collective-permute-done.2
  17.5 3.8 %collective-permute-start.5 = (bf16[1,96,640]{2,1,0:T(8,128)(2,1)S(1)}, bf16[1,96,640]{2,1,0:T(8,128)(2,1)S(1)}, u32[]{:S(2)}, u32[]{:S(2)}) collective-permute-start(bf16[1,96,640]{2,1,0:T(8,128)(2,1)S(1)} %bitcast.229), channel_id=1, source_target_pairs={{8,0},{9,1},{10,2},{11,3},{12,4},{13,5},{14,6},{15,7},{16,8},{17,9... | collective-permute-start | bytes 368648 | tf_op jit(solution)/shard_map/ppermute | solution.py:41
  22.3 13.3 %collective-permute-done.3.refs_2_ = bf16[512,768]{1,0:T(8,128)(2,1)S(1)} collective-permute-done((bf16[512,768]{1,0:T(8,128)(2,1)S(1)}, bf16[512,768]{1,0:T(8,128)(2,1)S(1)}, u32[]{:S(2)}, u32[]{:S(2)}) %collective-permute-start.3) | collective-permute-done | bytes 786464 | tf_op jit(solution)/shard_map/ppermute | solution.py:41
  35.6 1.3 pad_maximum_fusion
  37.1 1.2 sort.17
  38.5 1.6 collective-permute-start.9
  40.7 2.4 slice_bitcast_fusion.2
  43.0 3.6 %collective-permute-start.10 = (bf16[192,768]{1,0:T(8,128)(2,1)}, bf16[192,768]{1,0:T(8,128)(2,1)}, u32[]{:S(2)}, u32[]{:S(2)}) collective-permute-start(bf16[192,768]{1,0:T(8,128)(2,1)} %fusion.30), channel_id=1, source_target_pairs={{8,0},{9,1},{10,2},{11,3},{12,4},{13,5},{14,6},{15,7},{16,8},{17,9... | collective-permute-start | bytes 884744 | tf_op jit(solution)/shard_map/ppermute | solution.py:41
  46.6 1.2 collective-permute-start.12
  48.0 4.1 %collective-permute-done.9.refs_1_ = bf16[4,96,640]{2,1,0:T(8,128)(2,1)S(1)} collective-permute-done((bf16[4,96,640]{2,1,0:T(8,128)(2,1)S(1)}, bf16[4,96,640]{2,1,0:T(8,128)(2,1)S(1)}, u32[]{:S(2)}, u32[]{:S(2)}) %collective-permute-start.9) | collective-permute-done | bytes 491552 | tf_op jit(solution)/shard_map/ppermute | solution.py:41
  54.9 1.9 shard_map.161.refs_4_.refs_2_
  56.8 5.4 %shard_map.162 = (bf16[768,2048]{1,0:T(8,128)(2,1)S(1)}, bf16[576,2048]{1,0:T(8,128)(2,1)S(1)}) custom-call(bf16[512,768]{1,0:T(8,128)(2,1)S(1)} %copy-done, bf16[512,768]{1,0:T(8,128)(2,1)S(1)} %copy-done.4, bf16[512,768]{1,0:T(8,128)(2,1)S(1)} %collective-permute-done.3.refs_2_, bf16[512,768]{1,0:T(8,128)(2,1)S(1)} %get-tuple-element.146.refs_3_, ...), custom_call_target="tpu_custom_call" | custom-call | flops 1000000 | bytes 100000 | tf_op jit(solution)/shard_map/pallas_call | solution.py:429
  62.6 10.6 %collective-permute-done.11 = bf16[192,768]{1,0:T(8,128)(2,1)} collective-permute-done((bf16[192,768]{1,0:T(8,128)(2,1)}, bf16[192,768]{1,0:T(8,128)(2,1)}, u32[]{:S(2)}, u32[]{:S(2)}) %collective-permute-start.11) | collective-permute-done | bytes 294944 | tf_op jit(solution)/shard_map/ppermute | solution.py:41
  73.2 1.4 pad_maximum_fusion.1
  75.5 1.5 collective-permute-start.14
  77.1 15.1 %shard_map.163 = (bf16[4,192,512]{2,1,0:T(8,128)(2,1)S(1)}, f32[192,2048]{1,0:T(8,128)S(1)}, f32[8,2048]{1,0:T(8,128)S(1)}) custom-call(s32[17]{0:T(128)S(1)} %pad_add_fusion.meta_ref, bf16[576,2048]{1,0:T(8,128)(2,1)S(1)} %get-tuple-element.82.qkv_ref), custom_call_target="tpu_custom_call" | custom-call | flops 20999999488 | bytes 1000000 | tf_op jit(solution)/shard_map/pallas_call | solution.py:275
  92.2 1.5 copy-done.7
  93.7 1.3 collective-permute-start.16
  95.7 1.3 collective-permute-start.19
  98.7 4.5 %collective-permute-start.18 = (bf16[8,96,768]{2,1,0:T(8,128)(2,1)}, bf16[8,96,768]{2,1,0:T(8,128)(2,1)}, u32[]{:S(2)}, u32[]{:S(2)}) collective-permute-start(bf16[8,96,768]{2,1,0:T(8,128)(2,1)} %constant_dynamic-update-slice_fusion.refs_0_), channel_id=1, source_target_pairs={{4,0},{5,1},{6,2},{7,3},{0,4},{1,5},{2,6},{3,7},{12,8},{13,9},{14,... | collective-permute-start | bytes 3538952 | tf_op jit(solution)/shard_map/ppermute | solution.py:41
  103.4 3.8 %collective-permute-done.17 = bf16[192,512]{1,0:T(8,128)(2,1)S(1)} collective-permute-done((bf16[192,512]{1,0:T(8,128)(2,1)S(1)}, bf16[192,512]{1,0:T(8,128)(2,1)S(1)}, u32[]{:S(2)}, u32[]{:S(2)}) %collective-permute-start.17) | collective-permute-done | bytes 196640 | tf_op jit(solution)/shard_map/ppermute | solution.py:41
  108.2 1.8 all-gather.2.cloned.1.call-done
  110.0 2.4 fusion.54
  112.7 1.2 multiply_convert_fusion.refs_4_
  114.5 2.1 collective-permute-done.20.refs_5_
  116.5 16.2 %collective-permute-done.19.refs_3_.refs_1_ = bf16[8,96,768]{2,1,0:T(8,128)(2,1)} collective-permute-done((bf16[8,96,768]{2,1,0:T(8,128)(2,1)S(1)}, bf16[8,96,768]{2,1,0:T(8,128)(2,1)}, u32[]{:S(2)}, u32[]{:S(2)}) %collective-permute-start.19) | collective-permute-done | bytes 1179680 | tf_op jit(solution)/shard_map/ppermute | solution.py:41
  132.8 14.2 %shard_map.164 = (bf16[1024,1536]{1,0:T(8,128)(2,1)}, bf16[1024,1536]{1,0:T(8,128)(2,1)}, f32[512,768]{1,0:T(8,128)}, bf16[512,768]{1,0:T(8,128)(2,1)S(1)}) custom-call(s32[16]{0:T(128)S(1)} %stack.191.up_at, s32[16]{0:T(128)S(1)} %stack.192.down_at, bf16[8,96,768]{2,1,0:T(8,128)(2,1)} %constant_dynamic-update-slice_fusion.refs_0_, ...), custom_call_target="tpu_custom_call" | custom-call | flops 14000000000 | bytes 1000000 | tf_op jit(solution)/shard_map/pallas_call | solution.py:563
  147.0 5.6 %convolution_convert_fusion = bf16[768,1536]{1,0:T(8,128)(2,1)S(1)} fusion(bf16[1024,1536]{1,0:T(8,128)(2,1)} %get-tuple-element.101, bf16[512,768]{1,0:T(8,128)(2,1)} %collective-permute-done.20.refs_5_, bf16[512,768]{1,0:T(8,128)(2,1)} %multiply_convert_fusion.refs_4_), kind=kOutput, calls=%fused_computation | convolution fusion | flops 2420244480 | bytes 7077888 | tf_op jit(solution)/shard_map/dot_general | solution.py:596
  152.6 1.1 dynamic-slice_bitcast_fusion
  153.8 2.4 collective-permute-start.27
  156.8 3.1 %fusion.46 = (bf16[512,768]{1,0:T(8,128)(2,1)S(1)}, f32[512,768]{1,0:T(8,128)}) fusion(f32[512]{0:T(512)S(1)} %get-tuple-element.205, f32[512]{0:T(512)S(1)} %add_rsqrt_fusion.1, f32[512,768]{1,0:T(8,128)S(1)} %copy-done.20, f32[512]{0:T(512)S(1)} %broadcast_multiply_fusion.5, f32[512]{0:T(512)S(1)} %get-tuple-element.206, f32[768]{0:T(1024)S(1)} %get-tuple-element.139, ...), kind=kLoop, calls=%fused_computation.195 | loop fusion | flops 4718592 | bytes 7089152 | tf_op jit(solution)/shard_map/convert_element_type | solution.py:730
  163.3 1.2 collective-permute-start.24
  164.8 4.3 %convolution_convert_fusion.1 = bf16[1536,768]{1,0:T(8,128)(2,1)S(1)} fusion(bf16[1024,1536]{1,0:T(8,128)(2,1)S(1)} %copy-done.49, bf16[512,768]{1,0:T(8,128)(2,1)} %collective-permute-done.21.refs_7_, bf16[512,768]{1,0:T(8,128)(2,1)} %refs_6_.1), kind=kOutput, calls=%fused_computation.1 | convolution fusion | flops 2420244480 | bytes 7077888 | tf_op jit(solution)/shard_map/dot_general | solution.py:596
  169.2 1.2 constant_dynamic-slice_fusion.2
  170.4 1.2 copy.54
  171.6 2.2 collective-permute-done.25
  175.0 1.2 collective-permute-start.28
  177.3 1.4 copy-done.12
  178.7 17.4 %shard_map.165.right_ref.refs_0_ = bf16[2048,384]{1,0:T(8,128)(2,1)S(1)} custom-call(s32[17]{0:T(128)S(1)} %pad_add_fusion.meta_ref, bf16[576,2048]{1,0:T(8,128)(2,1)} %copy-done.7, bf16[4,192,512]{2,1,0:T(8,128)(2,1)S(1)} %pad_maximum_fusion.3.up_ref, f32[192,2048]{1,0:T(8,128)S(1)} %copy-done.12, f32[8,2048]{1,0:T(8,128)S(1)} %get-tuple-element.100.lse_ref), custom_call_target="tpu_custom_call" | custom-call | flops 25999998976 | bytes 100000 | tf_op jit(solution)/shard_map/pallas_call | solution.py:378
  196.2 2.2 fusion.1
  200.2 2.0 shard_map.166
  202.2 6.7 %collective-permute-start.30 = (bf16[4,96,576]{2,1,0:T(8,128)(2,1)S(1)}, bf16[4,96,576]{2,1,0:T(8,128)(2,1)S(1)}, u32[]{:S(2)}, u32[]{:S(2)}) collective-permute-start(bf16[4,96,576]{2,1,0:T(8,128)(2,1)S(1)} %get-tuple-element.108), channel_id=1, source_target_pairs={{4,0},{5,1},{6,2},{7,3},{0,4},{1,5},{2,6},{3,7},{12,8},{13,9},{14,... | collective-permute-start | bytes 1327112 | tf_op jit(solution)/shard_map/ppermute | solution.py:41
  209.1 3.5 %collective-permute-done.29 = bf16[4,2,96,768]{3,2,0,1:T(8,128)(2,1)} collective-permute-done((bf16[4,2,96,768]{3,2,0,1:T(8,128)(2,1)}, bf16[4,2,96,768]{3,2,0,1:T(8,128)(2,1)}, u32[]{:S(2)}, u32[]{:S(2)}) %collective-permute-start.29) | collective-permute-done | bytes 1179680 | tf_op jit(solution)/shard_map/ppermute | solution.py:41
  212.6 7.6 %shard_map.167.right_ref.refs_1_ = bf16[2048,192]{1,0:T(8,128)(2,1)S(1)} custom-call(s32[17]{0:T(128)S(1)} %pad_add_fusion.meta_ref, bf16[576,2048]{1,0:T(8,128)(2,1)S(1)} %copy-done.8, bf16[4,192,512]{2,1,0:T(8,128)(2,1)S(1)} %pad_maximum_fusion.3.up_ref, f32[192,2048]{1,0:T(8,128)S(1)} %copy-done.13, f32[8,2048]{1,0:T(8,128)S(1)} %get-tuple-element.100.lse_ref), custom_call_target="tpu_custom_call" | custom-call | flops 1000000 | bytes 100000 | tf_op jit(solution)/shard_map/pallas_call | solution.py:378
  222.2 5.2 %shard_map.169 = (bf16[2,512,768]{2,1,0:T(8,128)(2,1)S(1)}, bf16[2,512,768]{2,1,0:T(8,128)(2,1)}) custom-call(bf16[2048,384]{1,0:T(8,128)(2,1)} %copy-done.3, bf16[2048,192]{1,0:T(8,128)(2,1)S(1)} %shard_map.167.right_ref.refs_1_, bf16[768,640]{1,0:T(8,128)(2,1)S(1)} %shard_map.161.refs_4_.refs_2_), custom_call_target="tpu_custom_call" | custom-call | flops 1000000 | bytes 100000 | tf_op jit(solution)/shard_map/pallas_call | solution.py:495
  227.7 6.0 %collective-permute-start.32 = (bf16[4,96,192]{2,1,0:T(8,128)(2,1)}, bf16[4,96,192]{2,1,0:T(8,128)(2,1)S(1)}, u32[]{:S(2)}, u32[]{:S(2)}) collective-permute-start(bf16[4,96,192]{2,1,0:T(8,128)(2,1)} %copy-done.18), channel_id=1, source_target_pairs={{4,0},{5,1},{6,2},{7,3},{0,4},{1,5},{2,6},{3,7},{12,8},{13,9},{14,... | collective-permute-start | bytes 442376 | tf_op jit(solution)/shard_map/ppermute | solution.py:41
  233.8 2.0 fusion
  236.7 1.2 fusion.23
  239.9 1.4 concatenate.53
  242.4 1.8 add_convert_fusion
  244.3 1.3 collective-permute-start.39
  245.6 7.3 %collective-permute-done.35 = bf16[1,2,48,1536]{3,2,1,0:T(8,128)(2,1)} collective-permute-done((bf16[1,2,48,1536]{3,2,1,0:T(8,128)(2,1)}, bf16[1,2,48,1536]{3,2,1,0:T(8,128)(2,1)}, u32[]{:S(2)}, u32[]{:S(2)}) %collective-permute-start.35) | collective-permute-done | bytes 294944 | tf_op jit(solution)/shard_map/ppermute | solution.py:41
  252.9 4.6 %collective-permute-done.34 = bf16[2,96,768]{2,1,0:T(8,128)(2,1)S(1)} collective-permute-done((bf16[2,96,768]{2,1,0:T(8,128)(2,1)S(1)}, bf16[2,96,768]{2,1,0:T(8,128)(2,1)S(1)}, u32[]{:S(2)}, u32[]{:S(2)}) %collective-permute-start.34) | collective-permute-done | bytes 294944 | tf_op jit(solution)/shard_map/ppermute | solution.py:41
  257.5 1.2 fusion.22
  260.0 1.3 collective-permute-start.40
  261.3 1.2 collective-permute-start.38
  262.6 3.6 %shard_map.170 = bf16[1536,768]{1,0:T(8,128)(2,1)S(1)} custom-call(s32[16]{0:T(128)S(1)} %broadcast_multiply_fusion.6.offs_ref, bf16[8,96,768]{2,1,0:T(8,128)(2,1)S(1)} %copy-done.6, bf16[8,96,768]{2,1,0:T(8,128)(2,1)} %collective-permute-done.19.refs_3_.refs_1_), custom_call_target="tpu_custom_call" | custom-call | flops 1000000 | bytes 100000 | tf_op jit(solution)/shard_map/pallas_call | solution.py:107
  266.2 2.6 fusion.55
  270.2 1.6 collective-permute-start.45
  273.8 1.6 fusion.10
  275.4 2.9 %collective-permute-done.42 = f32[2,24,768]{2,1,0:T(8,128)S(1)} collective-permute-done((f32[2,24,768]{2,1,0:T(8,128)S(1)}, f32[2,24,768]{2,1,0:T(8,128)S(1)}, u32[]{:S(2)}, u32[]{:S(2)}) %collective-permute-start.42) | collective-permute-done | bytes 147488 | tf_op jit(solution)/shard_map/ppermute | solution.py:41
  283.6 2.5 fusion.13
  (271 shorter events, 40.3 us)
Async XLA Ops:
  7.2 5.4 %copy-start.37 = (bf16[24,3072]{1,0:T(8,128)(2,1)S(1)}, bf16[24,3072]{1,0:T(8,128)(2,1)}, u32[]{:S(2)}) copy-start(bf16[24,3072]{1,0:T(8,128)(2,1)} %param.15) | copy-start | bytes 442372
  7.2 102.8 %all-gather.2.cloned.1.call-start = ((), (), s32[]{:S(2)}) async-start(), calls=%async_computation | async-start | bytes 1216512 | tf_op jit(solution)/shard_map/all_gather | solution.py:669
  8.6 7.3 %copy-start = (bf16[512,768]{1,0:T(8,128)(2,1)S(1)}, bf16[512,768]{1,0:T(8,128)(2,1)}, u32[]{:S(2)}) copy-start(bf16[512,768]{1,0:T(8,128)(2,1)} %refs_0_.1) | copy-start | bytes 2359300
  9.1 7.7 %copy-start.42 = (bf16[96,768]{1,0:T(8,128)(2,1)S(1)}, bf16[96,768]{1,0:T(8,128)(2,1)}, u32[]{:S(2)}) copy-start(bf16[96,768]{1,0:T(8,128)(2,1)} %param.16) | copy-start | bytes 442372
  9.5 3.8 %collective-permute-start = (bf16[24,640]{1,0:T(8,128)(2,1)S(1)}, bf16[24,640]{1,0:T(8,128)(2,1)S(1)}, u32[]{:S(2)}, u32[]{:S(2)}) collective-permute-start(bf16[24,640]{1,0:T(8,128)(2,1)S(1)} %get-tuple-element.186), channel_id=1, source_target_pairs={{1,0},{0,1},{3,2},{2,3},{5,4},{4,5},{7,6},{6,7},{9,8},{8,9},{11,10... | collective-permute-start | bytes 92168 | tf_op jit(solution)/shard_map/ppermute | solution.py:41
  10.0 4.5 %collective-permute-start.1 = (bf16[24,640]{1,0:T(8,128)(2,1)S(1)}, bf16[24,640]{1,0:T(8,128)(2,1)S(1)}, u32[]{:S(2)}, u32[]{:S(2)}) collective-permute-start(bf16[24,640]{1,0:T(8,128)(2,1)S(1)} %get-tuple-element.185), channel_id=1, source_target_pairs={{2,0},{3,1},{0,2},{1,3},{6,4},{7,5},{4,6},{5,7},{10,8},{11,9},{8,1... | collective-permute-start | bytes 92168 | tf_op jit(solution)/shard_map/ppermute | solution.py:41
  12.6 3.3 %collective-permute-start.2 = (bf16[24,640]{1,0:T(8,128)(2,1)S(1)}, bf16[24,640]{1,0:T(8,128)(2,1)S(1)}, u32[]{:S(2)}, u32[]{:S(2)}) collective-permute-start(bf16[24,640]{1,0:T(8,128)(2,1)S(1)} %get-tuple-element.184), channel_id=1, source_target_pairs={{3,0},{2,1},{1,2},{0,3},{7,4},{6,5},{5,6},{4,7},{11,8},{10,9},{9,1... | collective-permute-start | bytes 92168 | tf_op jit(solution)/shard_map/ppermute | solution.py:41
  13.1 3.6 %collective-permute-start.4 = (bf16[24,1536]{1,0:T(8,128)(2,1)S(1)}, bf16[24,1536]{1,0:T(8,128)(2,1)S(1)}, u32[]{:S(2)}, u32[]{:S(2)}) collective-permute-start(bf16[24,1536]{1,0:T(8,128)(2,1)S(1)} %dynamic-slice_bitcast_fusion.12), channel_id=1, source_target_pairs={{1,0},{0,1},{3,2},{2,3},{5,4},{4,5},{7,6},{6,7},{9,8},{8,9},{11,10... | collective-permute-start | bytes 221192 | tf_op jit(solution)/shard_map/ppermute | solution.py:41
  15.9 19.7 %collective-permute-start.3 = (bf16[512,768]{1,0:T(8,128)(2,1)S(1)}, bf16[512,768]{1,0:T(8,128)(2,1)S(1)}, u32[]{:S(2)}, u32[]{:S(2)}) collective-permute-start(bf16[512,768]{1,0:T(8,128)(2,1)S(1)} %copy-done), channel_id=1, source_target_pairs={{2,0},{3,1},{0,2},{1,3},{6,4},{7,5},{4,6},{5,7},{10,8},{11,9},{8,1... | collective-permute-start | bytes 2359304 | tf_op jit(solution)/shard_map/ppermute | solution.py:41
  17.5 19.3 %collective-permute-start.5 = (bf16[1,96,640]{2,1,0:T(8,128)(2,1)S(1)}, bf16[1,96,640]{2,1,0:T(8,128)(2,1)S(1)}, u32[]{:S(2)}, u32[]{:S(2)}) collective-permute-start(bf16[1,96,640]{2,1,0:T(8,128)(2,1)S(1)} %bitcast.229), channel_id=1, source_target_pairs={{8,0},{9,1},{10,2},{11,3},{12,4},{13,5},{14,6},{15,7},{16,8},{17,9... | collective-permute-start | bytes 368648 | tf_op jit(solution)/shard_map/ppermute | solution.py:41
  21.3 15.6 %collective-permute-start.6 = (bf16[1,96,640]{2,1,0:T(8,128)(2,1)S(1)}, bf16[1,96,640]{2,1,0:T(8,128)(2,1)S(1)}, u32[]{:S(2)}, u32[]{:S(2)}) collective-permute-start(bf16[1,96,640]{2,1,0:T(8,128)(2,1)S(1)} %bitcast.230), channel_id=1, source_target_pairs={{16,0},{17,1},{18,2},{19,3},{20,4},{21,5},{22,6},{23,7},{24,8},{25... | collective-permute-start | bytes 368648 | tf_op jit(solution)/shard_map/ppermute | solution.py:41
  21.3 15.6 %collective-permute-start.7 = (bf16[1,96,640]{2,1,0:T(8,128)(2,1)S(1)}, bf16[1,96,640]{2,1,0:T(8,128)(2,1)S(1)}, u32[]{:S(2)}, u32[]{:S(2)}) collective-permute-start(bf16[1,96,640]{2,1,0:T(8,128)(2,1)S(1)} %bitcast.231), channel_id=1, source_target_pairs={{24,0},{25,1},{26,2},{27,3},{28,4},{29,5},{30,6},{31,7},{0,8},{1,9... | collective-permute-start | bytes 368648 | tf_op jit(solution)/shard_map/ppermute | solution.py:41
  36.9 3.8 %collective-permute-start.8 = (bf16[2,512,768]{2,1,0:T(8,128)(2,1)}, bf16[2,512,768]{2,1,0:T(8,128)(2,1)}, u32[]{:S(2)}, u32[]{:S(2)}) collective-permute-start(bf16[2,512,768]{2,1,0:T(8,128)(2,1)} %pad_maximum_fusion), channel_id=1, source_target_pairs={{1,0},{0,1},{3,2},{2,3},{5,4},{4,5},{7,6},{6,7},{9,8},{8,9},{11,10... | collective-permute-start | bytes 4718600 | tf_op jit(solution)/shard_map/ppermute | solution.py:41
  38.5 9.4 %copy-start.45 = (s32[1,2]{1,0:T(1,128)S(1)}, s32[1,2]{1,0:T(1,128)}, u32[]{:S(2)}) copy-start(s32[1,2]{1,0:T(1,128)} %param.11) | copy-start | bytes 28
  38.5 13.6 %collective-permute-start.9 = (bf16[4,96,640]{2,1,0:T(8,128)(2,1)S(1)}, bf16[4,96,640]{2,1,0:T(8,128)(2,1)S(1)}, u32[]{:S(2)}, u32[]{:S(2)}) collective-permute-start(bf16[4,96,640]{2,1,0:T(8,128)(2,1)S(1)} %pad_maximum_fusion.4.refs_0_), channel_id=1, source_target_pairs={{4,0},{5,1},{6,2},{7,3},{0,4},{1,5},{2,6},{3,7},{12,8},{13,9},{14,... | collective-permute-start | bytes 1474568 | tf_op jit(solution)/shard_map/ppermute | solution.py:41
  43.0 19.5 %collective-permute-start.10 = (bf16[192,768]{1,0:T(8,128)(2,1)}, bf16[192,768]{1,0:T(8,128)(2,1)}, u32[]{:S(2)}, u32[]{:S(2)}) collective-permute-start(bf16[192,768]{1,0:T(8,128)(2,1)} %fusion.30), channel_id=1, source_target_pairs={{8,0},{9,1},{10,2},{11,3},{12,4},{13,5},{14,6},{15,7},{16,8},{17,9... | collective-permute-start | bytes 884744 | tf_op jit(solution)/shard_map/ppermute | solution.py:41
  46.6 26.5 %collective-permute-start.11 = (bf16[192,768]{1,0:T(8,128)(2,1)}, bf16[192,768]{1,0:T(8,128)(2,1)}, u32[]{:S(2)}, u32[]{:S(2)}) collective-permute-start(bf16[192,768]{1,0:T(8,128)(2,1)} %fusion.30), channel_id=1, source_target_pairs={{16,0},{17,1},{18,2},{19,3},{20,4},{21,5},{22,6},{23,7},{24,8},{25... | collective-permute-start | bytes 884744 | tf_op jit(solution)/shard_map/ppermute | solution.py:41
  46.6 26.5 %collective-permute-start.12 = (bf16[192,768]{1,0:T(8,128)(2,1)}, bf16[192,768]{1,0:T(8,128)(2,1)}, u32[]{:S(2)}, u32[]{:S(2)}) collective-permute-start(bf16[192,768]{1,0:T(8,128)(2,1)} %fusion.30), channel_id=1, source_target_pairs={{24,0},{25,1},{26,2},{27,3},{28,4},{29,5},{30,6},{31,7},{0,8},{1,9... | collective-permute-start | bytes 884744 | tf_op jit(solution)/shard_map/ppermute | solution.py:41
  48.0 8.8 %copy-start.4 = (bf16[512,768]{1,0:T(8,128)(2,1)S(1)}, bf16[512,768]{1,0:T(8,128)(2,1)}, u32[]{:S(2)}) copy-start(bf16[512,768]{1,0:T(8,128)(2,1)} %get-tuple-element.147.refs_1_) | copy-start | bytes 2359300
  62.3 12.4 %copy-start.1 = (bf16[768,2048]{1,0:T(8,128)(2,1)}, bf16[768,2048]{1,0:T(8,128)(2,1)S(1)}, u32[]{:S(2)}) copy-start(bf16[768,2048]{1,0:T(8,128)(2,1)S(1)} %get-tuple-element.93.left_ref) | copy-start | bytes 9437188
  74.7 19.0 %collective-permute-start.13 = (bf16[4,96,768]{2,1,0:T(8,128)(2,1)S(1)}, bf16[4,96,768]{2,1,0:T(8,128)(2,1)S(1)}, u32[]{:S(2)}, u32[]{:S(2)}) collective-permute-start(bf16[4,96,768]{2,1,0:T(8,128)(2,1)S(1)} %get-tuple-element.85), channel_id=1, source_target_pairs={{2,0},{3,1},{0,2},{1,3},{6,4},{7,5},{4,6},{5,7},{10,8},{11,9},{8,1... | collective-permute-start | bytes 1769480 | tf_op jit(solution)/shard_map/ppermute | solution.py:41
  75.5 18.1 %collective-permute-start.14 = (bf16[4,96,768]{2,1,0:T(8,128)(2,1)S(1)}, bf16[4,96,768]{2,1,0:T(8,128)(2,1)S(1)}, u32[]{:S(2)}, u32[]{:S(2)}) collective-permute-start(bf16[4,96,768]{2,1,0:T(8,128)(2,1)S(1)} %get-tuple-element.87), channel_id=1, source_target_pairs={{4,0},{5,1},{6,2},{7,3},{0,4},{1,5},{2,6},{3,7},{12,8},{13,9},{14,... | collective-permute-start | bytes 1769480 | tf_op jit(solution)/shard_map/ppermute | solution.py:41
  93.7 9.5 %collective-permute-start.15 = (bf16[192,512]{1,0:T(8,128)(2,1)S(1)}, bf16[192,512]{1,0:T(8,128)(2,1)S(1)}, u32[]{:S(2)}, u32[]{:S(2)}) collective-permute-start(bf16[192,512]{1,0:T(8,128)(2,1)S(1)} %get-tuple-element.158), channel_id=1, source_target_pairs={{1,0},{0,1},{3,2},{2,3},{5,4},{4,5},{7,6},{6,7},{9,8},{8,9},{11,10... | collective-permute-start | bytes 589832 | tf_op jit(solution)/shard_map/ppermute | solution.py:41
  93.7 9.6 %collective-permute-start.16 = (bf16[192,512]{1,0:T(8,128)(2,1)S(1)}, bf16[192,512]{1,0:T(8,128)(2,1)S(1)}, u32[]{:S(2)}, u32[]{:S(2)}) collective-permute-start(bf16[192,512]{1,0:T(8,128)(2,1)S(1)} %get-tuple-element.160), channel_id=1, source_target_pairs={{2,0},{3,1},{0,2},{1,3},{6,4},{7,5},{4,6},{5,7},{10,8},{11,9},{8,1... | collective-permute-start | bytes 589832 | tf_op jit(solution)/shard_map/ppermute | solution.py:41
  95.0 12.2 %collective-permute-start.17 = (bf16[192,512]{1,0:T(8,128)(2,1)S(1)}, bf16[192,512]{1,0:T(8,128)(2,1)S(1)}, u32[]{:S(2)}, u32[]{:S(2)}) collective-permute-start(bf16[192,512]{1,0:T(8,128)(2,1)S(1)} %get-tuple-element.159), channel_id=1, source_target_pairs={{3,0},{2,1},{1,2},{0,3},{7,4},{6,5},{5,6},{4,7},{11,8},{10,9},{9,1... | collective-permute-start | bytes 589832 | tf_op jit(solution)/shard_map/ppermute | solution.py:41
  95.7 11.5 %copy-start.5 = (bf16[8,96,768]{2,1,0:T(8,128)(2,1)}, bf16[8,96,768]{2,1,0:T(8,128)(2,1)S(1)}, u32[]{:S(2)}) copy-start(bf16[8,96,768]{2,1,0:T(8,128)(2,1)S(1)} %constant_dynamic-update-slice_fusion.2.refs_2_.refs_0_) | copy-start | bytes 3538948
  95.7 37.0 %collective-permute-start.19 = (bf16[8,96,768]{2,1,0:T(8,128)(2,1)S(1)}, bf16[8,96,768]{2,1,0:T(8,128)(2,1)}, u32[]{:S(2)}, u32[]{:S(2)}) collective-permute-start(bf16[8,96,768]{2,1,0:T(8,128)(2,1)S(1)} %constant_dynamic-update-slice_fusion.2.refs_2_.refs_0_), channel_id=1, source_target_pairs={{2,0},{3,1},{0,2},{1,3},{6,4},{7,5},{4,6},{5,7},{10,8},{11,9},{8,1... | collective-permute-start | bytes 3538952 | tf_op jit(solution)/shard_map/ppermute | solution.py:41
  98.7 34.1 %collective-permute-start.18 = (bf16[8,96,768]{2,1,0:T(8,128)(2,1)}, bf16[8,96,768]{2,1,0:T(8,128)(2,1)}, u32[]{:S(2)}, u32[]{:S(2)}) collective-permute-start(bf16[8,96,768]{2,1,0:T(8,128)(2,1)} %constant_dynamic-update-slice_fusion.refs_0_), channel_id=1, source_target_pairs={{4,0},{5,1},{6,2},{7,3},{0,4},{1,5},{2,6},{3,7},{12,8},{13,9},{14,... | collective-permute-start | bytes 3538952 | tf_op jit(solution)/shard_map/ppermute | solution.py:41
  103.2 11.2 %collective-permute-start.21 = (bf16[512,768]{1,0:T(8,128)(2,1)}, bf16[512,768]{1,0:T(8,128)(2,1)}, u32[]{:S(2)}, u32[]{:S(2)}) collective-permute-start(bf16[512,768]{1,0:T(8,128)(2,1)} %refs_6_.1), channel_id=1, source_target_pairs={{1,0},{0,1},{3,2},{2,3},{5,4},{4,5},{7,6},{6,7},{9,8},{8,9},{11,10... | collective-permute-start | bytes 2359304 | tf_op jit(solution)/shard_map/ppermute | solution.py:41
  113.9 2.6 collective-permute-start.20
  146.9 9.2 %collective-permute-start.22 = (bf16[512,768]{1,0:T(8,128)(2,1)S(1)}, bf16[512,768]{1,0:T(8,128)(2,1)S(1)}, u32[]{:S(2)}, u32[]{:S(2)}) collective-permute-start(bf16[512,768]{1,0:T(8,128)(2,1)S(1)} %get-tuple-element.95), channel_id=1, source_target_pairs={{1,0},{0,1},{3,2},{2,3},{5,4},{4,5},{7,6},{6,7},{9,8},{8,9},{11,10... | collective-permute-start | bytes 2359304 | tf_op jit(solution)/shard_map/ppermute | solution.py:41
  147.0 9.1 %copy-start.22 = (f32[512,768]{1,0:T(8,128)S(1)}, f32[512,768]{1,0:T(8,128)}, u32[]{:S(2)}) copy-start(f32[512,768]{1,0:T(8,128)} %get-tuple-element.94) | copy-start | bytes 4718596
  153.8 42.4 %collective-permute-start.27 = (bf16[4,2,48,1536]{3,2,1,0:T(8,128)(2,1)}, bf16[4,2,48,1536]{3,2,1,0:T(8,128)(2,1)}, u32[]{:S(2)}, u32[]{:S(2)}) collective-permute-start(bf16[4,2,48,1536]{3,2,1,0:T(8,128)(2,1)} %dynamic-slice_bitcast_fusion), channel_id=1, source_target_pairs={{4,0},{5,1},{6,2},{7,3},{0,4},{1,5},{2,6},{3,7},{12,8},{13,9},{14,... | collective-permute-start | bytes 3538952 | tf_op jit(solution)/shard_map/ppermute | solution.py:41
  162.7 11.2 %collective-permute-start.26 = (bf16[768,384]{0,1:T(8,128)(2,1)S(1)}, bf16[768,384]{0,1:T(8,128)(2,1)S(1)}, u32[]{:S(2)}, u32[]{:S(2)}) collective-permute-start(bf16[768,384]{0,1:T(8,128)(2,1)S(1)} %dynamic-slice_bitcast_fusion.3), channel_id=1, source_target_pairs={{1,0},{0,1},{3,2},{2,3},{5,4},{4,5},{7,6},{6,7},{9,8},{8,9},{11,10... | collective-permute-start | bytes 1769480 | tf_op jit(solution)/shard_map/ppermute | solution.py:41
  163.0 8.6 %collective-permute-start.23 = (bf16[192,512]{1,0:T(8,128)(2,1)S(1)}, bf16[192,512]{1,0:T(8,128)(2,1)S(1)}, u32[]{:S(2)}, u32[]{:S(2)}) collective-permute-start(bf16[192,512]{1,0:T(8,128)(2,1)S(1)} %get-tuple-element.157), channel_id=1, source_target_pairs={{1,0},{0,1},{3,2},{2,3},{5,4},{4,5},{7,6},{6,7},{9,8},{8,9},{11,10... | collective-permute-start | bytes 589832 | tf_op jit(solution)/shard_map/ppermute | solution.py:41
  163.3 8.3 %collective-permute-start.24 = (bf16[192,512]{1,0:T(8,128)(2,1)S(1)}, bf16[192,512]{1,0:T(8,128)(2,1)S(1)}, u32[]{:S(2)}, u32[]{:S(2)}) collective-permute-start(bf16[192,512]{1,0:T(8,128)(2,1)S(1)} %get-tuple-element.156), channel_id=1, source_target_pairs={{2,0},{3,1},{0,2},{1,3},{6,4},{7,5},{4,6},{5,7},{10,8},{11,9},{8,1... | collective-permute-start | bytes 589832 | tf_op jit(solution)/shard_map/ppermute | solution.py:41
  164.5 9.3 %collective-permute-start.25 = (bf16[192,512]{1,0:T(8,128)(2,1)S(1)}, bf16[192,512]{1,0:T(8,128)(2,1)S(1)}, u32[]{:S(2)}, u32[]{:S(2)}) collective-permute-start(bf16[192,512]{1,0:T(8,128)(2,1)S(1)} %get-tuple-element.155), channel_id=1, source_target_pairs={{3,0},{2,1},{1,2},{0,3},{7,4},{6,5},{5,6},{4,7},{11,8},{10,9},{9,1... | collective-permute-start | bytes 589832 | tf_op jit(solution)/shard_map/ppermute | solution.py:41
  175.0 21.1 %collective-permute-start.28 = (bf16[768,192]{1,0:T(8,128)(2,1)}, bf16[768,192]{1,0:T(8,128)(2,1)}, u32[]{:S(2)}, u32[]{:S(2)}) collective-permute-start(bf16[768,192]{1,0:T(8,128)(2,1)} %bitcast.233), channel_id=1, source_target_pairs={{2,0},{3,1},{0,2},{1,3},{6,4},{7,5},{4,6},{5,7},{10,8},{11,9},{8,1... | collective-permute-start | bytes 884744 | tf_op jit(solution)/shard_map/ppermute | solution.py:41
  176.4 36.2 %collective-permute-start.29 = (bf16[4,2,96,768]{3,2,0,1:T(8,128)(2,1)}, bf16[4,2,96,768]{3,2,0,1:T(8,128)(2,1)}, u32[]{:S(2)}, u32[]{:S(2)}) collective-permute-start(bf16[4,2,96,768]{3,2,0,1:T(8,128)(2,1)} %bitcast.220), channel_id=1, source_target_pairs={{2,0},{3,1},{0,2},{1,3},{6,4},{7,5},{4,6},{5,7},{10,8},{11,9},{8,1... | collective-permute-start | bytes 3538952 | tf_op jit(solution)/shard_map/ppermute | solution.py:41
  178.7 17.5 %copy-start.29 = (bf16[768,1536]{1,0:T(8,128)(2,1)S(1)}, bf16[768,1536]{1,0:T(8,128)(2,1)}, u32[]{:S(2)}) copy-start(bf16[768,1536]{1,0:T(8,128)(2,1)} %copy-done.28) | copy-start | bytes 7077892
  198.4 22.0 %collective-permute-start.31 = (bf16[2,2,48,1536]{3,2,1,0:T(8,128)(2,1)S(1)}, bf16[2,2,48,1536]{3,2,1,0:T(8,128)(2,1)}, u32[]{:S(2)}, u32[]{:S(2)}) collective-permute-start(bf16[2,2,48,1536]{3,2,1,0:T(8,128)(2,1)S(1)} %dynamic-slice_bitcast_fusion.2), channel_id=1, source_target_pairs={{8,0},{9,1},{10,2},{11,3},{12,4},{13,5},{14,6},{15,7},{0,8},{1,9},... | collective-permute-start | bytes 1769480 | tf_op jit(solution)/shard_map/ppermute | solution.py:41
  200.1 12.5 %copy-start.8 = (bf16[576,2048]{1,0:T(8,128)(2,1)S(1)}, bf16[576,2048]{1,0:T(8,128)(2,1)}, u32[]{:S(2)}) copy-start(bf16[576,2048]{1,0:T(8,128)(2,1)} %copy-done.7) | copy-start | bytes 7077892
  200.1 12.5 %copy-start.13 = (f32[192,2048]{1,0:T(8,128)S(1)}, f32[192,2048]{1,0:T(8,128)}, u32[]{:S(2)}) copy-start(f32[192,2048]{1,0:T(8,128)} %copy-done.11) | copy-start | bytes 4718596
  202.2 18.1 %copy-start.14 = (bf16[4,96,576]{2,1,0:T(8,128)(2,1)}, bf16[4,96,576]{2,1,0:T(8,128)(2,1)S(1)}, u32[]{:S(2)}) copy-start(bf16[4,96,576]{2,1,0:T(8,128)(2,1)S(1)} %get-tuple-element.105) | copy-start | bytes 1327108
  202.2 18.2 %collective-permute-start.30 = (bf16[4,96,576]{2,1,0:T(8,128)(2,1)S(1)}, bf16[4,96,576]{2,1,0:T(8,128)(2,1)S(1)}, u32[]{:S(2)}, u32[]{:S(2)}) collective-permute-start(bf16[4,96,576]{2,1,0:T(8,128)(2,1)S(1)} %get-tuple-element.108), channel_id=1, source_target_pairs={{4,0},{5,1},{6,2},{7,3},{0,4},{1,5},{2,6},{3,7},{12,8},{13,9},{14,... | collective-permute-start | bytes 1327112 | tf_op jit(solution)/shard_map/ppermute | solution.py:41
  227.4 12.2 %collective-permute-start.33 = (bf16[2,512,768]{2,1,0:T(8,128)(2,1)}, bf16[2,512,768]{2,1,0:T(8,128)(2,1)}, u32[]{:S(2)}, u32[]{:S(2)}) collective-permute-start(bf16[2,512,768]{2,1,0:T(8,128)(2,1)} %get-tuple-element.114), channel_id=1, source_target_pairs={{1,0},{0,1},{3,2},{2,3},{5,4},{4,5},{7,6},{6,7},{9,8},{8,9},{11,10... | collective-permute-start | bytes 4718600 | tf_op jit(solution)/shard_map/ppermute | solution.py:41
  227.7 11.8 %collective-permute-start.32 = (bf16[4,96,192]{2,1,0:T(8,128)(2,1)}, bf16[4,96,192]{2,1,0:T(8,128)(2,1)S(1)}, u32[]{:S(2)}, u32[]{:S(2)}) collective-permute-start(bf16[4,96,192]{2,1,0:T(8,128)(2,1)} %copy-done.18), channel_id=1, source_target_pairs={{4,0},{5,1},{6,2},{7,3},{0,4},{1,5},{2,6},{3,7},{12,8},{13,9},{14,... | collective-permute-start | bytes 442376 | tf_op jit(solution)/shard_map/ppermute | solution.py:41
  236.7 16.2 %collective-permute-start.36 = (bf16[4,96,768]{2,1,0:T(8,128)(2,1)}, bf16[4,96,768]{2,1,0:T(8,128)(2,1)}, u32[]{:S(2)}, u32[]{:S(2)}) collective-permute-start(bf16[4,96,768]{2,1,0:T(8,128)(2,1)} %dynamic-slice_bitcast_fusion.1), channel_id=1, source_target_pairs={{4,0},{5,1},{6,2},{7,3},{0,4},{1,5},{2,6},{3,7},{12,8},{13,9},{14,... | collective-permute-start | bytes 1769480 | tf_op jit(solution)/shard_map/ppermute | solution.py:41
  238.8 14.1 %collective-permute-start.35 = (bf16[1,2,48,1536]{3,2,1,0:T(8,128)(2,1)}, bf16[1,2,48,1536]{3,2,1,0:T(8,128)(2,1)}, u32[]{:S(2)}, u32[]{:S(2)}) collective-permute-start(bf16[1,2,48,1536]{3,2,1,0:T(8,128)(2,1)} %constant_dynamic-slice_fusion.3), channel_id=1, source_target_pairs={{16,0},{17,1},{18,2},{19,3},{20,4},{21,5},{22,6},{23,7},{24,8},{25... | collective-permute-start | bytes 884744 | tf_op jit(solution)/shard_map/ppermute | solution.py:41
  242.3 15.1 %collective-permute-start.34 = (bf16[2,96,768]{2,1,0:T(8,128)(2,1)S(1)}, bf16[2,96,768]{2,1,0:T(8,128)(2,1)S(1)}, u32[]{:S(2)}, u32[]{:S(2)}) collective-permute-start(bf16[2,96,768]{2,1,0:T(8,128)(2,1)S(1)} %dynamic-slice_bitcast_fusion.5), channel_id=1, source_target_pairs={{8,0},{9,1},{10,2},{11,3},{12,4},{13,5},{14,6},{15,7},{0,8},{1,9},... | collective-permute-start | bytes 884744 | tf_op jit(solution)/shard_map/ppermute | solution.py:41
  244.2 13.3 %copy-start.25 = (bf16[4,2,96,768]{3,2,0,1:T(8,128)(2,1)S(1)}, bf16[4,2,96,768]{3,2,0,1:T(8,128)(2,1)}, u32[]{:S(2)}) copy-start(bf16[4,2,96,768]{3,2,0,1:T(8,128)(2,1)} %copy-done.24) | copy-start | bytes 3538948
  244.3 14.5 %copy-start.31 = (bf16[2,2,48,1536]{3,2,1,0:T(8,128)(2,1)S(1)}, bf16[2,2,48,1536]{3,2,1,0:T(8,128)(2,1)}, u32[]{:S(2)}) copy-start(bf16[2,2,48,1536]{3,2,1,0:T(8,128)(2,1)} %copy-done.30) | copy-start | bytes 1769476
  244.3 16.9 %copy-start.32 = (bf16[4,96,768]{2,1,0:T(8,128)(2,1)S(1)}, bf16[4,96,768]{2,1,0:T(8,128)(2,1)}, u32[]{:S(2)}) copy-start(bf16[4,96,768]{2,1,0:T(8,128)(2,1)} %concatenate.53) | copy-start | bytes 1769476
  244.3 25.8 %collective-permute-start.39 = (bf16[512,768]{1,0:T(8,128)(2,1)S(1)}, bf16[512,768]{1,0:T(8,128)(2,1)S(1)}, u32[]{:S(2)}, u32[]{:S(2)}) collective-permute-start(bf16[512,768]{1,0:T(8,128)(2,1)S(1)} %slice_bitcast_fusion), channel_id=1, source_target_pairs={{2,0},{3,1},{0,2},{1,3},{6,4},{7,5},{4,6},{5,7},{10,8},{11,9},{8,1... | collective-permute-start | bytes 2359304 | tf_op jit(solution)/shard_map/ppermute | solution.py:41
  258.7 11.4 %collective-permute-start.41 = (bf16[2,96,768]{2,1,0:T(8,128)(2,1)S(1)}, bf16[2,96,768]{2,1,0:T(8,128)(2,1)S(1)}, u32[]{:S(2)}, u32[]{:S(2)}) collective-permute-start(bf16[2,96,768]{2,1,0:T(8,128)(2,1)S(1)} %dynamic-slice_bitcast_fusion.4), channel_id=1, source_target_pairs={{8,0},{9,1},{10,2},{11,3},{12,4},{13,5},{14,6},{15,7},{0,8},{1,9},... | collective-permute-start | bytes 884744 | tf_op jit(solution)/shard_map/ppermute | solution.py:41
  260.0 9.9 %collective-permute-start.40 = (bf16[48,1536]{1,0:T(8,128)(2,1)S(1)}, bf16[48,1536]{1,0:T(8,128)(2,1)S(1)}, u32[]{:S(2)}, u32[]{:S(2)}) collective-permute-start(bf16[48,1536]{1,0:T(8,128)(2,1)S(1)} %dynamic-slice_bitcast_fusion.11), channel_id=1, source_target_pairs={{2,0},{3,1},{0,2},{1,3},{6,4},{7,5},{4,6},{5,7},{10,8},{11,9},{8,1... | collective-permute-start | bytes 442376 | tf_op jit(solution)/shard_map/ppermute | solution.py:41
  261.3 4.8 %copy-start.50 = (bf16[1024,1536]{1,0:T(8,128)(2,1)S(1)}, bf16[1024,1536]{1,0:T(8,128)(2,1)}, u32[]{:S(2)}) copy-start(bf16[1024,1536]{1,0:T(8,128)(2,1)} %get-tuple-element.121) | copy-start | bytes 9437188
  261.3 8.8 %collective-permute-start.38 = (bf16[1,96,768]{2,1,0:T(8,128)(2,1)S(1)}, bf16[1,96,768]{2,1,0:T(8,128)(2,1)S(1)}, u32[]{:S(2)}, u32[]{:S(2)}) collective-permute-start(bf16[1,96,768]{2,1,0:T(8,128)(2,1)S(1)} %constant_dynamic-slice_fusion.1), channel_id=1, source_target_pairs={{16,0},{17,1},{18,2},{19,3},{20,4},{21,5},{22,6},{23,7},{24,8},{25... | collective-permute-start | bytes 442376 | tf_op jit(solution)/shard_map/ppermute | solution.py:41
  268.8 6.6 %copy-start.33 = (f32[1024,768]{1,0:T(8,128)}, f32[1024,768]{1,0:T(8,128)S(1)}, u32[]{:S(2)}) copy-start(f32[1024,768]{1,0:T(8,128)S(1)} %fusion.55) | copy-start | bytes 9437188
  269.8 13.7 %collective-permute-start.37 = (bf16[512,768]{1,0:T(8,128)(2,1)}, bf16[512,768]{1,0:T(8,128)(2,1)S(1)}, u32[]{:S(2)}, u32[]{:S(2)}) collective-permute-start(bf16[512,768]{1,0:T(8,128)(2,1)} %slice.259), channel_id=1, source_target_pairs={{1,0},{0,1},{3,2},{2,3},{5,4},{4,5},{7,6},{6,7},{9,8},{8,9},{11,10... | collective-permute-start | bytes 2359304 | tf_op jit(solution)/shard_map/ppermute | solution.py:41
  270.2 10.1 %collective-permute-start.45 = (bf16[1,96,768]{2,1,0:T(8,128)(2,1)S(1)}, bf16[1,96,768]{2,1,0:T(8,128)(2,1)S(1)}, u32[]{:S(2)}, u32[]{:S(2)}) collective-permute-start(bf16[1,96,768]{2,1,0:T(8,128)(2,1)S(1)} %constant_dynamic-slice_fusion), channel_id=1, source_target_pairs={{16,0},{17,1},{18,2},{19,3},{20,4},{21,5},{22,6},{23,7},{24,8},{25... | collective-permute-start | bytes 442376 | tf_op jit(solution)/shard_map/ppermute | solution.py:41
  271.9 3.5 %collective-permute-start.43 = (f32[24,1536]{1,0:T(8,128)S(1)}, f32[24,1536]{1,0:T(8,128)S(1)}, u32[]{:S(2)}, u32[]{:S(2)}) collective-permute-start(f32[24,1536]{1,0:T(8,128)S(1)} %dynamic-slice_bitcast_fusion.9), channel_id=1, source_target_pairs={{1,0},{0,1},{3,2},{2,3},{5,4},{4,5},{7,6},{6,7},{9,8},{8,9},{11,10... | collective-permute-start | bytes 442376 | tf_op jit(solution)/shard_map/ppermute | solution.py:41
  272.2 6.1 %collective-permute-start.42 = (f32[2,24,768]{2,1,0:T(8,128)S(1)}, f32[2,24,768]{2,1,0:T(8,128)S(1)}, u32[]{:S(2)}, u32[]{:S(2)}) collective-permute-start(f32[2,24,768]{2,1,0:T(8,128)S(1)} %dynamic-slice_bitcast_fusion.10), channel_id=1, source_target_pairs={{2,0},{3,1},{0,2},{1,3},{6,4},{7,5},{4,6},{5,7},{10,8},{11,9},{8,1... | collective-permute-start | bytes 442376 | tf_op jit(solution)/shard_map/ppermute | solution.py:41
  279.5 2.1 collective-permute-start.44
  (34 other events, 83.0 us)
Sparse Core Ops, SparseCore 0:
  48.1 61.8 all-gather.1

commit v4 on v3

--- a/solution.py
+++ b/solution.py
@@ -205,7 +205,7 @@
         sorted_ref[:, b * BLK : (b + 1) * BLK] = qkv_ref[:, lane_tile(meta_ref[b] * BLK, BLK)]
     for h in range(heads):
         keys_ref[h] = sorted_ref[head_rows(sets, 1, h), :].astype(f32).T.astype(bf16)
-    doc_units = meta_ref[blocks] // unit
+    doc_units = jnp.maximum(meta_ref[blocks] // unit, 1)
     seen = lax.broadcasted_iota(jnp.int32, (tile, tile), 0) <= lax.broadcasted_iota(jnp.int32, (tile, tile), 1)
     lse_ref[...] = jnp.zeros_like(lse_ref)
     for i in range(row_len // tile):
@@ -313,7 +313,7 @@
         stats = [lse_ref[heads[h] : heads[h] + 1, :], delta, jnp.zeros((6, row_len), f32)]
         stat_ref[h] = jnp.concatenate(stats, axis=0).T
     dkv_ref[...] = jnp.zeros_like(dkv_ref)
-    doc_units = meta_ref[blocks] // unit
+    doc_units = jnp.maximum(meta_ref[blocks] // unit, 1)
     seen = lax.broadcasted_iota(jnp.int32, (tile, tile), 0) >= lax.broadcasted_iota(jnp.int32, (tile, tile), 1)
     for i in range(row_len // tile):
         at = slice(i * tile, (i + 1) * tile)
@@ -661,14 +661,15 @@
     group_qkv, both = together(group_qkv, both)
     got_hi = [grid.fetch(group_qkv[None], hi=r) for r in range(1, grid.sizes["hi"])]
     stack = tie(jnp.stack(by_x), *got_hi)
-    by_c = [by_x] + [list(grid.fetch(stack, c=r)) for r in range(1, nc)]
+    from_c = [grid.fetch(stack, c=r) for r in range(1, nc)]
+    by_c = [by_x] + [list(one) for one in from_c]
     row_tokens = [by_c[c][x] for x in range(nx) for c in range(nc)]
     qkv_stack = jnp.concatenate([group_qkv[None]] + got_hi, axis=0)
     full_qkv, _ = gather_rows(grid, None, ("lo",), {"place": row_tokens}, qkv_stack)
 
     full_out = lax.all_gather(tie(out_weight, *got_hi), ("pb", "ka"), axis=0, tiled=True)
 
-    both = tie(both, qkv_stack, *row_tokens)
+    both = tie(both, qkv_stack, *from_c)
     both = grid.gather(both, "hi")
 
     slots = tok_rows // BLK

time: 299 us -> 298 us (level)
  local copies, waits for them, and re-layouts: 26.4 us -> 23.4 us
    unnamed x106 -> x98, local copies, waits for them, and re-layouts: 8.82 us -> 6.7 us
  transfers between devices with their start and end apart: 47 -> 47, of which waited for: 20 -> 18; matrix products, arithmetic and copies ran while one was open for 21% -> 21% of each run, Pallas kernels for 18% -> 18%
where the time goes in v4:
time: 298 us; the launch traced here: 294 us
  waiting for transfers between devices  79.4 us (27%)
  Pallas kernels  73.4 us (25%)
  starting transfers between devices  54.4 us (18%)
  other arithmetic  30.7 us (10%)
  local copies, waits for them, and re-layouts  23.4 us (8%)
  matrix products  16.5 us (6%)
  between operations  16 us (5%)
    ppermute x46, waiting for transfers between devices, fetch(): return lax.ppermute(value, ('pb', 'ka'), pairs)  77.2 us
    ppermute x46, starting transfers between devices, fetch(): return lax.ppermute(value, ('pb', 'ka'), pairs)  54.3 us
    pallas_call x2, Pallas kernels, backward_attention(): pl.pallas_call(functools.partial(backward_kernel, sets, which, 256, 256,...  25.1 us
    dot_general x6, matrix products, mm(): lax.dot_general(a, b, ((dims[:1], dims[1:]), ((), ())), preferred_element...  16.5 us
    pallas_call x1, Pallas kernels, forward_attention(): pl.pallas_call(functools.partial(forward_kernel, sets, 256, 512, SEQ_UNIT...  15.1 us
    pallas_call x1, Pallas kernels, hidden_layer(): pl.pallas_call(functools.partial(hidden_kernel, (len(up_stacks), len(down...  14.2 us
    convert_element_type x12, other arithmetic, added(): return total if last else total.astype(own.dtype)  11.1 us
    unnamed x98, local copies, waits for them, and re-layouts  6.7 us
  transfers between devices with their start and end apart: 47, of which 18 were waited for; matrix products, arithmetic and copies ran while one was open for 21% of the time, Pallas kernels for 18%

profile of v4, /device:TPU:0, one launch (start us, length us, event | category | flops | bytes accessed | tf_op | source)
XLA Modules:
  0.0 293.9 jit_solution(13135324289496399661)
XLA Ops:
  10.0 2.6 collective-permute-start.1
  13.3 1.2 collective-permute-done.1
  14.5 1.4 collective-permute-done.2
  17.5 3.8 %collective-permute-start.5 = (bf16[1,96,640]{2,1,0:T(8,128)(2,1)S(1)}, bf16[1,96,640]{2,1,0:T(8,128)(2,1)S(1)}, u32[]{:S(2)}, u32[]{:S(2)}) collective-permute-start(bf16[1,96,640]{2,1,0:T(8,128)(2,1)S(1)} %bitcast.229), channel_id=1, source_target_pairs={{8,0},{9,1},{10,2},{11,3},{12,4},{13,5},{14,6},{15,7},{16,8},{17,9... | collective-permute-start | bytes 368648 | tf_op jit(solution)/shard_map/ppermute | solution.py:41
  22.3 13.3 %collective-permute-done.3.refs_2_ = bf16[512,768]{1,0:T(8,128)(2,1)S(1)} collective-permute-done((bf16[512,768]{1,0:T(8,128)(2,1)S(1)}, bf16[512,768]{1,0:T(8,128)(2,1)S(1)}, u32[]{:S(2)}, u32[]{:S(2)}) %collective-permute-start.3) | collective-permute-done | bytes 786464 | tf_op jit(solution)/shard_map/ppermute | solution.py:41
  35.6 1.3 pad_maximum_fusion
  37.1 1.2 sort.17
  38.6 1.6 collective-permute-start.9
  40.7 3.6 %collective-permute-start.10 = (bf16[192,768]{1,0:T(8,128)(2,1)}, bf16[192,768]{1,0:T(8,128)(2,1)S(1)}, u32[]{:S(2)}, u32[]{:S(2)}) collective-permute-start(bf16[192,768]{1,0:T(8,128)(2,1)} %fusion.30), channel_id=1, source_target_pairs={{8,0},{9,1},{10,2},{11,3},{12,4},{13,5},{14,6},{15,7},{16,8},{17,9... | collective-permute-start | bytes 884744 | tf_op jit(solution)/shard_map/ppermute | solution.py:41
  44.3 1.2 collective-permute-start.12
  45.5 1.5 slice_bitcast_fusion.2
  47.0 5.5 %collective-permute-done.9.refs_1_ = bf16[4,96,640]{2,1,0:T(8,128)(2,1)S(1)} collective-permute-done((bf16[4,96,640]{2,1,0:T(8,128)(2,1)S(1)}, bf16[4,96,640]{2,1,0:T(8,128)(2,1)S(1)}, u32[]{:S(2)}, u32[]{:S(2)}) %collective-permute-start.9) | collective-permute-done | bytes 491552 | tf_op jit(solution)/shard_map/ppermute | solution.py:41
  52.5 1.9 shard_map.161.refs_4_.refs_2_
  54.4 5.4 %shard_map.162 = (bf16[768,2048]{1,0:T(8,128)(2,1)S(1)}, bf16[576,2048]{1,0:T(8,128)(2,1)S(1)}) custom-call(bf16[512,768]{1,0:T(8,128)(2,1)S(1)} %copy-done, bf16[512,768]{1,0:T(8,128)(2,1)S(1)} %get-tuple-element.147.refs_1_, bf16[512,768]{1,0:T(8,128)(2,1)S(1)} %collective-permute-done.3.refs_2_, bf16[512,768]{1,0:T(8,128)(2,1)S(1)} %get-tuple-element.146.refs_3_, ...), custom_call_target="tpu_custom_call" | custom-call | flops 1000000 | bytes 100000 | tf_op jit(solution)/shard_map/pallas_call | solution.py:429
  60.1 10.6 %collective-permute-done.11 = bf16[192,768]{1,0:T(8,128)(2,1)S(1)} collective-permute-done((bf16[192,768]{1,0:T(8,128)(2,1)}, bf16[192,768]{1,0:T(8,128)(2,1)S(1)}, u32[]{:S(2)}, u32[]{:S(2)}) %collective-permute-start.11) | collective-permute-done | bytes 294944 | tf_op jit(solution)/shard_map/ppermute | solution.py:41
  72.9 1.5 collective-permute-start.14
  74.4 15.1 %shard_map.163 = (bf16[4,192,512]{2,1,0:T(8,128)(2,1)S(1)}, f32[192,2048]{1,0:T(8,128)S(1)}, f32[8,2048]{1,0:T(8,128)S(1)}) custom-call(s32[17]{0:T(128)S(1)} %pad_add_fusion.meta_ref, bf16[576,2048]{1,0:T(8,128)(2,1)S(1)} %get-tuple-element.82.qkv_ref), custom_call_target="tpu_custom_call" | custom-call | flops 20999999488 | bytes 1000000 | tf_op jit(solution)/shard_map/pallas_call | solution.py:275
  89.5 1.4 copy-done.6
  91.1 1.2 collective-permute-start.16
  93.1 1.2 collective-permute-start.19
  96.0 4.5 %collective-permute-start.18 = (bf16[8,96,768]{2,1,0:T(8,128)(2,1)}, bf16[8,96,768]{2,1,0:T(8,128)(2,1)}, u32[]{:S(2)}, u32[]{:S(2)}) collective-permute-start(bf16[8,96,768]{2,1,0:T(8,128)(2,1)} %constant_dynamic-update-slice_fusion.refs_0_), channel_id=1, source_target_pairs={{4,0},{5,1},{6,2},{7,3},{0,4},{1,5},{2,6},{3,7},{12,8},{13,9},{14,... | collective-permute-start | bytes 3538952 | tf_op jit(solution)/shard_map/ppermute | solution.py:41
  100.9 3.5 %collective-permute-done.17 = bf16[192,512]{1,0:T(8,128)(2,1)S(1)} collective-permute-done((bf16[192,512]{1,0:T(8,128)(2,1)S(1)}, bf16[192,512]{1,0:T(8,128)(2,1)S(1)}, u32[]{:S(2)}, u32[]{:S(2)}) %collective-permute-start.17) | collective-permute-done | bytes 196640 | tf_op jit(solution)/shard_map/ppermute | solution.py:41
  105.4 2.2 all-gather.2.cloned.1.call-done
  107.6 2.4 fusion.54
  110.3 1.2 multiply_convert_fusion.refs_4_
  112.0 2.1 collective-permute-done.20.refs_5_
  114.1 16.0 %collective-permute-done.19.refs_3_.refs_1_ = bf16[8,96,768]{2,1,0:T(8,128)(2,1)} collective-permute-done((bf16[8,96,768]{2,1,0:T(8,128)(2,1)S(1)}, bf16[8,96,768]{2,1,0:T(8,128)(2,1)}, u32[]{:S(2)}, u32[]{:S(2)}) %collective-permute-start.19) | collective-permute-done | bytes 1179680 | tf_op jit(solution)/shard_map/ppermute | solution.py:41
  130.1 14.2 %shard_map.164 = (bf16[1024,1536]{1,0:T(8,128)(2,1)}, bf16[1024,1536]{1,0:T(8,128)(2,1)}, f32[512,768]{1,0:T(8,128)}, bf16[512,768]{1,0:T(8,128)(2,1)S(1)}) custom-call(s32[16]{0:T(128)S(1)} %stack.191.up_at, s32[16]{0:T(128)S(1)} %stack.192.down_at, bf16[8,96,768]{2,1,0:T(8,128)(2,1)} %constant_dynamic-update-slice_fusion.refs_0_, ...), custom_call_target="tpu_custom_call" | custom-call | flops 14000000000 | bytes 1000000 | tf_op jit(solution)/shard_map/pallas_call | solution.py:563
  144.4 5.6 %convolution_convert_fusion = bf16[768,1536]{1,0:T(8,128)(2,1)S(1)} fusion(bf16[1024,1536]{1,0:T(8,128)(2,1)} %get-tuple-element.101, bf16[512,768]{1,0:T(8,128)(2,1)} %collective-permute-done.20.refs_5_, bf16[512,768]{1,0:T(8,128)(2,1)} %multiply_convert_fusion.refs_4_), kind=kOutput, calls=%fused_computation | convolution fusion | flops 2420244480 | bytes 7077888 | tf_op jit(solution)/shard_map/dot_general | solution.py:596
  150.0 1.1 dynamic-slice_bitcast_fusion
  151.1 2.3 collective-permute-start.27
  154.1 3.1 %fusion.46 = (bf16[512,768]{1,0:T(8,128)(2,1)S(1)}, f32[512,768]{1,0:T(8,128)}) fusion(f32[512]{0:T(512)S(1)} %get-tuple-element.205, f32[512]{0:T(512)S(1)} %add_rsqrt_fusion.1, f32[512,768]{1,0:T(8,128)S(1)} %copy-done.15, f32[512]{0:T(512)S(1)} %broadcast_multiply_fusion.5, f32[512]{0:T(512)S(1)} %get-tuple-element.206, f32[768]{0:T(1024)S(1)} %get-tuple-element.139, ...), kind=kLoop, calls=%fused_computation.195 | loop fusion | flops 4718592 | bytes 7089152 | tf_op jit(solution)/shard_map/convert_element_type | solution.py:731
  160.6 1.2 collective-permute-start.24
  162.2 4.3 %convolution_convert_fusion.1 = bf16[1536,768]{1,0:T(8,128)(2,1)S(1)} fusion(bf16[1024,1536]{1,0:T(8,128)(2,1)S(1)} %copy-done.45, bf16[512,768]{1,0:T(8,128)(2,1)} %collective-permute-done.21.refs_7_, bf16[512,768]{1,0:T(8,128)(2,1)} %refs_6_.1), kind=kOutput, calls=%fused_computation.1 | convolution fusion | flops 2420244480 | bytes 7077888 | tf_op jit(solution)/shard_map/dot_general | solution.py:596
  166.5 1.2 constant_dynamic-slice_fusion.2
  167.7 1.2 copy.54
  168.9 2.2 collective-permute-done.25
  172.3 1.2 collective-permute-start.28
  174.6 1.4 copy-done.9
  176.0 17.4 %shard_map.165.right_ref.refs_0_ = bf16[2048,384]{1,0:T(8,128)(2,1)S(1)} custom-call(s32[17]{0:T(128)S(1)} %pad_add_fusion.meta_ref, bf16[576,2048]{1,0:T(8,128)(2,1)} %copy-done.6, bf16[4,192,512]{2,1,0:T(8,128)(2,1)S(1)} %pad_maximum_fusion.3.up_ref, f32[192,2048]{1,0:T(8,128)S(1)} %copy-done.9, f32[8,2048]{1,0:T(8,128)S(1)} %get-tuple-element.100.lse_ref), custom_call_target="tpu_custom_call" | custom-call | flops 25999998976 | bytes 100000 | tf_op jit(solution)/shard_map/pallas_call | solution.py:378
  193.5 2.2 fusion.1
  195.7 7.4 %collective-permute-start.31 = (bf16[2,2,48,1536]{3,2,1,0:T(8,128)(2,1)S(1)}, bf16[2,2,48,1536]{3,2,1,0:T(8,128)(2,1)}, u32[]{:S(2)}, u32[]{:S(2)}) collective-permute-start(bf16[2,2,48,1536]{3,2,1,0:T(8,128)(2,1)S(1)} %dynamic-slice_bitcast_fusion.2), channel_id=1, source_target_pairs={{8,0},{9,1},{10,2},{11,3},{12,4},{13,5},{14,6},{15,7},{0,8},{1,9},... | collective-permute-start | bytes 1769480 | tf_op jit(solution)/shard_map/ppermute | solution.py:41
  204.3 2.0 shard_map.166
  206.6 3.3 %collective-permute-done.29 = bf16[4,2,96,768]{3,2,0,1:T(8,128)(2,1)} collective-permute-done((bf16[4,2,96,768]{3,2,0,1:T(8,128)(2,1)}, bf16[4,2,96,768]{3,2,0,1:T(8,128)(2,1)}, u32[]{:S(2)}, u32[]{:S(2)}) %collective-permute-start.29) | collective-permute-done | bytes 1179680 | tf_op jit(solution)/shard_map/ppermute | solution.py:41
  209.9 7.6 %shard_map.167.right_ref.refs_1_ = bf16[2048,192]{1,0:T(8,128)(2,1)S(1)} custom-call(s32[17]{0:T(128)S(1)} %pad_add_fusion.meta_ref, bf16[576,2048]{1,0:T(8,128)(2,1)S(1)} %copy-done.7, bf16[4,192,512]{2,1,0:T(8,128)(2,1)S(1)} %pad_maximum_fusion.3.up_ref, f32[192,2048]{1,0:T(8,128)S(1)} %copy-done.10, f32[8,2048]{1,0:T(8,128)S(1)} %get-tuple-element.100.lse_ref), custom_call_target="tpu_custom_call" | custom-call | flops 1000000 | bytes 100000 | tf_op jit(solution)/shard_map/pallas_call | solution.py:378
  217.6 1.8 collective-permute-done.30
  221.9 5.2 %shard_map.169 = (bf16[2,512,768]{2,1,0:T(8,128)(2,1)S(1)}, bf16[2,512,768]{2,1,0:T(8,128)(2,1)}) custom-call(bf16[2048,384]{1,0:T(8,128)(2,1)} %copy-done.3, bf16[2048,192]{1,0:T(8,128)(2,1)S(1)} %shard_map.167.right_ref.refs_1_, bf16[768,640]{1,0:T(8,128)(2,1)S(1)} %shard_map.161.refs_4_.refs_2_), custom_call_target="tpu_custom_call" | custom-call | flops 1000000 | bytes 100000 | tf_op jit(solution)/shard_map/pallas_call | solution.py:495
  227.5 4.4 %collective-permute-start.32 = (bf16[4,96,192]{2,1,0:T(8,128)(2,1)}, bf16[4,96,192]{2,1,0:T(8,128)(2,1)S(1)}, u32[]{:S(2)}, u32[]{:S(2)}) collective-permute-start(bf16[4,96,192]{2,1,0:T(8,128)(2,1)} %copy-done.13), channel_id=1, source_target_pairs={{4,0},{5,1},{6,2},{7,3},{0,4},{1,5},{2,6},{3,7},{12,8},{13,9},{14,... | collective-permute-start | bytes 442376 | tf_op jit(solution)/shard_map/ppermute | solution.py:41
  231.8 2.0 fusion
  234.8 1.2 fusion.23
  236.8 4.2 %collective-permute-start.35 = (bf16[1,2,48,1536]{3,2,1,0:T(8,128)(2,1)}, bf16[1,2,48,1536]{3,2,1,0:T(8,128)(2,1)}, u32[]{:S(2)}, u32[]{:S(2)}) collective-permute-start(bf16[1,2,48,1536]{3,2,1,0:T(8,128)(2,1)} %constant_dynamic-slice_fusion.3), channel_id=1, source_target_pairs={{16,0},{17,1},{18,2},{19,3},{20,4},{21,5},{22,6},{23,7},{24,8},{25... | collective-permute-start | bytes 884744 | tf_op jit(solution)/shard_map/ppermute | solution.py:41
  241.5 1.4 concatenate.53
  244.0 1.8 add_convert_fusion
  245.9 1.2 collective-permute-start.39
  247.1 7.9 %collective-permute-done.35 = bf16[1,2,48,1536]{3,2,1,0:T(8,128)(2,1)} collective-permute-done((bf16[1,2,48,1536]{3,2,1,0:T(8,128)(2,1)}, bf16[1,2,48,1536]{3,2,1,0:T(8,128)(2,1)}, u32[]{:S(2)}, u32[]{:S(2)}) %collective-permute-start.35) | collective-permute-done | bytes 294944 | tf_op jit(solution)/shard_map/ppermute | solution.py:41
  255.0 3.6 %collective-permute-done.34 = bf16[2,96,768]{2,1,0:T(8,128)(2,1)S(1)} collective-permute-done((bf16[2,96,768]{2,1,0:T(8,128)(2,1)S(1)}, bf16[2,96,768]{2,1,0:T(8,128)(2,1)S(1)}, u32[]{:S(2)}, u32[]{:S(2)}) %collective-permute-start.34) | collective-permute-done | bytes 294944 | tf_op jit(solution)/shard_map/ppermute | solution.py:41
  258.5 1.2 fusion.22
  261.0 1.2 collective-permute-start.40
  262.4 3.6 %shard_map.170 = bf16[1536,768]{1,0:T(8,128)(2,1)S(1)} custom-call(s32[16]{0:T(128)S(1)} %broadcast_multiply_fusion.6.offs_ref, bf16[8,96,768]{2,1,0:T(8,128)(2,1)S(1)} %copy-done.5, bf16[8,96,768]{2,1,0:T(8,128)(2,1)} %collective-permute-done.19.refs_3_.refs_1_), custom_call_target="tpu_custom_call" | custom-call | flops 1000000 | bytes 100000 | tf_op jit(solution)/shard_map/pallas_call | solution.py:107
  266.0 2.6 fusion.55
  270.9 1.9 collective-permute-start.45
  274.9 1.6 fusion.10
  276.4 2.9 collective-permute-done.42
  284.0 2.5 fusion.13
  (263 shorter events, 38.6 us)
Async XLA Ops:
  7.2 100.4 %all-gather.2.cloned.1.call-start = ((), (), s32[]{:S(2)}) async-start(), calls=%async_computation | async-start | bytes 1216512 | tf_op jit(solution)/shard_map/all_gather | solution.py:670
  8.6 7.3 %copy-start = (bf16[512,768]{1,0:T(8,128)(2,1)S(1)}, bf16[512,768]{1,0:T(8,128)(2,1)}, u32[]{:S(2)}) copy-start(bf16[512,768]{1,0:T(8,128)(2,1)} %refs_0_.1) | copy-start | bytes 2359300
  9.1 7.7 %copy-start.37 = (bf16[96,768]{1,0:T(8,128)(2,1)S(1)}, bf16[96,768]{1,0:T(8,128)(2,1)}, u32[]{:S(2)}) copy-start(bf16[96,768]{1,0:T(8,128)(2,1)} %param.16) | copy-start | bytes 442372
  9.5 3.8 %collective-permute-start = (bf16[24,640]{1,0:T(8,128)(2,1)S(1)}, bf16[24,640]{1,0:T(8,128)(2,1)S(1)}, u32[]{:S(2)}, u32[]{:S(2)}) collective-permute-start(bf16[24,640]{1,0:T(8,128)(2,1)S(1)} %get-tuple-element.186), channel_id=1, source_target_pairs={{1,0},{0,1},{3,2},{2,3},{5,4},{4,5},{7,6},{6,7},{9,8},{8,9},{11,10... | collective-permute-start | bytes 92168 | tf_op jit(solution)/shard_map/ppermute | solution.py:41
  10.0 4.5 %collective-permute-start.1 = (bf16[24,640]{1,0:T(8,128)(2,1)S(1)}, bf16[24,640]{1,0:T(8,128)(2,1)S(1)}, u32[]{:S(2)}, u32[]{:S(2)}) collective-permute-start(bf16[24,640]{1,0:T(8,128)(2,1)S(1)} %get-tuple-element.185), channel_id=1, source_target_pairs={{2,0},{3,1},{0,2},{1,3},{6,4},{7,5},{4,6},{5,7},{10,8},{11,9},{8,1... | collective-permute-start | bytes 92168 | tf_op jit(solution)/shard_map/ppermute | solution.py:41
  12.6 3.3 %collective-permute-start.2 = (bf16[24,640]{1,0:T(8,128)(2,1)S(1)}, bf16[24,640]{1,0:T(8,128)(2,1)S(1)}, u32[]{:S(2)}, u32[]{:S(2)}) collective-permute-start(bf16[24,640]{1,0:T(8,128)(2,1)S(1)} %get-tuple-element.184), channel_id=1, source_target_pairs={{3,0},{2,1},{1,2},{0,3},{7,4},{6,5},{5,6},{4,7},{11,8},{10,9},{9,1... | collective-permute-start | bytes 92168 | tf_op jit(solution)/shard_map/ppermute | solution.py:41
  13.1 3.6 %collective-permute-start.4 = (bf16[24,1536]{1,0:T(8,128)(2,1)S(1)}, bf16[24,1536]{1,0:T(8,128)(2,1)S(1)}, u32[]{:S(2)}, u32[]{:S(2)}) collective-permute-start(bf16[24,1536]{1,0:T(8,128)(2,1)S(1)} %dynamic-slice_bitcast_fusion.12), channel_id=1, source_target_pairs={{1,0},{0,1},{3,2},{2,3},{5,4},{4,5},{7,6},{6,7},{9,8},{8,9},{11,10... | collective-permute-start | bytes 221192 | tf_op jit(solution)/shard_map/ppermute | solution.py:41
  15.9 19.7 %collective-permute-start.3 = (bf16[512,768]{1,0:T(8,128)(2,1)S(1)}, bf16[512,768]{1,0:T(8,128)(2,1)S(1)}, u32[]{:S(2)}, u32[]{:S(2)}) collective-permute-start(bf16[512,768]{1,0:T(8,128)(2,1)S(1)} %copy-done), channel_id=1, source_target_pairs={{2,0},{3,1},{0,2},{1,3},{6,4},{7,5},{4,6},{5,7},{10,8},{11,9},{8,1... | collective-permute-start | bytes 2359304 | tf_op jit(solution)/shard_map/ppermute | solution.py:41
  17.5 19.3 %collective-permute-start.5 = (bf16[1,96,640]{2,1,0:T(8,128)(2,1)S(1)}, bf16[1,96,640]{2,1,0:T(8,128)(2,1)S(1)}, u32[]{:S(2)}, u32[]{:S(2)}) collective-permute-start(bf16[1,96,640]{2,1,0:T(8,128)(2,1)S(1)} %bitcast.229), channel_id=1, source_target_pairs={{8,0},{9,1},{10,2},{11,3},{12,4},{13,5},{14,6},{15,7},{16,8},{17,9... | collective-permute-start | bytes 368648 | tf_op jit(solution)/shard_map/ppermute | solution.py:41
  21.3 15.6 %collective-permute-start.6 = (bf16[1,96,640]{2,1,0:T(8,128)(2,1)S(1)}, bf16[1,96,640]{2,1,0:T(8,128)(2,1)S(1)}, u32[]{:S(2)}, u32[]{:S(2)}) collective-permute-start(bf16[1,96,640]{2,1,0:T(8,128)(2,1)S(1)} %bitcast.230), channel_id=1, source_target_pairs={{16,0},{17,1},{18,2},{19,3},{20,4},{21,5},{22,6},{23,7},{24,8},{25... | collective-permute-start | bytes 368648 | tf_op jit(solution)/shard_map/ppermute | solution.py:41
  21.3 15.6 %collective-permute-start.7 = (bf16[1,96,640]{2,1,0:T(8,128)(2,1)S(1)}, bf16[1,96,640]{2,1,0:T(8,128)(2,1)S(1)}, u32[]{:S(2)}, u32[]{:S(2)}) collective-permute-start(bf16[1,96,640]{2,1,0:T(8,128)(2,1)S(1)} %bitcast.231), channel_id=1, source_target_pairs={{24,0},{25,1},{26,2},{27,3},{28,4},{29,5},{30,6},{31,7},{0,8},{1,9... | collective-permute-start | bytes 368648 | tf_op jit(solution)/shard_map/ppermute | solution.py:41
  36.9 3.8 %collective-permute-start.8 = (bf16[2,512,768]{2,1,0:T(8,128)(2,1)}, bf16[2,512,768]{2,1,0:T(8,128)(2,1)}, u32[]{:S(2)}, u32[]{:S(2)}) collective-permute-start(bf16[2,512,768]{2,1,0:T(8,128)(2,1)} %pad_maximum_fusion), channel_id=1, source_target_pairs={{1,0},{0,1},{3,2},{2,3},{5,4},{4,5},{7,6},{6,7},{9,8},{8,9},{11,10... | collective-permute-start | bytes 4718600 | tf_op jit(solution)/shard_map/ppermute | solution.py:41
  38.6 13.8 %collective-permute-start.9 = (bf16[4,96,640]{2,1,0:T(8,128)(2,1)S(1)}, bf16[4,96,640]{2,1,0:T(8,128)(2,1)S(1)}, u32[]{:S(2)}, u32[]{:S(2)}) collective-permute-start(bf16[4,96,640]{2,1,0:T(8,128)(2,1)S(1)} %pad_maximum_fusion.4.refs_0_), channel_id=1, source_target_pairs={{4,0},{5,1},{6,2},{7,3},{0,4},{1,5},{2,6},{3,7},{12,8},{13,9},{14,... | collective-permute-start | bytes 1474568 | tf_op jit(solution)/shard_map/ppermute | solution.py:41
  40.7 19.4 %collective-permute-start.10 = (bf16[192,768]{1,0:T(8,128)(2,1)}, bf16[192,768]{1,0:T(8,128)(2,1)S(1)}, u32[]{:S(2)}, u32[]{:S(2)}) collective-permute-start(bf16[192,768]{1,0:T(8,128)(2,1)} %fusion.30), channel_id=1, source_target_pairs={{8,0},{9,1},{10,2},{11,3},{12,4},{13,5},{14,6},{15,7},{16,8},{17,9... | collective-permute-start | bytes 884744 | tf_op jit(solution)/shard_map/ppermute | solution.py:41
  44.3 26.5 %collective-permute-start.11 = (bf16[192,768]{1,0:T(8,128)(2,1)}, bf16[192,768]{1,0:T(8,128)(2,1)S(1)}, u32[]{:S(2)}, u32[]{:S(2)}) collective-permute-start(bf16[192,768]{1,0:T(8,128)(2,1)} %fusion.30), channel_id=1, source_target_pairs={{16,0},{17,1},{18,2},{19,3},{20,4},{21,5},{22,6},{23,7},{24,8},{25... | collective-permute-start | bytes 884744 | tf_op jit(solution)/shard_map/ppermute | solution.py:41
  44.3 26.5 %collective-permute-start.12 = (bf16[192,768]{1,0:T(8,128)(2,1)}, bf16[192,768]{1,0:T(8,128)(2,1)S(1)}, u32[]{:S(2)}, u32[]{:S(2)}) collective-permute-start(bf16[192,768]{1,0:T(8,128)(2,1)} %fusion.30), channel_id=1, source_target_pairs={{24,0},{25,1},{26,2},{27,3},{28,4},{29,5},{30,6},{31,7},{0,8},{1,9... | collective-permute-start | bytes 884744 | tf_op jit(solution)/shard_map/ppermute | solution.py:41
  59.8 12.2 %copy-start.1 = (bf16[768,2048]{1,0:T(8,128)(2,1)}, bf16[768,2048]{1,0:T(8,128)(2,1)S(1)}, u32[]{:S(2)}) copy-start(bf16[768,2048]{1,0:T(8,128)(2,1)S(1)} %get-tuple-element.93.left_ref) | copy-start | bytes 9437188
  71.9 19.0 %collective-permute-start.13 = (bf16[4,96,768]{2,1,0:T(8,128)(2,1)S(1)}, bf16[4,96,768]{2,1,0:T(8,128)(2,1)S(1)}, u32[]{:S(2)}, u32[]{:S(2)}) collective-permute-start(bf16[4,96,768]{2,1,0:T(8,128)(2,1)S(1)} %get-tuple-element.85), channel_id=1, source_target_pairs={{2,0},{3,1},{0,2},{1,3},{6,4},{7,5},{4,6},{5,7},{10,8},{11,9},{8,1... | collective-permute-start | bytes 1769480 | tf_op jit(solution)/shard_map/ppermute | solution.py:41
  72.9 18.1 %collective-permute-start.14 = (bf16[4,96,768]{2,1,0:T(8,128)(2,1)S(1)}, bf16[4,96,768]{2,1,0:T(8,128)(2,1)S(1)}, u32[]{:S(2)}, u32[]{:S(2)}) collective-permute-start(bf16[4,96,768]{2,1,0:T(8,128)(2,1)S(1)} %get-tuple-element.87), channel_id=1, source_target_pairs={{4,0},{5,1},{6,2},{7,3},{0,4},{1,5},{2,6},{3,7},{12,8},{13,9},{14,... | collective-permute-start | bytes 1769480 | tf_op jit(solution)/shard_map/ppermute | solution.py:41
  91.0 9.5 %collective-permute-start.15 = (bf16[192,512]{1,0:T(8,128)(2,1)S(1)}, bf16[192,512]{1,0:T(8,128)(2,1)S(1)}, u32[]{:S(2)}, u32[]{:S(2)}) collective-permute-start(bf16[192,512]{1,0:T(8,128)(2,1)S(1)} %get-tuple-element.158), channel_id=1, source_target_pairs={{1,0},{0,1},{3,2},{2,3},{5,4},{4,5},{7,6},{6,7},{9,8},{8,9},{11,10... | collective-permute-start | bytes 589832 | tf_op jit(solution)/shard_map/ppermute | solution.py:41
  91.1 9.8 %collective-permute-start.16 = (bf16[192,512]{1,0:T(8,128)(2,1)S(1)}, bf16[192,512]{1,0:T(8,128)(2,1)S(1)}, u32[]{:S(2)}, u32[]{:S(2)}) collective-permute-start(bf16[192,512]{1,0:T(8,128)(2,1)S(1)} %get-tuple-element.160), channel_id=1, source_target_pairs={{2,0},{3,1},{0,2},{1,3},{6,4},{7,5},{4,6},{5,7},{10,8},{11,9},{8,1... | collective-permute-start | bytes 589832 | tf_op jit(solution)/shard_map/ppermute | solution.py:41
  92.3 12.1 %collective-permute-start.17 = (bf16[192,512]{1,0:T(8,128)(2,1)S(1)}, bf16[192,512]{1,0:T(8,128)(2,1)S(1)}, u32[]{:S(2)}, u32[]{:S(2)}) collective-permute-start(bf16[192,512]{1,0:T(8,128)(2,1)S(1)} %get-tuple-element.159), channel_id=1, source_target_pairs={{3,0},{2,1},{1,2},{0,3},{7,4},{6,5},{5,6},{4,7},{11,8},{10,9},{9,1... | collective-permute-start | bytes 589832 | tf_op jit(solution)/shard_map/ppermute | solution.py:41
  93.1 11.4 %copy-start.4 = (bf16[8,96,768]{2,1,0:T(8,128)(2,1)}, bf16[8,96,768]{2,1,0:T(8,128)(2,1)S(1)}, u32[]{:S(2)}) copy-start(bf16[8,96,768]{2,1,0:T(8,128)(2,1)S(1)} %constant_dynamic-update-slice_fusion.2.refs_2_.refs_0_) | copy-start | bytes 3538948
  93.1 37.0 %collective-permute-start.19 = (bf16[8,96,768]{2,1,0:T(8,128)(2,1)S(1)}, bf16[8,96,768]{2,1,0:T(8,128)(2,1)}, u32[]{:S(2)}, u32[]{:S(2)}) collective-permute-start(bf16[8,96,768]{2,1,0:T(8,128)(2,1)S(1)} %constant_dynamic-update-slice_fusion.2.refs_2_.refs_0_), channel_id=1, source_target_pairs={{2,0},{3,1},{0,2},{1,3},{6,4},{7,5},{4,6},{5,7},{10,8},{11,9},{8,1... | collective-permute-start | bytes 3538952 | tf_op jit(solution)/shard_map/ppermute | solution.py:41
  96.0 34.1 %collective-permute-start.18 = (bf16[8,96,768]{2,1,0:T(8,128)(2,1)}, bf16[8,96,768]{2,1,0:T(8,128)(2,1)}, u32[]{:S(2)}, u32[]{:S(2)}) collective-permute-start(bf16[8,96,768]{2,1,0:T(8,128)(2,1)} %constant_dynamic-update-slice_fusion.refs_0_), channel_id=1, source_target_pairs={{4,0},{5,1},{6,2},{7,3},{0,4},{1,5},{2,6},{3,7},{12,8},{13,9},{14,... | collective-permute-start | bytes 3538952 | tf_op jit(solution)/shard_map/ppermute | solution.py:41
  100.5 11.5 %collective-permute-start.21 = (bf16[512,768]{1,0:T(8,128)(2,1)}, bf16[512,768]{1,0:T(8,128)(2,1)}, u32[]{:S(2)}, u32[]{:S(2)}) collective-permute-start(bf16[512,768]{1,0:T(8,128)(2,1)} %refs_6_.1), channel_id=1, source_target_pairs={{1,0},{0,1},{3,2},{2,3},{5,4},{4,5},{7,6},{6,7},{9,8},{8,9},{11,10... | collective-permute-start | bytes 2359304 | tf_op jit(solution)/shard_map/ppermute | solution.py:41
  111.5 2.6 collective-permute-start.20
  144.3 9.2 %collective-permute-start.22 = (bf16[512,768]{1,0:T(8,128)(2,1)S(1)}, bf16[512,768]{1,0:T(8,128)(2,1)S(1)}, u32[]{:S(2)}, u32[]{:S(2)}) collective-permute-start(bf16[512,768]{1,0:T(8,128)(2,1)S(1)} %get-tuple-element.95), channel_id=1, source_target_pairs={{1,0},{0,1},{3,2},{2,3},{5,4},{4,5},{7,6},{6,7},{9,8},{8,9},{11,10... | collective-permute-start | bytes 2359304 | tf_op jit(solution)/shard_map/ppermute | solution.py:41
  144.4 9.1 %copy-start.17 = (f32[512,768]{1,0:T(8,128)S(1)}, f32[512,768]{1,0:T(8,128)}, u32[]{:S(2)}) copy-start(f32[512,768]{1,0:T(8,128)} %get-tuple-element.94) | copy-start | bytes 4718596
  151.1 42.4 %collective-permute-start.27 = (bf16[4,2,48,1536]{3,2,1,0:T(8,128)(2,1)}, bf16[4,2,48,1536]{3,2,1,0:T(8,128)(2,1)}, u32[]{:S(2)}, u32[]{:S(2)}) collective-permute-start(bf16[4,2,48,1536]{3,2,1,0:T(8,128)(2,1)} %dynamic-slice_bitcast_fusion), channel_id=1, source_target_pairs={{4,0},{5,1},{6,2},{7,3},{0,4},{1,5},{2,6},{3,7},{12,8},{13,9},{14,... | collective-permute-start | bytes 3538952 | tf_op jit(solution)/shard_map/ppermute | solution.py:41
  160.0 11.2 %collective-permute-start.26 = (bf16[768,384]{0,1:T(8,128)(2,1)S(1)}, bf16[768,384]{0,1:T(8,128)(2,1)S(1)}, u32[]{:S(2)}, u32[]{:S(2)}) collective-permute-start(bf16[768,384]{0,1:T(8,128)(2,1)S(1)} %dynamic-slice_bitcast_fusion.3), channel_id=1, source_target_pairs={{1,0},{0,1},{3,2},{2,3},{5,4},{4,5},{7,6},{6,7},{9,8},{8,9},{11,10... | collective-permute-start | bytes 1769480 | tf_op jit(solution)/shard_map/ppermute | solution.py:41
  160.3 8.6 %collective-permute-start.23 = (bf16[192,512]{1,0:T(8,128)(2,1)S(1)}, bf16[192,512]{1,0:T(8,128)(2,1)S(1)}, u32[]{:S(2)}, u32[]{:S(2)}) collective-permute-start(bf16[192,512]{1,0:T(8,128)(2,1)S(1)} %get-tuple-element.157), channel_id=1, source_target_pairs={{1,0},{0,1},{3,2},{2,3},{5,4},{4,5},{7,6},{6,7},{9,8},{8,9},{11,10... | collective-permute-start | bytes 589832 | tf_op jit(solution)/shard_map/ppermute | solution.py:41
  160.6 8.3 %collective-permute-start.24 = (bf16[192,512]{1,0:T(8,128)(2,1)S(1)}, bf16[192,512]{1,0:T(8,128)(2,1)S(1)}, u32[]{:S(2)}, u32[]{:S(2)}) collective-permute-start(bf16[192,512]{1,0:T(8,128)(2,1)S(1)} %get-tuple-element.156), channel_id=1, source_target_pairs={{2,0},{3,1},{0,2},{1,3},{6,4},{7,5},{4,6},{5,7},{10,8},{11,9},{8,1... | collective-permute-start | bytes 589832 | tf_op jit(solution)/shard_map/ppermute | solution.py:41
  161.8 9.3 %collective-permute-start.25 = (bf16[192,512]{1,0:T(8,128)(2,1)S(1)}, bf16[192,512]{1,0:T(8,128)(2,1)S(1)}, u32[]{:S(2)}, u32[]{:S(2)}) collective-permute-start(bf16[192,512]{1,0:T(8,128)(2,1)S(1)} %get-tuple-element.155), channel_id=1, source_target_pairs={{3,0},{2,1},{1,2},{0,3},{7,4},{6,5},{5,6},{4,7},{11,8},{10,9},{9,1... | collective-permute-start | bytes 589832 | tf_op jit(solution)/shard_map/ppermute | solution.py:41
  172.3 21.1 %collective-permute-start.28 = (bf16[768,192]{1,0:T(8,128)(2,1)}, bf16[768,192]{1,0:T(8,128)(2,1)}, u32[]{:S(2)}, u32[]{:S(2)}) collective-permute-start(bf16[768,192]{1,0:T(8,128)(2,1)} %bitcast.233), channel_id=1, source_target_pairs={{2,0},{3,1},{0,2},{1,3},{6,4},{7,5},{4,6},{5,7},{10,8},{11,9},{8,1... | collective-permute-start | bytes 884744 | tf_op jit(solution)/shard_map/ppermute | solution.py:41
  173.7 36.2 %collective-permute-start.29 = (bf16[4,2,96,768]{3,2,0,1:T(8,128)(2,1)}, bf16[4,2,96,768]{3,2,0,1:T(8,128)(2,1)}, u32[]{:S(2)}, u32[]{:S(2)}) collective-permute-start(bf16[4,2,96,768]{3,2,0,1:T(8,128)(2,1)} %bitcast.220), channel_id=1, source_target_pairs={{2,0},{3,1},{0,2},{1,3},{6,4},{7,5},{4,6},{5,7},{10,8},{11,9},{8,1... | collective-permute-start | bytes 3538952 | tf_op jit(solution)/shard_map/ppermute | solution.py:41
  176.0 17.5 %copy-start.24 = (bf16[768,1536]{1,0:T(8,128)(2,1)S(1)}, bf16[768,1536]{1,0:T(8,128)(2,1)}, u32[]{:S(2)}) copy-start(bf16[768,1536]{1,0:T(8,128)(2,1)} %copy-done.23) | copy-start | bytes 7077892
  193.5 10.8 %copy-start.3 = (bf16[2048,384]{1,0:T(8,128)(2,1)}, bf16[2048,384]{1,0:T(8,128)(2,1)S(1)}, u32[]{:S(2)}) copy-start(bf16[2048,384]{1,0:T(8,128)(2,1)S(1)} %shard_map.165.right_ref.refs_0_) | copy-start | bytes 4718596
  193.5 10.7 %copy-start.2 = (bf16[768,2048]{1,0:T(8,128)(2,1)S(1)}, bf16[768,2048]{1,0:T(8,128)(2,1)}, u32[]{:S(2)}) copy-start(bf16[768,2048]{1,0:T(8,128)(2,1)} %copy-done.1) | copy-start | bytes 9437188
  195.7 10.6 %copy-start.21 = (bf16[4,2,48,1536]{3,2,1,0:T(8,128)(2,1)}, bf16[4,2,48,1536]{3,2,1,0:T(8,128)(2,1)S(1)}, u32[]{:S(2)}) copy-start(bf16[4,2,48,1536]{3,2,1,0:T(8,128)(2,1)S(1)} %fusion.1) | copy-start | bytes 3538948
  195.7 24.4 %collective-permute-start.31 = (bf16[2,2,48,1536]{3,2,1,0:T(8,128)(2,1)S(1)}, bf16[2,2,48,1536]{3,2,1,0:T(8,128)(2,1)}, u32[]{:S(2)}, u32[]{:S(2)}) collective-permute-start(bf16[2,2,48,1536]{3,2,1,0:T(8,128)(2,1)S(1)} %dynamic-slice_bitcast_fusion.2), channel_id=1, source_target_pairs={{8,0},{9,1},{10,2},{11,3},{12,4},{13,5},{14,6},{15,7},{0,8},{1,9},... | collective-permute-start | bytes 1769480 | tf_op jit(solution)/shard_map/ppermute | solution.py:41
  204.2 5.7 %copy-start.7 = (bf16[576,2048]{1,0:T(8,128)(2,1)S(1)}, bf16[576,2048]{1,0:T(8,128)(2,1)}, u32[]{:S(2)}) copy-start(bf16[576,2048]{1,0:T(8,128)(2,1)} %copy-done.6) | copy-start | bytes 7077892
  206.3 11.3 %copy-start.11 = (bf16[4,96,576]{2,1,0:T(8,128)(2,1)}, bf16[4,96,576]{2,1,0:T(8,128)(2,1)S(1)}, u32[]{:S(2)}) copy-start(bf16[4,96,576]{2,1,0:T(8,128)(2,1)S(1)} %get-tuple-element.105) | copy-start | bytes 1327108
  206.3 13.1 %collective-permute-start.30 = (bf16[4,96,576]{2,1,0:T(8,128)(2,1)S(1)}, bf16[4,96,576]{2,1,0:T(8,128)(2,1)S(1)}, u32[]{:S(2)}, u32[]{:S(2)}) collective-permute-start(bf16[4,96,576]{2,1,0:T(8,128)(2,1)S(1)} %get-tuple-element.108), channel_id=1, source_target_pairs={{4,0},{5,1},{6,2},{7,3},{0,4},{1,5},{2,6},{3,7},{12,8},{13,9},{14,... | collective-permute-start | bytes 1327112 | tf_op jit(solution)/shard_map/ppermute | solution.py:41
  227.1 14.0 %collective-permute-start.33 = (bf16[2,512,768]{2,1,0:T(8,128)(2,1)}, bf16[2,512,768]{2,1,0:T(8,128)(2,1)}, u32[]{:S(2)}, u32[]{:S(2)}) collective-permute-start(bf16[2,512,768]{2,1,0:T(8,128)(2,1)} %get-tuple-element.114), channel_id=1, source_target_pairs={{1,0},{0,1},{3,2},{2,3},{5,4},{4,5},{7,6},{6,7},{9,8},{8,9},{11,10... | collective-permute-start | bytes 4718600 | tf_op jit(solution)/shard_map/ppermute | solution.py:41
  227.5 13.6 %collective-permute-start.32 = (bf16[4,96,192]{2,1,0:T(8,128)(2,1)}, bf16[4,96,192]{2,1,0:T(8,128)(2,1)S(1)}, u32[]{:S(2)}, u32[]{:S(2)}) collective-permute-start(bf16[4,96,192]{2,1,0:T(8,128)(2,1)} %copy-done.13), channel_id=1, source_target_pairs={{4,0},{5,1},{6,2},{7,3},{0,4},{1,5},{2,6},{3,7},{12,8},{13,9},{14,... | collective-permute-start | bytes 442376 | tf_op jit(solution)/shard_map/ppermute | solution.py:41
  233.9 7.2 %copy-start.12 = (bf16[4,96,576]{2,1,0:T(8,128)(2,1)S(1)}, bf16[4,96,576]{2,1,0:T(8,128)(2,1)}, u32[]{:S(2)}) copy-start(bf16[4,96,576]{2,1,0:T(8,128)(2,1)} %copy-done.11) | copy-start | bytes 1327108
  233.9 7.2 %copy-start.35 = (bf16[4,96,576]{2,1,0:T(8,128)(2,1)S(1)}, bf16[4,96,576]{2,1,0:T(8,128)(2,1)}, u32[]{:S(2)}) copy-start(bf16[4,96,576]{2,1,0:T(8,128)(2,1)} %copy-done.34) | copy-start | bytes 1327108
  234.7 20.2 %collective-permute-start.36 = (bf16[4,96,768]{2,1,0:T(8,128)(2,1)}, bf16[4,96,768]{2,1,0:T(8,128)(2,1)}, u32[]{:S(2)}, u32[]{:S(2)}) collective-permute-start(bf16[4,96,768]{2,1,0:T(8,128)(2,1)} %dynamic-slice_bitcast_fusion.1), channel_id=1, source_target_pairs={{4,0},{5,1},{6,2},{7,3},{0,4},{1,5},{2,6},{3,7},{12,8},{13,9},{14,... | collective-permute-start | bytes 1769480 | tf_op jit(solution)/shard_map/ppermute | solution.py:41
  236.8 18.1 %collective-permute-start.35 = (bf16[1,2,48,1536]{3,2,1,0:T(8,128)(2,1)}, bf16[1,2,48,1536]{3,2,1,0:T(8,128)(2,1)}, u32[]{:S(2)}, u32[]{:S(2)}) collective-permute-start(bf16[1,2,48,1536]{3,2,1,0:T(8,128)(2,1)} %constant_dynamic-slice_fusion.3), channel_id=1, source_target_pairs={{16,0},{17,1},{18,2},{19,3},{20,4},{21,5},{22,6},{23,7},{24,8},{25... | collective-permute-start | bytes 884744 | tf_op jit(solution)/shard_map/ppermute | solution.py:41
  243.9 14.6 %collective-permute-start.34 = (bf16[2,96,768]{2,1,0:T(8,128)(2,1)S(1)}, bf16[2,96,768]{2,1,0:T(8,128)(2,1)S(1)}, u32[]{:S(2)}, u32[]{:S(2)}) collective-permute-start(bf16[2,96,768]{2,1,0:T(8,128)(2,1)S(1)} %dynamic-slice_bitcast_fusion.5), channel_id=1, source_target_pairs={{8,0},{9,1},{10,2},{11,3},{12,4},{13,5},{14,6},{15,7},{0,8},{1,9},... | collective-permute-start | bytes 884744 | tf_op jit(solution)/shard_map/ppermute | solution.py:41
  245.8 12.8 %copy-start.20 = (bf16[4,2,96,768]{3,2,0,1:T(8,128)(2,1)S(1)}, bf16[4,2,96,768]{3,2,0,1:T(8,128)(2,1)}, u32[]{:S(2)}) copy-start(bf16[4,2,96,768]{3,2,0,1:T(8,128)(2,1)} %copy-done.19) | copy-start | bytes 3538948
  245.8 14.0 %copy-start.26 = (bf16[2,2,48,1536]{3,2,1,0:T(8,128)(2,1)S(1)}, bf16[2,2,48,1536]{3,2,1,0:T(8,128)(2,1)}, u32[]{:S(2)}) copy-start(bf16[2,2,48,1536]{3,2,1,0:T(8,128)(2,1)} %copy-done.25) | copy-start | bytes 1769476
  245.9 16.3 %copy-start.27 = (bf16[4,96,768]{2,1,0:T(8,128)(2,1)S(1)}, bf16[4,96,768]{2,1,0:T(8,128)(2,1)}, u32[]{:S(2)}) copy-start(bf16[4,96,768]{2,1,0:T(8,128)(2,1)} %concatenate.53) | copy-start | bytes 1769476
  245.9 24.9 %collective-permute-start.39 = (bf16[512,768]{1,0:T(8,128)(2,1)S(1)}, bf16[512,768]{1,0:T(8,128)(2,1)S(1)}, u32[]{:S(2)}, u32[]{:S(2)}) collective-permute-start(bf16[512,768]{1,0:T(8,128)(2,1)S(1)} %slice_bitcast_fusion), channel_id=1, source_target_pairs={{2,0},{3,1},{0,2},{1,3},{6,4},{7,5},{4,6},{5,7},{10,8},{11,9},{8,1... | collective-permute-start | bytes 2359304 | tf_op jit(solution)/shard_map/ppermute | solution.py:41
  259.8 11.0 %collective-permute-start.41 = (bf16[2,96,768]{2,1,0:T(8,128)(2,1)S(1)}, bf16[2,96,768]{2,1,0:T(8,128)(2,1)S(1)}, u32[]{:S(2)}, u32[]{:S(2)}) collective-permute-start(bf16[2,96,768]{2,1,0:T(8,128)(2,1)S(1)} %dynamic-slice_bitcast_fusion.4), channel_id=1, source_target_pairs={{8,0},{9,1},{10,2},{11,3},{12,4},{13,5},{14,6},{15,7},{0,8},{1,9},... | collective-permute-start | bytes 884744 | tf_op jit(solution)/shard_map/ppermute | solution.py:41
  261.0 8.6 %collective-permute-start.40 = (bf16[48,1536]{1,0:T(8,128)(2,1)S(1)}, bf16[48,1536]{1,0:T(8,128)(2,1)S(1)}, u32[]{:S(2)}, u32[]{:S(2)}) collective-permute-start(bf16[48,1536]{1,0:T(8,128)(2,1)S(1)} %dynamic-slice_bitcast_fusion.11), channel_id=1, source_target_pairs={{2,0},{3,1},{0,2},{1,3},{6,4},{7,5},{4,6},{5,7},{10,8},{11,9},{8,1... | collective-permute-start | bytes 442376 | tf_op jit(solution)/shard_map/ppermute | solution.py:41
  262.3 8.5 %collective-permute-start.38 = (bf16[1,96,768]{2,1,0:T(8,128)(2,1)S(1)}, bf16[1,96,768]{2,1,0:T(8,128)(2,1)S(1)}, u32[]{:S(2)}, u32[]{:S(2)}) collective-permute-start(bf16[1,96,768]{2,1,0:T(8,128)(2,1)S(1)} %constant_dynamic-slice_fusion.1), channel_id=1, source_target_pairs={{16,0},{17,1},{18,2},{19,3},{20,4},{21,5},{22,6},{23,7},{24,8},{25... | collective-permute-start | bytes 442376 | tf_op jit(solution)/shard_map/ppermute | solution.py:41
  268.6 7.8 %copy-start.28 = (f32[1024,768]{1,0:T(8,128)}, f32[1024,768]{1,0:T(8,128)S(1)}, u32[]{:S(2)}) copy-start(f32[1024,768]{1,0:T(8,128)S(1)} %fusion.55) | copy-start | bytes 9437188
  269.6 14.3 %collective-permute-start.37 = (bf16[512,768]{1,0:T(8,128)(2,1)}, bf16[512,768]{1,0:T(8,128)(2,1)S(1)}, u32[]{:S(2)}, u32[]{:S(2)}) collective-permute-start(bf16[512,768]{1,0:T(8,128)(2,1)} %slice.259), channel_id=1, source_target_pairs={{1,0},{0,1},{3,2},{2,3},{5,4},{4,5},{7,6},{6,7},{9,8},{8,9},{11,10... | collective-permute-start | bytes 2359304 | tf_op jit(solution)/shard_map/ppermute | solution.py:41
  270.9 9.9 %collective-permute-start.45 = (bf16[1,96,768]{2,1,0:T(8,128)(2,1)S(1)}, bf16[1,96,768]{2,1,0:T(8,128)(2,1)S(1)}, u32[]{:S(2)}, u32[]{:S(2)}) collective-permute-start(bf16[1,96,768]{2,1,0:T(8,128)(2,1)S(1)} %constant_dynamic-slice_fusion), channel_id=1, source_target_pairs={{16,0},{17,1},{18,2},{19,3},{20,4},{21,5},{22,6},{23,7},{24,8},{25... | collective-permute-start | bytes 442376 | tf_op jit(solution)/shard_map/ppermute | solution.py:41
  272.8 3.6 %collective-permute-start.43 = (f32[24,1536]{1,0:T(8,128)S(1)}, f32[24,1536]{1,0:T(8,128)S(1)}, u32[]{:S(2)}, u32[]{:S(2)}) collective-permute-start(f32[24,1536]{1,0:T(8,128)S(1)} %dynamic-slice_bitcast_fusion.9), channel_id=1, source_target_pairs={{1,0},{0,1},{3,2},{2,3},{5,4},{4,5},{7,6},{6,7},{9,8},{8,9},{11,10... | collective-permute-start | bytes 442376 | tf_op jit(solution)/shard_map/ppermute | solution.py:41
  273.2 6.1 %collective-permute-start.42 = (f32[2,24,768]{2,1,0:T(8,128)S(1)}, f32[2,24,768]{2,1,0:T(8,128)S(1)}, u32[]{:S(2)}, u32[]{:S(2)}) collective-permute-start(f32[2,24,768]{2,1,0:T(8,128)S(1)} %dynamic-slice_bitcast_fusion.10), channel_id=1, source_target_pairs={{2,0},{3,1},{0,2},{1,3},{6,4},{7,5},{4,6},{5,7},{10,8},{11,9},{8,1... | collective-permute-start | bytes 442376 | tf_op jit(solution)/shard_map/ppermute | solution.py:41
  280.5 1.5 collective-permute-start.44
  (30 other events, 76.7 us)
Sparse Core Ops, SparseCore 0:
  40.4 67.1 all-gather.1

commit v5 on v4

--- a/solution.py
+++ b/solution.py
@@ -522,18 +522,30 @@
         for i in range(ref.shape[0]):
             at = pl.multiple_of(down_at[len(later)] * strip, strip)
             later.append(pltpu.make_async_copy(ref.at[i], down_ref.at[pl.ds(at, strip), :], down_sem.at[len(later)]))
-    for copy in copies + later:
+    waiting = [copies[f::folds] for f in range(folds)]
+    for copy in waiting[0] + later + [copy for fold in waiting[1:] for copy in fold]:
         copy.start()
-    for copy in copies + later:
-        copy.wait()
+
+    def arrive(group):
+        while group:
+            group.pop().wait()
+
     half = h2_refs[0].shape[0]
     hidden = up_ref.shape[1]
     width = 256
     root = (2.0 / math.pi) ** 0.5
 
+    def before(item):
+        i, at = item
+        arrive(waiting[at // model])
+        return jnp.dot(h2_refs[i][...], up_ref[:, at : at + width], preferred_element_type=f32)
+
+    ahead = {(0, at): before((0, at)) for at in range(0, model, width)}
+    arrive(later)
+
     def first(item):
         i, at = item
-        pre = jnp.dot(h2_refs[i][...], up_ref[:, at : at + width], preferred_element_type=f32)
+        pre = ahead.pop(item) if item in ahead else before(item)
         back = lax.dot_general(cot_refs[i][...], down_ref[at : at + width, :], (((1,), (1,)), ((), ())), preferred_element_type=f32)
         return pre, back
 

time: 298 us -> 298 us (level)
  starting transfers between devices: 54.4 us -> 38.2 us
  Pallas kernels: 73.4 us -> 87.2 us
    ppermute x46, starting transfers between devices: 54.3 us -> 38.2 us  [fetch(): return lax.ppermute(value, ('pb', 'ka'), pairs)]
    pallas_call x2, Pallas kernels: 25.1 us -> 34.4 us  [backward_attention(): pl.pallas_call(functools.partial(backward_kernel, sets, which, 256, 256,...]
    pallas_call x1, Pallas kernels: 15.1 us -> 19.1 us  [forward_attention(): pl.pallas_call(functools.partial(forward_kernel, sets, 256, 512, SEQ_UNIT...]
    ppermute x46, waiting for transfers between devices: 77.2 us -> 80.6 us  [fetch(): return lax.ppermute(value, ('pb', 'ka'), pairs)]
  transfers between devices with their start and end apart: 47 -> 47, of which waited for: 18 -> 17; matrix products, arithmetic and copies ran while one was open for 21% -> 21% of each run, Pallas kernels for 18% -> 23%
where the time goes in v5:
time: 298 us; the launch traced here: 295 us
  Pallas kernels  87.2 us (29%)
  waiting for transfers between devices  80.9 us (27%)
  starting transfers between devices  38.2 us (13%)
  other arithmetic  31 us (10%)
  local copies, waits for them, and re-layouts  24.8 us (8%)
  matrix products  16.5 us (6%)
  between operations  16.1 us (5%)
    ppermute x46, waiting for transfers between devices, fetch(): return lax.ppermute(value, ('pb', 'ka'), pairs)  80.6 us
    ppermute x46, starting transfers between devices, fetch(): return lax.ppermute(value, ('pb', 'ka'), pairs)  38.2 us
    pallas_call x2, Pallas kernels, backward_attention(): pl.pallas_call(functools.partial(backward_kernel, sets, which, 256, 256,...  34.4 us
    pallas_call x1, Pallas kernels, forward_attention(): pl.pallas_call(functools.partial(forward_kernel, sets, 256, 512, SEQ_UNIT...  19.1 us
    dot_general x6, matrix products, mm(): lax.dot_general(a, b, ((dims[:1], dims[1:]), ((), ())), preferred_element...  16.5 us
    pallas_call x1, Pallas kernels, hidden_layer(): pl.pallas_call(functools.partial(hidden_kernel, (len(up_stacks), len(down...  14.6 us
    convert_element_type x12, other arithmetic, added(): return total if last else total.astype(own.dtype)  11.3 us
    unnamed x98, local copies, waits for them, and re-layouts  8.11 us
  transfers between devices with their start and end apart: 47, of which 17 were waited for; matrix products, arithmetic and copies ran while one was open for 21% of the time, Pallas kernels for 23%

profile of v5, /device:TPU:0, one launch (start us, length us, event | category | flops | bytes accessed | tf_op | source)
XLA Modules:
  0.0 294.6 jit_solution(728096694524999547)
XLA Ops:
  7.4 1.1 reshape_reshape.3
  10.0 2.6 collective-permute-start.1
  13.3 1.2 collective-permute-done.1
  14.5 1.4 collective-permute-done.2
  17.5 3.8 %collective-permute-start.5 = (bf16[1,96,640]{2,1,0:T(8,128)(2,1)S(1)}, bf16[1,96,640]{2,1,0:T(8,128)(2,1)S(1)}, u32[]{:S(2)}, u32[]{:S(2)}) collective-permute-start(bf16[1,96,640]{2,1,0:T(8,128)(2,1)S(1)} %bitcast.229), channel_id=1, source_target_pairs={{8,0},{9,1},{10,2},{11,3},{12,4},{13,5},{14,6},{15,7},{16,8},{17,9... | collective-permute-start | bytes 368648 | tf_op jit(solution)/shard_map/ppermute | solution.py:41
  22.3 13.3 %collective-permute-done.3.refs_2_ = bf16[512,768]{1,0:T(8,128)(2,1)S(1)} collective-permute-done((bf16[512,768]{1,0:T(8,128)(2,1)S(1)}, bf16[512,768]{1,0:T(8,128)(2,1)S(1)}, u32[]{:S(2)}, u32[]{:S(2)}) %collective-permute-start.3) | collective-permute-done | bytes 786464 | tf_op jit(solution)/shard_map/ppermute | solution.py:41
  35.6 1.3 pad_maximum_fusion
  37.1 1.2 sort.17
  38.6 1.6 collective-permute-start.9
  40.7 3.6 %collective-permute-start.10 = (bf16[192,768]{1,0:T(8,128)(2,1)}, bf16[192,768]{1,0:T(8,128)(2,1)S(1)}, u32[]{:S(2)}, u32[]{:S(2)}) collective-permute-start(bf16[192,768]{1,0:T(8,128)(2,1)} %fusion.30), channel_id=1, source_target_pairs={{8,0},{9,1},{10,2},{11,3},{12,4},{13,5},{14,6},{15,7},{16,8},{17,9... | collective-permute-start | bytes 884744 | tf_op jit(solution)/shard_map/ppermute | solution.py:41
  44.3 1.2 collective-permute-start.12
  45.5 1.5 slice_bitcast_fusion.2
  47.0 5.5 %collective-permute-done.9.refs_1_ = bf16[4,96,640]{2,1,0:T(8,128)(2,1)S(1)} collective-permute-done((bf16[4,96,640]{2,1,0:T(8,128)(2,1)S(1)}, bf16[4,96,640]{2,1,0:T(8,128)(2,1)S(1)}, u32[]{:S(2)}, u32[]{:S(2)}) %collective-permute-start.9) | collective-permute-done | bytes 491552 | tf_op jit(solution)/shard_map/ppermute | solution.py:41
  52.5 1.9 shard_map.161.refs_4_.refs_2_
  54.4 5.4 %shard_map.162 = (bf16[768,2048]{1,0:T(8,128)(2,1)S(1)}, bf16[576,2048]{1,0:T(8,128)(2,1)S(1)}) custom-call(bf16[512,768]{1,0:T(8,128)(2,1)S(1)} %copy-done, bf16[512,768]{1,0:T(8,128)(2,1)S(1)} %get-tuple-element.147.refs_1_, bf16[512,768]{1,0:T(8,128)(2,1)S(1)} %collective-permute-done.3.refs_2_, bf16[512,768]{1,0:T(8,128)(2,1)S(1)} %get-tuple-element.146.refs_3_, ...), custom_call_target="tpu_custom_call" | custom-call | flops 1000000 | bytes 100000 | tf_op jit(solution)/shard_map/pallas_call | solution.py:429
  60.1 10.6 %collective-permute-done.11 = bf16[192,768]{1,0:T(8,128)(2,1)S(1)} collective-permute-done((bf16[192,768]{1,0:T(8,128)(2,1)}, bf16[192,768]{1,0:T(8,128)(2,1)S(1)}, u32[]{:S(2)}, u32[]{:S(2)}) %collective-permute-start.11) | collective-permute-done | bytes 294944 | tf_op jit(solution)/shard_map/ppermute | solution.py:41
  70.7 1.1 pad_maximum_fusion.1
  72.9 1.5 collective-permute-start.14
  74.4 19.1 %shard_map.163 = (bf16[4,192,512]{2,1,0:T(8,128)(2,1)S(1)}, f32[192,2048]{1,0:T(8,128)S(1)}, f32[8,2048]{1,0:T(8,128)S(1)}) custom-call(s32[17]{0:T(128)S(1)} %pad_add_fusion.meta_ref, bf16[576,2048]{1,0:T(8,128)(2,1)S(1)} %get-tuple-element.82.qkv_ref), custom_call_target="tpu_custom_call" | custom-call | flops 20999999488 | bytes 1000000 | tf_op jit(solution)/shard_map/pallas_call | solution.py:275
  93.5 1.4 copy-done.6
  95.1 1.2 collective-permute-start.16
  97.1 1.2 collective-permute-start.19
  100.0 2.8 collective-permute-done.16
  102.9 3.3 %collective-permute-done.17 = bf16[192,512]{1,0:T(8,128)(2,1)S(1)} collective-permute-done((bf16[192,512]{1,0:T(8,128)(2,1)S(1)}, bf16[192,512]{1,0:T(8,128)(2,1)S(1)}, u32[]{:S(2)}, u32[]{:S(2)}) %collective-permute-start.17) | collective-permute-done | bytes 196640 | tf_op jit(solution)/shard_map/ppermute | solution.py:41
  107.4 2.4 fusion.54
  110.2 1.2 multiply_convert_fusion.refs_4_
  112.5 2.0 collective-permute-done.20.refs_5_
  114.5 17.5 %collective-permute-done.19.refs_3_.refs_1_ = bf16[8,96,768]{2,1,0:T(8,128)(2,1)} collective-permute-done((bf16[8,96,768]{2,1,0:T(8,128)(2,1)S(1)}, bf16[8,96,768]{2,1,0:T(8,128)(2,1)}, u32[]{:S(2)}, u32[]{:S(2)}) %collective-permute-start.19) | collective-permute-done | bytes 1179680 | tf_op jit(solution)/shard_map/ppermute | solution.py:41
  132.0 14.6 %shard_map.164 = (bf16[1024,1536]{1,0:T(8,128)(2,1)}, bf16[1024,1536]{1,0:T(8,128)(2,1)}, f32[512,768]{1,0:T(8,128)}, bf16[512,768]{1,0:T(8,128)(2,1)S(1)}) custom-call(s32[16]{0:T(128)S(1)} %stack.191.up_at, s32[16]{0:T(128)S(1)} %stack.192.down_at, bf16[8,96,768]{2,1,0:T(8,128)(2,1)} %constant_dynamic-update-slice_fusion.refs_0_, ...), custom_call_target="tpu_custom_call" | custom-call | flops 14000000000 | bytes 1000000 | tf_op jit(solution)/shard_map/pallas_call | solution.py:575
  146.7 5.5 %convolution_convert_fusion = bf16[768,1536]{1,0:T(8,128)(2,1)S(1)} fusion(bf16[1024,1536]{1,0:T(8,128)(2,1)} %get-tuple-element.101, bf16[512,768]{1,0:T(8,128)(2,1)} %collective-permute-done.20.refs_5_, bf16[512,768]{1,0:T(8,128)(2,1)} %multiply_convert_fusion.refs_4_), kind=kOutput, calls=%fused_computation | convolution fusion | flops 2420244480 | bytes 7077888 | tf_op jit(solution)/shard_map/dot_general | solution.py:608
  152.3 1.1 dynamic-slice_bitcast_fusion
  153.4 1.4 copy-done.15
  155.5 3.1 %fusion.46 = (bf16[512,768]{1,0:T(8,128)(2,1)S(1)}, f32[512,768]{1,0:T(8,128)}) fusion(f32[512]{0:T(512)S(1)} %get-tuple-element.205, f32[512]{0:T(512)S(1)} %add_rsqrt_fusion.1, f32[512,768]{1,0:T(8,128)S(1)} %copy-done.15, f32[512]{0:T(512)S(1)} %broadcast_multiply_fusion.5, f32[512]{0:T(512)S(1)} %get-tuple-element.206, f32[768]{0:T(1024)S(1)} %get-tuple-element.139, ...), kind=kLoop, calls=%fused_computation.195 | loop fusion | flops 4718592 | bytes 7089152 | tf_op jit(solution)/shard_map/convert_element_type | solution.py:743
  163.8 4.3 %convolution_convert_fusion.1 = bf16[1536,768]{1,0:T(8,128)(2,1)S(1)} fusion(bf16[1024,1536]{1,0:T(8,128)(2,1)S(1)} %copy-done.45, bf16[512,768]{1,0:T(8,128)(2,1)} %collective-permute-done.21.refs_7_, bf16[512,768]{1,0:T(8,128)(2,1)} %refs_6_.1), kind=kOutput, calls=%fused_computation.1 | convolution fusion | flops 2420244480 | bytes 7077888 | tf_op jit(solution)/shard_map/dot_general | solution.py:608
  168.2 1.2 constant_dynamic-slice_fusion.2
  169.4 1.2 copy.54
  170.6 2.5 collective-permute-done.25
  176.6 1.4 copy-done.9
  178.0 22.3 %shard_map.165.right_ref.refs_0_ = bf16[2048,384]{1,0:T(8,128)(2,1)S(1)} custom-call(s32[17]{0:T(128)S(1)} %pad_add_fusion.meta_ref, bf16[576,2048]{1,0:T(8,128)(2,1)} %copy-done.6, bf16[4,192,512]{2,1,0:T(8,128)(2,1)S(1)} %pad_maximum_fusion.3.up_ref, f32[192,2048]{1,0:T(8,128)S(1)} %copy-done.9, f32[8,2048]{1,0:T(8,128)S(1)} %get-tuple-element.100.lse_ref), custom_call_target="tpu_custom_call" | custom-call | flops 25999998976 | bytes 100000 | tf_op jit(solution)/shard_map/pallas_call | solution.py:378
  200.3 2.2 fusion.1
  202.7 1.4 fusion.25.refs_0_
  204.1 2.0 shard_map.166
  206.1 1.2 collective-permute-start.30
  207.5 4.1 %collective-permute-done.29 = bf16[4,2,96,768]{3,2,0,1:T(8,128)(2,1)} collective-permute-done((bf16[4,2,96,768]{3,2,0,1:T(8,128)(2,1)}, bf16[4,2,96,768]{3,2,0,1:T(8,128)(2,1)}, u32[]{:S(2)}, u32[]{:S(2)}) %collective-permute-start.29) | collective-permute-done | bytes 1179680 | tf_op jit(solution)/shard_map/ppermute | solution.py:41
  211.6 12.0 %shard_map.167.right_ref.refs_1_ = bf16[2048,192]{1,0:T(8,128)(2,1)S(1)} custom-call(s32[17]{0:T(128)S(1)} %pad_add_fusion.meta_ref, bf16[576,2048]{1,0:T(8,128)(2,1)S(1)} %copy-done.7, bf16[4,192,512]{2,1,0:T(8,128)(2,1)S(1)} %pad_maximum_fusion.3.up_ref, f32[192,2048]{1,0:T(8,128)S(1)} %copy-done.10, f32[8,2048]{1,0:T(8,128)S(1)} %get-tuple-element.100.lse_ref), custom_call_target="tpu_custom_call" | custom-call | flops 1000000 | bytes 100000 | tf_op jit(solution)/shard_map/pallas_call | solution.py:378
  226.2 5.2 %shard_map.169 = (bf16[2,512,768]{2,1,0:T(8,128)(2,1)S(1)}, bf16[2,512,768]{2,1,0:T(8,128)(2,1)}) custom-call(bf16[2048,384]{1,0:T(8,128)(2,1)} %copy-done.3, bf16[2048,192]{1,0:T(8,128)(2,1)S(1)} %shard_map.167.right_ref.refs_1_, bf16[768,640]{1,0:T(8,128)(2,1)S(1)} %shard_map.161.refs_4_.refs_2_), custom_call_target="tpu_custom_call" | custom-call | flops 1000000 | bytes 100000 | tf_op jit(solution)/shard_map/pallas_call | solution.py:495
  231.8 2.0 fusion
  234.7 2.0 collective-permute-start.36
  236.8 1.2 fusion.23
  238.8 2.7 collective-permute-start.35
  241.9 1.4 concatenate.53
  244.4 1.8 add_convert_fusion
  246.3 1.2 collective-permute-start.39
  247.5 7.0 %collective-permute-done.35 = bf16[1,2,48,1536]{3,2,1,0:T(8,128)(2,1)} collective-permute-done((bf16[1,2,48,1536]{3,2,1,0:T(8,128)(2,1)}, bf16[1,2,48,1536]{3,2,1,0:T(8,128)(2,1)}, u32[]{:S(2)}, u32[]{:S(2)}) %collective-permute-start.35) | collective-permute-done | bytes 294944 | tf_op jit(solution)/shard_map/ppermute | solution.py:41
  254.5 4.7 %collective-permute-done.34 = bf16[2,96,768]{2,1,0:T(8,128)(2,1)S(1)} collective-permute-done((bf16[2,96,768]{2,1,0:T(8,128)(2,1)S(1)}, bf16[2,96,768]{2,1,0:T(8,128)(2,1)S(1)}, u32[]{:S(2)}, u32[]{:S(2)}) %collective-permute-start.34) | collective-permute-done | bytes 294944 | tf_op jit(solution)/shard_map/ppermute | solution.py:41
  259.2 1.2 fusion.22
  261.7 1.2 collective-permute-start.40
  263.1 3.6 %shard_map.170 = bf16[1536,768]{1,0:T(8,128)(2,1)S(1)} custom-call(s32[16]{0:T(128)S(1)} %broadcast_multiply_fusion.6.offs_ref, bf16[8,96,768]{2,1,0:T(8,128)(2,1)S(1)} %copy-done.5, bf16[8,96,768]{2,1,0:T(8,128)(2,1)} %collective-permute-done.19.refs_3_.refs_1_), custom_call_target="tpu_custom_call" | custom-call | flops 1000000 | bytes 100000 | tf_op jit(solution)/shard_map/pallas_call | solution.py:107
  266.7 2.6 fusion.55
  270.4 1.4 collective-permute-done.38
  271.9 1.6 collective-permute-start.45
  275.5 1.6 fusion.10
  277.1 2.9 collective-permute-done.42
  284.7 2.5 fusion.13
  (263 shorter events, 37.3 us)
Async XLA Ops:
  7.2 5.4 %copy-start.32 = (bf16[24,3072]{1,0:T(8,128)(2,1)S(1)}, bf16[24,3072]{1,0:T(8,128)(2,1)}, u32[]{:S(2)}) copy-start(bf16[24,3072]{1,0:T(8,128)(2,1)} %param.15) | copy-start | bytes 442372
  7.2 100.2 %all-gather.2.cloned.1.call-start = ((), (), s32[]{:S(2)}) async-start(), calls=%async_computation | async-start | bytes 1216512 | tf_op jit(solution)/shard_map/all_gather | solution.py:682
  8.6 7.3 %copy-start = (bf16[512,768]{1,0:T(8,128)(2,1)S(1)}, bf16[512,768]{1,0:T(8,128)(2,1)}, u32[]{:S(2)}) copy-start(bf16[512,768]{1,0:T(8,128)(2,1)} %refs_0_.1) | copy-start | bytes 2359300
  9.1 7.7 %copy-start.37 = (bf16[96,768]{1,0:T(8,128)(2,1)S(1)}, bf16[96,768]{1,0:T(8,128)(2,1)}, u32[]{:S(2)}) copy-start(bf16[96,768]{1,0:T(8,128)(2,1)} %param.16) | copy-start | bytes 442372
  9.5 3.8 %collective-permute-start = (bf16[24,640]{1,0:T(8,128)(2,1)S(1)}, bf16[24,640]{1,0:T(8,128)(2,1)S(1)}, u32[]{:S(2)}, u32[]{:S(2)}) collective-permute-start(bf16[24,640]{1,0:T(8,128)(2,1)S(1)} %get-tuple-element.186), channel_id=1, source_target_pairs={{1,0},{0,1},{3,2},{2,3},{5,4},{4,5},{7,6},{6,7},{9,8},{8,9},{11,10... | collective-permute-start | bytes 92168 | tf_op jit(solution)/shard_map/ppermute | solution.py:41
  10.0 4.5 %collective-permute-start.1 = (bf16[24,640]{1,0:T(8,128)(2,1)S(1)}, bf16[24,640]{1,0:T(8,128)(2,1)S(1)}, u32[]{:S(2)}, u32[]{:S(2)}) collective-permute-start(bf16[24,640]{1,0:T(8,128)(2,1)S(1)} %get-tuple-element.185), channel_id=1, source_target_pairs={{2,0},{3,1},{0,2},{1,3},{6,4},{7,5},{4,6},{5,7},{10,8},{11,9},{8,1... | collective-permute-start | bytes 92168 | tf_op jit(solution)/shard_map/ppermute | solution.py:41
  12.6 3.3 %collective-permute-start.2 = (bf16[24,640]{1,0:T(8,128)(2,1)S(1)}, bf16[24,640]{1,0:T(8,128)(2,1)S(1)}, u32[]{:S(2)}, u32[]{:S(2)}) collective-permute-start(bf16[24,640]{1,0:T(8,128)(2,1)S(1)} %get-tuple-element.184), channel_id=1, source_target_pairs={{3,0},{2,1},{1,2},{0,3},{7,4},{6,5},{5,6},{4,7},{11,8},{10,9},{9,1... | collective-permute-start | bytes 92168 | tf_op jit(solution)/shard_map/ppermute | solution.py:41
  13.1 3.6 %collective-permute-start.4 = (bf16[24,1536]{1,0:T(8,128)(2,1)S(1)}, bf16[24,1536]{1,0:T(8,128)(2,1)S(1)}, u32[]{:S(2)}, u32[]{:S(2)}) collective-permute-start(bf16[24,1536]{1,0:T(8,128)(2,1)S(1)} %dynamic-slice_bitcast_fusion.12), channel_id=1, source_target_pairs={{1,0},{0,1},{3,2},{2,3},{5,4},{4,5},{7,6},{6,7},{9,8},{8,9},{11,10... | collective-permute-start | bytes 221192 | tf_op jit(solution)/shard_map/ppermute | solution.py:41
  15.9 19.7 %collective-permute-start.3 = (bf16[512,768]{1,0:T(8,128)(2,1)S(1)}, bf16[512,768]{1,0:T(8,128)(2,1)S(1)}, u32[]{:S(2)}, u32[]{:S(2)}) collective-permute-start(bf16[512,768]{1,0:T(8,128)(2,1)S(1)} %copy-done), channel_id=1, source_target_pairs={{2,0},{3,1},{0,2},{1,3},{6,4},{7,5},{4,6},{5,7},{10,8},{11,9},{8,1... | collective-permute-start | bytes 2359304 | tf_op jit(solution)/shard_map/ppermute | solution.py:41
  17.5 19.3 %collective-permute-start.5 = (bf16[1,96,640]{2,1,0:T(8,128)(2,1)S(1)}, bf16[1,96,640]{2,1,0:T(8,128)(2,1)S(1)}, u32[]{:S(2)}, u32[]{:S(2)}) collective-permute-start(bf16[1,96,640]{2,1,0:T(8,128)(2,1)S(1)} %bitcast.229), channel_id=1, source_target_pairs={{8,0},{9,1},{10,2},{11,3},{12,4},{13,5},{14,6},{15,7},{16,8},{17,9... | collective-permute-start | bytes 368648 | tf_op jit(solution)/shard_map/ppermute | solution.py:41
  21.3 15.6 %collective-permute-start.6 = (bf16[1,96,640]{2,1,0:T(8,128)(2,1)S(1)}, bf16[1,96,640]{2,1,0:T(8,128)(2,1)S(1)}, u32[]{:S(2)}, u32[]{:S(2)}) collective-permute-start(bf16[1,96,640]{2,1,0:T(8,128)(2,1)S(1)} %bitcast.230), channel_id=1, source_target_pairs={{16,0},{17,1},{18,2},{19,3},{20,4},{21,5},{22,6},{23,7},{24,8},{25... | collective-permute-start | bytes 368648 | tf_op jit(solution)/shard_map/ppermute | solution.py:41
  21.3 15.6 %collective-permute-start.7 = (bf16[1,96,640]{2,1,0:T(8,128)(2,1)S(1)}, bf16[1,96,640]{2,1,0:T(8,128)(2,1)S(1)}, u32[]{:S(2)}, u32[]{:S(2)}) collective-permute-start(bf16[1,96,640]{2,1,0:T(8,128)(2,1)S(1)} %bitcast.231), channel_id=1, source_target_pairs={{24,0},{25,1},{26,2},{27,3},{28,4},{29,5},{30,6},{31,7},{0,8},{1,9... | collective-permute-start | bytes 368648 | tf_op jit(solution)/shard_map/ppermute | solution.py:41
  36.9 3.8 %collective-permute-start.8 = (bf16[2,512,768]{2,1,0:T(8,128)(2,1)}, bf16[2,512,768]{2,1,0:T(8,128)(2,1)}, u32[]{:S(2)}, u32[]{:S(2)}) collective-permute-start(bf16[2,512,768]{2,1,0:T(8,128)(2,1)} %pad_maximum_fusion), channel_id=1, source_target_pairs={{1,0},{0,1},{3,2},{2,3},{5,4},{4,5},{7,6},{6,7},{9,8},{8,9},{11,10... | collective-permute-start | bytes 4718600 | tf_op jit(solution)/shard_map/ppermute | solution.py:41
  38.6 13.8 %collective-permute-start.9 = (bf16[4,96,640]{2,1,0:T(8,128)(2,1)S(1)}, bf16[4,96,640]{2,1,0:T(8,128)(2,1)S(1)}, u32[]{:S(2)}, u32[]{:S(2)}) collective-permute-start(bf16[4,96,640]{2,1,0:T(8,128)(2,1)S(1)} %pad_maximum_fusion.4.refs_0_), channel_id=1, source_target_pairs={{4,0},{5,1},{6,2},{7,3},{0,4},{1,5},{2,6},{3,7},{12,8},{13,9},{14,... | collective-permute-start | bytes 1474568 | tf_op jit(solution)/shard_map/ppermute | solution.py:41
  40.7 19.4 %collective-permute-start.10 = (bf16[192,768]{1,0:T(8,128)(2,1)}, bf16[192,768]{1,0:T(8,128)(2,1)S(1)}, u32[]{:S(2)}, u32[]{:S(2)}) collective-permute-start(bf16[192,768]{1,0:T(8,128)(2,1)} %fusion.30), channel_id=1, source_target_pairs={{8,0},{9,1},{10,2},{11,3},{12,4},{13,5},{14,6},{15,7},{16,8},{17,9... | collective-permute-start | bytes 884744 | tf_op jit(solution)/shard_map/ppermute | solution.py:41
  44.3 26.5 %collective-permute-start.11 = (bf16[192,768]{1,0:T(8,128)(2,1)}, bf16[192,768]{1,0:T(8,128)(2,1)S(1)}, u32[]{:S(2)}, u32[]{:S(2)}) collective-permute-start(bf16[192,768]{1,0:T(8,128)(2,1)} %fusion.30), channel_id=1, source_target_pairs={{16,0},{17,1},{18,2},{19,3},{20,4},{21,5},{22,6},{23,7},{24,8},{25... | collective-permute-start | bytes 884744 | tf_op jit(solution)/shard_map/ppermute | solution.py:41
  44.3 26.5 %collective-permute-start.12 = (bf16[192,768]{1,0:T(8,128)(2,1)}, bf16[192,768]{1,0:T(8,128)(2,1)S(1)}, u32[]{:S(2)}, u32[]{:S(2)}) collective-permute-start(bf16[192,768]{1,0:T(8,128)(2,1)} %fusion.30), channel_id=1, source_target_pairs={{24,0},{25,1},{26,2},{27,3},{28,4},{29,5},{30,6},{31,7},{0,8},{1,9... | collective-permute-start | bytes 884744 | tf_op jit(solution)/shard_map/ppermute | solution.py:41
  59.8 12.2 %copy-start.1 = (bf16[768,2048]{1,0:T(8,128)(2,1)}, bf16[768,2048]{1,0:T(8,128)(2,1)S(1)}, u32[]{:S(2)}) copy-start(bf16[768,2048]{1,0:T(8,128)(2,1)S(1)} %get-tuple-element.93.left_ref) | copy-start | bytes 9437188
  71.9 23.0 %collective-permute-start.13 = (bf16[4,96,768]{2,1,0:T(8,128)(2,1)S(1)}, bf16[4,96,768]{2,1,0:T(8,128)(2,1)S(1)}, u32[]{:S(2)}, u32[]{:S(2)}) collective-permute-start(bf16[4,96,768]{2,1,0:T(8,128)(2,1)S(1)} %get-tuple-element.85), channel_id=1, source_target_pairs={{2,0},{3,1},{0,2},{1,3},{6,4},{7,5},{4,6},{5,7},{10,8},{11,9},{8,1... | collective-permute-start | bytes 1769480 | tf_op jit(solution)/shard_map/ppermute | solution.py:41
  72.9 22.1 %collective-permute-start.14 = (bf16[4,96,768]{2,1,0:T(8,128)(2,1)S(1)}, bf16[4,96,768]{2,1,0:T(8,128)(2,1)S(1)}, u32[]{:S(2)}, u32[]{:S(2)}) collective-permute-start(bf16[4,96,768]{2,1,0:T(8,128)(2,1)S(1)} %get-tuple-element.87), channel_id=1, source_target_pairs={{4,0},{5,1},{6,2},{7,3},{0,4},{1,5},{2,6},{3,7},{12,8},{13,9},{14,... | collective-permute-start | bytes 1769480 | tf_op jit(solution)/shard_map/ppermute | solution.py:41
  95.0 5.0 %collective-permute-start.15 = (bf16[192,512]{1,0:T(8,128)(2,1)S(1)}, bf16[192,512]{1,0:T(8,128)(2,1)S(1)}, u32[]{:S(2)}, u32[]{:S(2)}) collective-permute-start(bf16[192,512]{1,0:T(8,128)(2,1)S(1)} %get-tuple-element.158), channel_id=1, source_target_pairs={{1,0},{0,1},{3,2},{2,3},{5,4},{4,5},{7,6},{6,7},{9,8},{8,9},{11,10... | collective-permute-start | bytes 589832 | tf_op jit(solution)/shard_map/ppermute | solution.py:41
  95.1 7.8 %collective-permute-start.16 = (bf16[192,512]{1,0:T(8,128)(2,1)S(1)}, bf16[192,512]{1,0:T(8,128)(2,1)S(1)}, u32[]{:S(2)}, u32[]{:S(2)}) collective-permute-start(bf16[192,512]{1,0:T(8,128)(2,1)S(1)} %get-tuple-element.160), channel_id=1, source_target_pairs={{2,0},{3,1},{0,2},{1,3},{6,4},{7,5},{4,6},{5,7},{10,8},{11,9},{8,1... | collective-permute-start | bytes 589832 | tf_op jit(solution)/shard_map/ppermute | solution.py:41
  96.3 9.9 %collective-permute-start.17 = (bf16[192,512]{1,0:T(8,128)(2,1)S(1)}, bf16[192,512]{1,0:T(8,128)(2,1)S(1)}, u32[]{:S(2)}, u32[]{:S(2)}) collective-permute-start(bf16[192,512]{1,0:T(8,128)(2,1)S(1)} %get-tuple-element.159), channel_id=1, source_target_pairs={{3,0},{2,1},{1,2},{0,3},{7,4},{6,5},{5,6},{4,7},{11,8},{10,9},{9,1... | collective-permute-start | bytes 589832 | tf_op jit(solution)/shard_map/ppermute | solution.py:41
  97.1 9.2 %copy-start.4 = (bf16[8,96,768]{2,1,0:T(8,128)(2,1)}, bf16[8,96,768]{2,1,0:T(8,128)(2,1)S(1)}, u32[]{:S(2)}) copy-start(bf16[8,96,768]{2,1,0:T(8,128)(2,1)S(1)} %constant_dynamic-update-slice_fusion.2.refs_2_.refs_0_) | copy-start | bytes 3538948
  97.1 34.9 %collective-permute-start.19 = (bf16[8,96,768]{2,1,0:T(8,128)(2,1)S(1)}, bf16[8,96,768]{2,1,0:T(8,128)(2,1)}, u32[]{:S(2)}, u32[]{:S(2)}) collective-permute-start(bf16[8,96,768]{2,1,0:T(8,128)(2,1)S(1)} %constant_dynamic-update-slice_fusion.2.refs_2_.refs_0_), channel_id=1, source_target_pairs={{2,0},{3,1},{0,2},{1,3},{6,4},{7,5},{4,6},{5,7},{10,8},{11,9},{8,1... | collective-permute-start | bytes 3538952 | tf_op jit(solution)/shard_map/ppermute | solution.py:41
  100.0 32.1 %collective-permute-start.18 = (bf16[8,96,768]{2,1,0:T(8,128)(2,1)}, bf16[8,96,768]{2,1,0:T(8,128)(2,1)}, u32[]{:S(2)}, u32[]{:S(2)}) collective-permute-start(bf16[8,96,768]{2,1,0:T(8,128)(2,1)} %constant_dynamic-update-slice_fusion.refs_0_), channel_id=1, source_target_pairs={{4,0},{5,1},{6,2},{7,3},{0,4},{1,5},{2,6},{3,7},{12,8},{13,9},{14,... | collective-permute-start | bytes 3538952 | tf_op jit(solution)/shard_map/ppermute | solution.py:41
  100.0 12.5 %collective-permute-start.21 = (bf16[512,768]{1,0:T(8,128)(2,1)}, bf16[512,768]{1,0:T(8,128)(2,1)}, u32[]{:S(2)}, u32[]{:S(2)}) collective-permute-start(bf16[512,768]{1,0:T(8,128)(2,1)} %refs_6_.1), channel_id=1, source_target_pairs={{1,0},{0,1},{3,2},{2,3},{5,4},{4,5},{7,6},{6,7},{9,8},{8,9},{11,10... | collective-permute-start | bytes 2359304 | tf_op jit(solution)/shard_map/ppermute | solution.py:41
  111.3 3.2 %collective-permute-start.20 = (bf16[512,768]{1,0:T(8,128)(2,1)}, bf16[512,768]{1,0:T(8,128)(2,1)}, u32[]{:S(2)}, u32[]{:S(2)}) collective-permute-start(bf16[512,768]{1,0:T(8,128)(2,1)} %multiply_convert_fusion.refs_4_), channel_id=1, source_target_pairs={{1,0},{0,1},{3,2},{2,3},{5,4},{4,5},{7,6},{6,7},{9,8},{8,9},{11,10... | collective-permute-start | bytes 2359304 | tf_op jit(solution)/shard_map/ppermute | solution.py:41
  146.6 6.8 %collective-permute-start.22 = (bf16[512,768]{1,0:T(8,128)(2,1)S(1)}, bf16[512,768]{1,0:T(8,128)(2,1)S(1)}, u32[]{:S(2)}, u32[]{:S(2)}) collective-permute-start(bf16[512,768]{1,0:T(8,128)(2,1)S(1)} %get-tuple-element.95), channel_id=1, source_target_pairs={{1,0},{0,1},{3,2},{2,3},{5,4},{4,5},{7,6},{6,7},{9,8},{8,9},{11,10... | collective-permute-start | bytes 2359304 | tf_op jit(solution)/shard_map/ppermute | solution.py:41
  146.7 6.7 %copy-start.17 = (f32[512,768]{1,0:T(8,128)S(1)}, f32[512,768]{1,0:T(8,128)}, u32[]{:S(2)}) copy-start(f32[512,768]{1,0:T(8,128)} %get-tuple-element.94) | copy-start | bytes 4718596
  153.4 46.9 %collective-permute-start.27 = (bf16[4,2,48,1536]{3,2,1,0:T(8,128)(2,1)}, bf16[4,2,48,1536]{3,2,1,0:T(8,128)(2,1)}, u32[]{:S(2)}, u32[]{:S(2)}) collective-permute-start(bf16[4,2,48,1536]{3,2,1,0:T(8,128)(2,1)} %dynamic-slice_bitcast_fusion), channel_id=1, source_target_pairs={{4,0},{5,1},{6,2},{7,3},{0,4},{1,5},{2,6},{3,7},{12,8},{13,9},{14,... | collective-permute-start | bytes 3538952 | tf_op jit(solution)/shard_map/ppermute | solution.py:41
  161.4 11.7 %collective-permute-start.26 = (bf16[768,384]{0,1:T(8,128)(2,1)S(1)}, bf16[768,384]{0,1:T(8,128)(2,1)S(1)}, u32[]{:S(2)}, u32[]{:S(2)}) collective-permute-start(bf16[768,384]{0,1:T(8,128)(2,1)S(1)} %dynamic-slice_bitcast_fusion.3), channel_id=1, source_target_pairs={{1,0},{0,1},{3,2},{2,3},{5,4},{4,5},{7,6},{6,7},{9,8},{8,9},{11,10... | collective-permute-start | bytes 1769480 | tf_op jit(solution)/shard_map/ppermute | solution.py:41
  162.0 8.6 %collective-permute-start.23 = (bf16[192,512]{1,0:T(8,128)(2,1)S(1)}, bf16[192,512]{1,0:T(8,128)(2,1)S(1)}, u32[]{:S(2)}, u32[]{:S(2)}) collective-permute-start(bf16[192,512]{1,0:T(8,128)(2,1)S(1)} %get-tuple-element.157), channel_id=1, source_target_pairs={{1,0},{0,1},{3,2},{2,3},{5,4},{4,5},{7,6},{6,7},{9,8},{8,9},{11,10... | collective-permute-start | bytes 589832 | tf_op jit(solution)/shard_map/ppermute | solution.py:41
  162.0 8.5 %collective-permute-start.24 = (bf16[192,512]{1,0:T(8,128)(2,1)S(1)}, bf16[192,512]{1,0:T(8,128)(2,1)S(1)}, u32[]{:S(2)}, u32[]{:S(2)}) collective-permute-start(bf16[192,512]{1,0:T(8,128)(2,1)S(1)} %get-tuple-element.156), channel_id=1, source_target_pairs={{2,0},{3,1},{0,2},{1,3},{6,4},{7,5},{4,6},{5,7},{10,8},{11,9},{8,1... | collective-permute-start | bytes 589832 | tf_op jit(solution)/shard_map/ppermute | solution.py:41
  163.2 9.9 %collective-permute-start.25 = (bf16[192,512]{1,0:T(8,128)(2,1)S(1)}, bf16[192,512]{1,0:T(8,128)(2,1)S(1)}, u32[]{:S(2)}, u32[]{:S(2)}) collective-permute-start(bf16[192,512]{1,0:T(8,128)(2,1)S(1)} %get-tuple-element.155), channel_id=1, source_target_pairs={{3,0},{2,1},{1,2},{0,3},{7,4},{6,5},{5,6},{4,7},{11,8},{10,9},{9,1... | collective-permute-start | bytes 589832 | tf_op jit(solution)/shard_map/ppermute | solution.py:41
  174.3 26.0 %collective-permute-start.28 = (bf16[768,192]{1,0:T(8,128)(2,1)}, bf16[768,192]{1,0:T(8,128)(2,1)}, u32[]{:S(2)}, u32[]{:S(2)}) collective-permute-start(bf16[768,192]{1,0:T(8,128)(2,1)} %bitcast.233), channel_id=1, source_target_pairs={{2,0},{3,1},{0,2},{1,3},{6,4},{7,5},{4,6},{5,7},{10,8},{11,9},{8,1... | collective-permute-start | bytes 884744 | tf_op jit(solution)/shard_map/ppermute | solution.py:41
  175.6 36.0 %collective-permute-start.29 = (bf16[4,2,96,768]{3,2,0,1:T(8,128)(2,1)}, bf16[4,2,96,768]{3,2,0,1:T(8,128)(2,1)}, u32[]{:S(2)}, u32[]{:S(2)}) collective-permute-start(bf16[4,2,96,768]{3,2,0,1:T(8,128)(2,1)} %bitcast.220), channel_id=1, source_target_pairs={{2,0},{3,1},{0,2},{1,3},{6,4},{7,5},{4,6},{5,7},{10,8},{11,9},{8,1... | collective-permute-start | bytes 3538952 | tf_op jit(solution)/shard_map/ppermute | solution.py:41
  178.0 22.4 %copy-start.24 = (bf16[768,1536]{1,0:T(8,128)(2,1)S(1)}, bf16[768,1536]{1,0:T(8,128)(2,1)}, u32[]{:S(2)}) copy-start(bf16[768,1536]{1,0:T(8,128)(2,1)} %copy-done.23) | copy-start | bytes 7077892
  202.6 21.9 %collective-permute-start.31 = (bf16[2,2,48,1536]{3,2,1,0:T(8,128)(2,1)S(1)}, bf16[2,2,48,1536]{3,2,1,0:T(8,128)(2,1)}, u32[]{:S(2)}, u32[]{:S(2)}) collective-permute-start(bf16[2,2,48,1536]{3,2,1,0:T(8,128)(2,1)S(1)} %dynamic-slice_bitcast_fusion.2), channel_id=1, source_target_pairs={{8,0},{9,1},{10,2},{11,3},{12,4},{13,5},{14,6},{15,7},{0,8},{1,9},... | collective-permute-start | bytes 1769480 | tf_op jit(solution)/shard_map/ppermute | solution.py:41
  204.1 7.5 %copy-start.7 = (bf16[576,2048]{1,0:T(8,128)(2,1)S(1)}, bf16[576,2048]{1,0:T(8,128)(2,1)}, u32[]{:S(2)}) copy-start(bf16[576,2048]{1,0:T(8,128)(2,1)} %copy-done.6) | copy-start | bytes 7077892
  204.1 7.5 %copy-start.10 = (f32[192,2048]{1,0:T(8,128)S(1)}, f32[192,2048]{1,0:T(8,128)}, u32[]{:S(2)}) copy-start(f32[192,2048]{1,0:T(8,128)} %copy-done.8) | copy-start | bytes 4718596
  206.1 17.5 %copy-start.11 = (bf16[4,96,576]{2,1,0:T(8,128)(2,1)}, bf16[4,96,576]{2,1,0:T(8,128)(2,1)S(1)}, u32[]{:S(2)}) copy-start(bf16[4,96,576]{2,1,0:T(8,128)(2,1)S(1)} %get-tuple-element.105) | copy-start | bytes 1327108
  206.1 17.5 %collective-permute-start.30 = (bf16[4,96,576]{2,1,0:T(8,128)(2,1)S(1)}, bf16[4,96,576]{2,1,0:T(8,128)(2,1)S(1)}, u32[]{:S(2)}, u32[]{:S(2)}) collective-permute-start(bf16[4,96,576]{2,1,0:T(8,128)(2,1)S(1)} %get-tuple-element.108), channel_id=1, source_target_pairs={{4,0},{5,1},{6,2},{7,3},{0,4},{1,5},{2,6},{3,7},{12,8},{13,9},{14,... | collective-permute-start | bytes 1327112 | tf_op jit(solution)/shard_map/ppermute | solution.py:41
  231.4 10.1 %collective-permute-start.33 = (bf16[2,512,768]{2,1,0:T(8,128)(2,1)}, bf16[2,512,768]{2,1,0:T(8,128)(2,1)}, u32[]{:S(2)}, u32[]{:S(2)}) collective-permute-start(bf16[2,512,768]{2,1,0:T(8,128)(2,1)} %get-tuple-element.114), channel_id=1, source_target_pairs={{1,0},{0,1},{3,2},{2,3},{5,4},{4,5},{7,6},{6,7},{9,8},{8,9},{11,10... | collective-permute-start | bytes 4718600 | tf_op jit(solution)/shard_map/ppermute | solution.py:41
  231.8 9.8 %collective-permute-start.32 = (bf16[4,96,192]{2,1,0:T(8,128)(2,1)}, bf16[4,96,192]{2,1,0:T(8,128)(2,1)S(1)}, u32[]{:S(2)}, u32[]{:S(2)}) collective-permute-start(bf16[4,96,192]{2,1,0:T(8,128)(2,1)} %copy-done.13), channel_id=1, source_target_pairs={{4,0},{5,1},{6,2},{7,3},{0,4},{1,5},{2,6},{3,7},{12,8},{13,9},{14,... | collective-permute-start | bytes 442376 | tf_op jit(solution)/shard_map/ppermute | solution.py:41
  233.9 4.9 %copy-start.19 = (bf16[4,2,96,768]{3,2,0,1:T(8,128)(2,1)}, bf16[4,2,96,768]{3,2,0,1:T(8,128)(2,1)S(1)}, u32[]{:S(2)}) copy-start(bf16[4,2,96,768]{3,2,0,1:T(8,128)(2,1)S(1)} %fusion) | copy-start | bytes 3538948
  233.9 7.7 %copy-start.12 = (bf16[4,96,576]{2,1,0:T(8,128)(2,1)S(1)}, bf16[4,96,576]{2,1,0:T(8,128)(2,1)}, u32[]{:S(2)}) copy-start(bf16[4,96,576]{2,1,0:T(8,128)(2,1)} %copy-done.11) | copy-start | bytes 1327108
  233.9 7.7 %copy-start.35 = (bf16[4,96,576]{2,1,0:T(8,128)(2,1)S(1)}, bf16[4,96,576]{2,1,0:T(8,128)(2,1)}, u32[]{:S(2)}) copy-start(bf16[4,96,576]{2,1,0:T(8,128)(2,1)} %copy-done.34) | copy-start | bytes 1327108
  234.7 19.7 %collective-permute-start.36 = (bf16[4,96,768]{2,1,0:T(8,128)(2,1)}, bf16[4,96,768]{2,1,0:T(8,128)(2,1)}, u32[]{:S(2)}, u32[]{:S(2)}) collective-permute-start(bf16[4,96,768]{2,1,0:T(8,128)(2,1)} %dynamic-slice_bitcast_fusion.1), channel_id=1, source_target_pairs={{4,0},{5,1},{6,2},{7,3},{0,4},{1,5},{2,6},{3,7},{12,8},{13,9},{14,... | collective-permute-start | bytes 1769480 | tf_op jit(solution)/shard_map/ppermute | solution.py:41
  238.8 15.7 %collective-permute-start.35 = (bf16[1,2,48,1536]{3,2,1,0:T(8,128)(2,1)}, bf16[1,2,48,1536]{3,2,1,0:T(8,128)(2,1)}, u32[]{:S(2)}, u32[]{:S(2)}) collective-permute-start(bf16[1,2,48,1536]{3,2,1,0:T(8,128)(2,1)} %constant_dynamic-slice_fusion.3), channel_id=1, source_target_pairs={{16,0},{17,1},{18,2},{19,3},{20,4},{21,5},{22,6},{23,7},{24,8},{25... | collective-permute-start | bytes 884744 | tf_op jit(solution)/shard_map/ppermute | solution.py:41
  244.3 14.9 %collective-permute-start.34 = (bf16[2,96,768]{2,1,0:T(8,128)(2,1)S(1)}, bf16[2,96,768]{2,1,0:T(8,128)(2,1)S(1)}, u32[]{:S(2)}, u32[]{:S(2)}) collective-permute-start(bf16[2,96,768]{2,1,0:T(8,128)(2,1)S(1)} %dynamic-slice_bitcast_fusion.5), channel_id=1, source_target_pairs={{8,0},{9,1},{10,2},{11,3},{12,4},{13,5},{14,6},{15,7},{0,8},{1,9},... | collective-permute-start | bytes 884744 | tf_op jit(solution)/shard_map/ppermute | solution.py:41
  246.2 13.0 %copy-start.20 = (bf16[4,2,96,768]{3,2,0,1:T(8,128)(2,1)S(1)}, bf16[4,2,96,768]{3,2,0,1:T(8,128)(2,1)}, u32[]{:S(2)}) copy-start(bf16[4,2,96,768]{3,2,0,1:T(8,128)(2,1)} %copy-done.19) | copy-start | bytes 3538948
  246.3 14.3 %copy-start.26 = (bf16[2,2,48,1536]{3,2,1,0:T(8,128)(2,1)S(1)}, bf16[2,2,48,1536]{3,2,1,0:T(8,128)(2,1)}, u32[]{:S(2)}) copy-start(bf16[2,2,48,1536]{3,2,1,0:T(8,128)(2,1)} %copy-done.25) | copy-start | bytes 1769476
  246.3 16.6 %copy-start.27 = (bf16[4,96,768]{2,1,0:T(8,128)(2,1)S(1)}, bf16[4,96,768]{2,1,0:T(8,128)(2,1)}, u32[]{:S(2)}) copy-start(bf16[4,96,768]{2,1,0:T(8,128)(2,1)} %concatenate.53) | copy-start | bytes 1769476
  246.3 25.4 %collective-permute-start.39 = (bf16[512,768]{1,0:T(8,128)(2,1)S(1)}, bf16[512,768]{1,0:T(8,128)(2,1)S(1)}, u32[]{:S(2)}, u32[]{:S(2)}) collective-permute-start(bf16[512,768]{1,0:T(8,128)(2,1)S(1)} %slice_bitcast_fusion), channel_id=1, source_target_pairs={{2,0},{3,1},{0,2},{1,3},{6,4},{7,5},{4,6},{5,7},{10,8},{11,9},{8,1... | collective-permute-start | bytes 2359304 | tf_op jit(solution)/shard_map/ppermute | solution.py:41
  260.5 11.3 %collective-permute-start.41 = (bf16[2,96,768]{2,1,0:T(8,128)(2,1)S(1)}, bf16[2,96,768]{2,1,0:T(8,128)(2,1)S(1)}, u32[]{:S(2)}, u32[]{:S(2)}) collective-permute-start(bf16[2,96,768]{2,1,0:T(8,128)(2,1)S(1)} %dynamic-slice_bitcast_fusion.4), channel_id=1, source_target_pairs={{8,0},{9,1},{10,2},{11,3},{12,4},{13,5},{14,6},{15,7},{0,8},{1,9},... | collective-permute-start | bytes 884744 | tf_op jit(solution)/shard_map/ppermute | solution.py:41
  261.7 8.7 %collective-permute-start.40 = (bf16[48,1536]{1,0:T(8,128)(2,1)S(1)}, bf16[48,1536]{1,0:T(8,128)(2,1)S(1)}, u32[]{:S(2)}, u32[]{:S(2)}) collective-permute-start(bf16[48,1536]{1,0:T(8,128)(2,1)S(1)} %dynamic-slice_bitcast_fusion.11), channel_id=1, source_target_pairs={{2,0},{3,1},{0,2},{1,3},{6,4},{7,5},{4,6},{5,7},{10,8},{11,9},{8,1... | collective-permute-start | bytes 442376 | tf_op jit(solution)/shard_map/ppermute | solution.py:41
  263.0 8.7 %collective-permute-start.38 = (bf16[1,96,768]{2,1,0:T(8,128)(2,1)S(1)}, bf16[1,96,768]{2,1,0:T(8,128)(2,1)S(1)}, u32[]{:S(2)}, u32[]{:S(2)}) collective-permute-start(bf16[1,96,768]{2,1,0:T(8,128)(2,1)S(1)} %constant_dynamic-slice_fusion.1), channel_id=1, source_target_pairs={{16,0},{17,1},{18,2},{19,3},{20,4},{21,5},{22,6},{23,7},{24,8},{25... | collective-permute-start | bytes 442376 | tf_op jit(solution)/shard_map/ppermute | solution.py:41
  269.3 7.8 %copy-start.28 = (f32[1024,768]{1,0:T(8,128)}, f32[1024,768]{1,0:T(8,128)S(1)}, u32[]{:S(2)}) copy-start(f32[1024,768]{1,0:T(8,128)S(1)} %fusion.55) | copy-start | bytes 9437188
  270.4 14.3 %collective-permute-start.37 = (bf16[512,768]{1,0:T(8,128)(2,1)}, bf16[512,768]{1,0:T(8,128)(2,1)S(1)}, u32[]{:S(2)}, u32[]{:S(2)}) collective-permute-start(bf16[512,768]{1,0:T(8,128)(2,1)} %slice.259), channel_id=1, source_target_pairs={{1,0},{0,1},{3,2},{2,3},{5,4},{4,5},{7,6},{6,7},{9,8},{8,9},{11,10... | collective-permute-start | bytes 2359304 | tf_op jit(solution)/shard_map/ppermute | solution.py:41
  271.9 9.6 %collective-permute-start.45 = (bf16[1,96,768]{2,1,0:T(8,128)(2,1)S(1)}, bf16[1,96,768]{2,1,0:T(8,128)(2,1)S(1)}, u32[]{:S(2)}, u32[]{:S(2)}) collective-permute-start(bf16[1,96,768]{2,1,0:T(8,128)(2,1)S(1)} %constant_dynamic-slice_fusion), channel_id=1, source_target_pairs={{16,0},{17,1},{18,2},{19,3},{20,4},{21,5},{22,6},{23,7},{24,8},{25... | collective-permute-start | bytes 442376 | tf_op jit(solution)/shard_map/ppermute | solution.py:41
  273.5 3.6 %collective-permute-start.43 = (f32[24,1536]{1,0:T(8,128)S(1)}, f32[24,1536]{1,0:T(8,128)S(1)}, u32[]{:S(2)}, u32[]{:S(2)}) collective-permute-start(f32[24,1536]{1,0:T(8,128)S(1)} %dynamic-slice_bitcast_fusion.9), channel_id=1, source_target_pairs={{1,0},{0,1},{3,2},{2,3},{5,4},{4,5},{7,6},{6,7},{9,8},{8,9},{11,10... | collective-permute-start | bytes 442376 | tf_op jit(solution)/shard_map/ppermute | solution.py:41
  273.9 6.1 %collective-permute-start.42 = (f32[2,24,768]{2,1,0:T(8,128)S(1)}, f32[2,24,768]{2,1,0:T(8,128)S(1)}, u32[]{:S(2)}, u32[]{:S(2)}) collective-permute-start(f32[2,24,768]{2,1,0:T(8,128)S(1)} %dynamic-slice_bitcast_fusion.10), channel_id=1, source_target_pairs={{2,0},{3,1},{0,2},{1,3},{6,4},{7,5},{4,6},{5,7},{10,8},{11,9},{8,1... | collective-permute-start | bytes 442376 | tf_op jit(solution)/shard_map/ppermute | solution.py:41
  281.2 1.5 collective-permute-start.44
  (30 other events, 72.6 us)
Sparse Core Ops, SparseCore 0:
  40.4 66.9 all-gather.1
